TPU v7x, 512 devices: a whole 4x8x8 slice. The times are simulated.
512 devices in a mesh: row: 32 (over x, y), col: 16 (over z, core).
Axes of the slice: x: 4, y: 8, z: 8, core: 2. Of those that a mesh axis runs over, the one named last changes fastest.
Arguments:
- vectors: float32 [16384, 16384], P('row', 'col'), may hold values from -6 to 6
- reflectors_first: float32 [256, 16384], P('col', 'row'), may hold values from -0.1875 to 0.1875
- reflectors_second: float32 [256, 16384], P('col', 'row'), may hold values from -0.1875 to 0.1875
- factor_first: float32 [256, 256], replicated, as said below
- factor_second: float32 [256, 256], replicated, as said below
Outputs:
- transformed: float32 [16384, 16384], P('row', 'col')
Inputs may be any that keep to these rules, and one draw needn't show every extreme that they name: `factor_first`: upper triangular: zero below the diagonal, diagonal between 1 and 2. `factor_second`: upper triangular: zero below the diagonal, diagonal between 1 and 2.
All inputs are finite; a program needn't handle non-finite values.
Results may differ from a plain program's by a relative error of at most 0.00014.
Values sent between devices are 32-bit elements; how exact they have to be, the bound alone decides.
No kernel may reach another device: no remote copies, remote signals or barrier semaphores. Data moves between devices by JAX's collectives and lax.ppermute only.
A program may use at most 64 MiB of HBM per device.

v0:
```python
import jax
import jax.numpy as jnp
from jax import lax
from jax.sharding import PartitionSpec as P


def times_left(left, right):
    return jnp.dot(left, right, precision=lax.Precision.HIGHEST, preferred_element_type=jnp.float32)


def spread_back(panel, coeff):
    return lax.dot_general(
        panel,
        coeff,
        (((0,), (0,)), ((), ())),
        precision=lax.Precision.HIGHEST,
        preferred_element_type=jnp.float32,
    )


def fetch_panel(shard):
    return lax.all_gather(shard, "col", axis=0, tiled=True)


def apply_apart(block, panel, factor):
    partial_value = times_left(panel, block)
    proj = lax.psum(partial_value, "row")
    coeff = times_left(factor, proj)
    return block - spread_back(panel, coeff)


def local(vectors, reflectors_first, reflectors_second, factor_first, factor_second):
    whole_second = fetch_panel(reflectors_second)
    middle = apply_apart(vectors, whole_second, factor_second)
    whole_first = fetch_panel(reflectors_first)
    result = apply_apart(middle, whole_first, factor_first)
    return result


def solution(mesh):
    return jax.shard_map(
        local,
        mesh=mesh,
        in_specs=(P("row", "col"), P("col", "row"), P("col", "row"), P(), P()),
        out_specs=P("row", "col"),
        check_vma=False,
    )
```

profile of v0, /device:TPU:1, one launch (start us, length us, event | category | flops | bytes accessed | tf_op | source)
XLA Modules:
  0.0 371.6 jit_solution(13075525277667710809)
XLA Ops:
  6.5 0.0 copy-start
  6.5 0.0 all-reduce.3.cloned.1.call-start
  6.5 26.3 %all_gather.6 = f32[256,512]{1,0:T(8,128)S(1)} all-gather(f32[16,512]{1,0:T(8,128)} %param.7), channel_id=1, replica_groups=mesh['row'=32,'col'=16] {'col'}, dimensions={0}, use_global_device_ids=true | all-gather | bytes 557056 | tf_op jit(solution)/shard_map/all_gather | solution.py:22
  32.8 4.7 %fusion = f32[256,1024]{1,0:T(8,128)} fusion(f32[256,512]{1,0:T(8,128)S(1)} %all_gather.6, f32[512,1024]{1,0:T(8,128)} %param.5), kind=kOutput, calls=%fused_computation.3 | convolution fusion | flops 1610612736 | bytes 3670016 | tf_op jit(solution)/shard_map/dot_general | solution.py:8
  37.5 0.0 all-reduce.3.cloned.1.call-update
  37.5 0.0 copy-start.4
  37.5 0.0 all-reduce.5.cloned.1.call-start
  37.6 0.0 copy-done.1
  37.6 1.8 copy.6
  39.4 0.0 copy-done.4
  39.4 15.9 %all_gather.7 = f32[256,512]{1,0:T(8,128)S(1)} all-gather(f32[16,512]{1,0:T(8,128)S(1)} %copy-done.4), channel_id=1, replica_groups=mesh['row'=32,'col'=16] {'col'}, dimensions={0}, use_global_device_ids=true | all-gather | bytes 557056 | tf_op jit(solution)/shard_map/all_gather | solution.py:22
  55.3 134.9 %all-reduce.3.cloned.1.call-done = f32[256,1024]{1,0:T(8,128)} async-done(((f32[256,1024]{1,0:T(8,128)}), f32[256,1024]{1,0:T(8,128)}) %all-reduce.3.cloned.1.call-update) | async-done | bytes 1048592 | tf_op jit(solution)/shard_map/psum | solution.py:27
  190.2 0.0 copy-done
  190.2 3.2 fusion.1
  193.4 0.0 copy-done.2
  193.4 1.9 bitcast_subtract_fusion.1
  195.3 0.0 copy-start.3
  195.3 2.8 convolution_bitcast_fusion
  198.1 0.0 all-reduce.5.cloned.1.call-update
  198.1 158.3 %all-reduce.5.cloned.1.call-done = f32[256,1024]{0,1:T(8,128)} async-done(((f32[256,1024]{0,1:T(8,128)}), f32[256,1024]{0,1:T(8,128)}) %all-reduce.5.cloned.1.call-update) | async-done | bytes 1048592 | tf_op jit(solution)/shard_map/psum | solution.py:27
  356.4 0.0 copy-done.3
  356.4 2.3 fusion.2
  358.7 3.2 bitcast_subtract_fusion
  361.8 2.9 copy.7
  (2 shorter events, 0.0 us)
Async XLA Ops:
  6.5 183.7 %copy-start = (f32[256,256]{1,0:T(8,128)S(1)}, f32[256,256]{1,0:T(8,128)}, u32[]{:S(2)}) copy-start(f32[256,256]{1,0:T(8,128)} %param.9) | copy-start | bytes 786436
  6.5 183.6 %all-reduce.3.cloned.1.call-start = ((), (), s32[]{:S(2)}) async-start(), calls=%async_computation | async-start | bytes 2097152 | tf_op jit(solution)/shard_map/psum | solution.py:27
  32.8 4.7 %copy-start.1 = (f32[512,1024]{1,0:T(8,128)S(1)}, f32[512,1024]{1,0:T(8,128)}, u32[]{:S(2)}) copy-start(f32[512,1024]{1,0:T(8,128)} %param.5) | copy-start | bytes 6291460
  37.5 1.9 copy-start.4
  37.5 318.9 %all-reduce.5.cloned.1.call-start = ((), (), s32[]{:S(2)}) async-start(), calls=%async_computation.1 | async-start | bytes 2097152 | tf_op jit(solution)/shard_map/psum | solution.py:27
  190.2 3.2 copy-start.2
  195.3 161.1 %copy-start.3 = (f32[256,256]{1,0:T(8,128)S(1)}, f32[256,256]{1,0:T(8,128)}, u32[]{:S(2)}) copy-start(f32[256,256]{1,0:T(8,128)} %param.8) | copy-start | bytes 786436
Sparse Core Ops, SparseCore 0:
  37.6 152.5 all-reduce.2
  198.3 158.0 all-reduce.4
where the time goes:
time: 375 us; the launch traced here: 372 us
  waiting for transfers between devices  293 us (78%)
  blocking collectives  42.2 us (11%)
  matrix products  18 us (5%)
  between operations  13.5 us (4%)
  local copies, waits for them, and re-layouts  4.72 us (1%)
    psum x2, waiting for transfers between devices, apply_apart(): proj = lax.psum(partial_value, 'row')  293 us
    all_gather x2, blocking collectives, fetch_panel(): return lax.all_gather(shard, 'col', axis=0, tiled=True)  42.2 us
    dot_general x4, matrix products, times_left(): jnp.dot(left, right, precision=lax.Precision.HIGHEST, preferred_element_t...  12.9 us
  transfers between devices with their start and end apart: 2, of which 2 were waited for; matrix products, arithmetic and copies ran while one was open for 0% of the time, Pallas kernels for 0%

commit v1 on v0

v1 whole, which is shorter than its diff:
```python
import jax
import jax.numpy as jnp
from jax import lax
from jax.sharding import Mesh, PartitionSpec as P

ROW = ("x", "y")
COL = ("z", "core")
SIZES = {"x": 4, "y": 8, "z": 8, "core": 2}


def dot(left, right, dims):
    return lax.dot_general(
        left, right, (dims, ((), ())), precision=lax.Precision.HIGH, preferred_element_type=jnp.float32
    )


def scatter_sum(value, axis):
    n = SIZES[axis]
    pieces = value.reshape(n, value.shape[0] // n, value.shape[1])
    return jnp.sum(lax.all_to_all(pieces, axis, 0, 0), axis=0)


def spread(value, axis):
    n = SIZES[axis]
    copies = jnp.broadcast_to(value[None], (n,) + value.shape)
    return lax.all_to_all(copies, axis, 0, 0).reshape(n * value.shape[0], value.shape[1])


def sum_over_rows(value):
    share = scatter_sum(scatter_sum(value, "x"), "y")
    return spread(spread(share, "y"), "x")


def fetch_panel(shard):
    return lax.all_gather(shard, COL, axis=0, tiled=True)


def local(vectors, reflectors_first, reflectors_second, factor_first, factor_second):
    second = fetch_panel(reflectors_second)
    proj_second = sum_over_rows(dot(second, vectors, ((1,), (0,))))
    first = fetch_panel(reflectors_first)
    proj_first = sum_over_rows(dot(first, vectors, ((1,), (0,))))
    cross_share = dot(reflectors_first, second, ((1,), (1,)))
    cross_share = jnp.sum(lax.all_gather(cross_share, ROW, axis=0, tiled=False), axis=0)
    cross = fetch_panel(cross_share)
    w_first = dot(factor_first, first, ((0,), (0,)))
    w_second = dot(factor_second, second - dot(cross, w_first, ((0,), (0,))), ((0,), (0,)))
    middle = vectors - dot(w_second, proj_second, ((0,), (0,)))
    return middle - dot(w_first, proj_first, ((0,), (0,)))


def solution(mesh):
    fine = Mesh(mesh.devices.reshape(4, 8, 8, 2), ("x", "y", "z", "core"))
    return jax.shard_map(
        local,
        mesh=fine,
        in_specs=(P(ROW, COL), P(COL, ROW), P(COL, ROW), P(), P()),
        out_specs=P(ROW, COL),
        check_vma=False,
    )
```

time: 375 us -> 244 us (0.65)
  waiting for transfers between devices: 293 us -> 46.2 us
  blocking collectives: 42.2 us -> 134 us
  starting transfers between devices: 0.04 us -> 32.1 us
  between operations: 13.5 us -> 0.1 us
  other arithmetic: 0 us -> 7.07 us
    psum x2 -> x0, waiting for transfers between devices: 293 us -> none  [apply_apart(): proj = lax.psum(partial_value, 'row')]
    all_gather x2 -> x4, blocking collectives: 42.2 us -> 122 us  [the longest x3 78.2 us: fetch_panel(): return lax.all_gather(shard, COL, axis=0, tiled=True)]
    all_to_all x0 -> x7, waiting for transfers between devices: none -> 46.2 us  [the longest x4 29.2 us: scatter_sum(): return jnp.sum(lax.all_to_all(pieces, axis, 0, 0), axis=0)]
    all_to_all x0 -> x7, starting transfers between devices: none -> 32.1 us  [the longest x4 19.6 us: scatter_sum(): return jnp.sum(lax.all_to_all(pieces, axis, 0, 0), axis=0)]
    all_to_all x0 -> x1, blocking collectives: none -> 12.4 us  [spread(): lax.all_to_all(copies, axis, 0, 0)]
    reduce_sum x0 -> x5, other arithmetic: none -> 7.07 us  [the longest x4 5.98 us: scatter_sum(): return jnp.sum(lax.all_to_all(pieces, axis, 0, 0), axis=0)]
    broadcast_in_dim x0 -> x4, local copies, waits for them, and re-layouts: none -> 4.92 us  [spread(): copies = jnp.broadcast_to(value[None], (n,) + value.shape)]
    dot_general x6 -> x8, matrix products: 18 us -> 18.2 us  [dot(): lax.dot_general(left, right, (dims, ((), ())), precision=lax.Precision.HI...]
  transfers between devices with their start and end apart: 2 -> 7, of which waited for: 2 -> 5; matrix products, arithmetic and copies ran while one was open for 0% -> 7% of each run, Pallas kernels for 0% -> 0%
where the time goes in v1:
time: 244 us; the launch traced here: 243 us
  blocking collectives  134 us (55%)
  waiting for transfers between devices  46.2 us (19%)
  starting transfers between devices  32.1 us (13%)
  matrix products  18.2 us (7%)
  other arithmetic  7.07 us (3%)
  local copies, waits for them, and re-layouts  4.93 us (2%)
    all_gather x3, blocking collectives, fetch_panel(): return lax.all_gather(shard, COL, axis=0, tiled=True)  78.2 us
    all_gather x1, blocking collectives, local(): lax.all_gather(cross_share, ROW, axis=0, tiled=False)  43.9 us
    all_to_all x4, waiting for transfers between devices, scatter_sum(): return jnp.sum(lax.all_to_all(pieces, axis, 0, 0), axis=0)  29.2 us
    all_to_all x4, starting transfers between devices, scatter_sum(): return jnp.sum(lax.all_to_all(pieces, axis, 0, 0), axis=0)  19.6 us
    dot_general x8, matrix products, dot(): lax.dot_general(left, right, (dims, ((), ())), precision=lax.Precision.HI...  18.2 us
    all_to_all x3, waiting for transfers between devices, spread(): lax.all_to_all(copies, axis, 0, 0)  17 us
    all_to_all x3, starting transfers between devices, spread(): lax.all_to_all(copies, axis, 0, 0)  12.5 us
    all_to_all x1, blocking collectives, spread(): lax.all_to_all(copies, axis, 0, 0)  12.4 us
  transfers between devices with their start and end apart: 7, of which 5 were waited for; matrix products, arithmetic and copies ran while one was open for 7% of the time, Pallas kernels for 0%

profile of v1, /device:TPU:1, one launch (start us, length us, event | category | flops | bytes accessed | tf_op | source)
XLA Modules:
  0.0 243.0 jit_solution(1313414182677814591)
XLA Ops:
  0.0 26.3 %all_gather.15 = f32[256,512]{1,0:T(8,128)S(1)} all-gather(f32[16,512]{1,0:T(8,128)} %param.7), channel_id=1, replica_groups=mesh['x'=4,'y'=8,'z'=8,'core'=2] {'z','core'}, dimensions={0}, use_global_device_ids=true | all-gather | bytes 557056 | tf_op jit(solution)/shard_map/all_gather | solution.py:35
  26.3 3.6 %fusion.3 = f32[256,1024]{1,0:T(8,128)} fusion(f32[256,512]{1,0:T(8,128)S(1)} %all_gather.15, f32[512,1024]{1,0:T(8,128)} %param.5), kind=kOutput, calls=%fused_computation.5 | convolution fusion | flops 805306368 | bytes 3670016 | tf_op jit(solution)/shard_map/dot_general | solution.py:12
  29.9 4.4 %all-to-all-start = ((f32[4,64,1024]{2,1,0:T(8,128)}), f32[4,64,1024]{2,1,0:T(8,128)}, u32[]{:S(2)}, u32[]{:S(2)}) async-start(f32[4,64,1024]{2,1,0:T(8,128)} %bitcast.26), calls=%async_computation | async-start | bytes 2097152 | tf_op jit(solution)/shard_map/all_to_all | solution.py:20
  34.3 15.9 %all_gather.19 = f32[256,512]{1,0:T(8,128)S(1)} all-gather(f32[16,512]{1,0:T(8,128)S(1)} %copy-done.3), channel_id=1, replica_groups=mesh['x'=4,'y'=8,'z'=8,'core'=2] {'z','core'}, dimensions={0}, use_global_device_ids=true | all-gather | bytes 557056 | tf_op jit(solution)/shard_map/all_gather | solution.py:35
  50.2 2.1 fusion.5
  52.3 4.3 %all-to-all-start.4 = ((f32[4,64,1024]{2,1,0:T(8,128)}), f32[4,64,1024]{2,1,0:T(8,128)}, u32[]{:S(2)}, u32[]{:S(2)}) async-start(f32[4,64,1024]{2,1,0:T(8,128)} %bitcast.25), calls=%async_computation.4 | async-start | bytes 2097152 | tf_op jit(solution)/shard_map/all_to_all | solution.py:20
  58.7 12.9 %all-to-all-done.4 = f32[4,64,1024]{2,1,0:T(8,128)} async-done(((f32[4,64,1024]{2,1,0:T(8,128)}), f32[4,64,1024]{2,1,0:T(8,128)}, u32[]{:S(2)}, u32[]{:S(2)}) %all-to-all-start.4) | async-done | bytes 1048608 | tf_op jit(solution)/shard_map/all_to_all | solution.py:20
  71.6 6.8 %all-to-all-start.1 = ((f32[8,8,1024]{2,1,0:T(8,128)}), f32[8,8,1024]{2,1,0:T(8,128)}, u32[]{:S(2)}, u32[]{:S(2)}) async-start(f32[8,8,1024]{2,1,0:T(8,128)} %bitcast.29), calls=%async_computation.1 | async-start | bytes 524288 | tf_op jit(solution)/shard_map/all_to_all | solution.py:20
  78.4 2.0 reduce_sum.48
  80.4 7.9 %all-to-all-done.1 = f32[8,8,1024]{2,1,0:T(8,128)} async-done(((f32[8,8,1024]{2,1,0:T(8,128)}), f32[8,8,1024]{2,1,0:T(8,128)}, u32[]{:S(2)}, u32[]{:S(2)}) %all-to-all-start.1) | async-done | bytes 262176 | tf_op jit(solution)/shard_map/all_to_all | solution.py:20
  88.3 4.0 %all-to-all-start.5 = ((f32[8,8,1024]{2,1,0:T(8,128)}), f32[8,8,1024]{2,1,0:T(8,128)}, u32[]{:S(2)}, u32[]{:S(2)}) async-start(f32[8,8,1024]{2,1,0:T(8,128)} %bitcast.30), calls=%async_computation.5 | async-start | bytes 524288 | tf_op jit(solution)/shard_map/all_to_all | solution.py:20
  93.4 8.4 %all-to-all-done.5 = f32[8,8,1024]{2,1,0:T(8,128)} async-done(((f32[8,8,1024]{2,1,0:T(8,128)}), f32[8,8,1024]{2,1,0:T(8,128)}, u32[]{:S(2)}, u32[]{:S(2)}) %all-to-all-start.5) | async-done | bytes 262176 | tf_op jit(solution)/shard_map/all_to_all | solution.py:20
  102.5 4.1 %all-to-all-start.2 = ((f32[8,8,1024]{2,1,0:T(8,128)}), f32[8,8,1024]{2,1,0:T(8,128)}, u32[]{:S(2)}, u32[]{:S(2)}) async-start(f32[8,8,1024]{2,1,0:T(8,128)} %broadcast_in_dim.12), calls=%async_computation.2 | async-start | bytes 524288 | tf_op jit(solution)/shard_map/all_to_all | solution.py:26
  107.5 8.4 %all-to-all-done.2 = f32[8,8,1024]{2,1,0:T(8,128)} async-done(((f32[8,8,1024]{2,1,0:T(8,128)}), f32[8,8,1024]{2,1,0:T(8,128)}, u32[]{:S(2)}, u32[]{:S(2)}) %all-to-all-start.2) | async-done | bytes 262176 | tf_op jit(solution)/shard_map/all_to_all | solution.py:26
  115.9 12.4 %all_to_all.40 = f32[8,8,1024]{2,1,0:T(8,128)} all-to-all(f32[8,8,1024]{2,1,0:T(8,128)S(1)} %broadcast_in_dim.29), channel_id=1, replica_groups=mesh['x'=4,'y'=8,'z'=8,'core'=2] {'y'}, dimensions={0} | all-to-all | bytes 524288 | tf_op jit(solution)/shard_map/all_to_all | solution.py:26
  128.3 2.0 broadcast_in_dim.28
  130.3 4.2 %all-to-all-start.3 = ((f32[4,64,1024]{2,1,0:T(8,128)}), f32[4,64,1024]{2,1,0:T(8,128)}, u32[]{:S(2)}, u32[]{:S(2)}) async-start(f32[4,64,1024]{2,1,0:T(8,128)} %broadcast_in_dim.28), calls=%async_computation.3 | async-start | bytes 2097152 | tf_op jit(solution)/shard_map/all_to_all | solution.py:26
  134.9 43.9 %all-gather = f32[512,256]{1,0:T(8,128)} all-gather(f32[16,256]{1,0:T(8,128)S(1)} %fusion), channel_id=2, replica_groups=mesh['x'=4,'y'=8,'z'=8,'core'=2] {'x','y'}, dimensions={0}, use_global_device_ids=true | all-gather | bytes 540672 | tf_op jit(solution)/shard_map/all_gather | solution.py:44
  179.8 36.0 %all_gather.18 = f32[256,256]{1,0:T(8,128)} all-gather(f32[16,256]{1,0:T(8,128)S(1)} %reduce_sum.45), channel_id=1, replica_groups=mesh['x'=4,'y'=8,'z'=8,'core'=2] {'z','core'}, dimensions={0}, use_global_device_ids=true | all-gather | bytes 278528 | tf_op jit(solution)/shard_map/all_gather | solution.py:35
  217.0 2.1 broadcast_in_dim.31
  219.2 4.3 %all-to-all-start.7 = ((f32[4,64,1024]{2,1,0:T(8,128)}), f32[4,64,1024]{2,1,0:T(8,128)}, u32[]{:S(2)}, u32[]{:S(2)}) async-start(f32[4,64,1024]{2,1,0:T(8,128)} %broadcast_in_dim.31), calls=%async_computation.7 | async-start | bytes 2097152 | tf_op jit(solution)/shard_map/all_to_all | solution.py:26
  226.4 3.5 %fusion.4 = f32[512,1024]{1,0:T(8,128)} fusion(f32[512,256]{1,0:T(8,128)S(1)} %fusion.2, f32[256,1024]{1,0:T(8,128)} %bitcast.4), kind=kOutput, calls=%fused_computation.6 | convolution fusion | flops 805306368 | bytes 3670016 | tf_op jit(solution)/shard_map/dot_general | solution.py:12
  230.0 8.6 %all-to-all-done.7 = f32[4,64,1024]{2,1,0:T(8,128)} async-done(((f32[4,64,1024]{2,1,0:T(8,128)}), f32[4,64,1024]{2,1,0:T(8,128)}, u32[]{:S(2)}, u32[]{:S(2)}) %all-to-all-start.7) | async-done | bytes 1048608 | tf_op jit(solution)/shard_map/all_to_all | solution.py:26
  238.6 4.4 %subtract_subtract_fusion = f32[512,1024]{1,0:T(8,128)} fusion(f32[512,1024]{1,0:T(8,128)S(1)} %copy-done.1, f32[512,1024]{1,0:T(8,128)} %fusion.4, f32[256,512]{1,0:T(8,128)S(1)} %copy-done.2, f32[256,1024]{1,0:T(8,128)} %bitcast.8), kind=kOutput, calls=%fused_computation | convolution fusion | flops 806354944 | bytes 7864320 | tf_op jit(solution)/shard_map/dot_general | solution.py:12
  (20 shorter events, 10.3 us)
Async XLA Ops:
  0.0 215.8 %copy-start = (f32[256,256]{1,0:T(8,128)S(1)}, f32[256,256]{1,0:T(8,128)}, u32[]{:S(2)}) copy-start(f32[256,256]{1,0:T(8,128)} %param.8) | copy-start | bytes 786436
  26.3 8.0 %copy-start.3 = (f32[16,512]{1,0:T(8,128)S(1)}, f32[16,512]{1,0:T(8,128)}, u32[]{:S(2)}) copy-start(f32[16,512]{1,0:T(8,128)} %param.6) | copy-start | bytes 98308
  29.9 20.3 %copy-start.1 = (f32[512,1024]{1,0:T(8,128)S(1)}, f32[512,1024]{1,0:T(8,128)}, u32[]{:S(2)}) copy-start(f32[512,1024]{1,0:T(8,128)} %param.5) | copy-start | bytes 6291460
  29.9 22.4 %all-to-all-start = ((f32[4,64,1024]{2,1,0:T(8,128)}), f32[4,64,1024]{2,1,0:T(8,128)}, u32[]{:S(2)}, u32[]{:S(2)}) async-start(f32[4,64,1024]{2,1,0:T(8,128)} %bitcast.26), calls=%async_computation | async-start | bytes 2097152 | tf_op jit(solution)/shard_map/all_to_all | solution.py:20
  52.3 19.2 %all-to-all-start.4 = ((f32[4,64,1024]{2,1,0:T(8,128)}), f32[4,64,1024]{2,1,0:T(8,128)}, u32[]{:S(2)}, u32[]{:S(2)}) async-start(f32[4,64,1024]{2,1,0:T(8,128)} %bitcast.25), calls=%async_computation.4 | async-start | bytes 2097152 | tf_op jit(solution)/shard_map/all_to_all | solution.py:20
  71.6 16.8 %all-to-all-start.1 = ((f32[8,8,1024]{2,1,0:T(8,128)}), f32[8,8,1024]{2,1,0:T(8,128)}, u32[]{:S(2)}, u32[]{:S(2)}) async-start(f32[8,8,1024]{2,1,0:T(8,128)} %bitcast.29), calls=%async_computation.1 | async-start | bytes 524288 | tf_op jit(solution)/shard_map/all_to_all | solution.py:20
  88.3 13.4 %all-to-all-start.5 = ((f32[8,8,1024]{2,1,0:T(8,128)}), f32[8,8,1024]{2,1,0:T(8,128)}, u32[]{:S(2)}, u32[]{:S(2)}) async-start(f32[8,8,1024]{2,1,0:T(8,128)} %bitcast.30), calls=%async_computation.5 | async-start | bytes 524288 | tf_op jit(solution)/shard_map/all_to_all | solution.py:20
  102.5 13.4 %all-to-all-start.2 = ((f32[8,8,1024]{2,1,0:T(8,128)}), f32[8,8,1024]{2,1,0:T(8,128)}, u32[]{:S(2)}, u32[]{:S(2)}) async-start(f32[8,8,1024]{2,1,0:T(8,128)} %broadcast_in_dim.12), calls=%async_computation.2 | async-start | bytes 524288 | tf_op jit(solution)/shard_map/all_to_all | solution.py:26
  130.3 86.7 %all-to-all-start.3 = ((f32[4,64,1024]{2,1,0:T(8,128)}), f32[4,64,1024]{2,1,0:T(8,128)}, u32[]{:S(2)}, u32[]{:S(2)}) async-start(f32[4,64,1024]{2,1,0:T(8,128)} %broadcast_in_dim.28), calls=%async_computation.3 | async-start | bytes 2097152 | tf_op jit(solution)/shard_map/all_to_all | solution.py:26
  217.0 6.4 %copy-start.2 = (f32[256,512]{1,0:T(8,128)S(1)}, f32[256,512]{1,0:T(8,128)}, u32[]{:S(2)}) copy-start(f32[256,512]{1,0:T(8,128)} %fusion.1) | copy-start | bytes 1572868
  219.2 19.4 %all-to-all-start.7 = ((f32[4,64,1024]{2,1,0:T(8,128)}), f32[4,64,1024]{2,1,0:T(8,128)}, u32[]{:S(2)}, u32[]{:S(2)}) async-start(f32[4,64,1024]{2,1,0:T(8,128)} %broadcast_in_dim.31), calls=%async_computation.7 | async-start | bytes 2097152 | tf_op jit(solution)/shard_map/all_to_all | solution.py:26

commit v2 on v1

v2 whole, which is shorter than its diff:
```python
import jax
import jax.numpy as jnp
from jax import lax
from jax.experimental import pallas as pl
from jax.experimental.pallas import tpu as pltpu
from jax.sharding import Mesh, PartitionSpec as P

ROW = ("x", "y")
COL = ("z", "core")
NX, NY, NZ = 4, 8, 8
F32, BF16 = jnp.float32, jnp.bfloat16
VMEM = pl.BlockSpec(memory_space=pltpu.VMEM)
SMEM = pl.BlockSpec(memory_space=pltpu.SMEM)
PARAMS = pltpu.CompilerParams(vmem_limit_bytes=40 * 2**20)

STRIDED = [
    [(sx + dx) * NY + sy + dy for dx in range(0, NX, 2) for dy in range(0, NY, 2)]
    for sx in range(2)
    for sy in range(2)
]


def partner(i, n, start):
    return (i + 1) % n if (i - start) % 2 == 0 else (i - 1) % n


def exchange(values, start):
    got = []
    for d in (1, 2, 3):
        pairs = []
        for x in range(NX):
            for y in range(NY):
                px = partner(x, NX, start) if d & 2 else x
                py = partner(y, NY, start) if d & 1 else y
                pairs.append((x * NY + y, px * NY + py))
        got.append(lax.ppermute(values[d - 1], ROW, pairs))
    return got


def split(value):
    high = value.astype(BF16)
    return high, (value - high.astype(F32)).astype(BF16)


def mul(a, b):
    return jnp.dot(a, b, preferred_element_type=F32)


def mul3(a, b):
    return mul(a[0], b[0]) + (mul(a[0], b[1]) + mul(a[1], b[0]))


def project_kernel(j_ref, second_ref, first_ref, own_ref, block_ref, *refs):
    outs, (high, low) = refs[:8], refs[8:]
    j = j_ref[0]
    for panel, ref in enumerate((second_ref, first_ref)):
        for d in range(4):
            h, l = split(ref[pl.ds(pl.multiple_of((j ^ d) * 64, 64), 64), :])
            at = pl.ds(panel * 256 + d * 64, 64)
            high[at, :] = h
            low[at, :] = l
    for t in range(4):
        cols = pl.ds(t * 256, 256)
        value = mul3((high[...], low[...]), split(block_ref[:, cols]))
        for s in range(8):
            outs[s][:64, cols] = value[s * 64 : (s + 1) * 64]
    own = split(own_ref[...])
    whole = split(second_ref[...])
    nt = lambda a, b: lax.dot_general(a, b, (((1,), (1,)), ((), ())), preferred_element_type=F32)
    cross = nt(own[0], whole[0]) + (nt(own[0], whole[1]) + nt(own[1], whole[0]))
    for d in range(4):
        outs[d][64:, :256] = cross[:8]
        outs[d][64:, 256:512] = cross[8:]
        outs[d][64:, 512:] = jnp.zeros((8, 512), F32)


def near_kernel(*refs):
    parts, out = refs[:8], refs[8]
    total = [
        (parts[4 * p][...] + parts[4 * p + 1][...]) + (parts[4 * p + 2][...] + parts[4 * p + 3][...]) for p in range(2)
    ]
    cross = total[0][64:]
    for m in range(8):
        out[m, :8, :1024] = total[0][m * 8 : m * 8 + 8]
        out[m, 8:, :1024] = total[1][m * 8 : m * 8 + 8]
        out[m, :8, 1024:] = cross[:, :256]
        out[m, 8:, 1024:] = cross[:, 256:512]


def far_kernel(parts, out, cross):
    total = ((parts[0] + parts[1]) + (parts[2] + parts[3])) + ((parts[4] + parts[5]) + (parts[6] + parts[7]))
    for m in range(8):
        out[m] = total[:, :1024]
    cross[...] = total[:, 1024:]


def part_kernel(shares, out_second, out_first):
    for m in range(8):
        out_second[m * 8 : m * 8 + 8] = shares[m, :8]
        out_first[m * 8 : m * 8 + 8] = shares[m, 8:]


def weight_kernel(j_ref, second_ref, first_ref, high, low, rows):
    j = j_ref[0]
    for panel, ref in enumerate((second_ref, first_ref)):
        for d in range(4):
            rows[pl.ds(panel * 256 + d * 64, 64), :] = ref[pl.ds(pl.multiple_of((j ^ d) * 64, 64), 64), :]
    h, l = split(rows[...].T)
    high[...] = h
    low[...] = l


def update_kernel(block_ref, wh_ref, wl_ref, *refs):
    parts, (out, high, low) = refs[:8], refs[8:]
    for s in range(8):
        h, l = split(parts[s][...])
        high[pl.ds(s * 64, 64), :] = h
        low[pl.ds(s * 64, 64), :] = l
    for t in range(4):
        cols = pl.ds(t * 256, 256)
        out[:, cols] = block_ref[:, cols] - mul3((wh_ref[...], wl_ref[...]), (high[:, cols], low[:, cols]))


def call(kernel, outs, args, scratch=(), scalars=0):
    single = not isinstance(outs, list)
    return pl.pallas_call(
        kernel,
        out_shape=outs,
        in_specs=[SMEM] * scalars + [VMEM] * (len(args) - scalars),
        out_specs=VMEM if single else [VMEM] * len(outs),
        scratch_shapes=list(scratch),
        compiler_params=PARAMS,
    )(*args)


def shape(*dims, dtype=F32):
    return jax.ShapeDtypeStruct(dims, dtype)


def exact(left, right, dims):
    return lax.dot_general(left, right, (dims, ((), ())), precision=lax.Precision.HIGHEST, preferred_element_type=F32)


def fetch_beside(shard, core):
    mine = lax.all_to_all(jnp.broadcast_to(shard[None], (NZ,) + shard.shape), "z", 0, 0)
    other = lax.ppermute(mine, "core", [(0, 1), (1, 0)])
    low = jnp.where(core == 0, mine, other)
    high = jnp.where(core == 0, other, mine)
    return jnp.stack([low, high], axis=1).reshape(-1, shard.shape[1])


def local(vectors, reflectors_first, reflectors_second, factor_first, factor_second):
    core = lax.axis_index("core")
    j = ((lax.axis_index("x") % 2) * 2 + lax.axis_index("y") % 2).astype(jnp.int32).reshape(1)
    second = lax.all_gather(reflectors_second, COL, axis=0, tiled=True)
    first = fetch_beside(reflectors_first, core)
    wide = pltpu.VMEM((512, 512), BF16)
    parts = call(
        project_kernel,
        [shape(72, 1024)] * 4 + [shape(64, 1024)] * 4,
        (j, second, first, reflectors_first, vectors),
        scratch=(wide, wide),
        scalars=1,
    )
    got_second = exchange(parts[1:4], 0)
    got_first = exchange(parts[5:8], 1)
    pieces = call(near_kernel, shape(8, 16, 1280), (parts[0], *got_second, parts[4], *got_first))
    pieces = lax.all_to_all(pieces, ROW, 0, 0, axis_index_groups=STRIDED)
    copies, cross = call(far_kernel, [shape(8, 16, 1024), shape(16, 256)], (pieces,))
    shares = lax.all_to_all(copies, ROW, 0, 0, axis_index_groups=STRIDED)
    cross = lax.all_gather(cross, COL, axis=0, tiled=True)
    share_second, share_first = call(part_kernel, [shape(64, 1024)] * 2, (shares,))
    got_second = exchange([share_second] * 3, 0)
    got_first = exchange([share_first] * 3, 1)
    w_first = exact(factor_first, first, ((0,), (0,)))
    w_second = exact(factor_second, second - exact(cross, w_first, ((0,), (0,))), ((0,), (0,)))
    weights = call(
        weight_kernel,
        [shape(512, 512, dtype=BF16)] * 2,
        (j, w_second, w_first),
        scratch=(pltpu.VMEM((512, 512), F32),),
        scalars=1,
    )
    tall = pltpu.VMEM((512, 1024), BF16)
    return call(
        update_kernel,
        shape(512, 1024),
        (vectors, *weights, share_second, *got_second, share_first, *got_first),
        scratch=(tall, tall),
    )


def solution(mesh):
    fine = Mesh(mesh.devices.reshape(NX, NY, NZ, 2), ROW + COL)
    return jax.shard_map(
        local,
        mesh=fine,
        in_specs=(P(ROW, COL), P(COL, ROW), P(COL, ROW), P(), P()),
        out_specs=P(ROW, COL),
        check_vma=False,
    )
```

time: 244 us -> 174 us (0.71)
  blocking collectives: 134 us -> 91.5 us
  waiting for transfers between devices: 46.2 us -> 13.9 us
  starting transfers between devices: 32.1 us -> 52.9 us
  matrix products: 18.2 us -> 4.54 us
  Pallas kernels: 0 us -> 7.33 us
  other arithmetic: 7.07 us -> 0.09 us
    all_gather x4 -> x2, blocking collectives: 122 us -> 36 us  [the longest x1 19.8 us: local(): cross = lax.all_gather(cross, COL, axis=0, tiled=True)]
    ppermute x0 -> x13, starting transfers between devices: none -> 52.9 us  [the longest x12 48.5 us: exchange(): got.append(lax.ppermute(values[d - 1], ROW, pairs))]
    all_to_all x7 -> x0, waiting for transfers between devices: 46.2 us -> none  [the longest x4 29.2 us: scatter_sum(): return jnp.sum(lax.all_to_all(pieces, axis, 0, 0), axis=0)]
    all_to_all x1 -> x3, blocking collectives: 12.4 us -> 55.5 us  [the longest x1 21 us: fetch_beside(): lax.all_to_all(jnp.broadcast_to(shard[None], (NZ,) + shard.shape), 'z', 0...]
    all_to_all x7 -> x0, starting transfers between devices: 32.1 us -> none  [the longest x4 19.6 us: scatter_sum(): return jnp.sum(lax.all_to_all(pieces, axis, 0, 0), axis=0)]
    ppermute x0 -> x13, waiting for transfers between devices: none -> 13.9 us  [the longest x12 13.9 us: exchange(): got.append(lax.ppermute(values[d - 1], ROW, pairs))]
    dot_general x8 -> x3, matrix products: 18.2 us -> 4.54 us  [exact(): lax.dot_general(left, right, (dims, ((), ())), precision=lax.Precision.HI...]
    pallas_call x0 -> x6, Pallas kernels: none -> 7.33 us  [call(): pl.pallas_call(kernel, out_shape=outs, in_specs=[SMEM] * scalars + [VMEM]...]
  transfers between devices with their start and end apart: 7 -> 13, of which waited for: 5 -> 3; matrix products, arithmetic and copies ran while one was open for 7% -> 3% of each run, Pallas kernels for 0% -> 0%
where the time goes in v2:
time: 174 us
  blocking collectives  91.5 us (53%)
  starting transfers between devices  52.9 us (30%)
  waiting for transfers between devices  13.9 us (8%)
  Pallas kernels  7.33 us (4%)
  matrix products  4.54 us (3%)
  local copies, waits for them, and re-layouts  2.88 us (2%)
    ppermute x12, starting transfers between devices, exchange(): got.append(lax.ppermute(values[d - 1], ROW, pairs))  48.5 us
    all_to_all x1, blocking collectives, fetch_beside(): lax.all_to_all(jnp.broadcast_to(shard[None], (NZ,) + shard.shape), 'z', 0...  21 us
    all_gather x1, blocking collectives, local(): cross = lax.all_gather(cross, COL, axis=0, tiled=True)  19.8 us
    all_to_all x1, blocking collectives, local(): pieces = lax.all_to_all(pieces, ROW, 0, 0, axis_index_groups=STRIDED)  18.9 us
    all_gather x1, blocking collectives, local(): second = lax.all_gather(reflectors_second, COL, axis=0, tiled=True)  16.2 us
    all_to_all x1, blocking collectives, local(): shares = lax.all_to_all(copies, ROW, 0, 0, axis_index_groups=STRIDED)  15.6 us
    ppermute x12, waiting for transfers between devices, exchange(): got.append(lax.ppermute(values[d - 1], ROW, pairs))  13.9 us
    pallas_call x6, Pallas kernels, call(): pl.pallas_call(kernel, out_shape=outs, in_specs=[SMEM] * scalars + [VMEM]...  7.33 us
  transfers between devices with their start and end apart: 13, of which 3 were waited for; matrix products, arithmetic and copies ran while one was open for 3% of the time, Pallas kernels for 0%

profile of v2, /device:TPU:1, one launch (start us, length us, event | category | flops | bytes accessed | tf_op | source)
XLA Modules:
  0.0 173.5 jit_solution(17135367757064877468)
XLA Ops:
  0.9 21.0 %all_to_all.15 = f32[8,16,512]{2,1,0:T(8,128)S(1)} all-to-all(f32[8,16,512]{2,1,0:T(8,128)S(1)} %broadcast_in_dim.2), channel_id=1, replica_groups=mesh['x'=4,'y'=8,'z'=8,'core'=2] {'z'}, dimensions={0} | all-to-all | bytes 524288 | tf_op jit(solution)/shard_map/all_to_all | solution.py:145
  22.0 4.4 %collective-permute-start = (f32[8,16,512]{2,1,0:T(8,128)S(1)}, f32[8,16,512]{2,1,0:T(8,128)S(1)}, u32[]{:S(2)}, u32[]{:S(2)}) collective-permute-start(f32[8,16,512]{2,1,0:T(8,128)S(1)} %all_to_all.15), channel_id=1, source_target_pairs={{0,1},{1,0},{2,3},{3,2},{4,5},{5,4},{6,7},{7,6},{8,9},{9,8},{10,11... | collective-permute-start | bytes 786440 | tf_op jit(solution)/shard_map/ppermute | solution.py:146
  26.4 16.2 %all_gather.6.second_ref = f32[256,512]{1,0:T(8,128)S(1)} all-gather(f32[16,512]{1,0:T(8,128)} %param.7), channel_id=1, replica_groups=mesh['x'=4,'y'=8,'z'=8,'core'=2] {'z','core'}, dimensions={0}, use_global_device_ids=true | all-gather | bytes 557056 | tf_op jit(solution)/shard_map/all_gather | solution.py:155
  42.7 2.0 %shard_map.55 = (f32[72,1024]{1,0:T(8,128)S(1)}, f32[72,1024]{1,0:T(8,128)S(1)}, f32[72,1024]{1,0:T(8,128)S(1)}, f32[72,1024]{1,0:T(8,128)S(1)}, f32[64,1024]{1,...) custom-call(s32[1]{0:T(128)} %bitcast.j_ref, ...), custom_call_target="tpu_custom_call" | custom-call | tf_op jit(solution)/shard_map/pallas_call | solution.py:126
  44.7 5.1 %collective-permute-start.4 = (f32[64,1024]{1,0:T(8,128)S(1)}, f32[64,1024]{1,0:T(8,128)S(1)}, u32[]{:S(2)}, u32[]{:S(2)}) collective-permute-start(f32[64,1024]{1,0:T(8,128)S(1)} %get-tuple-element.24), channel_id=1, source_target_pairs={{0,112},{16,32},{32,16},{48,64},{64,48},{80,96},{96,80},{112,0},{1... | collective-permute-start | bytes 786440 | tf_op jit(solution)/shard_map/ppermute | solution.py:36
  49.8 1.9 %collective-permute-start.1 = (f32[72,1024]{1,0:T(8,128)S(1)}, f32[72,1024]{1,0:T(8,128)S(1)}, u32[]{:S(2)}, u32[]{:S(2)}) collective-permute-start(f32[72,1024]{1,0:T(8,128)S(1)} %get-tuple-element.20), channel_id=1, source_target_pairs={{0,16},{16,0},{32,48},{48,32},{64,80},{80,64},{96,112},{112,96},{1... | collective-permute-start | bytes 884744 | tf_op jit(solution)/shard_map/ppermute | solution.py:36
  51.7 3.1 %collective-permute-start.2 = (f32[72,1024]{1,0:T(8,128)S(1)}, f32[72,1024]{1,0:T(8,128)S(1)}, u32[]{:S(2)}, u32[]{:S(2)}) collective-permute-start(f32[72,1024]{1,0:T(8,128)S(1)} %get-tuple-element.21), channel_id=1, source_target_pairs={{0,128},{16,144},{32,160},{48,176},{64,192},{80,208},{96,224},{112... | collective-permute-start | bytes 884744 | tf_op jit(solution)/shard_map/ppermute | solution.py:36
  54.8 3.3 %collective-permute-start.3 = (f32[72,1024]{1,0:T(8,128)S(1)}, f32[72,1024]{1,0:T(8,128)S(1)}, u32[]{:S(2)}, u32[]{:S(2)}) collective-permute-start(f32[72,1024]{1,0:T(8,128)S(1)} %get-tuple-element.22), channel_id=1, source_target_pairs={{0,144},{16,128},{32,176},{48,160},{64,208},{80,192},{96,240},{112... | collective-permute-start | bytes 884744 | tf_op jit(solution)/shard_map/ppermute | solution.py:36
  58.2 4.4 %collective-permute-start.5 = (f32[64,1024]{1,0:T(8,128)S(1)}, f32[64,1024]{1,0:T(8,128)S(1)}, u32[]{:S(2)}, u32[]{:S(2)}) collective-permute-start(f32[64,1024]{1,0:T(8,128)S(1)} %get-tuple-element.25), channel_id=1, source_target_pairs={{0,384},{16,400},{32,416},{48,432},{64,448},{80,464},{96,480},{112... | collective-permute-start | bytes 786440 | tf_op jit(solution)/shard_map/ppermute | solution.py:36
  62.6 2.5 %collective-permute-start.6 = (f32[64,1024]{1,0:T(8,128)S(1)}, f32[64,1024]{1,0:T(8,128)S(1)}, u32[]{:S(2)}, u32[]{:S(2)}) collective-permute-start(f32[64,1024]{1,0:T(8,128)S(1)} %get-tuple-element.26), channel_id=1, source_target_pairs={{0,496},{16,416},{32,400},{48,448},{64,432},{80,480},{96,464},{112... | collective-permute-start | bytes 786440 | tf_op jit(solution)/shard_map/ppermute | solution.py:36
  65.1 2.7 %collective-permute-done.5.refs_6_ = f32[64,1024]{1,0:T(8,128)S(1)} collective-permute-done((f32[64,1024]{1,0:T(8,128)S(1)}, f32[64,1024]{1,0:T(8,128)S(1)}, u32[]{:S(2)}, u32[]{:S(2)}) %collective-permute-start.5) | collective-permute-done | bytes 262176 | tf_op jit(solution)/shard_map/ppermute | solution.py:36
  67.8 6.2 %collective-permute-done.6.refs_7_ = f32[64,1024]{1,0:T(8,128)S(1)} collective-permute-done((f32[64,1024]{1,0:T(8,128)S(1)}, f32[64,1024]{1,0:T(8,128)S(1)}, u32[]{:S(2)}, u32[]{:S(2)}) %collective-permute-start.6) | collective-permute-done | bytes 262176 | tf_op jit(solution)/shard_map/ppermute | solution.py:36
  74.2 18.9 %all_to_all.16.parts = f32[8,16,1280]{2,1,0:T(8,128)S(1)} all-to-all(f32[8,16,1280]{2,1,0:T(8,128)S(1)} %shard_map.56), channel_id=1, replica_groups={{0,32,64,96,256,288,320,352},{16,48,80,112,272,304,336,368},{128,160,19..., dimensions={0} | all-to-all | bytes 1310720 | tf_op jit(solution)/shard_map/all_to_all | solution.py:168
  93.2 15.6 %all_to_all.17.shares = f32[8,16,1024]{2,1,0:T(8,128)S(1)} all-to-all(f32[8,16,1024]{2,1,0:T(8,128)S(1)} %get-tuple-element.30), channel_id=1, replica_groups={{0,32,64,96,256,288,320,352},{16,48,80,112,272,304,336,368},{128,160,19..., dimensions={0} | all-to-all | bytes 1048576 | tf_op jit(solution)/shard_map/all_to_all | solution.py:170
  110.1 13.4 %collective-permute-start.9 = (f32[64,1024]{1,0:T(8,128)}, f32[64,1024]{1,0:T(8,128)}, u32[]{:S(2)}, u32[]{:S(2)}) collective-permute-start(f32[64,1024]{1,0:T(8,128)} %get-tuple-element.31.refs_0_), channel_id=1, source_target_pairs={{0,144},{16,128},{32,176},{48,160},{64,208},{80,192},{96,240},{112... | collective-permute-start | bytes 786440 | tf_op jit(solution)/shard_map/ppermute | solution.py:36
  126.6 19.8 %all_gather.7 = f32[256,256]{1,0:T(8,128)S(1)} all-gather(f32[16,256]{1,0:T(8,128)S(1)} %get-tuple-element.27), channel_id=1, replica_groups=mesh['x'=4,'y'=8,'z'=8,'core'=2] {'z','core'}, dimensions={0}, use_global_device_ids=true | all-gather | bytes 278528 | tf_op jit(solution)/shard_map/all_gather | solution.py:171
  146.4 1.9 %collective-permute-start.8 = (f32[64,1024]{1,0:T(8,128)}, f32[64,1024]{1,0:T(8,128)S(1)}, u32[]{:S(2)}, u32[]{:S(2)}) collective-permute-start(f32[64,1024]{1,0:T(8,128)} %get-tuple-element.31.refs_0_), channel_id=1, source_target_pairs={{0,128},{16,144},{32,160},{48,176},{64,192},{80,208},{96,224},{112... | collective-permute-start | bytes 786440 | tf_op jit(solution)/shard_map/ppermute | solution.py:36
  148.3 1.9 %collective-permute-start.7 = (f32[64,1024]{1,0:T(8,128)}, f32[64,1024]{1,0:T(8,128)S(1)}, u32[]{:S(2)}, u32[]{:S(2)}) collective-permute-start(f32[64,1024]{1,0:T(8,128)} %get-tuple-element.31.refs_0_), channel_id=1, source_target_pairs={{0,16},{16,0},{32,48},{48,32},{64,80},{80,64},{96,112},{112,96},{1... | collective-permute-start | bytes 786440 | tf_op jit(solution)/shard_map/ppermute | solution.py:36
  150.2 2.1 %collective-permute-start.12 = (f32[64,1024]{1,0:T(8,128)}, f32[64,1024]{1,0:T(8,128)S(1)}, u32[]{:S(2)}, u32[]{:S(2)}) collective-permute-start(f32[64,1024]{1,0:T(8,128)} %copy-done.2), channel_id=1, source_target_pairs={{0,496},{16,416},{32,400},{48,448},{64,432},{80,480},{96,464},{112... | collective-permute-start | bytes 786440 | tf_op jit(solution)/shard_map/ppermute | solution.py:36
  152.3 3.1 %collective-permute-start.11 = (f32[64,1024]{1,0:T(8,128)}, f32[64,1024]{1,0:T(8,128)S(1)}, u32[]{:S(2)}, u32[]{:S(2)}) collective-permute-start(f32[64,1024]{1,0:T(8,128)} %copy-done.2), channel_id=1, source_target_pairs={{0,384},{16,400},{32,416},{48,432},{64,448},{80,464},{96,480},{112... | collective-permute-start | bytes 786440 | tf_op jit(solution)/shard_map/ppermute | solution.py:36
  155.4 5.8 %collective-permute-start.10 = (f32[64,1024]{1,0:T(8,128)}, f32[64,1024]{1,0:T(8,128)S(1)}, u32[]{:S(2)}, u32[]{:S(2)}) collective-permute-start(f32[64,1024]{1,0:T(8,128)} %copy-done.2), channel_id=1, source_target_pairs={{0,112},{16,32},{32,16},{48,64},{64,48},{80,96},{96,80},{112,0},{1... | collective-permute-start | bytes 786440 | tf_op jit(solution)/shard_map/ppermute | solution.py:36
  161.2 2.1 %convolution_subtract_fusion = f32[256,512]{1,0:T(8,128)S(1)} fusion(f32[256,512]{1,0:T(8,128)S(1)} %all_gather.6.second_ref, f32[256,256]{1,0:T(8,128)S(1)} %all_gather.7, f32[512,256]{1,0:T(8,128)} %fusion), kind=kOutput, calls=%fused_computation.1 | convolution fusion | flops 402784256 | bytes 1835008 | tf_op jit(solution)/shard_map/dot_general | solution.py:141
  164.4 5.0 %collective-permute-done.11.refs_6_ = f32[64,1024]{1,0:T(8,128)S(1)} collective-permute-done((f32[64,1024]{1,0:T(8,128)}, f32[64,1024]{1,0:T(8,128)S(1)}, u32[]{:S(2)}, u32[]{:S(2)}) %collective-permute-start.11) | collective-permute-done | bytes 262176 | tf_op jit(solution)/shard_map/ppermute | solution.py:36
  169.4 4.1 %shard_map.60 = f32[512,1024]{1,0:T(8,128)} custom-call(f32[512,1024]{1,0:T(8,128)S(1)} %copy-done.1, bf16[512,512]{1,0:T(8,128)(2,1)S(1)} %get-tuple-element.28.wh_ref, bf16[512,512]{1,0:T(8,128)(2,1)S(1)} %get-tuple-element.29.wl_ref, f32[64,1024]{1,0:T(8,128)} %get-tuple-element.31.refs_0_, f32[64,1024]{1,0:T(8,128)S(1)} %collective-permute-done.7.refs_1_, ...), custom_call_target="tpu_custom_call" | custom-call | tf_op jit(solution)/shard_map/pallas_call | solution.py:126
  (32 shorter events, 6.7 us)
Async XLA Ops:
  0.0 123.5 %copy-start = (f32[256,256]{1,0:T(8,128)S(1)}, f32[256,256]{1,0:T(8,128)}, u32[]{:S(2)}) copy-start(f32[256,256]{1,0:T(8,128)} %param.8) | copy-start | bytes 786436
  0.0 42.7 %copy-start.4 = (f32[16,512]{1,0:T(8,128)S(1)}, f32[16,512]{1,0:T(8,128)}, u32[]{:S(2)}) copy-start(f32[16,512]{1,0:T(8,128)} %own_ref.1) | copy-start | bytes 98308
  0.0 42.7 %copy-start.1 = (f32[512,1024]{1,0:T(8,128)S(1)}, f32[512,1024]{1,0:T(8,128)}, u32[]{:S(2)}) copy-start(f32[512,1024]{1,0:T(8,128)} %block_ref.3) | copy-start | bytes 6291460
  22.0 20.6 %collective-permute-start = (f32[8,16,512]{2,1,0:T(8,128)S(1)}, f32[8,16,512]{2,1,0:T(8,128)S(1)}, u32[]{:S(2)}, u32[]{:S(2)}) collective-permute-start(f32[8,16,512]{2,1,0:T(8,128)S(1)} %all_to_all.15), channel_id=1, source_target_pairs={{0,1},{1,0},{2,3},{3,2},{4,5},{5,4},{6,7},{7,6},{8,9},{9,8},{10,11... | collective-permute-start | bytes 786440 | tf_op jit(solution)/shard_map/ppermute | solution.py:146
  44.7 17.9 %collective-permute-start.4 = (f32[64,1024]{1,0:T(8,128)S(1)}, f32[64,1024]{1,0:T(8,128)S(1)}, u32[]{:S(2)}, u32[]{:S(2)}) collective-permute-start(f32[64,1024]{1,0:T(8,128)S(1)} %get-tuple-element.24), channel_id=1, source_target_pairs={{0,112},{16,32},{32,16},{48,64},{64,48},{80,96},{96,80},{112,0},{1... | collective-permute-start | bytes 786440 | tf_op jit(solution)/shard_map/ppermute | solution.py:36
  49.8 24.3 %collective-permute-start.1 = (f32[72,1024]{1,0:T(8,128)S(1)}, f32[72,1024]{1,0:T(8,128)S(1)}, u32[]{:S(2)}, u32[]{:S(2)}) collective-permute-start(f32[72,1024]{1,0:T(8,128)S(1)} %get-tuple-element.20), channel_id=1, source_target_pairs={{0,16},{16,0},{32,48},{48,32},{64,80},{80,64},{96,112},{112,96},{1... | collective-permute-start | bytes 884744 | tf_op jit(solution)/shard_map/ppermute | solution.py:36
  51.7 22.3 %collective-permute-start.2 = (f32[72,1024]{1,0:T(8,128)S(1)}, f32[72,1024]{1,0:T(8,128)S(1)}, u32[]{:S(2)}, u32[]{:S(2)}) collective-permute-start(f32[72,1024]{1,0:T(8,128)S(1)} %get-tuple-element.21), channel_id=1, source_target_pairs={{0,128},{16,144},{32,160},{48,176},{64,192},{80,208},{96,224},{112... | collective-permute-start | bytes 884744 | tf_op jit(solution)/shard_map/ppermute | solution.py:36
  54.8 19.2 %collective-permute-start.3 = (f32[72,1024]{1,0:T(8,128)S(1)}, f32[72,1024]{1,0:T(8,128)S(1)}, u32[]{:S(2)}, u32[]{:S(2)}) collective-permute-start(f32[72,1024]{1,0:T(8,128)S(1)} %get-tuple-element.22), channel_id=1, source_target_pairs={{0,144},{16,128},{32,176},{48,160},{64,208},{80,192},{96,240},{112... | collective-permute-start | bytes 884744 | tf_op jit(solution)/shard_map/ppermute | solution.py:36
  58.2 9.6 %collective-permute-start.5 = (f32[64,1024]{1,0:T(8,128)S(1)}, f32[64,1024]{1,0:T(8,128)S(1)}, u32[]{:S(2)}, u32[]{:S(2)}) collective-permute-start(f32[64,1024]{1,0:T(8,128)S(1)} %get-tuple-element.25), channel_id=1, source_target_pairs={{0,384},{16,400},{32,416},{48,432},{64,448},{80,464},{96,480},{112... | collective-permute-start | bytes 786440 | tf_op jit(solution)/shard_map/ppermute | solution.py:36
  62.6 11.4 %collective-permute-start.6 = (f32[64,1024]{1,0:T(8,128)S(1)}, f32[64,1024]{1,0:T(8,128)S(1)}, u32[]{:S(2)}, u32[]{:S(2)}) collective-permute-start(f32[64,1024]{1,0:T(8,128)S(1)} %get-tuple-element.26), channel_id=1, source_target_pairs={{0,496},{16,416},{32,400},{48,448},{64,432},{80,480},{96,464},{112... | collective-permute-start | bytes 786440 | tf_op jit(solution)/shard_map/ppermute | solution.py:36
  109.4 0.7 copy-start.2
  110.1 45.3 %collective-permute-start.9 = (f32[64,1024]{1,0:T(8,128)}, f32[64,1024]{1,0:T(8,128)}, u32[]{:S(2)}, u32[]{:S(2)}) collective-permute-start(f32[64,1024]{1,0:T(8,128)} %get-tuple-element.31.refs_0_), channel_id=1, source_target_pairs={{0,144},{16,128},{32,176},{48,160},{64,208},{80,192},{96,240},{112... | collective-permute-start | bytes 786440 | tf_op jit(solution)/shard_map/ppermute | solution.py:36
  126.6 36.7 %copy-start.5 = (f32[256,256]{1,0:T(8,128)S(1)}, f32[256,256]{1,0:T(8,128)}, u32[]{:S(2)}) copy-start(f32[256,256]{1,0:T(8,128)} %param.9) | copy-start | bytes 786436
  146.4 17.9 %collective-permute-start.8 = (f32[64,1024]{1,0:T(8,128)}, f32[64,1024]{1,0:T(8,128)S(1)}, u32[]{:S(2)}, u32[]{:S(2)}) collective-permute-start(f32[64,1024]{1,0:T(8,128)} %get-tuple-element.31.refs_0_), channel_id=1, source_target_pairs={{0,128},{16,144},{32,160},{48,176},{64,192},{80,208},{96,224},{112... | collective-permute-start | bytes 786440 | tf_op jit(solution)/shard_map/ppermute | solution.py:36
  148.3 16.0 %collective-permute-start.7 = (f32[64,1024]{1,0:T(8,128)}, f32[64,1024]{1,0:T(8,128)S(1)}, u32[]{:S(2)}, u32[]{:S(2)}) collective-permute-start(f32[64,1024]{1,0:T(8,128)} %get-tuple-element.31.refs_0_), channel_id=1, source_target_pairs={{0,16},{16,0},{32,48},{48,32},{64,80},{80,64},{96,112},{112,96},{1... | collective-permute-start | bytes 786440 | tf_op jit(solution)/shard_map/ppermute | solution.py:36
  150.2 19.1 %copy-start.3 = (f32[64,1024]{1,0:T(8,128)S(1)}, f32[64,1024]{1,0:T(8,128)}, u32[]{:S(2)}) copy-start(f32[64,1024]{1,0:T(8,128)} %copy-done.2) | copy-start | bytes 786436
  150.2 14.1 %collective-permute-start.12 = (f32[64,1024]{1,0:T(8,128)}, f32[64,1024]{1,0:T(8,128)S(1)}, u32[]{:S(2)}, u32[]{:S(2)}) collective-permute-start(f32[64,1024]{1,0:T(8,128)} %copy-done.2), channel_id=1, source_target_pairs={{0,496},{16,416},{32,400},{48,448},{64,432},{80,480},{96,464},{112... | collective-permute-start | bytes 786440 | tf_op jit(solution)/shard_map/ppermute | solution.py:36
  152.3 17.0 %collective-permute-start.11 = (f32[64,1024]{1,0:T(8,128)}, f32[64,1024]{1,0:T(8,128)S(1)}, u32[]{:S(2)}, u32[]{:S(2)}) collective-permute-start(f32[64,1024]{1,0:T(8,128)} %copy-done.2), channel_id=1, source_target_pairs={{0,384},{16,400},{32,416},{48,432},{64,448},{80,464},{96,480},{112... | collective-permute-start | bytes 786440 | tf_op jit(solution)/shard_map/ppermute | solution.py:36
  155.4 13.9 %collective-permute-start.10 = (f32[64,1024]{1,0:T(8,128)}, f32[64,1024]{1,0:T(8,128)S(1)}, u32[]{:S(2)}, u32[]{:S(2)}) collective-permute-start(f32[64,1024]{1,0:T(8,128)} %copy-done.2), channel_id=1, source_target_pairs={{0,112},{16,32},{32,16},{48,64},{64,48},{80,96},{96,80},{112,0},{1... | collective-permute-start | bytes 786440 | tf_op jit(solution)/shard_map/ppermute | solution.py:36

commit v3 on v1

v3 whole, which is shorter than its diff:
```python
import jax
import jax.numpy as jnp
from jax import lax
from jax.experimental import pallas as pl
from jax.experimental.pallas import tpu as pltpu
from jax.sharding import Mesh, PartitionSpec as P

ROW = ("x", "y")
COL = ("z", "core")
NX, NY, NZ = 4, 8, 8
F32, BF16 = jnp.float32, jnp.bfloat16
VMEM = pl.BlockSpec(memory_space=pltpu.VMEM)
PARAMS = pltpu.CompilerParams(vmem_limit_bytes=48 * 2**20)

NEAR = [[x * NY + y + dy for x in range(NX) for dy in range(2)] for y in range(0, NY, 2)]
FAR = [[x * NY + y for y in range(parity, NY, 2)] for x in range(NX) for parity in range(2)]


def split(value):
    high = value.astype(BF16)
    return high, (value - high.astype(F32)).astype(BF16)


def mul(a, b):
    return jnp.dot(a, b, preferred_element_type=F32)


def mul_nt(a, b):
    return lax.dot_general(a, b, (((1,), (1,)), ((), ())), preferred_element_type=F32)


def mul3(a, b, mul=mul):
    return mul(a[0], b[0]) + (mul(a[0], b[1]) + mul(a[1], b[0]))


def project_kernel(second_ref, first_ref, own_ref, block_ref, out, high, low):
    for panel, ref in enumerate((second_ref, first_ref)):
        h, l = split(ref[...])
        high[pl.ds(panel * 256, 256), :] = h
        low[pl.ds(panel * 256, 256), :] = l
    for t in range(4):
        value = mul3((high[...], low[...]), split(block_ref[:, t * 256 : (t + 1) * 256]))
        for m in range(8):
            for half in range(2):
                at = (2 * t + half) * 64
                out[m, at : at + 64, :] = value[m * 64 : (m + 1) * 64, half * 128 : (half + 1) * 128]
    cross = mul3(split(own_ref[...]), (high[:256], low[:256]), mul_nt)
    for m in range(8):
        out[m, 512:528, :] = cross[:, :128]
        out[m, 528:544, :] = cross[:, 128:]


def near_kernel(parts, out):
    total = ((parts[0] + parts[1]) + (parts[2] + parts[3])) + ((parts[4] + parts[5]) + (parts[6] + parts[7]))
    for m in range(4):
        out[m, :128, :] = total[m * 128 : (m + 1) * 128]
        out[m, 128:, :] = total[512:]


def far_kernel(parts, out, cross):
    total = (parts[0] + parts[1]) + (parts[2] + parts[3])
    for m in range(4):
        out[m] = total[:128]
    cross[:, :128] = total[128:144]
    cross[:, 128:] = total[144:]


def copy_kernel(share, out):
    for m in range(8):
        out[m] = share[...]


def weight_kernel(second_ref, first_ref, high, low):
    for panel, ref in enumerate((second_ref, first_ref)):
        h, l = split(ref[...].T)
        high[:, panel * 256 : (panel + 1) * 256] = h
        low[:, panel * 256 : (panel + 1) * 256] = l


def update_kernel(block_ref, wh_ref, wl_ref, proj_ref, out):
    proj = jnp.concatenate(
        [jnp.concatenate([proj_ref[m, :64], proj_ref[m, 64:]], axis=1) for m in range(8)], axis=0
    )
    out[...] = block_ref[...] - mul3((wh_ref[...], wl_ref[...]), split(proj))


def call(kernel, outs, args, scratch=()):
    single = not isinstance(outs, list)
    return pl.pallas_call(
        kernel,
        out_shape=outs,
        in_specs=[VMEM] * len(args),
        out_specs=VMEM if single else [VMEM] * len(outs),
        scratch_shapes=list(scratch),
        compiler_params=PARAMS,
    )(*args)


def shape(*dims, dtype=F32):
    return jax.ShapeDtypeStruct(dims, dtype)


def exact(left, right):
    dims = (((0,), (0,)), ((), ()))
    return lax.dot_general(left, right, dims, precision=lax.Precision.HIGHEST, preferred_element_type=F32)


def trade(pieces, groups):
    return lax.all_to_all(pieces, ROW, 0, 0, axis_index_groups=groups)


def local(vectors, reflectors_first, reflectors_second, factor_first, factor_second):
    copies = jnp.broadcast_to(reflectors_first[None], (2 * NZ,) + reflectors_first.shape)
    first = lax.all_to_all(copies, COL, 0, 0).reshape(256, 512)
    second = lax.all_gather(reflectors_second, COL, axis=0, tiled=True)
    wide = pltpu.VMEM((512, 512), BF16)
    parts = call(project_kernel, shape(8, 544, 128), (second, first, reflectors_first, vectors), (wide, wide))
    parts = call(near_kernel, shape(4, 160, 128), (trade(parts, NEAR),))
    share, cross = call(far_kernel, [shape(4, 128, 128), shape(16, 256)], (trade(parts, FAR),))
    share = trade(share, FAR).reshape(512, 128)
    proj = trade(call(copy_kernel, shape(8, 512, 128), (share,)), NEAR)
    cross = lax.all_gather(cross, COL, axis=0, tiled=True)
    w_first = exact(factor_first, first)
    w_second = exact(factor_second, second - exact(cross, w_first))
    weights = call(weight_kernel, [shape(512, 512, dtype=BF16)] * 2, (w_second, w_first))
    return pl.pallas_call(
        update_kernel,
        out_shape=shape(512, 1024),
        grid=(4,),
        in_specs=[
            pl.BlockSpec((512, 256), lambda t: (0, t)),
            pl.BlockSpec((512, 512), lambda t: (0, 0)),
            pl.BlockSpec((512, 512), lambda t: (0, 0)),
            pl.BlockSpec((8, 128, 128), lambda t: (0, t, 0)),
        ],
        out_specs=pl.BlockSpec((512, 256), lambda t: (0, t)),
        compiler_params=PARAMS,
    )(vectors, *weights, proj)


def solution(mesh):
    fine = Mesh(mesh.devices.reshape(NX, NY, NZ, 2), ROW + COL)
    return jax.shard_map(
        local,
        mesh=fine,
        in_specs=(P(ROW, COL), P(COL, ROW), P(COL, ROW), P(), P()),
        out_specs=P(ROW, COL),
        check_vma=False,
    )
```

time: 244 us -> 140 us (0.57)
  waiting for transfers between devices: 46.2 us -> 2.15 us
  blocking collectives: 134 us -> 107 us
  starting transfers between devices: 32.1 us -> 15.4 us
  matrix products: 18.2 us -> 1.92 us
  other arithmetic: 7.07 us -> 0 us
  Pallas kernels: 0 us -> 6.14 us
    all_gather x4 -> x2, blocking collectives: 122 us -> 46.1 us  [the longest x1 27.4 us: local(): second = lax.all_gather(reflectors_second, COL, axis=0, tiled=True)]
    all_to_all x1 -> x3, blocking collectives: 12.4 us -> 60.5 us  [trade(): return lax.all_to_all(pieces, ROW, 0, 0, axis_index_groups=groups)]
    all_to_all x7 -> x2, waiting for transfers between devices: 46.2 us -> 2.15 us  [the longest x1 2.15 us: trade(): return lax.all_to_all(pieces, ROW, 0, 0, axis_index_groups=groups)]
    all_to_all x7 -> x2, starting transfers between devices: 32.1 us -> 15.4 us  [the longest x1 11.8 us: local(): first = lax.all_to_all(copies, COL, 0, 0).reshape(256, 512)]
    dot_general x8 -> x3, matrix products: 18.2 us -> 1.92 us  [exact(): lax.dot_general(left, right, dims, precision=lax.Precision.HIGHEST, prefe...]
    reduce_sum x5 -> x0, other arithmetic: 7.07 us -> none  [the longest x4 5.98 us: scatter_sum(): return jnp.sum(lax.all_to_all(pieces, axis, 0, 0), axis=0)]
    pallas_call x0 -> x6, Pallas kernels: none -> 6.14 us  [the longest x1 3.58 us: local(): pl.pallas_call(update_kernel, out_shape=shape(512, 1024), grid=(4,), in_s...]
    broadcast_in_dim x4 -> x1, local copies, waits for them, and re-layouts: 4.92 us -> 1.76 us  [local(): jnp.broadcast_to(reflectors_first[None], (2 * NZ,) + reflectors_first.shape)]
  transfers between devices with their start and end apart: 7 -> 2, of which waited for: 5 -> 1; matrix products, arithmetic and copies ran while one was open for 7% -> 1% of each run, Pallas kernels for 0% -> 0%
where the time goes in v3:
time: 140 us; the launch traced here: 137 us
  blocking collectives  107 us (76%)
  starting transfers between devices  15.4 us (11%)
  Pallas kernels  6.14 us (4%)
  local copies, waits for them, and re-layouts  4.68 us (3%)
  waiting for transfers between devices  2.15 us (2%)
  matrix products  1.92 us (1%)
    all_to_all x3, blocking collectives, trade(): return lax.all_to_all(pieces, ROW, 0, 0, axis_index_groups=groups)  60.5 us
    all_gather x1, blocking collectives, local(): second = lax.all_gather(reflectors_second, COL, axis=0, tiled=True)  27.4 us
    all_gather x1, blocking collectives, local(): cross = lax.all_gather(cross, COL, axis=0, tiled=True)  18.8 us
    all_to_all x1, starting transfers between devices, local(): first = lax.all_to_all(copies, COL, 0, 0).reshape(256, 512)  11.8 us
    all_to_all x1, starting transfers between devices, trade(): return lax.all_to_all(pieces, ROW, 0, 0, axis_index_groups=groups)  3.6 us
    pallas_call x1, Pallas kernels, local(): pl.pallas_call(update_kernel, out_shape=shape(512, 1024), grid=(4,), in_s...  3.58 us
    unnamed x12, local copies, waits for them, and re-layouts  2.92 us
  transfers between devices with their start and end apart: 2, of which 1 were waited for; matrix products, arithmetic and copies ran while one was open for 1% of the time, Pallas kernels for 0%

profile of v3, /device:TPU:1, one launch (start us, length us, event | category | flops | bytes accessed | tf_op | source)
XLA Modules:
  0.0 137.1 jit_solution(17198053774643887556)
XLA Ops:
  0.0 0.0 copy-start
  0.0 1.8 %broadcast_in_dim.2 = f32[16,16,512]{2,1,0:T(8,128)} broadcast(f32[16,512]{1,0:T(8,128)} %own_ref.1), dimensions={1,2} | broadcast | bytes 557056 | tf_op jit(solution)/shard_map/broadcast_in_dim | solution.py:113
  1.8 11.8 %all-to-all-start = ((f32[16,16,512]{2,1,0:T(8,128)}), f32[16,16,512]{2,1,0:T(8,128)S(1)}, u32[]{:S(2)}, u32[]{:S(2)}) async-start(f32[16,16,512]{2,1,0:T(8,128)} %broadcast_in_dim.2), calls=%async_computation | async-start | bytes 1048576 | tf_op jit(solution)/shard_map/all_to_all | solution.py:114
  13.6 27.4 %all_gather.6.second_ref = f32[256,512]{1,0:T(8,128)S(1)} all-gather(f32[16,512]{1,0:T(8,128)} %param.7), channel_id=1, replica_groups=mesh['x'=4,'y'=8,'z'=8,'core'=2] {'z','core'}, dimensions={0}, use_global_device_ids=true | all-gather | bytes 557056 | tf_op jit(solution)/shard_map/all_gather | solution.py:115
  41.0 0.0 all-to-all-done
  41.0 0.0 copy-done.1
  41.0 2.0 %shard_map.55 = f32[8,544,128]{2,1,0:T(8,128)S(1)} custom-call(f32[256,512]{1,0:T(8,128)S(1)} %all_gather.6.second_ref, f32[256,512]{1,0:T(8,128)S(1)} %bitcast.10, f32[16,512]{1,0:T(8,128)S(1)} %copy-done.4, f32[512,1024]{1,0:T(8,128)S(1)} %copy-done.1), custom_call_target="tpu_custom_call" | custom-call | tf_op jit(solution)/shard_map/pallas_call | solution.py:89
  42.9 32.8 %all_to_all.25.parts = f32[8,544,128]{2,1,0:T(8,128)S(1)} all-to-all(f32[8,544,128]{2,1,0:T(8,128)S(1)} %shard_map.55), channel_id=1, replica_groups={{0,16,128,144,256,272,384,400},{32,48,160,176,288,304,416,432},{64,80,1..., dimensions={0} | all-to-all | bytes 4456448 | tf_op jit(solution)/shard_map/all_to_all | solution.py:109
  75.8 0.1 shard_map.56
  75.9 14.7 %all_to_all.26.parts = f32[4,160,128]{2,1,0:T(8,128)S(1)} all-to-all(f32[4,160,128]{2,1,0:T(8,128)S(1)} %shard_map.56), channel_id=1, replica_groups={{0,32,64,96},{16,48,80,112},{128,160,192,224},{144,176,208,240},{256,28..., dimensions={0} | all-to-all | bytes 655360 | tf_op jit(solution)/shard_map/all_to_all | solution.py:109
  90.6 13.0 %all_to_all.27 = f32[4,128,128]{2,1,0:T(8,128)S(1)} all-to-all(f32[4,128,128]{2,1,0:T(8,128)S(1)} %get-tuple-element.12), channel_id=1, replica_groups={{0,32,64,96},{16,48,80,112},{128,160,192,224},{144,176,208,240},{256,28..., dimensions={0} | all-to-all | bytes 524288 | tf_op jit(solution)/shard_map/all_to_all | solution.py:109
  103.6 0.1 shard_map.59
  103.8 0.0 copy-start.3
  103.8 1.3 copy-done.3
  105.1 3.6 %all-to-all-start.4 = ((f32[8,512,128]{2,1,0:T(8,128)}), f32[8,512,128]{2,1,0:T(8,128)S(1)}, u32[]{:S(2)}, u32[]{:S(2)}) async-start(f32[8,512,128]{2,1,0:T(8,128)} %copy-done.3), calls=%async_computation.4 | async-start | bytes 4194304 | tf_op jit(solution)/shard_map/all_to_all | solution.py:109
  108.7 0.0 copy-start.5
  108.7 0.6 fusion.first_ref
  109.3 18.8 %all_gather.7 = f32[256,256]{1,0:T(8,128)S(1)} all-gather(f32[16,256]{1,0:T(8,128)S(1)} %get-tuple-element.9), channel_id=1, replica_groups=mesh['x'=4,'y'=8,'z'=8,'core'=2] {'z','core'}, dimensions={0}, use_global_device_ids=true | all-gather | bytes 278528 | tf_op jit(solution)/shard_map/all_gather | solution.py:122
  128.1 0.6 convolution_subtract_fusion
  128.8 0.7 convolution_bitcast_fusion.second_ref
  129.4 0.3 shard_map.58
  129.8 2.1 %all-to-all-done.4.proj_ref = f32[8,512,128]{2,1,0:T(8,128)S(1)} async-done(((f32[8,512,128]{2,1,0:T(8,128)}), f32[8,512,128]{2,1,0:T(8,128)S(1)}, u32[]{:S(2)}, u32[]{:S(2)}) %all-to-all-start.4) | async-done | bytes 2097184 | tf_op jit(solution)/shard_map/all_to_all | solution.py:109
  131.9 1.6 %copy-done.2 = f32[512,1024]{1,0:T(8,128)S(1)} copy-done((f32[512,1024]{1,0:T(8,128)S(1)}, f32[512,1024]{1,0:T(8,128)}, u32[]{:S(2)}) %copy-start.2) | copy-done | bytes 2097176
  133.5 3.6 %shard_map.60 = f32[512,1024]{1,0:T(8,128)} custom-call(f32[512,1024]{1,0:T(8,128)S(1)} %copy-done.2, bf16[512,512]{1,0:T(8,128)(2,1)S(1)} %get-tuple-element.10.wh_ref, bf16[512,512]{1,0:T(8,128)(2,1)S(1)} %get-tuple-element.11.wl_ref, f32[8,512,128]{2,1,0:T(8,128)S(1)} %all-to-all-done.4.proj_ref), custom_call_target="tpu_custom_call" | custom-call | tf_op jit(solution)/shard_map/pallas_call | solution.py:126
  (7 shorter events, 0.0 us)
Async XLA Ops:
  0.0 108.7 %copy-start = (f32[256,256]{1,0:T(8,128)S(1)}, f32[256,256]{1,0:T(8,128)}, u32[]{:S(2)}) copy-start(f32[256,256]{1,0:T(8,128)} %param.8) | copy-start | bytes 786436
  0.0 41.0 %copy-start.4 = (f32[16,512]{1,0:T(8,128)S(1)}, f32[16,512]{1,0:T(8,128)}, u32[]{:S(2)}) copy-start(f32[16,512]{1,0:T(8,128)} %own_ref.1) | copy-start | bytes 98308
  0.0 41.0 %copy-start.1 = (f32[512,1024]{1,0:T(8,128)S(1)}, f32[512,1024]{1,0:T(8,128)}, u32[]{:S(2)}) copy-start(f32[512,1024]{1,0:T(8,128)} %block_ref.3) | copy-start | bytes 6291460
  1.8 39.2 %all-to-all-start = ((f32[16,16,512]{2,1,0:T(8,128)}), f32[16,16,512]{2,1,0:T(8,128)S(1)}, u32[]{:S(2)}, u32[]{:S(2)}) async-start(f32[16,16,512]{2,1,0:T(8,128)} %broadcast_in_dim.2), calls=%async_computation | async-start | bytes 1048576 | tf_op jit(solution)/shard_map/all_to_all | solution.py:114
  103.8 1.3 copy-start.3
  105.1 26.9 %all-to-all-start.4 = ((f32[8,512,128]{2,1,0:T(8,128)}), f32[8,512,128]{2,1,0:T(8,128)S(1)}, u32[]{:S(2)}, u32[]{:S(2)}) async-start(f32[8,512,128]{2,1,0:T(8,128)} %copy-done.3), calls=%async_computation.4 | async-start | bytes 4194304 | tf_op jit(solution)/shard_map/all_to_all | solution.py:109
  108.7 20.1 %copy-start.5 = (f32[256,256]{1,0:T(8,128)S(1)}, f32[256,256]{1,0:T(8,128)}, u32[]{:S(2)}) copy-start(f32[256,256]{1,0:T(8,128)} %param.9) | copy-start | bytes 786436
  131.9 1.6 %copy-start.2 = (f32[512,1024]{1,0:T(8,128)S(1)}, f32[512,1024]{1,0:T(8,128)}, u32[]{:S(2)}) copy-start(f32[512,1024]{1,0:T(8,128)} %block_ref.3) | copy-start | bytes 6291460

commit v4 on v3

v4 whole, which is shorter than its diff:
```python
import jax
import jax.numpy as jnp
from jax import lax
from jax.experimental import pallas as pl
from jax.experimental.pallas import tpu as pltpu
from jax.sharding import Mesh, PartitionSpec as P

ROW = ("x", "y")
COL = ("z", "core")
NX, NY, NZ = 4, 8, 8
F32, BF16 = jnp.float32, jnp.bfloat16
VMEM = pl.BlockSpec(memory_space=pltpu.VMEM)
PARAMS = pltpu.CompilerParams(vmem_limit_bytes=24 * 2**20)

NEAR = [[x * NY + y + dy for x in range(NX) for dy in range(2)] for y in range(0, NY, 2)]
FAR = [[x * NY + y for y in range(parity, NY, 2)] for x in range(NX) for parity in range(2)]


def split(value):
    high = value.astype(BF16)
    return high, (value - high.astype(F32)).astype(BF16)


def mul(a, b):
    return jnp.dot(a, b, preferred_element_type=F32)


def mul_nt(a, b):
    return lax.dot_general(a, b, (((1,), (1,)), ((), ())), preferred_element_type=F32)


def mul3(a, b, mul=mul):
    return mul(a[0], b[0]) + (mul(a[0], b[1]) + mul(a[1], b[0]))


def project(panel, block_ref, out):
    for t in range(4):
        value = mul3(panel, split(block_ref[:, t * 256 : (t + 1) * 256]))
        for m in range(8):
            for half in range(2):
                at = (2 * t + half) * 32
                out[m, at : at + 32, :] = value[m * 32 : (m + 1) * 32, half * 128 : (half + 1) * 128]


def second_kernel(second_ref, own_ref, block_ref, out):
    panel = split(second_ref[...])
    project(panel, block_ref, out)
    cross = mul3(split(own_ref[...]), panel, mul_nt)
    for m in range(8):
        out[m, 256:272, :] = cross[:, :128]
        out[m, 272:288, :] = cross[:, 128:]


def first_kernel(first_ref, block_ref, out):
    project(split(first_ref[...]), block_ref, out)


def sum8(parts):
    return ((parts[0] + parts[1]) + (parts[2] + parts[3])) + ((parts[4] + parts[5]) + (parts[6] + parts[7]))


def near_kernel(second_parts, first_parts, out):
    second, first = sum8(second_parts), sum8(first_parts)
    for m in range(4):
        out[m, :64, :] = second[m * 64 : (m + 1) * 64]
        out[m, 64:128, :] = first[m * 64 : (m + 1) * 64]
        out[m, 128:, :] = second[256:]


def far_kernel(parts, out, cross):
    total = (parts[0] + parts[1]) + (parts[2] + parts[3])
    for m in range(4):
        out[m] = total[:128]
    cross[:, :128] = total[128:144]
    cross[:, 128:] = total[144:]


def copy_kernel(share, out):
    for m in range(8):
        for n in range(4):
            out[m, n * 64 : (n + 1) * 64, :] = share[n, :64]
            out[m, 256 + n * 64 : 256 + (n + 1) * 64, :] = share[n, 64:]


def weight_kernel(second_ref, first_ref, high, low):
    for panel, ref in enumerate((second_ref, first_ref)):
        h, l = split(ref[...].T)
        high[:, panel * 256 : (panel + 1) * 256] = h
        low[:, panel * 256 : (panel + 1) * 256] = l


def update_kernel(block_ref, wh_ref, wl_ref, second_ref, first_ref, out):
    rows = [jnp.concatenate([ref[m, :32], ref[m, 32:]], axis=1) for ref in (second_ref, first_ref) for m in range(8)]
    proj = split(jnp.concatenate(rows, axis=0))
    out[...] = block_ref[...] - mul3((wh_ref[...], wl_ref[...]), proj)


def call(kernel, outs, args, scratch=()):
    single = not isinstance(outs, list)
    return pl.pallas_call(
        kernel,
        out_shape=outs,
        in_specs=[VMEM] * len(args),
        out_specs=VMEM if single else [VMEM] * len(outs),
        scratch_shapes=list(scratch),
        compiler_params=PARAMS,
    )(*args)


def shape(*dims, dtype=F32):
    return jax.ShapeDtypeStruct(dims, dtype)


def exact(left, right):
    dims = (((0,), (0,)), ((), ()))
    return lax.dot_general(left, right, dims, precision=lax.Precision.HIGHEST, preferred_element_type=F32)


def trade(pieces, groups):
    return lax.all_to_all(pieces, ROW, 0, 0, axis_index_groups=groups)


def local(vectors, reflectors_first, reflectors_second, factor_first, factor_second):
    second = lax.all_gather(reflectors_second, COL, axis=0, tiled=True)
    second_parts = call(second_kernel, shape(8, 288, 128), (second, reflectors_first, vectors))
    second_parts = trade(second_parts, NEAR)
    first = lax.all_gather(reflectors_first, COL, axis=0, tiled=True)
    first_parts = trade(call(first_kernel, shape(8, 256, 128), (first, vectors)), NEAR)
    parts = call(near_kernel, shape(4, 160, 128), (second_parts, first_parts))
    share, cross = call(far_kernel, [shape(4, 128, 128), shape(16, 256)], (trade(parts, FAR),))
    proj = trade(call(copy_kernel, shape(8, 512, 128), (trade(share, FAR),)), NEAR)
    cross = lax.all_gather(cross, COL, axis=0, tiled=True)
    w_first = exact(factor_first, first)
    w_second = exact(factor_second, second - exact(cross, w_first))
    weights = call(weight_kernel, [shape(512, 512, dtype=BF16)] * 2, (w_second, w_first))
    return pl.pallas_call(
        update_kernel,
        out_shape=shape(512, 1024),
        grid=(4,),
        in_specs=[
            pl.BlockSpec((512, 256), lambda t: (0, t)),
            pl.BlockSpec((512, 512), lambda t: (0, 0)),
            pl.BlockSpec((512, 512), lambda t: (0, 0)),
            pl.BlockSpec((8, 64, 128), lambda t: (0, t, 0)),
            pl.BlockSpec((8, 64, 128), lambda t: (0, t + 4, 0)),
        ],
        out_specs=pl.BlockSpec((512, 256), lambda t: (0, t)),
        compiler_params=PARAMS,
    )(vectors, *weights, proj, proj)


def solution(mesh):
    fine = Mesh(mesh.devices.reshape(NX, NY, NZ, 2), ROW + COL)
    return jax.shard_map(
        local,
        mesh=fine,
        in_specs=(P(ROW, COL), P(COL, ROW), P(COL, ROW), P(), P()),
        out_specs=P(ROW, COL),
        check_vma=False,
    )
```

time: 140 us -> 143 us (1.021)
  the two profiles are of different devices: /device:TPU:1 before, /device:TPU:64 now
where the time goes in v4:
time: 143 us; the launch traced here: 142 us
  blocking collectives  109 us (76%)
  starting transfers between devices  9.79 us (7%)
  Pallas kernels  8.93 us (6%)
  local copies, waits for them, and re-layouts  6.77 us (5%)
  waiting for transfers between devices  6.05 us (4%)
  matrix products  1.93 us (1%)
    all_to_all x3, blocking collectives, trade(): return lax.all_to_all(pieces, ROW, 0, 0, axis_index_groups=groups)  53.4 us
    all_gather x1, blocking collectives, local(): first = lax.all_gather(reflectors_first, COL, axis=0, tiled=True)  21.9 us
    all_gather x1, blocking collectives, local(): second = lax.all_gather(reflectors_second, COL, axis=0, tiled=True)  18.3 us
    all_gather x1, blocking collectives, local(): cross = lax.all_gather(cross, COL, axis=0, tiled=True)  15 us
    all_to_all x2, starting transfers between devices, trade(): return lax.all_to_all(pieces, ROW, 0, 0, axis_index_groups=groups)  9.79 us
    unnamed x22, local copies, waits for them, and re-layouts  6.77 us
    all_to_all x2, waiting for transfers between devices, trade(): return lax.all_to_all(pieces, ROW, 0, 0, axis_index_groups=groups)  6.05 us
    pallas_call x1, Pallas kernels, local(): pl.pallas_call(update_kernel, out_shape=shape(512, 1024), grid=(4,), in_s...  4.96 us
  transfers between devices with their start and end apart: 2, of which 1 were waited for; matrix products, arithmetic and copies ran while one was open for 1% of the time, Pallas kernels for 1%

profile of v4, /device:TPU:64, one launch (start us, length us, event | category | flops | bytes accessed | tf_op | source)
XLA Modules:
  0.0 142.2 jit_solution(5113705814783371326)
XLA Ops:
  0.0 21.9 %all_gather.10.first_ref = f32[256,512]{1,0:T(8,128)S(1)} all-gather(f32[16,512]{1,0:T(8,128)} %own_ref.1), channel_id=1, replica_groups=mesh['x'=4,'y'=8,'z'=8,'core'=2] {'z','core'}, dimensions={0}, use_global_device_ids=true | all-gather | bytes 557056 | tf_op jit(solution)/shard_map/all_gather | solution.py:127
  21.9 1.6 %copy-done.1 = f32[512,1024]{1,0:T(8,128)S(1)} copy-done((f32[512,1024]{1,0:T(8,128)S(1)}, f32[512,1024]{1,0:T(8,128)}, u32[]{:S(2)}) %copy-start.1) | copy-done | bytes 2097176
  23.5 1.0 shard_map.56
  24.5 1.0 copy-done.5
  25.5 5.4 %all-to-all-start.1 = ((f32[8,256,128]{2,1,0:T(8,128)}), f32[8,256,128]{2,1,0:T(8,128)}, u32[]{:S(2)}, u32[]{:S(2)}) async-start(f32[8,256,128]{2,1,0:T(8,128)} %copy-done.5), calls=%async_computation.1 | async-start | bytes 2097152 | tf_op jit(solution)/shard_map/all_to_all | solution.py:120
  30.9 18.3 %all_gather.9.second_ref = f32[256,512]{1,0:T(8,128)S(1)} all-gather(f32[16,512]{1,0:T(8,128)S(1)} %copy-done.10), channel_id=1, replica_groups=mesh['x'=4,'y'=8,'z'=8,'core'=2] {'z','core'}, dimensions={0}, use_global_device_ids=true | all-gather | bytes 557056 | tf_op jit(solution)/shard_map/all_gather | solution.py:124
  49.2 1.1 shard_map.55
  50.4 1.0 copy-done.4
  51.4 23.4 %all_to_all.25.second_parts = f32[8,288,128]{2,1,0:T(8,128)S(1)} all-to-all(f32[8,288,128]{2,1,0:T(8,128)} %copy-done.4), channel_id=1, replica_groups={{0,16,128,144,256,272,384,400},{32,48,160,176,288,304,416,432},{64,80,1..., dimensions={0} | all-to-all | bytes 2359296 | tf_op jit(solution)/shard_map/all_to_all | solution.py:120
  74.8 1.3 shard_map.57
  76.1 17.8 %all_to_all.26.parts = f32[4,160,128]{2,1,0:T(8,128)S(1)} all-to-all(f32[4,160,128]{2,1,0:T(8,128)S(1)} %shard_map.57), channel_id=1, replica_groups={{0,32,64,96},{16,48,80,112},{128,160,192,224},{144,176,208,240},{256,28..., dimensions={0} | all-to-all | bytes 655360 | tf_op jit(solution)/shard_map/all_to_all | solution.py:120
  94.0 12.2 %all_to_all.27.share = f32[4,128,128]{2,1,0:T(8,128)S(1)} all-to-all(f32[4,128,128]{2,1,0:T(8,128)S(1)} %get-tuple-element.12), channel_id=1, replica_groups={{0,32,64,96},{16,48,80,112},{128,160,192,224},{144,176,208,240},{256,28..., dimensions={0} | all-to-all | bytes 524288 | tf_op jit(solution)/shard_map/all_to_all | solution.py:120
  106.2 0.1 shard_map.60
  106.3 1.3 copy-done.3
  107.6 4.3 %all-to-all-start.4 = ((f32[8,512,128]{2,1,0:T(8,128)}), f32[8,512,128]{2,1,0:T(8,128)}, u32[]{:S(2)}, u32[]{:S(2)}) async-start(f32[8,512,128]{2,1,0:T(8,128)} %copy-done.3), calls=%async_computation.4 | async-start | bytes 4194304 | tf_op jit(solution)/shard_map/all_to_all | solution.py:120
  112.0 0.6 fusion.first_ref
  112.6 15.0 %all_gather.11 = f32[256,256]{1,0:T(8,128)S(1)} all-gather(f32[16,256]{1,0:T(8,128)S(1)} %get-tuple-element.9), channel_id=1, replica_groups=mesh['x'=4,'y'=8,'z'=8,'core'=2] {'z','core'}, dimensions={0}, use_global_device_ids=true | all-gather | bytes 278528 | tf_op jit(solution)/shard_map/all_gather | solution.py:132
  127.6 0.6 convolution_subtract_fusion
  128.3 0.7 convolution_bitcast_fusion.second_ref
  129.0 0.3 shard_map.59
  129.3 0.8 copy-done.6
  130.1 6.0 %all-to-all-done.4.second_ref.first_ref = f32[8,512,128]{2,1,0:T(8,128)} async-done(((f32[8,512,128]{2,1,0:T(8,128)}), f32[8,512,128]{2,1,0:T(8,128)}, u32[]{:S(2)}, u32[]{:S(2)}) %all-to-all-start.4) | async-done | bytes 2097184 | tf_op jit(solution)/shard_map/all_to_all | solution.py:120
  136.2 1.0 copy-done.7
  137.2 5.0 %shard_map.61 = f32[512,1024]{1,0:T(8,128)} custom-call(f32[512,1024]{1,0:T(8,128)S(1)} %copy-done.2, bf16[512,512]{1,0:T(8,128)(2,1)S(1)} %get-tuple-element.10.wh_ref, bf16[512,512]{1,0:T(8,128)(2,1)S(1)} %copy-done.7, f32[8,512,128]{2,1,0:T(8,128)} %all-to-all-done.4.second_ref.first_ref, f32[8,512,128]{2,1,0:T(8,128)} %all-to-all-done.4.second_ref.first_ref), custom_call_target="tpu_custom_call" | custom-call | tf_op jit(solution)/shard_map/pallas_call | solution.py:136
  (18 shorter events, 0.1 us)
Async XLA Ops:
  0.0 112.0 %copy-start = (f32[256,256]{1,0:T(8,128)S(1)}, f32[256,256]{1,0:T(8,128)}, u32[]{:S(2)}) copy-start(f32[256,256]{1,0:T(8,128)} %param.8) | copy-start | bytes 786436
  21.9 1.6 %copy-start.1 = (f32[512,1024]{1,0:T(8,128)S(1)}, f32[512,1024]{1,0:T(8,128)}, u32[]{:S(2)}) copy-start(f32[512,1024]{1,0:T(8,128)} %block_ref.5) | copy-start | bytes 6291460
  23.5 7.5 %copy-start.10 = (f32[16,512]{1,0:T(8,128)S(1)}, f32[16,512]{1,0:T(8,128)}, u32[]{:S(2)}) copy-start(f32[16,512]{1,0:T(8,128)} %param.7) | copy-start | bytes 98308
  24.5 1.0 copy-start.5
  25.5 23.7 %copy-start.2 = (f32[512,1024]{1,0:T(8,128)S(1)}, f32[512,1024]{1,0:T(8,128)}, u32[]{:S(2)}) copy-start(f32[512,1024]{1,0:T(8,128)} %block_ref.5) | copy-start | bytes 6291460
  25.5 23.7 %copy-start.8 = (f32[16,512]{1,0:T(8,128)S(1)}, f32[16,512]{1,0:T(8,128)}, u32[]{:S(2)}) copy-start(f32[16,512]{1,0:T(8,128)} %own_ref.1) | copy-start | bytes 98308
  25.5 25.9 %all-to-all-start.1 = ((f32[8,256,128]{2,1,0:T(8,128)}), f32[8,256,128]{2,1,0:T(8,128)}, u32[]{:S(2)}, u32[]{:S(2)}) async-start(f32[8,256,128]{2,1,0:T(8,128)} %copy-done.5), calls=%async_computation.1 | async-start | bytes 2097152 | tf_op jit(solution)/shard_map/all_to_all | solution.py:120
  50.4 1.0 copy-start.4
  106.3 1.3 copy-start.3
  107.6 28.6 %all-to-all-start.4 = ((f32[8,512,128]{2,1,0:T(8,128)}), f32[8,512,128]{2,1,0:T(8,128)}, u32[]{:S(2)}, u32[]{:S(2)}) async-start(f32[8,512,128]{2,1,0:T(8,128)} %copy-done.3), calls=%async_computation.4 | async-start | bytes 4194304 | tf_op jit(solution)/shard_map/all_to_all | solution.py:120
  112.0 16.3 %copy-start.9 = (f32[256,256]{1,0:T(8,128)S(1)}, f32[256,256]{1,0:T(8,128)}, u32[]{:S(2)}) copy-start(f32[256,256]{1,0:T(8,128)} %param.9) | copy-start | bytes 786436
  129.3 0.8 copy-start.6
  136.2 1.0 copy-start.7

commit v5 on v3

v5 whole, which is shorter than its diff:
```python
import jax
import jax.numpy as jnp
from jax import lax
from jax.experimental import pallas as pl
from jax.experimental.pallas import tpu as pltpu
from jax.sharding import Mesh, PartitionSpec as P

ROW = ("x", "y")
COL = ("z", "core")
NX, NY, NZ = 4, 8, 8
F32, BF16 = jnp.float32, jnp.bfloat16
VMEM = pl.BlockSpec(memory_space=pltpu.VMEM)
SMEM = pl.BlockSpec(memory_space=pltpu.SMEM)
HBM = pl.BlockSpec(memory_space=pltpu.HBM)
PARAMS = pltpu.CompilerParams(vmem_limit_bytes=48 * 2**20)

NEAR = [[x * NY + y + dy for x in range(NX) for dy in range(2)] for y in range(0, NY, 2)]
FAR = [[x * NY + y for y in range(parity, NY, 2)] for x in range(NX) for parity in range(2)]


def split(value):
    high = value.astype(BF16)
    return high, (value - high.astype(F32)).astype(BF16)


def mul(a, b):
    return jnp.dot(a, b, preferred_element_type=F32)


def mul_nt(a, b):
    return lax.dot_general(a, b, (((1,), (1,)), ((), ())), preferred_element_type=F32)


def mul3(a, b, mul=mul):
    return mul(a[0], b[0]) + (mul(a[0], b[1]) + mul(a[1], b[0]))


def split_kernel(block_ref, high, low):
    high[...], low[...] = split(block_ref[...])


def project_kernel(core_ref, mine_ref, other_ref, own_ref, block_high, block_low, out, high, low, both):
    core = core_ref[0]
    both[0] = mine_ref[...]
    both[1] = other_ref[...]
    for c in range(2):
        from_core = both.at[core ^ c]
        for z in range(8):
            for panel in range(2):
                h, l = split(from_core[z, panel * 16 : panel * 16 + 16, :])
                at = panel * 256 + z * 32 + c * 16
                high[at : at + 16, :] = h
                low[at : at + 16, :] = l
    for t in range(4):
        at = slice(t * 256, (t + 1) * 256)
        value = mul3((high[...], low[...]), (block_high[:, at], block_low[:, at]))
        for m in range(8):
            for half in range(2):
                at = (2 * t + half) * 64
                out[m, at : at + 64, :] = value[m * 64 : (m + 1) * 64, half * 128 : (half + 1) * 128]
    cross = mul3(split(own_ref[...]), (high[:256], low[:256]), mul_nt)
    for m in range(8):
        out[m, 512:528, :] = cross[:, :128]
        out[m, 528:544, :] = cross[:, 128:]


def near_kernel(parts, out):
    total = ((parts[0] + parts[1]) + (parts[2] + parts[3])) + ((parts[4] + parts[5]) + (parts[6] + parts[7]))
    for m in range(4):
        out[m, :128, :] = total[m * 128 : (m + 1) * 128]
        out[m, 128:, :] = total[512:]


def far_kernel(parts, out, cross):
    total = (parts[0] + parts[1]) + (parts[2] + parts[3])
    for m in range(4):
        out[m] = total[:128]
    cross[:, :128] = total[128:144]
    cross[:, 128:] = total[144:]


def copy_kernel(share, out, sems):
    copies = [pltpu.make_async_copy(share, out.at[m], sems.at[m]) for m in range(8)]
    for copy in copies:
        copy.start()
    for copy in copies:
        copy.wait()


def weight_kernel(second_ref, first_ref, out):
    for panel, ref in enumerate((second_ref, first_ref)):
        out[0, :, panel * 256 : (panel + 1) * 256], out[1, :, panel * 256 : (panel + 1) * 256] = split(ref[...].T)


def update_kernel(block_ref, w_ref, proj_ref, out_ref, block, parts, out, block_sems, part_sems, out_sems):
    at = [slice(t * 256, (t + 1) * 256) for t in range(4)]
    rows = [slice(t * 128, (t + 1) * 128) for t in range(4)]
    reads = [pltpu.make_async_copy(proj_ref.at[:, rows[t]], parts.at[:, rows[t]], part_sems.at[t]) for t in range(4)]
    reads += [pltpu.make_async_copy(block_ref.at[:, at[t]], block.at[:, at[t]], block_sems.at[t]) for t in range(4)]
    writes = [pltpu.make_async_copy(out.at[:, at[t]], out_ref.at[:, at[t]], out_sems.at[t]) for t in range(4)]
    for read in reads:
        read.start()
    for t in range(4):
        first = t * 128
        reads[t].wait()
        proj = jnp.concatenate(
            [
                jnp.concatenate([parts[m, first : first + 64], parts[m, first + 64 : first + 128]], axis=1)
                for m in range(8)
            ],
            axis=0,
        )
        change = mul3((w_ref[0], w_ref[1]), split(proj))
        reads[4 + t].wait()
        out[:, at[t]] = block[:, at[t]] - change
        writes[t].start()
    for write in writes:
        write.wait()


def call(kernel, outs, args, scratch=(), scalars=0, inputs=None, out_spec=VMEM):
    single = not isinstance(outs, list)
    return pl.pallas_call(
        kernel,
        out_shape=outs,
        in_specs=inputs or [SMEM] * scalars + [VMEM] * (len(args) - scalars),
        out_specs=out_spec if single else [out_spec] * len(outs),
        scratch_shapes=list(scratch),
        compiler_params=PARAMS,
    )(*args)


def shape(*dims, dtype=F32):
    return jax.ShapeDtypeStruct(dims, dtype)


def exact(left, right):
    dims = (((0,), (0,)), ((), ()))
    return lax.dot_general(left, right, dims, precision=lax.Precision.HIGHEST, preferred_element_type=F32)


def trade(pieces, groups):
    return lax.all_to_all(pieces, ROW, 0, 0, axis_index_groups=groups)


def local(vectors, reflectors_first, reflectors_second, factor_first, factor_second):
    core = lax.axis_index("core")
    shards = jnp.concatenate([reflectors_second, reflectors_first], axis=0)
    mine = lax.all_to_all(jnp.broadcast_to(shards[None], (NZ,) + shards.shape), "z", 0, 0)
    other = lax.ppermute(mine, "core", [(0, 1), (1, 0)])
    wide = pltpu.VMEM((512, 512), BF16)
    block = call(split_kernel, [shape(512, 1024, dtype=BF16)] * 2, (vectors,))
    parts = call(
        project_kernel,
        shape(8, 544, 128),
        (core.astype(jnp.int32).reshape(1), mine, other, reflectors_first, *block),
        (wide, wide, pltpu.VMEM((2, 8, 32, 512), F32)),
        scalars=1,
    )
    parts = call(near_kernel, shape(4, 160, 128), (trade(parts, NEAR),))
    share, cross = call(far_kernel, [shape(4, 128, 128), shape(16, 256)], (trade(parts, FAR),))
    share = trade(share, FAR).reshape(512, 128)
    copies = call(copy_kernel, shape(8, 512, 128), (share,), (pltpu.SemaphoreType.DMA((8,)),), out_spec=HBM)
    proj = trade(copies, NEAR)
    cross = lax.all_gather(cross, COL, axis=0, tiled=True)
    by_core = jnp.stack([jnp.where(core == 0, mine, other), jnp.where(core == 0, other, mine)], axis=1)
    second = by_core[:, :, :16].reshape(256, 512)
    first = by_core[:, :, 16:].reshape(256, 512)
    w_first = exact(factor_first, first)
    w_second = exact(factor_second, second - exact(cross, w_first))
    weights = call(weight_kernel, shape(2, 512, 512, dtype=BF16), (w_second, w_first))
    whole = pltpu.VMEM((512, 1024), F32)
    four = pltpu.SemaphoreType.DMA((4,))
    return call(
        update_kernel,
        shape(512, 1024),
        (vectors, weights, proj),
        (whole, pltpu.VMEM((8, 512, 128), F32), whole, four, four, four),
        inputs=[HBM, VMEM, HBM],
        out_spec=HBM,
    )


def solution(mesh):
    fine = Mesh(mesh.devices.reshape(NX, NY, NZ, 2), ROW + COL)
    return jax.shard_map(
        local,
        mesh=fine,
        in_specs=(P(ROW, COL), P(COL, ROW), P(COL, ROW), P(), P()),
        out_specs=P(ROW, COL),
        check_vma=False,
    )
```

time: 140 us -> 136 us (0.971)
  starting transfers between devices: 15.4 us -> 8.72 us
  Pallas kernels: 6.14 us -> 10.2 us
  local copies, waits for them, and re-layouts: 4.68 us -> 2.76 us
    all_gather x1 -> x0, blocking collectives: 27.4 us -> none  [local(): second = lax.all_gather(reflectors_second, COL, axis=0, tiled=True)]
    all_to_all x0 -> x1, blocking collectives: none -> 26.7 us  [local(): lax.all_to_all(jnp.broadcast_to(shards[None], (NZ,) + shards.shape), 'z',...]
    all_to_all x1 -> x0, starting transfers between devices: 11.8 us -> none  [local(): first = lax.all_to_all(copies, COL, 0, 0).reshape(256, 512)]
    ppermute x0 -> x1, starting transfers between devices: none -> 4.35 us  [local(): other = lax.ppermute(mine, 'core', [(0, 1), (1, 0)])]
    pallas_call x6 -> x7, Pallas kernels: 6.14 us -> 10.2 us  [call(): pl.pallas_call(kernel, out_shape=outs, in_specs=inputs or [SMEM] * scalar...]
    broadcast_in_dim x1, local copies, waits for them, and re-layouts: 1.76 us -> 0.05 us  [local(): jnp.broadcast_to(shards[None], (NZ,) + shards.shape)]
  transfers between devices with their start and end apart: 2 -> 2, of which waited for: 1 -> 1; matrix products, arithmetic and copies ran while one was open for 1% -> 3% of each run, Pallas kernels for 0% -> 0%
where the time goes in v5:
time: 136 us; the launch traced here: 134 us
  blocking collectives  106 us (78%)
  Pallas kernels  10.2 us (7%)
  starting transfers between devices  8.72 us (6%)
  local copies, waits for them, and re-layouts  2.76 us (2%)
  matrix products  2.72 us (2%)
  waiting for transfers between devices  2.08 us (2%)
    all_to_all x3, blocking collectives, trade(): return lax.all_to_all(pieces, ROW, 0, 0, axis_index_groups=groups)  61.8 us
    all_to_all x1, blocking collectives, local(): lax.all_to_all(jnp.broadcast_to(shards[None], (NZ,) + shards.shape), 'z',...  26.7 us
    all_gather x1, blocking collectives, local(): cross = lax.all_gather(cross, COL, axis=0, tiled=True)  17.7 us
    pallas_call x7, Pallas kernels, call(): pl.pallas_call(kernel, out_shape=outs, in_specs=inputs or [SMEM] * scalar...  10.2 us
    all_to_all x1, starting transfers between devices, trade(): return lax.all_to_all(pieces, ROW, 0, 0, axis_index_groups=groups)  4.37 us
    ppermute x1, starting transfers between devices, local(): other = lax.ppermute(mine, 'core', [(0, 1), (1, 0)])  4.35 us
  transfers between devices with their start and end apart: 2, of which 1 were waited for; matrix products, arithmetic and copies ran while one was open for 3% of the time, Pallas kernels for 0%

profile of v5, /device:TPU:1, one launch (start us, length us, event | category | flops | bytes accessed | tf_op | source)
XLA Modules:
  0.0 133.9 jit_solution(179089360169035)
XLA Ops:
  0.0 0.8 pad_maximum_fusion.1
  0.9 26.7 %all_to_all.25.mine_ref = f32[8,32,512]{2,1,0:T(8,128)S(1)} all-to-all(f32[8,32,512]{2,1,0:T(8,128)S(1)} %broadcast_in_dim.2), channel_id=1, replica_groups=mesh['x'=4,'y'=8,'z'=8,'core'=2] {'z'}, dimensions={0} | all-to-all | bytes 1048576 | tf_op jit(solution)/shard_map/all_to_all | solution.py:149
  27.6 4.4 %collective-permute-start = (f32[8,32,512]{2,1,0:T(8,128)S(1)}, f32[8,32,512]{2,1,0:T(8,128)S(1)}, u32[]{:S(2)}, u32[]{:S(2)}) collective-permute-start(f32[8,32,512]{2,1,0:T(8,128)S(1)} %all_to_all.25.mine_ref), channel_id=1, source_target_pairs={{0,1},{1,0},{2,3},{3,2},{4,5},{5,4},{6,7},{7,6},{8,9},{9,8},{10,11... | collective-permute-start | bytes 1572872 | tf_op jit(solution)/shard_map/ppermute | solution.py:150
  31.9 0.0 copy-start.1
  31.9 1.6 %copy-done.1 = f32[512,1024]{1,0:T(8,128)S(1)} copy-done((f32[512,1024]{1,0:T(8,128)S(1)}, f32[512,1024]{1,0:T(8,128)}, u32[]{:S(2)}) %copy-start.1) | copy-done | bytes 2097176
  33.5 0.3 shard_map.55
  33.8 2.0 %shard_map.56 = f32[8,544,128]{2,1,0:T(8,128)S(1)} custom-call(s32[1]{0:T(128)} %bitcast.3.core_ref, f32[8,32,512]{2,1,0:T(8,128)S(1)} %all_to_all.25.mine_ref, f32[8,32,512]{2,1,0:T(8,128)S(1)} %collective-permute-done.other_ref, f32[16,512]{1,0:T(8,128)S(1)} %copy-done.4, bf16[512,1024]{1,0:T(8,128)(2,1)S(1)} %get-tuple-element.9.block_high, ...), custom_call_target="tpu_custom_call" | custom-call | tf_op jit(solution)/shard_map/pallas_call | solution.py:123
  35.9 33.0 %all_to_all.26.parts = f32[8,544,128]{2,1,0:T(8,128)S(1)} all-to-all(f32[8,544,128]{2,1,0:T(8,128)S(1)} %shard_map.56), channel_id=1, replica_groups={{0,16,128,144,256,272,384,400},{32,48,160,176,288,304,416,432},{64,80,1..., dimensions={0} | all-to-all | bytes 4456448 | tf_op jit(solution)/shard_map/all_to_all | solution.py:143
  68.9 0.1 shard_map.57
  69.0 15.2 %all_to_all.27.parts = f32[4,160,128]{2,1,0:T(8,128)S(1)} all-to-all(f32[4,160,128]{2,1,0:T(8,128)S(1)} %shard_map.57), channel_id=1, replica_groups={{0,32,64,96},{16,48,80,112},{128,160,192,224},{144,176,208,240},{256,28..., dimensions={0} | all-to-all | bytes 655360 | tf_op jit(solution)/shard_map/all_to_all | solution.py:143
  84.2 13.6 %all_to_all.28 = f32[4,128,128]{2,1,0:T(8,128)S(1)} all-to-all(f32[4,128,128]{2,1,0:T(8,128)S(1)} %get-tuple-element.12), channel_id=1, replica_groups={{0,32,64,96},{16,48,80,112},{128,160,192,224},{144,176,208,240},{256,28..., dimensions={0} | all-to-all | bytes 524288 | tf_op jit(solution)/shard_map/all_to_all | solution.py:143
  97.8 1.4 %shard_map.60 = f32[8,512,128]{2,1,0:T(8,128)} custom-call(f32[512,128]{1,0:T(8,128)S(1)} %bitcast.18), custom_call_target="tpu_custom_call" | custom-call | tf_op jit(solution)/shard_map/pallas_call | solution.py:123
  99.2 4.4 %all-to-all-start.4 = ((f32[8,512,128]{2,1,0:T(8,128)}), f32[8,512,128]{2,1,0:T(8,128)}, u32[]{:S(2)}, u32[]{:S(2)}) async-start(f32[8,512,128]{2,1,0:T(8,128)} %shard_map.60), calls=%async_computation.4 | async-start | bytes 4194304 | tf_op jit(solution)/shard_map/all_to_all | solution.py:143
  103.6 0.1 select_bitcast_fusion
  103.7 0.1 pad_maximum_fusion
  103.9 1.0 fusion.1
  105.0 1.0 copy.11
  106.0 17.7 %all_gather.3 = f32[256,256]{1,0:T(8,128)S(1)} all-gather(f32[16,256]{1,0:T(8,128)S(1)} %get-tuple-element.11), channel_id=1, replica_groups=mesh['x'=4,'y'=8,'z'=8,'core'=2] {'z','core'}, dimensions={0}, use_global_device_ids=true | all-gather | bytes 278528 | tf_op jit(solution)/shard_map/all_gather | solution.py:165
  123.7 1.0 convolution_subtract_fusion
  124.7 0.0 copy-start.2
  124.8 0.7 convolution_bitcast_fusion.second_ref
  125.4 0.3 shard_map.59.w_ref
  125.8 2.1 %all-to-all-done.4.proj_ref = f32[8,512,128]{2,1,0:T(8,128)} async-done(((f32[8,512,128]{2,1,0:T(8,128)}), f32[8,512,128]{2,1,0:T(8,128)}, u32[]{:S(2)}, u32[]{:S(2)}) %all-to-all-start.4) | async-done | bytes 2097184 | tf_op jit(solution)/shard_map/all_to_all | solution.py:143
  127.9 6.1 %shard_map.61 = f32[512,1024]{1,0:T(8,128)} custom-call(f32[512,1024]{1,0:T(8,128)S(1)} %copy-done.2, bf16[2,512,512]{2,1,0:T(8,128)(2,1)S(1)} %shard_map.59.w_ref, f32[8,512,128]{2,1,0:T(8,128)} %all-to-all-done.4.proj_ref), custom_call_target="tpu_custom_call" | custom-call | tf_op jit(solution)/shard_map/pallas_call | solution.py:123
  (14 shorter events, 0.2 us)
Async XLA Ops:
  0.0 103.9 %copy-start = (f32[256,256]{1,0:T(8,128)S(1)}, f32[256,256]{1,0:T(8,128)}, u32[]{:S(2)}) copy-start(f32[256,256]{1,0:T(8,128)} %param.8) | copy-start | bytes 786436
  0.0 33.8 %copy-start.4 = (f32[16,512]{1,0:T(8,128)S(1)}, f32[16,512]{1,0:T(8,128)}, u32[]{:S(2)}) copy-start(f32[16,512]{1,0:T(8,128)} %own_ref.1) | copy-start | bytes 98308
  27.6 6.3 %collective-permute-start = (f32[8,32,512]{2,1,0:T(8,128)S(1)}, f32[8,32,512]{2,1,0:T(8,128)S(1)}, u32[]{:S(2)}, u32[]{:S(2)}) collective-permute-start(f32[8,32,512]{2,1,0:T(8,128)S(1)} %all_to_all.25.mine_ref), channel_id=1, source_target_pairs={{0,1},{1,0},{2,3},{3,2},{4,5},{5,4},{6,7},{7,6},{8,9},{9,8},{10,11... | collective-permute-start | bytes 1572872 | tf_op jit(solution)/shard_map/ppermute | solution.py:150
  31.9 1.6 %copy-start.1 = (f32[512,1024]{1,0:T(8,128)S(1)}, f32[512,1024]{1,0:T(8,128)}, u32[]{:S(2)}) copy-start(f32[512,1024]{1,0:T(8,128)} %block_ref.3) | copy-start | bytes 6291460
  99.2 28.7 %all-to-all-start.4 = ((f32[8,512,128]{2,1,0:T(8,128)}), f32[8,512,128]{2,1,0:T(8,128)}, u32[]{:S(2)}, u32[]{:S(2)}) async-start(f32[8,512,128]{2,1,0:T(8,128)} %shard_map.60), calls=%async_computation.4 | async-start | bytes 4194304 | tf_op jit(solution)/shard_map/all_to_all | solution.py:143
  103.9 20.8 %copy-start.5 = (f32[256,256]{1,0:T(8,128)S(1)}, f32[256,256]{1,0:T(8,128)}, u32[]{:S(2)}) copy-start(f32[256,256]{1,0:T(8,128)} %param.9) | copy-start | bytes 786436
  106.0 19.5 %copy-start.3 = (f32[512,256]{0,1:T(8,128)S(1)}, f32[512,256]{0,1:T(8,128)}, u32[]{:S(2)}) copy-start(f32[512,256]{0,1:T(8,128)} %copy.11) | copy-start | bytes 1572868
  124.7 3.1 %copy-start.2 = (f32[512,1024]{1,0:T(8,128)S(1)}, f32[512,1024]{1,0:T(8,128)}, u32[]{:S(2)}) copy-start(f32[512,1024]{1,0:T(8,128)} %block_ref.3) | copy-start | bytes 6291460

commit v6 on v3

v6 whole, which is shorter than its diff:
```python
import jax
import jax.numpy as jnp
from jax import lax
from jax.experimental import pallas as pl
from jax.experimental.pallas import tpu as pltpu
from jax.sharding import Mesh, PartitionSpec as P

ROW = ("x", "y")
COL = ("z", "core")
NX, NY, NZ = 4, 8, 8
F32, BF16 = jnp.float32, jnp.bfloat16
VMEM = pl.BlockSpec(memory_space=pltpu.VMEM)
SMEM = pl.BlockSpec(memory_space=pltpu.SMEM)
HBM = pl.BlockSpec(memory_space=pltpu.HBM)

NEAR = [[x * NY + y + dy for x in range(NX) for dy in range(2)] for y in range(0, NY, 2)]


def split(value):
    high = value.astype(BF16)
    return high, (value - high.astype(F32)).astype(BF16)


def mul(a, b):
    return jnp.dot(a, b, preferred_element_type=F32)


def mul_nt(a, b):
    return lax.dot_general(a, b, (((1,), (1,)), ((), ())), preferred_element_type=F32)


def mul3(a, b, mul=mul):
    return mul(a[0], b[0]) + (mul(a[0], b[1]) + mul(a[1], b[0]))


def split_kernel(block_ref, high, low):
    high[...], low[...] = split(block_ref[...])


def project(chain, block_high, block_low, out):
    for t in range(4):
        at = slice(t * 256, (t + 1) * 256)
        value = mul3(chain, (block_high[:, at], block_low[:, at]))
        for m in range(8):
            for half in range(2):
                to = (2 * t + half) * 32
                out[m, to : to + 32, :] = value[m * 32 : (m + 1) * 32, half * 128 : (half + 1) * 128]


def mine_kernel(mine_ref, block_high, block_low, out):
    project(split(mine_ref[...]), block_high, block_low, out)


def other_kernel(core_ref, mine_ref, other_ref, own_ref, block_high, block_low, out, both, second):
    project(split(other_ref[...]), block_high, block_low, out)
    core = core_ref[0]
    both[0] = mine_ref[...]
    both[1] = other_ref[...]
    for c in range(2):
        from_core = both.at[core ^ c]
        for z in range(8):
            second[z * 32 + c * 16 : z * 32 + c * 16 + 16, :] = from_core[z * 32 : z * 32 + 16, :]
    cross = mul3(split(own_ref[...]), split(second[...]), mul_nt)
    for m in range(8):
        out[m, 256:272, :] = cross[:, :128]
        out[m, 272:288, :] = cross[:, 128:]


def near_kernel(parts, out):
    out[...] = ((parts[0] + parts[1]) + (parts[2] + parts[3])) + ((parts[4] + parts[5]) + (parts[6] + parts[7]))


def add_kernel(share, got, out):
    out[...] = share[...] + got[...]


def mine_copy_kernel(share, got, out):
    total = share[...] + got[...]
    for m in range(8):
        out[m] = total


def other_copy_kernel(share, got, out, cross):
    total = share[...] + got[...]
    for m in range(8):
        out[m] = total[:256]
    cross[:, :128] = total[256:272]
    cross[:, 128:] = total[272:]


def natural(parts):
    return jnp.concatenate(
        [jnp.concatenate([parts[m, t * 32 : (t + 1) * 32] for t in range(8)], axis=1) for m in range(8)], axis=0
    )


def prepare_kernel(core_ref, second_ref, first_ref, parts, out, rows):
    core = core_ref[0]
    for c in range(2):
        for z in range(8):
            at = pl.ds(pl.multiple_of(z * 32 + (core ^ c) * 16, 16), 16)
            to = c * 256 + z * 32
            rows[to : to + 16, :] = second_ref[at, :]
            rows[to + 16 : to + 32, :] = first_ref[at, :]
    out[0], out[1] = split(rows[...].T)
    high, low = split(natural(parts))
    for half in range(2):
        out[2, half * 256 : (half + 1) * 256] = high[:, half * 512 : (half + 1) * 512]
        out[3, half * 256 : (half + 1) * 256] = low[:, half * 512 : (half + 1) * 512]


def update_kernel(block_ref, ready_ref, parts_ref, out_ref, block, ready, parts, high, low, out, reads, writes):
    loads = [pltpu.make_async_copy(parts_ref, parts, reads.at[0])]
    loads.append(pltpu.make_async_copy(ready_ref, ready, reads.at[1]))
    for t in range(2):
        rows = slice(t * 256, (t + 1) * 256)
        loads.append(pltpu.make_async_copy(block_ref.at[rows], block.at[rows], reads.at[2 + t]))
    for load in loads:
        load.start()
    loads[0].wait()
    high[256:], low[256:] = split(natural(parts))
    loads[1].wait()
    for half in range(2):
        at = slice(half * 512, (half + 1) * 512)
        high[:256, at] = ready[2, half * 256 : (half + 1) * 256]
        low[:256, at] = ready[3, half * 256 : (half + 1) * 256]
    stores = []
    for t in range(2):
        rows = slice(t * 256, (t + 1) * 256)
        loads[2 + t].wait()
        for u in range(4):
            at = slice(u * 256, (u + 1) * 256)
            change = mul3((ready[0, rows], ready[1, rows]), (high[:, at], low[:, at]))
            out[rows, at] = block[rows, at] - change
        stores.append(pltpu.make_async_copy(out.at[rows], out_ref.at[rows], writes.at[t]))
        stores[t].start()
    for store in stores:
        store.wait()


def call(kernel, outs, args, scratch=(), scalars=0, inputs=None, out_spec=VMEM, limit=48):
    single = not isinstance(outs, list)
    return pl.pallas_call(
        kernel,
        out_shape=outs,
        in_specs=inputs or [SMEM] * scalars + [VMEM] * (len(args) - scalars),
        out_specs=out_spec if single else [out_spec] * len(outs),
        scratch_shapes=list(scratch),
        compiler_params=pltpu.CompilerParams(vmem_limit_bytes=limit * 2**20),
    )(*args)


def shape(*dims, dtype=F32):
    return jax.ShapeDtypeStruct(dims, dtype)


def exact(left, right):
    dims = (((0,), (0,)), ((), ()))
    return lax.dot_general(left, right, dims, precision=lax.Precision.HIGHEST, preferred_element_type=F32)


def trade(pieces):
    return lax.all_to_all(pieces, ROW, 0, 0, axis_index_groups=NEAR)


def across(value, distance):
    return lax.ppermute(value, "y", [(y, y ^ distance) for y in range(NY)])


def local(vectors, reflectors_first, reflectors_second, factor_first, factor_second):
    core = lax.axis_index("core")
    scalar = core.astype(jnp.int32).reshape(1)
    shards = jnp.concatenate([reflectors_second, reflectors_first], axis=0)
    mine = lax.all_to_all(jnp.broadcast_to(shards[None], (NZ,) + shards.shape), "z", 0, 0).reshape(256, 512)
    other = lax.ppermute(mine, "core", [(0, 1), (1, 0)])
    block = call(split_kernel, [shape(512, 1024, dtype=BF16)] * 2, (vectors,))
    mine_parts = trade(call(mine_kernel, shape(8, 256, 128), (mine, *block)))
    panel = pltpu.VMEM((256, 512), F32)
    other_parts = trade(
        call(
            other_kernel,
            shape(8, 288, 128),
            (scalar, mine, other, reflectors_first, *block),
            (pltpu.VMEM((2, 256, 512), F32), panel),
            scalars=1,
        )
    )
    share = call(near_kernel, shape(256, 128), (mine_parts,))
    share = call(add_kernel, shape(256, 128), (share, across(share, 2)))
    mine_proj = trade(call(mine_copy_kernel, shape(8, 256, 128), (share, across(share, 4))))
    share = call(near_kernel, shape(288, 128), (other_parts,))
    share = call(add_kernel, shape(288, 128), (share, across(share, 2)))
    copies, cross = call(other_copy_kernel, [shape(8, 256, 128), shape(16, 256)], (share, across(share, 4)))
    other_proj = trade(copies)
    cross = lax.all_gather(cross, COL, axis=0, tiled=True)
    both = jnp.stack([jnp.where(core == 0, mine, other), jnp.where(core == 0, other, mine)]).reshape(2, 8, 32, 512)
    by_core = both.transpose(1, 0, 2, 3)
    second = by_core[:, :, :16].reshape(256, 512)
    first = by_core[:, :, 16:].reshape(256, 512)
    w_first = exact(factor_first, first)
    w_second = exact(factor_second, second - exact(cross, w_first))
    ready = call(
        prepare_kernel,
        shape(4, 512, 512, dtype=BF16),
        (scalar, w_second, w_first, mine_proj),
        (pltpu.VMEM((512, 512), F32),),
        scalars=1,
    )
    whole = pltpu.VMEM((512, 1024), F32)
    tall = pltpu.VMEM((512, 1024), BF16)
    return call(
        update_kernel,
        shape(512, 1024),
        (vectors, ready, other_proj),
        (
            whole,
            pltpu.VMEM((4, 512, 512), BF16),
            pltpu.VMEM((8, 256, 128), F32),
            tall,
            tall,
            whole,
            pltpu.SemaphoreType.DMA((4,)),
            pltpu.SemaphoreType.DMA((2,)),
        ),
        inputs=[HBM] * 3,
        out_spec=HBM,
        limit=58,
    )


def solution(mesh):
    fine = Mesh(mesh.devices.reshape(NX, NY, NZ, 2), ROW + COL)
    return jax.shard_map(
        local,
        mesh=fine,
        in_specs=(P(ROW, COL), P(COL, ROW), P(COL, ROW), P(), P()),
        out_specs=P(ROW, COL),
        check_vma=False,
    )
```

time: 140 us -> 151 us (1.079); the launches traced: 137 us -> 151 us
  blocking collectives: 107 us -> 21.5 us
  waiting for transfers between devices: 2.15 us -> 53.2 us
  starting transfers between devices: 15.4 us -> 54.1 us
  Pallas kernels: 6.14 us -> 11.7 us
    all_to_all x3 -> x0, blocking collectives: 60.5 us -> none  [trade(): return lax.all_to_all(pieces, ROW, 0, 0, axis_index_groups=groups)]
    ppermute x0 -> x5, waiting for transfers between devices: none -> 28.4 us  [the longest x4 26.9 us: across(): return lax.ppermute(value, 'y', [(y, y ^ distance) for y in range(NY)])]
    all_gather x1 -> x0, blocking collectives: 27.4 us -> none  [local(): second = lax.all_gather(reflectors_second, COL, axis=0, tiled=True)]
    all_to_all x2 -> x5, waiting for transfers between devices: 2.15 us -> 24.8 us  [the longest x1 16.1 us: local(): lax.all_to_all(jnp.broadcast_to(shards[None], (NZ,) + shards.shape), 'z',...]
    ppermute x0 -> x5, starting transfers between devices: none -> 19.6 us  [the longest x4 16.9 us: across(): return lax.ppermute(value, 'y', [(y, y ^ distance) for y in range(NY)])]
    all_to_all x2 -> x5, starting transfers between devices: 15.4 us -> 34.5 us  [the longest x4 23.6 us: trade(): return lax.all_to_all(pieces, ROW, 0, 0, axis_index_groups=NEAR)]
    pallas_call x6 -> x11, Pallas kernels: 6.14 us -> 11.7 us  [call(): pl.pallas_call(kernel, out_shape=outs, in_specs=inputs or [SMEM] * scalar...]
    all_gather x1, blocking collectives: 18.8 us -> 21.5 us  [local(): cross = lax.all_gather(cross, COL, axis=0, tiled=True)]
  transfers between devices with their start and end apart: 2 -> 10, of which waited for: 1 -> 7; matrix products, arithmetic and copies ran while one was open for 1% -> 2% of each run, Pallas kernels for 0% -> 4%
where the time goes in v6:
time: 151 us
  starting transfers between devices  54.1 us (36%)
  waiting for transfers between devices  53.2 us (35%)
  blocking collectives  21.5 us (14%)
  Pallas kernels  11.7 us (8%)
  local copies, waits for them, and re-layouts  6.02 us (4%)
  matrix products  2.74 us (2%)
    ppermute x4, waiting for transfers between devices, across(): return lax.ppermute(value, 'y', [(y, y ^ distance) for y in range(NY)])  26.9 us
    all_to_all x4, starting transfers between devices, trade(): return lax.all_to_all(pieces, ROW, 0, 0, axis_index_groups=NEAR)  23.6 us
    all_gather x1, blocking collectives, local(): cross = lax.all_gather(cross, COL, axis=0, tiled=True)  21.5 us
    ppermute x4, starting transfers between devices, across(): return lax.ppermute(value, 'y', [(y, y ^ distance) for y in range(NY)])  16.9 us
    all_to_all x1, waiting for transfers between devices, local(): lax.all_to_all(jnp.broadcast_to(shards[None], (NZ,) + shards.shape), 'z',...  16.1 us
    pallas_call x11, Pallas kernels, call(): pl.pallas_call(kernel, out_shape=outs, in_specs=inputs or [SMEM] * scalar...  11.7 us
    all_to_all x1, starting transfers between devices, local(): lax.all_to_all(jnp.broadcast_to(shards[None], (NZ,) + shards.shape), 'z',...  10.9 us
    all_to_all x4, waiting for transfers between devices, trade(): return lax.all_to_all(pieces, ROW, 0, 0, axis_index_groups=NEAR)  8.77 us
  transfers between devices with their start and end apart: 10, of which 7 were waited for; matrix products, arithmetic and copies ran while one was open for 2% of the time, Pallas kernels for 4%

profile of v6, /device:TPU:1, one launch (start us, length us, event | category | flops | bytes accessed | tf_op | source)
XLA Modules:
  0.0 150.5 jit_solution(10992517215618982813)
XLA Ops:
  1.7 10.9 %all-to-all-start = ((f32[8,32,512]{2,1,0:T(8,128)}), f32[8,32,512]{2,1,0:T(8,128)S(1)}, u32[]{:S(2)}, u32[]{:S(2)}) async-start(f32[8,32,512]{2,1,0:T(8,128)} %broadcast_in_dim.2), calls=%async_computation | async-start | bytes 1048576 | tf_op jit(solution)/shard_map/all_to_all | solution.py:174
  12.6 1.6 %copy-done.1 = f32[512,1024]{1,0:T(8,128)S(1)} copy-done((f32[512,1024]{1,0:T(8,128)S(1)}, f32[512,1024]{1,0:T(8,128)}, u32[]{:S(2)}) %copy-start.1) | copy-done | bytes 2097176
  14.4 16.1 %all-to-all-done = f32[8,32,512]{2,1,0:T(8,128)S(1)} async-done(((f32[8,32,512]{2,1,0:T(8,128)}), f32[8,32,512]{2,1,0:T(8,128)S(1)}, u32[]{:S(2)}, u32[]{:S(2)}) %all-to-all-start) | async-done | bytes 524320 | tf_op jit(solution)/shard_map/all_to_all | solution.py:174
  32.5 5.0 %all-to-all-start.2 = ((f32[8,256,128]{2,1,0:T(8,128)}), f32[8,256,128]{2,1,0:T(8,128)}, u32[]{:S(2)}, u32[]{:S(2)}) async-start(f32[8,256,128]{2,1,0:T(8,128)} %copy-done.3), calls=%async_computation.2 | async-start | bytes 2097152 | tf_op jit(solution)/shard_map/all_to_all | solution.py:163
  37.5 2.7 %collective-permute-start = (f32[256,512]{1,0:T(8,128)S(1)}, f32[256,512]{1,0:T(8,128)S(1)}, u32[]{:S(2)}, u32[]{:S(2)}) collective-permute-start(f32[256,512]{1,0:T(8,128)S(1)} %bitcast.24), channel_id=1, source_target_pairs={{0,1},{1,0},{2,3},{3,2},{4,5},{5,4},{6,7},{7,6},{8,9},{9,8},{10,11... | collective-permute-start | bytes 1572872 | tf_op jit(solution)/shard_map/ppermute | solution.py:175
  40.2 1.5 %collective-permute-done.other_ref = f32[256,512]{1,0:T(8,128)S(1)} collective-permute-done((f32[256,512]{1,0:T(8,128)S(1)}, f32[256,512]{1,0:T(8,128)S(1)}, u32[]{:S(2)}, u32[]{:S(2)}) %collective-permute-start) | collective-permute-done | bytes 524320 | tf_op jit(solution)/shard_map/ppermute | solution.py:175
  41.7 2.2 %shard_map.56 = f32[8,288,128]{2,1,0:T(8,128)} custom-call(s32[1]{0:T(128)} %bitcast.core_ref, f32[256,512]{1,0:T(8,128)S(1)} %bitcast.25, f32[256,512]{1,0:T(8,128)S(1)} %collective-permute-done.other_ref, f32[16,512]{1,0:T(8,128)S(1)} %copy-done.5, bf16[512,1024]{1,0:T(8,128)(2,1)S(1)} %get-tuple-element.9.block_high, ...), custom_call_target="tpu_custom_call" | custom-call | tf_op jit(solution)/shard_map/pallas_call | solution.py:143
  43.9 8.8 %all-to-all-done.2.parts = f32[8,256,128]{2,1,0:T(8,128)} async-done(((f32[8,256,128]{2,1,0:T(8,128)}), f32[8,256,128]{2,1,0:T(8,128)}, u32[]{:S(2)}, u32[]{:S(2)}) %all-to-all-start.2) | async-done | bytes 1048608 | tf_op jit(solution)/shard_map/all_to_all | solution.py:163
  52.6 3.6 %all-to-all-start.1 = ((f32[8,288,128]{2,1,0:T(8,128)}), f32[8,288,128]{2,1,0:T(8,128)S(1)}, u32[]{:S(2)}, u32[]{:S(2)}) async-start(f32[8,288,128]{2,1,0:T(8,128)} %shard_map.56), calls=%async_computation.1 | async-start | bytes 2359296 | tf_op jit(solution)/shard_map/all_to_all | solution.py:163
  56.2 1.3 shard_map.61.share
  57.5 4.2 %collective-permute-start.3 = (f32[256,128]{1,0:T(8,128)S(1)}, f32[256,128]{1,0:T(8,128)S(1)}, u32[]{:S(2)}, u32[]{:S(2)}) collective-permute-start(f32[256,128]{1,0:T(8,128)S(1)} %shard_map.61.share), channel_id=1, source_target_pairs={{0,32},{16,48},{32,0},{48,16},{64,96},{80,112},{96,64},{112,80},{1... | collective-permute-start | bytes 393224 | tf_op jit(solution)/shard_map/ppermute | solution.py:167
  61.7 8.8 %collective-permute-done.3.got = f32[256,128]{1,0:T(8,128)S(1)} collective-permute-done((f32[256,128]{1,0:T(8,128)S(1)}, f32[256,128]{1,0:T(8,128)S(1)}, u32[]{:S(2)}, u32[]{:S(2)}) %collective-permute-start.3) | collective-permute-done | bytes 131104 | tf_op jit(solution)/shard_map/ppermute | solution.py:167
  70.6 6.5 %collective-permute-start.4 = (f32[256,128]{1,0:T(8,128)S(1)}, f32[256,128]{1,0:T(8,128)S(1)}, u32[]{:S(2)}, u32[]{:S(2)}) collective-permute-start(f32[256,128]{1,0:T(8,128)S(1)} %shard_map.62.share), channel_id=1, source_target_pairs={{0,64},{16,80},{32,96},{48,112},{64,0},{80,16},{96,32},{112,48},{1... | collective-permute-start | bytes 393224 | tf_op jit(solution)/shard_map/ppermute | solution.py:167
  77.1 3.1 %collective-permute-done.4.got = f32[256,128]{1,0:T(8,128)S(1)} collective-permute-done((f32[256,128]{1,0:T(8,128)S(1)}, f32[256,128]{1,0:T(8,128)S(1)}, u32[]{:S(2)}, u32[]{:S(2)}) %collective-permute-start.4) | collective-permute-done | bytes 131104 | tf_op jit(solution)/shard_map/ppermute | solution.py:167
  81.3 8.4 %all-to-all-start.3 = ((f32[8,256,128]{2,1,0:T(8,128)}), f32[8,256,128]{2,1,0:T(8,128)S(1)}, u32[]{:S(2)}, u32[]{:S(2)}) async-start(f32[8,256,128]{2,1,0:T(8,128)} %copy-done.4), calls=%async_computation.3 | async-start | bytes 2097152 | tf_op jit(solution)/shard_map/all_to_all | solution.py:163
  89.8 1.9 %collective-permute-start.1 = (f32[288,128]{1,0:T(8,128)S(1)}, f32[288,128]{1,0:T(8,128)S(1)}, u32[]{:S(2)}, u32[]{:S(2)}) collective-permute-start(f32[288,128]{1,0:T(8,128)S(1)} %shard_map.57.share), channel_id=1, source_target_pairs={{0,32},{16,48},{32,0},{48,16},{64,96},{80,112},{96,64},{112,80},{1... | collective-permute-start | bytes 442376 | tf_op jit(solution)/shard_map/ppermute | solution.py:167
  91.7 9.4 %collective-permute-done.1.got = f32[288,128]{1,0:T(8,128)S(1)} collective-permute-done((f32[288,128]{1,0:T(8,128)S(1)}, f32[288,128]{1,0:T(8,128)S(1)}, u32[]{:S(2)}, u32[]{:S(2)}) %collective-permute-start.1) | collective-permute-done | bytes 147488 | tf_op jit(solution)/shard_map/ppermute | solution.py:167
  101.1 4.3 %collective-permute-start.2 = (f32[288,128]{1,0:T(8,128)S(1)}, f32[288,128]{1,0:T(8,128)S(1)}, u32[]{:S(2)}, u32[]{:S(2)}) collective-permute-start(f32[288,128]{1,0:T(8,128)S(1)} %shard_map.58.share), channel_id=1, source_target_pairs={{0,64},{16,80},{32,96},{48,112},{64,0},{80,16},{96,32},{112,48},{1... | collective-permute-start | bytes 442376 | tf_op jit(solution)/shard_map/ppermute | solution.py:167
  105.4 5.6 %collective-permute-done.2.got = f32[288,128]{1,0:T(8,128)S(1)} collective-permute-done((f32[288,128]{1,0:T(8,128)S(1)}, f32[288,128]{1,0:T(8,128)S(1)}, u32[]{:S(2)}, u32[]{:S(2)}) %collective-permute-start.2) | collective-permute-done | bytes 147488 | tf_op jit(solution)/shard_map/ppermute | solution.py:167
  112.0 6.6 %all-to-all-start.4 = ((f32[8,256,128]{2,1,0:T(8,128)}), f32[8,256,128]{2,1,0:T(8,128)}, u32[]{:S(2)}, u32[]{:S(2)}) async-start(f32[8,256,128]{2,1,0:T(8,128)} %get-tuple-element.12), calls=%async_computation.4 | async-start | bytes 2097152 | tf_op jit(solution)/shard_map/all_to_all | solution.py:163
  120.2 21.5 %all_gather.3 = f32[256,256]{1,0:T(8,128)S(1)} all-gather(f32[16,256]{1,0:T(8,128)S(1)} %get-tuple-element.11), channel_id=1, replica_groups=mesh['x'=4,'y'=8,'z'=8,'core'=2] {'z','core'}, dimensions={0}, use_global_device_ids=true | all-gather | bytes 278528 | tf_op jit(solution)/shard_map/all_gather | solution.py:195
  141.7 1.1 convolution_subtract_fusion
  144.1 1.3 copy-done.2
  145.4 5.1 %shard_map.65 = f32[512,1024]{1,0:T(8,128)} custom-call(f32[512,1024]{1,0:T(8,128)} %block_ref.3, bf16[4,512,512]{2,1,0:T(8,128)(2,1)} %copy-done.2, f32[8,256,128]{2,1,0:T(8,128)} %all-to-all-done.4.parts_ref), custom_call_target="tpu_custom_call" | custom-call | tf_op jit(solution)/shard_map/pallas_call | solution.py:143
  (31 shorter events, 8.9 us)
Async XLA Ops:
  0.0 118.9 %copy-start = (f32[256,256]{1,0:T(8,128)S(1)}, f32[256,256]{1,0:T(8,128)}, u32[]{:S(2)}) copy-start(f32[256,256]{1,0:T(8,128)} %param.8) | copy-start | bytes 786436
  1.7 28.8 %all-to-all-start = ((f32[8,32,512]{2,1,0:T(8,128)}), f32[8,32,512]{2,1,0:T(8,128)S(1)}, u32[]{:S(2)}, u32[]{:S(2)}) async-start(f32[8,32,512]{2,1,0:T(8,128)} %broadcast_in_dim.2), calls=%async_computation | async-start | bytes 1048576 | tf_op jit(solution)/shard_map/all_to_all | solution.py:174
  12.5 1.6 %copy-start.1 = (f32[512,1024]{1,0:T(8,128)S(1)}, f32[512,1024]{1,0:T(8,128)}, u32[]{:S(2)}) copy-start(f32[512,1024]{1,0:T(8,128)} %block_ref.3) | copy-start | bytes 6291460
  30.5 11.2 %copy-start.5 = (f32[16,512]{1,0:T(8,128)S(1)}, f32[16,512]{1,0:T(8,128)}, u32[]{:S(2)}) copy-start(f32[16,512]{1,0:T(8,128)} %own_ref.1) | copy-start | bytes 98308
  31.5 1.0 copy-start.3
  32.5 20.2 %all-to-all-start.2 = ((f32[8,256,128]{2,1,0:T(8,128)}), f32[8,256,128]{2,1,0:T(8,128)}, u32[]{:S(2)}, u32[]{:S(2)}) async-start(f32[8,256,128]{2,1,0:T(8,128)} %copy-done.3), calls=%async_computation.2 | async-start | bytes 2097152 | tf_op jit(solution)/shard_map/all_to_all | solution.py:163
  37.5 4.2 %collective-permute-start = (f32[256,512]{1,0:T(8,128)S(1)}, f32[256,512]{1,0:T(8,128)S(1)}, u32[]{:S(2)}, u32[]{:S(2)}) collective-permute-start(f32[256,512]{1,0:T(8,128)S(1)} %bitcast.24), channel_id=1, source_target_pairs={{0,1},{1,0},{2,3},{3,2},{4,5},{5,4},{6,7},{7,6},{8,9},{9,8},{10,11... | collective-permute-start | bytes 1572872 | tf_op jit(solution)/shard_map/ppermute | solution.py:175
  52.6 28.7 %all-to-all-start.1 = ((f32[8,288,128]{2,1,0:T(8,128)}), f32[8,288,128]{2,1,0:T(8,128)S(1)}, u32[]{:S(2)}, u32[]{:S(2)}) async-start(f32[8,288,128]{2,1,0:T(8,128)} %shard_map.56), calls=%async_computation.1 | async-start | bytes 2359296 | tf_op jit(solution)/shard_map/all_to_all | solution.py:163
  57.5 13.0 %collective-permute-start.3 = (f32[256,128]{1,0:T(8,128)S(1)}, f32[256,128]{1,0:T(8,128)S(1)}, u32[]{:S(2)}, u32[]{:S(2)}) collective-permute-start(f32[256,128]{1,0:T(8,128)S(1)} %shard_map.61.share), channel_id=1, source_target_pairs={{0,32},{16,48},{32,0},{48,16},{64,96},{80,112},{96,64},{112,80},{1... | collective-permute-start | bytes 393224 | tf_op jit(solution)/shard_map/ppermute | solution.py:167
  70.6 9.7 %collective-permute-start.4 = (f32[256,128]{1,0:T(8,128)S(1)}, f32[256,128]{1,0:T(8,128)S(1)}, u32[]{:S(2)}, u32[]{:S(2)}) collective-permute-start(f32[256,128]{1,0:T(8,128)S(1)} %shard_map.62.share), channel_id=1, source_target_pairs={{0,64},{16,80},{32,96},{48,112},{64,0},{80,16},{96,32},{112,48},{1... | collective-permute-start | bytes 393224 | tf_op jit(solution)/shard_map/ppermute | solution.py:167
  80.3 1.0 copy-start.4
  81.3 30.7 %all-to-all-start.3 = ((f32[8,256,128]{2,1,0:T(8,128)}), f32[8,256,128]{2,1,0:T(8,128)S(1)}, u32[]{:S(2)}, u32[]{:S(2)}) async-start(f32[8,256,128]{2,1,0:T(8,128)} %copy-done.4), calls=%async_computation.3 | async-start | bytes 2097152 | tf_op jit(solution)/shard_map/all_to_all | solution.py:163
  89.8 11.3 %collective-permute-start.1 = (f32[288,128]{1,0:T(8,128)S(1)}, f32[288,128]{1,0:T(8,128)S(1)}, u32[]{:S(2)}, u32[]{:S(2)}) collective-permute-start(f32[288,128]{1,0:T(8,128)S(1)} %shard_map.57.share), channel_id=1, source_target_pairs={{0,32},{16,48},{32,0},{48,16},{64,96},{80,112},{96,64},{112,80},{1... | collective-permute-start | bytes 442376 | tf_op jit(solution)/shard_map/ppermute | solution.py:167
  101.1 9.9 %collective-permute-start.2 = (f32[288,128]{1,0:T(8,128)S(1)}, f32[288,128]{1,0:T(8,128)S(1)}, u32[]{:S(2)}, u32[]{:S(2)}) collective-permute-start(f32[288,128]{1,0:T(8,128)S(1)} %shard_map.58.share), channel_id=1, source_target_pairs={{0,64},{16,80},{32,96},{48,112},{64,0},{80,16},{96,32},{112,48},{1... | collective-permute-start | bytes 442376 | tf_op jit(solution)/shard_map/ppermute | solution.py:167
  112.0 33.4 %all-to-all-start.4 = ((f32[8,256,128]{2,1,0:T(8,128)}), f32[8,256,128]{2,1,0:T(8,128)}, u32[]{:S(2)}, u32[]{:S(2)}) async-start(f32[8,256,128]{2,1,0:T(8,128)} %get-tuple-element.12), calls=%async_computation.4 | async-start | bytes 2097152 | tf_op jit(solution)/shard_map/all_to_all | solution.py:163
  118.9 23.8 %copy-start.6 = (f32[256,256]{1,0:T(8,128)S(1)}, f32[256,256]{1,0:T(8,128)}, u32[]{:S(2)}) copy-start(f32[256,256]{1,0:T(8,128)} %param.9) | copy-start | bytes 786436
  144.1 1.3 copy-start.2

commit v7 on v5

v7 whole, which is shorter than its diff:
```python
import jax
import jax.numpy as jnp
from jax import lax
from jax.experimental import pallas as pl
from jax.experimental.pallas import tpu as pltpu
from jax.sharding import Mesh, PartitionSpec as P

ROW = ("x", "y")
COL = ("z", "core")
NX, NY, NZ = 4, 8, 8
F32, BF16 = jnp.float32, jnp.bfloat16
VMEM = pl.BlockSpec(memory_space=pltpu.VMEM)
SMEM = pl.BlockSpec(memory_space=pltpu.SMEM)
HBM = pl.BlockSpec(memory_space=pltpu.HBM)
PARAMS = pltpu.CompilerParams(vmem_limit_bytes=48 * 2**20)


def device(x, y, z, core):
    return ((x % NX * NY + y % NY) * NZ + z) * 2 + core


NEAR = [
    [device(bx + (px ^ core) + core, by + (py ^ core) + core, z, core) for px in range(2) for py in range(2)]
    for z in range(NZ)
    for core in range(2)
    for bx in range(0, NX, 2)
    for by in range(0, NY, 2)
]
FAR = [
    [device(px + dx, py + dy, z, core) for dx in range(0, NX, 2) for dy in range(0, NY, 2)]
    for z in range(NZ)
    for core in range(2)
    for px in range(2)
    for py in range(2)
]


def split(value):
    high = value.astype(BF16)
    return high, (value - high.astype(F32)).astype(BF16)


def mul(a, b):
    return jnp.dot(a, b, preferred_element_type=F32)


def mul_nt(a, b):
    return lax.dot_general(a, b, (((1,), (1,)), ((), ())), preferred_element_type=F32)


def mul3(a, b, mul=mul):
    return mul(a[0], b[0]) + (mul(a[0], b[1]) + mul(a[1], b[0]))


def split_kernel(block_ref, high, low):
    high[...], low[...] = split(block_ref[...])


def project_kernel(core_ref, mine_ref, other_ref, own_ref, block_high, block_low, out, high, low, both):
    core = core_ref[0]
    both[0] = mine_ref[...]
    both[1] = other_ref[...]
    for c in range(2):
        from_core = both.at[core ^ c]
        for z in range(8):
            for panel in range(2):
                h, l = split(from_core[z, panel * 16 : panel * 16 + 16, :])
                at = panel * 256 + z * 32 + c * 16
                high[at : at + 16, :] = h
                low[at : at + 16, :] = l
    for t in range(4):
        at = slice(t * 256, (t + 1) * 256)
        value = mul3((high[...], low[...]), (block_high[:, at], block_low[:, at]))
        for m in range(4):
            for half in range(2):
                to = (2 * t + half) * 128
                out[m, to : to + 128, :] = value[m * 128 : (m + 1) * 128, half * 128 : (half + 1) * 128]
    cross = mul3(split(own_ref[...]), (high[:256], low[:256]), mul_nt)
    for m in range(4):
        out[m, 1024:1040, :] = cross[:, :128]
        out[m, 1040:, :] = cross[:, 128:]


def near_kernel(parts, out):
    total = (parts[0] + parts[1]) + (parts[2] + parts[3])
    for m in range(8):
        out[m, :128, :] = total[m * 128 : (m + 1) * 128]
        out[m, 128:, :] = total[1024:]


def far_kernel(parts, out, cross):
    total = ((parts[0] + parts[1]) + (parts[2] + parts[3])) + ((parts[4] + parts[5]) + (parts[6] + parts[7]))
    for m in range(8):
        out[m] = total[:128]
    cross[:, :128] = total[128:144]
    cross[:, 128:] = total[144:]


def copy_kernel(share, after, out, sems):
    copies = [pltpu.make_async_copy(share, out.at[m], sems.at[m]) for m in range(4)]
    for copy in copies:
        copy.start()
    for copy in copies:
        copy.wait()


def weight_kernel(second_ref, first_ref, out):
    for panel, ref in enumerate((second_ref, first_ref)):
        out[0, :, panel * 256 : (panel + 1) * 256], out[1, :, panel * 256 : (panel + 1) * 256] = split(ref[...].T)


def update_kernel(block_ref, w_ref, parts, out_ref, block, out, reads, writes):
    rows = [slice(t * 256, (t + 1) * 256) for t in range(2)]
    loads = [pltpu.make_async_copy(block_ref.at[rows[t]], block.at[rows[t]], reads.at[t]) for t in range(2)]
    stores = [pltpu.make_async_copy(out.at[rows[t]], out_ref.at[rows[t]], writes.at[t]) for t in range(2)]
    for load in loads:
        load.start()
    whole = [jnp.concatenate([parts[m, j * 128 : (j + 1) * 128] for j in range(8)], axis=1) for m in range(4)]
    proj = split(jnp.concatenate(whole, axis=0))
    for t in range(2):
        change = mul3((w_ref[0, rows[t]], w_ref[1, rows[t]]), proj)
        loads[t].wait()
        out[rows[t]] = block[rows[t]] - change
        stores[t].start()
    for store in stores:
        store.wait()


def call(kernel, outs, args, scratch=(), scalars=0, inputs=None, out_spec=VMEM):
    single = not isinstance(outs, list)
    return pl.pallas_call(
        kernel,
        out_shape=outs,
        in_specs=inputs or [SMEM] * scalars + [VMEM] * (len(args) - scalars),
        out_specs=out_spec if single else [out_spec] * len(outs),
        scratch_shapes=list(scratch),
        compiler_params=PARAMS,
    )(*args)


def shape(*dims, dtype=F32):
    return jax.ShapeDtypeStruct(dims, dtype)


def exact(left, right):
    dims = (((0,), (0,)), ((), ()))
    return lax.dot_general(left, right, dims, precision=lax.Precision.HIGHEST, preferred_element_type=F32)


def trade(pieces, groups):
    return lax.all_to_all(pieces, ROW + COL, 0, 0, axis_index_groups=groups)


def local(vectors, reflectors_first, reflectors_second, factor_first, factor_second):
    core = lax.axis_index("core")
    shards = jnp.concatenate([reflectors_second, reflectors_first], axis=0)
    mine = lax.all_to_all(jnp.broadcast_to(shards[None], (NZ,) + shards.shape), "z", 0, 0)
    other = lax.ppermute(mine, "core", [(0, 1), (1, 0)])
    wide = pltpu.VMEM((512, 512), BF16)
    block = call(split_kernel, [shape(512, 1024, dtype=BF16)] * 2, (vectors,))
    parts = call(
        project_kernel,
        shape(4, 1056, 128),
        (core.astype(jnp.int32).reshape(1), mine, other, reflectors_first, *block),
        (wide, wide, pltpu.VMEM((2, 8, 32, 512), F32)),
        scalars=1,
    )
    parts = call(near_kernel, shape(8, 160, 128), (trade(parts, NEAR),))
    share, cross = call(far_kernel, [shape(8, 128, 128), shape(16, 256)], (trade(parts, FAR),))
    share = trade(share, FAR).reshape(1024, 128)
    cross = lax.all_gather(cross, COL, axis=0, tiled=True)
    copies = call(
        copy_kernel,
        shape(4, 1024, 128),
        (share, cross),
        (pltpu.SemaphoreType.DMA((4,)),),
        inputs=[VMEM, HBM],
        out_spec=HBM,
    )
    proj = trade(copies, NEAR)
    by_core = jnp.stack([jnp.where(core == 0, mine, other), jnp.where(core == 0, other, mine)], axis=1)
    second = by_core[:, :, :16].reshape(256, 512)
    first = by_core[:, :, 16:].reshape(256, 512)
    w_first = exact(factor_first, first)
    w_second = exact(factor_second, second - exact(cross, w_first))
    weights = call(weight_kernel, shape(2, 512, 512, dtype=BF16), (w_second, w_first))
    whole = pltpu.VMEM((512, 1024), F32)
    two = pltpu.SemaphoreType.DMA((2,))
    return call(
        update_kernel,
        shape(512, 1024),
        (vectors, weights, proj),
        (whole, whole, two, two),
        inputs=[HBM, VMEM, VMEM],
        out_spec=HBM,
    )


def solution(mesh):
    fine = Mesh(mesh.devices.reshape(NX, NY, NZ, 2), ROW + COL)
    return jax.shard_map(
        local,
        mesh=fine,
        in_specs=(P(ROW, COL), P(COL, ROW), P(COL, ROW), P(), P()),
        out_specs=P(ROW, COL),
        check_vma=False,
    )
```

time: 136 us -> 133 us (0.978); the launches traced: 134 us -> 132 us
  blocking collectives: 106 us -> 91.3 us
  waiting for transfers between devices: 2.08 us -> 11 us
  starting transfers between devices: 8.72 us -> 13.5 us
    all_to_all x3 -> x2, blocking collectives: 61.8 us -> 48.8 us  [trade(): return lax.all_to_all(pieces, ROW + COL, 0, 0, axis_index_groups=groups)]
    all_to_all x1 -> x2, waiting for transfers between devices: 2.08 us -> 11 us  [trade(): return lax.all_to_all(pieces, ROW + COL, 0, 0, axis_index_groups=groups)]
    all_to_all x1 -> x2, starting transfers between devices: 4.37 us -> 9.17 us  [trade(): return lax.all_to_all(pieces, ROW + COL, 0, 0, axis_index_groups=groups)]
    all_gather x1, blocking collectives: 17.7 us -> 15.8 us  [local(): cross = lax.all_gather(cross, COL, axis=0, tiled=True)]
  transfers between devices with their start and end apart: 2 -> 3, of which waited for: 1 -> 2; matrix products, arithmetic and copies ran while one was open for 3% -> 3% of each run, Pallas kernels for 0% -> 0%
where the time goes in v7:
time: 133 us; the launch traced here: 132 us
  blocking collectives  91.3 us (69%)
  starting transfers between devices  13.5 us (10%)
  waiting for transfers between devices  11 us (8%)
  Pallas kernels  10 us (8%)
  local copies, waits for them, and re-layouts  2.74 us (2%)
  matrix products  2.72 us (2%)
    all_to_all x2, blocking collectives, trade(): return lax.all_to_all(pieces, ROW + COL, 0, 0, axis_index_groups=groups)  48.8 us
    all_to_all x1, blocking collectives, local(): lax.all_to_all(jnp.broadcast_to(shards[None], (NZ,) + shards.shape), 'z',...  26.7 us
    all_gather x1, blocking collectives, local(): cross = lax.all_gather(cross, COL, axis=0, tiled=True)  15.8 us
    all_to_all x2, waiting for transfers between devices, trade(): return lax.all_to_all(pieces, ROW + COL, 0, 0, axis_index_groups=groups)  11 us
    pallas_call x7, Pallas kernels, call(): pl.pallas_call(kernel, out_shape=outs, in_specs=inputs or [SMEM] * scalar...  10 us
    all_to_all x2, starting transfers between devices, trade(): return lax.all_to_all(pieces, ROW + COL, 0, 0, axis_index_groups=groups)  9.17 us
    ppermute x1, starting transfers between devices, local(): other = lax.ppermute(mine, 'core', [(0, 1), (1, 0)])  4.35 us
    dot_general x3, matrix products, exact(): lax.dot_general(left, right, dims, precision=lax.Precision.HIGHEST, prefe...  2.72 us
  transfers between devices with their start and end apart: 3, of which 2 were waited for; matrix products, arithmetic and copies ran while one was open for 3% of the time, Pallas kernels for 0%

profile of v7, /device:TPU:1, one launch (start us, length us, event | category | flops | bytes accessed | tf_op | source)
XLA Modules:
  0.0 132.5 jit_solution(14447937165018686327)
XLA Ops:
  0.0 0.8 pad_maximum_fusion.1
  0.9 26.7 %all_to_all.25.mine_ref = f32[8,32,512]{2,1,0:T(8,128)S(1)} all-to-all(f32[8,32,512]{2,1,0:T(8,128)S(1)} %broadcast_in_dim.2), channel_id=1, replica_groups=mesh['x'=4,'y'=8,'z'=8,'core'=2] {'z'}, dimensions={0} | all-to-all | bytes 1048576 | tf_op jit(solution)/shard_map/all_to_all | solution.py:157
  27.6 4.4 %collective-permute-start = (f32[8,32,512]{2,1,0:T(8,128)S(1)}, f32[8,32,512]{2,1,0:T(8,128)S(1)}, u32[]{:S(2)}, u32[]{:S(2)}) collective-permute-start(f32[8,32,512]{2,1,0:T(8,128)S(1)} %all_to_all.25.mine_ref), channel_id=1, source_target_pairs={{0,1},{1,0},{2,3},{3,2},{4,5},{5,4},{6,7},{7,6},{8,9},{9,8},{10,11... | collective-permute-start | bytes 1572872 | tf_op jit(solution)/shard_map/ppermute | solution.py:158
  31.9 1.6 %copy-done.1 = f32[512,1024]{1,0:T(8,128)S(1)} copy-done((f32[512,1024]{1,0:T(8,128)S(1)}, f32[512,1024]{1,0:T(8,128)}, u32[]{:S(2)}) %copy-start.1) | copy-done | bytes 2097176
  33.5 0.3 shard_map.55
  33.8 2.0 %shard_map.56 = f32[4,1056,128]{2,1,0:T(8,128)S(1)} custom-call(s32[1]{0:T(128)} %bitcast.3.core_ref, f32[8,32,512]{2,1,0:T(8,128)S(1)} %all_to_all.25.mine_ref, f32[8,32,512]{2,1,0:T(8,128)S(1)} %collective-permute-done.other_ref, f32[16,512]{1,0:T(8,128)S(1)} %copy-done.4, bf16[512,1024]{1,0:T(8,128)(2,1)S(1)} %get-tuple-element.9.block_high, ...), custom_call_target="tpu_custom_call" | custom-call | tf_op jit(solution)/shard_map/pallas_call | solution.py:131
  35.9 23.8 %all_to_all.26.parts = f32[4,1056,128]{2,1,0:T(8,128)S(1)} all-to-all(f32[4,1056,128]{2,1,0:T(8,128)S(1)} %shard_map.56), channel_id=1, replica_groups={{0,16,128,144},{32,48,160,176},{64,80,192,208},{96,112,224,240},{256,27..., dimensions={0} | all-to-all | bytes 4325376 | tf_op jit(solution)/shard_map/all_to_all | solution.py:151
  59.7 0.1 shard_map.57
  59.8 25.0 %all_to_all.27.parts = f32[8,160,128]{2,1,0:T(8,128)S(1)} all-to-all(f32[8,160,128]{2,1,0:T(8,128)S(1)} %shard_map.57), channel_id=1, replica_groups={{0,32,64,96,256,288,320,352},{16,48,80,112,272,304,336,368},{128,160,19..., dimensions={0} | all-to-all | bytes 1310720 | tf_op jit(solution)/shard_map/all_to_all | solution.py:151
  84.8 0.8 shard_map.58
  85.6 3.5 %all-to-all-start.3 = ((f32[8,128,128]{2,1,0:T(8,128)}), f32[8,128,128]{2,1,0:T(8,128)S(1)}, u32[]{:S(2)}, u32[]{:S(2)}) async-start(f32[8,128,128]{2,1,0:T(8,128)} %get-tuple-element.12), calls=%async_computation.3 | async-start | bytes 1048576 | tf_op jit(solution)/shard_map/all_to_all | solution.py:151
  89.1 15.8 %all_gather.3.after = f32[256,256]{1,0:T(8,128)S(1)} all-gather(f32[16,256]{1,0:T(8,128)S(1)} %get-tuple-element.11), channel_id=1, replica_groups=mesh['x'=4,'y'=8,'z'=8,'core'=2] {'z','core'}, dimensions={0}, use_global_device_ids=true | all-gather | bytes 278528 | tf_op jit(solution)/shard_map/all_gather | solution.py:171
  104.9 0.2 all-to-all-done.3
  105.2 1.3 %shard_map.60 = f32[4,1024,128]{2,1,0:T(8,128)} custom-call(f32[1024,128]{1,0:T(8,128)S(1)} %bitcast.17, f32[256,256]{1,0:T(8,128)S(1)} %all_gather.3.after), custom_call_target="tpu_custom_call" | custom-call | tf_op jit(solution)/shard_map/pallas_call | solution.py:131
  106.5 5.7 %all-to-all-start.4 = ((f32[4,1024,128]{2,1,0:T(8,128)}), f32[4,1024,128]{2,1,0:T(8,128)}, u32[]{:S(2)}, u32[]{:S(2)}) async-start(f32[4,1024,128]{2,1,0:T(8,128)} %shard_map.60), calls=%async_computation.4 | async-start | bytes 4194304 | tf_op jit(solution)/shard_map/all_to_all | solution.py:151
  112.2 0.1 select_bitcast_fusion
  112.3 0.1 pad_maximum_fusion
  112.5 1.0 fusion.1
  113.5 1.0 copy.11
  114.5 1.0 convolution_subtract_fusion
  115.6 0.7 convolution_bitcast_fusion.second_ref
  116.3 0.3 shard_map.59.w_ref
  116.6 10.8 %all-to-all-done.4.parts = f32[4,1024,128]{2,1,0:T(8,128)} async-done(((f32[4,1024,128]{2,1,0:T(8,128)}), f32[4,1024,128]{2,1,0:T(8,128)}, u32[]{:S(2)}, u32[]{:S(2)}) %all-to-all-start.4) | async-done | bytes 2097184 | tf_op jit(solution)/shard_map/all_to_all | solution.py:151
  127.4 5.1 %shard_map.61 = f32[512,1024]{1,0:T(8,128)} custom-call(f32[512,1024]{1,0:T(8,128)S(1)} %copy-done.2, bf16[2,512,512]{2,1,0:T(8,128)(2,1)S(1)} %shard_map.59.w_ref, f32[4,1024,128]{2,1,0:T(8,128)} %all-to-all-done.4.parts), custom_call_target="tpu_custom_call" | custom-call | tf_op jit(solution)/shard_map/pallas_call | solution.py:131
  (15 shorter events, 0.2 us)
Async XLA Ops:
  0.0 112.5 %copy-start = (f32[256,256]{1,0:T(8,128)S(1)}, f32[256,256]{1,0:T(8,128)}, u32[]{:S(2)}) copy-start(f32[256,256]{1,0:T(8,128)} %param.8) | copy-start | bytes 786436
  0.0 33.8 %copy-start.4 = (f32[16,512]{1,0:T(8,128)S(1)}, f32[16,512]{1,0:T(8,128)}, u32[]{:S(2)}) copy-start(f32[16,512]{1,0:T(8,128)} %own_ref.1) | copy-start | bytes 98308
  27.6 6.3 %collective-permute-start = (f32[8,32,512]{2,1,0:T(8,128)S(1)}, f32[8,32,512]{2,1,0:T(8,128)S(1)}, u32[]{:S(2)}, u32[]{:S(2)}) collective-permute-start(f32[8,32,512]{2,1,0:T(8,128)S(1)} %all_to_all.25.mine_ref), channel_id=1, source_target_pairs={{0,1},{1,0},{2,3},{3,2},{4,5},{5,4},{6,7},{7,6},{8,9},{9,8},{10,11... | collective-permute-start | bytes 1572872 | tf_op jit(solution)/shard_map/ppermute | solution.py:158
  31.9 1.6 %copy-start.1 = (f32[512,1024]{1,0:T(8,128)S(1)}, f32[512,1024]{1,0:T(8,128)}, u32[]{:S(2)}) copy-start(f32[512,1024]{1,0:T(8,128)} %block_ref.3) | copy-start | bytes 6291460
  85.6 19.5 %all-to-all-start.3 = ((f32[8,128,128]{2,1,0:T(8,128)}), f32[8,128,128]{2,1,0:T(8,128)S(1)}, u32[]{:S(2)}, u32[]{:S(2)}) async-start(f32[8,128,128]{2,1,0:T(8,128)} %get-tuple-element.12), calls=%async_computation.3 | async-start | bytes 1048576 | tf_op jit(solution)/shard_map/all_to_all | solution.py:151
  106.5 20.9 %all-to-all-start.4 = ((f32[4,1024,128]{2,1,0:T(8,128)}), f32[4,1024,128]{2,1,0:T(8,128)}, u32[]{:S(2)}, u32[]{:S(2)}) async-start(f32[4,1024,128]{2,1,0:T(8,128)} %shard_map.60), calls=%async_computation.4 | async-start | bytes 4194304 | tf_op jit(solution)/shard_map/all_to_all | solution.py:151
  112.5 3.1 %copy-start.5 = (f32[256,256]{1,0:T(8,128)S(1)}, f32[256,256]{1,0:T(8,128)}, u32[]{:S(2)}) copy-start(f32[256,256]{1,0:T(8,128)} %param.9) | copy-start | bytes 786436
  114.5 1.7 %copy-start.3 = (f32[512,256]{0,1:T(8,128)S(1)}, f32[512,256]{0,1:T(8,128)}, u32[]{:S(2)}) copy-start(f32[512,256]{0,1:T(8,128)} %copy.11) | copy-start | bytes 1572868
  115.6 11.8 %copy-start.2 = (f32[512,1024]{1,0:T(8,128)S(1)}, f32[512,1024]{1,0:T(8,128)}, u32[]{:S(2)}) copy-start(f32[512,1024]{1,0:T(8,128)} %block_ref.3) | copy-start | bytes 6291460

commit v8 on v5

--- a/solution.py
+++ b/solution.py
@@ -12,10 +12,25 @@
 VMEM = pl.BlockSpec(memory_space=pltpu.VMEM)
 SMEM = pl.BlockSpec(memory_space=pltpu.SMEM)
 HBM = pl.BlockSpec(memory_space=pltpu.HBM)
-PARAMS = pltpu.CompilerParams(vmem_limit_bytes=48 * 2**20)
-
-NEAR = [[x * NY + y + dy for x in range(NX) for dy in range(2)] for y in range(0, NY, 2)]
-FAR = [[x * NY + y for y in range(parity, NY, 2)] for x in range(NX) for parity in range(2)]
+
+
+def device(x, y, z, core):
+    return ((x * NY + y % NY) * NZ + z) * 2 + core
+
+
+NEAR = [
+    [device(x, y + (parity ^ core) + core, z, core) for x in range(NX) for parity in range(2)]
+    for z in range(NZ)
+    for core in range(2)
+    for y in range(0, NY, 2)
+]
+FAR = [
+    [device(x, y, z, core) for y in range(parity, NY, 2)]
+    for z in range(NZ)
+    for core in range(2)
+    for x in range(NX)
+    for parity in range(2)
+]
 
 
 def split(value):
@@ -92,33 +107,26 @@
         out[0, :, panel * 256 : (panel + 1) * 256], out[1, :, panel * 256 : (panel + 1) * 256] = split(ref[...].T)
 
 
-def update_kernel(block_ref, w_ref, proj_ref, out_ref, block, parts, out, block_sems, part_sems, out_sems):
-    at = [slice(t * 256, (t + 1) * 256) for t in range(4)]
-    rows = [slice(t * 128, (t + 1) * 128) for t in range(4)]
-    reads = [pltpu.make_async_copy(proj_ref.at[:, rows[t]], parts.at[:, rows[t]], part_sems.at[t]) for t in range(4)]
-    reads += [pltpu.make_async_copy(block_ref.at[:, at[t]], block.at[:, at[t]], block_sems.at[t]) for t in range(4)]
-    writes = [pltpu.make_async_copy(out.at[:, at[t]], out_ref.at[:, at[t]], out_sems.at[t]) for t in range(4)]
-    for read in reads:
-        read.start()
+def update_kernel(block, w_ref, parts_ref, out_ref, parts, high, low, out, reads, writes):
+    loads = [pltpu.make_async_copy(parts_ref.at[m], parts.at[m], reads.at[m]) for m in range(8)]
+    for load in loads:
+        load.start()
+    for m in range(8):
+        loads[m].wait()
+        rows = slice(m * 64, (m + 1) * 64)
+        high[rows], low[rows] = split(jnp.concatenate([parts[m, j * 64 : (j + 1) * 64] for j in range(8)], axis=1))
+    stores = []
     for t in range(4):
-        first = t * 128
-        reads[t].wait()
-        proj = jnp.concatenate(
-            [
-                jnp.concatenate([parts[m, first : first + 64], parts[m, first + 64 : first + 128]], axis=1)
-                for m in range(8)
-            ],
-            axis=0,
-        )
-        change = mul3((w_ref[0], w_ref[1]), split(proj))
-        reads[4 + t].wait()
-        out[:, at[t]] = block[:, at[t]] - change
-        writes[t].start()
-    for write in writes:
-        write.wait()
-
-
-def call(kernel, outs, args, scratch=(), scalars=0, inputs=None, out_spec=VMEM):
+        rows = slice(t * 128, (t + 1) * 128)
+        change = mul3((w_ref[0, rows], w_ref[1, rows]), (high[...], low[...]))
+        out[rows] = block[rows] - change
+        stores.append(pltpu.make_async_copy(out.at[rows], out_ref.at[rows], writes.at[t]))
+        stores[t].start()
+    for store in stores:
+        store.wait()
+
+
+def call(kernel, outs, args, scratch=(), scalars=0, inputs=None, out_spec=VMEM, limit=48):
     single = not isinstance(outs, list)
     return pl.pallas_call(
         kernel,
@@ -126,7 +134,7 @@
         in_specs=inputs or [SMEM] * scalars + [VMEM] * (len(args) - scalars),
         out_specs=out_spec if single else [out_spec] * len(outs),
         scratch_shapes=list(scratch),
-        compiler_params=PARAMS,
+        compiler_params=pltpu.CompilerParams(vmem_limit_bytes=limit * 2**20),
     )(*args)
 
 
@@ -140,7 +148,7 @@
 
 
 def trade(pieces, groups):
-    return lax.all_to_all(pieces, ROW, 0, 0, axis_index_groups=groups)
+    return lax.all_to_all(pieces, ROW + COL, 0, 0, axis_index_groups=groups)
 
 
 def local(vectors, reflectors_first, reflectors_second, factor_first, factor_second):
@@ -169,14 +177,20 @@
     w_first = exact(factor_first, first)
     w_second = exact(factor_second, second - exact(cross, w_first))
     weights = call(weight_kernel, shape(2, 512, 512, dtype=BF16), (w_second, w_first))
-    whole = pltpu.VMEM((512, 1024), F32)
-    four = pltpu.SemaphoreType.DMA((4,))
+    tall = pltpu.VMEM((512, 1024), BF16)
     return call(
         update_kernel,
         shape(512, 1024),
         (vectors, weights, proj),
-        (whole, pltpu.VMEM((8, 512, 128), F32), whole, four, four, four),
-        inputs=[HBM, VMEM, HBM],
+        (
+            pltpu.VMEM((8, 512, 128), F32),
+            tall,
+            tall,
+            pltpu.VMEM((512, 1024), F32),
+            pltpu.SemaphoreType.DMA((8,)),
+            pltpu.SemaphoreType.DMA((4,)),
+        ),
+        inputs=[VMEM, VMEM, HBM],
         out_spec=HBM,
     )
 

time: 136 us -> 133 us (0.978)
  waiting for transfers between devices: 2.08 us -> 0.01 us
  Pallas kernels: 10.2 us -> 8.37 us
    all_to_all x1, waiting for transfers between devices: 2.08 us -> 0.01 us  [trade(): return lax.all_to_all(pieces, ROW + COL, 0, 0, axis_index_groups=groups)]
    pallas_call x7, Pallas kernels: 10.2 us -> 8.37 us  [call(): pl.pallas_call(kernel, out_shape=outs, in_specs=inputs or [SMEM] * scalar...]
    all_gather x1, blocking collectives: 17.7 us -> 19.5 us  [local(): cross = lax.all_gather(cross, COL, axis=0, tiled=True)]
  transfers between devices with their start and end apart: 2 -> 2, of which waited for: 1 -> 0; matrix products, arithmetic and copies ran while one was open for 3% -> 3% of each run, Pallas kernels for 0% -> 0%
where the time goes in v8:
time: 133 us; the launch traced here: 132 us
  blocking collectives  107 us (80%)
  starting transfers between devices  8.72 us (7%)
  Pallas kernels  8.37 us (6%)
  local copies, waits for them, and re-layouts  3.3 us (2%)
  matrix products  2.72 us (2%)
    all_to_all x3, blocking collectives, trade(): return lax.all_to_all(pieces, ROW + COL, 0, 0, axis_index_groups=groups)  61 us
    all_to_all x1, blocking collectives, local(): lax.all_to_all(jnp.broadcast_to(shards[None], (NZ,) + shards.shape), 'z',...  26.7 us
    all_gather x1, blocking collectives, local(): cross = lax.all_gather(cross, COL, axis=0, tiled=True)  19.5 us
    pallas_call x7, Pallas kernels, call(): pl.pallas_call(kernel, out_shape=outs, in_specs=inputs or [SMEM] * scalar...  8.37 us
    all_to_all x1, starting transfers between devices, trade(): return lax.all_to_all(pieces, ROW + COL, 0, 0, axis_index_groups=groups)  4.37 us
    ppermute x1, starting transfers between devices, local(): other = lax.ppermute(mine, 'core', [(0, 1), (1, 0)])  4.35 us
    dot_general x3, matrix products, exact(): lax.dot_general(left, right, dims, precision=lax.Precision.HIGHEST, prefe...  2.72 us
  transfers between devices with their start and end apart: 2, of which 0 were waited for; matrix products, arithmetic and copies ran while one was open for 3% of the time, Pallas kernels for 0%

profile of v8, /device:TPU:1, one launch (start us, length us, event | category | flops | bytes accessed | tf_op | source)
XLA Modules:
  0.0 131.5 jit_solution(8639062450941633637)
XLA Ops:
  0.0 0.8 pad_maximum_fusion.1
  0.9 26.7 %all_to_all.25.mine_ref = f32[8,32,512]{2,1,0:T(8,128)S(1)} all-to-all(f32[8,32,512]{2,1,0:T(8,128)S(1)} %broadcast_in_dim.2), channel_id=1, replica_groups=mesh['x'=4,'y'=8,'z'=8,'core'=2] {'z'}, dimensions={0} | all-to-all | bytes 1048576 | tf_op jit(solution)/shard_map/all_to_all | solution.py:157
  27.6 4.4 %collective-permute-start = (f32[8,32,512]{2,1,0:T(8,128)S(1)}, f32[8,32,512]{2,1,0:T(8,128)S(1)}, u32[]{:S(2)}, u32[]{:S(2)}) collective-permute-start(f32[8,32,512]{2,1,0:T(8,128)S(1)} %all_to_all.25.mine_ref), channel_id=1, source_target_pairs={{0,1},{1,0},{2,3},{3,2},{4,5},{5,4},{6,7},{7,6},{8,9},{9,8},{10,11... | collective-permute-start | bytes 1572872 | tf_op jit(solution)/shard_map/ppermute | solution.py:158
  31.9 0.0 copy-start.1
  31.9 1.6 %copy-done.1 = f32[512,1024]{1,0:T(8,128)S(1)} copy-done((f32[512,1024]{1,0:T(8,128)S(1)}, f32[512,1024]{1,0:T(8,128)}, u32[]{:S(2)}) %copy-start.1) | copy-done | bytes 2097176
  33.5 0.3 shard_map.55
  33.8 2.0 %shard_map.56 = f32[8,544,128]{2,1,0:T(8,128)S(1)} custom-call(s32[1]{0:T(128)} %bitcast.3.core_ref, f32[8,32,512]{2,1,0:T(8,128)S(1)} %all_to_all.25.mine_ref, f32[8,32,512]{2,1,0:T(8,128)S(1)} %collective-permute-done.other_ref, f32[16,512]{1,0:T(8,128)S(1)} %copy-done.4, bf16[512,1024]{1,0:T(8,128)(2,1)S(1)} %get-tuple-element.9.block_high, ...), custom_call_target="tpu_custom_call" | custom-call | tf_op jit(solution)/shard_map/pallas_call | solution.py:131
  35.9 33.6 %all_to_all.26.parts = f32[8,544,128]{2,1,0:T(8,128)S(1)} all-to-all(f32[8,544,128]{2,1,0:T(8,128)S(1)} %shard_map.56), channel_id=1, replica_groups={{0,16,128,144,256,272,384,400},{32,48,160,176,288,304,416,432},{64,80,1..., dimensions={0} | all-to-all | bytes 4456448 | tf_op jit(solution)/shard_map/all_to_all | solution.py:151
  69.5 0.1 shard_map.57
  69.6 13.2 %all_to_all.27.parts = f32[4,160,128]{2,1,0:T(8,128)S(1)} all-to-all(f32[4,160,128]{2,1,0:T(8,128)S(1)} %shard_map.57), channel_id=1, replica_groups={{0,32,64,96},{16,48,80,112},{128,160,192,224},{144,176,208,240},{256,28..., dimensions={0} | all-to-all | bytes 655360 | tf_op jit(solution)/shard_map/all_to_all | solution.py:151
  82.8 14.2 %all_to_all.28 = f32[4,128,128]{2,1,0:T(8,128)S(1)} all-to-all(f32[4,128,128]{2,1,0:T(8,128)S(1)} %get-tuple-element.12), channel_id=1, replica_groups={{0,32,64,96},{16,48,80,112},{128,160,192,224},{144,176,208,240},{256,28..., dimensions={0} | all-to-all | bytes 524288 | tf_op jit(solution)/shard_map/all_to_all | solution.py:151
  97.0 1.4 %shard_map.60 = f32[8,512,128]{2,1,0:T(8,128)} custom-call(f32[512,128]{1,0:T(8,128)S(1)} %bitcast.18), custom_call_target="tpu_custom_call" | custom-call | tf_op jit(solution)/shard_map/pallas_call | solution.py:131
  98.4 4.4 %all-to-all-start.4 = ((f32[8,512,128]{2,1,0:T(8,128)}), f32[8,512,128]{2,1,0:T(8,128)}, u32[]{:S(2)}, u32[]{:S(2)}) async-start(f32[8,512,128]{2,1,0:T(8,128)} %shard_map.60), calls=%async_computation.4 | async-start | bytes 4194304 | tf_op jit(solution)/shard_map/all_to_all | solution.py:151
  102.8 0.1 select_bitcast_fusion
  102.9 0.1 pad_maximum_fusion
  103.1 0.0 copy-start.5
  103.1 1.0 fusion.1
  104.1 1.0 copy.11
  105.2 19.5 %all_gather.3 = f32[256,256]{1,0:T(8,128)S(1)} all-gather(f32[16,256]{1,0:T(8,128)S(1)} %get-tuple-element.11), channel_id=1, replica_groups=mesh['x'=4,'y'=8,'z'=8,'core'=2] {'z','core'}, dimensions={0}, use_global_device_ids=true | all-gather | bytes 278528 | tf_op jit(solution)/shard_map/all_gather | solution.py:173
  124.7 1.0 convolution_subtract_fusion
  125.8 0.7 convolution_bitcast_fusion.second_ref
  126.4 0.3 shard_map.59.w_ref
  126.8 0.5 copy-done.2
  127.4 4.2 %shard_map.61 = f32[512,1024]{1,0:T(8,128)} custom-call(f32[512,1024]{1,0:T(8,128)S(1)} %copy-done.2, bf16[2,512,512]{2,1,0:T(8,128)(2,1)S(1)} %shard_map.59.w_ref, f32[8,512,128]{2,1,0:T(8,128)} %all-to-all-done.4.parts_ref), custom_call_target="tpu_custom_call" | custom-call | tf_op jit(solution)/shard_map/pallas_call | solution.py:131
  (14 shorter events, 0.2 us)
Async XLA Ops:
  0.0 103.1 %copy-start = (f32[256,256]{1,0:T(8,128)S(1)}, f32[256,256]{1,0:T(8,128)}, u32[]{:S(2)}) copy-start(f32[256,256]{1,0:T(8,128)} %param.8) | copy-start | bytes 786436
  0.0 33.8 %copy-start.4 = (f32[16,512]{1,0:T(8,128)S(1)}, f32[16,512]{1,0:T(8,128)}, u32[]{:S(2)}) copy-start(f32[16,512]{1,0:T(8,128)} %own_ref.1) | copy-start | bytes 98308
  27.6 6.3 %collective-permute-start = (f32[8,32,512]{2,1,0:T(8,128)S(1)}, f32[8,32,512]{2,1,0:T(8,128)S(1)}, u32[]{:S(2)}, u32[]{:S(2)}) collective-permute-start(f32[8,32,512]{2,1,0:T(8,128)S(1)} %all_to_all.25.mine_ref), channel_id=1, source_target_pairs={{0,1},{1,0},{2,3},{3,2},{4,5},{5,4},{6,7},{7,6},{8,9},{9,8},{10,11... | collective-permute-start | bytes 1572872 | tf_op jit(solution)/shard_map/ppermute | solution.py:158
  31.9 1.6 %copy-start.1 = (f32[512,1024]{1,0:T(8,128)S(1)}, f32[512,1024]{1,0:T(8,128)}, u32[]{:S(2)}) copy-start(f32[512,1024]{1,0:T(8,128)} %block.1) | copy-start | bytes 6291460
  98.4 28.4 %all-to-all-start.4 = ((f32[8,512,128]{2,1,0:T(8,128)}), f32[8,512,128]{2,1,0:T(8,128)}, u32[]{:S(2)}, u32[]{:S(2)}) async-start(f32[8,512,128]{2,1,0:T(8,128)} %shard_map.60), calls=%async_computation.4 | async-start | bytes 4194304 | tf_op jit(solution)/shard_map/all_to_all | solution.py:151
  103.1 22.6 %copy-start.5 = (f32[256,256]{1,0:T(8,128)S(1)}, f32[256,256]{1,0:T(8,128)}, u32[]{:S(2)}) copy-start(f32[256,256]{1,0:T(8,128)} %param.9) | copy-start | bytes 786436
  105.1 21.3 %copy-start.3 = (f32[512,256]{0,1:T(8,128)S(1)}, f32[512,256]{0,1:T(8,128)}, u32[]{:S(2)}) copy-start(f32[512,256]{0,1:T(8,128)} %copy.11) | copy-start | bytes 1572868
  125.8 1.6 %copy-start.2 = (f32[512,1024]{1,0:T(8,128)S(1)}, f32[512,1024]{1,0:T(8,128)}, u32[]{:S(2)}) copy-start(f32[512,1024]{1,0:T(8,128)} %block.1) | copy-start | bytes 6291460

commit v9 on v7

v9 whole, which is shorter than its diff:
```python
import jax
import jax.numpy as jnp
from jax import lax
from jax.experimental import pallas as pl
from jax.experimental.pallas import tpu as pltpu
from jax.sharding import Mesh, PartitionSpec as P

ROW = ("x", "y")
COL = ("z", "core")
NX, NY, NZ = 4, 8, 8
F32, BF16 = jnp.float32, jnp.bfloat16
VMEM = pl.BlockSpec(memory_space=pltpu.VMEM)
SMEM = pl.BlockSpec(memory_space=pltpu.SMEM)
HBM = pl.BlockSpec(memory_space=pltpu.HBM)
PARAMS = pltpu.CompilerParams(vmem_limit_bytes=48 * 2**20)


def device(x, y, z, core):
    return ((x % NX * NY + y % NY) * NZ + z) * 2 + core


NEAR = [
    [device(bx + (px ^ core) + core, by + (py ^ core) + core, z, core) for px in range(2) for py in range(2)]
    for z in range(NZ)
    for core in range(2)
    for bx in range(0, NX, 2)
    for by in range(0, NY, 2)
]
FAR = [
    [device(px + dx, py + dy, z, core) for dx in range(0, NX, 2) for dy in range(0, NY, 2)]
    for z in range(NZ)
    for core in range(2)
    for px in range(2)
    for py in range(2)
]


def split(value):
    high = value.astype(BF16)
    return high, (value - high.astype(F32)).astype(BF16)


def mul(a, b):
    return jnp.dot(a, b, preferred_element_type=F32)


def mul_nt(a, b):
    return lax.dot_general(a, b, (((1,), (1,)), ((), ())), preferred_element_type=F32)


def mul3(a, b, mul=mul):
    return mul(a[0], b[0]) + (mul(a[0], b[1]) + mul(a[1], b[0]))


def split_kernel(block_ref, high, low):
    high[...], low[...] = split(block_ref[...])


def mine_kernel(mine_ref, block_high, block_low, out):
    out[...] = mul3(split(mine_ref[...]), (block_high[...], block_low[...]))


def other_kernel(core_ref, mine_ref, other_ref, own_ref, proj_ref, block_high, block_low, out, both, second):
    other = split(other_ref[...])
    for t in range(4):
        at = slice(t * 256, (t + 1) * 256)
        proj = mul3(other, (block_high[:, at], block_low[:, at]))
        for half in range(2):
            to = slice((2 * t + half) * 128, (2 * t + half + 1) * 128)
            at = slice(half * 128, (half + 1) * 128)
            for m in range(2):
                out[m, to, :] = proj_ref[m * 128 : (m + 1) * 128, to]
                out[2 + m, to, :] = proj[m * 128 : (m + 1) * 128, at]
    core = core_ref[0]
    both[0] = mine_ref[...]
    both[1] = other_ref[...]
    for c in range(2):
        from_core = both.at[core ^ c]
        for z in range(8):
            second[z * 32 + c * 16 : z * 32 + c * 16 + 16, :] = from_core[z * 32 : z * 32 + 16, :]
    cross = mul3(split(own_ref[...]), split(second[...]), mul_nt)
    for m in range(4):
        out[m, 1024:1040, :] = cross[:, :128]
        out[m, 1040:, :] = cross[:, 128:]


def near_kernel(parts, out):
    total = (parts[0] + parts[1]) + (parts[2] + parts[3])
    for m in range(8):
        out[m, :128, :] = total[m * 128 : (m + 1) * 128]
        out[m, 128:, :] = total[1024:]


def far_kernel(parts, out, cross):
    total = ((parts[0] + parts[1]) + (parts[2] + parts[3])) + ((parts[4] + parts[5]) + (parts[6] + parts[7]))
    for m in range(8):
        out[m] = total[:128]
    cross[:, :128] = total[128:144]
    cross[:, 128:] = total[144:]


def pass_kernel(share, after, out):
    out[...] = share[...]


ORDER = (0, 2, 1, 3)


def weight_kernel(core_ref, j_ref, second_ref, first_ref, out, rows, ordered):
    core, j = core_ref[0], j_ref[0]
    for c in range(2):
        for z in range(8):
            at = pl.ds(pl.multiple_of(z * 32 + (core ^ c) * 16, 16), 16)
            to = c * 256 + z * 32
            rows[to : to + 16, :] = second_ref[at, :]
            rows[to + 16 : to + 32, :] = first_ref[at, :]
    for place, d in enumerate(ORDER):
        ordered[place * 128 : (place + 1) * 128, :] = rows[pl.ds(pl.multiple_of((j ^ d) * 128, 128), 128), :]
    out[0], out[1] = split(ordered[...].T)


def natural(parts):
    return jnp.concatenate(
        [jnp.concatenate([part[t * 128 : (t + 1) * 128, :] for t in range(8)], axis=1) for part in parts], axis=0
    )


def middle_kernel(block, w_ref, own, got, out):
    proj = split(natural((own, got)))
    for t in range(2):
        rows = slice(t * 256, (t + 1) * 256)
        out[rows] = block[rows] - mul3((w_ref[0, rows, :256], w_ref[1, rows, :256]), proj)


def update_kernel(middle, w_ref, got, last, out_ref, out, sems):
    proj = split(natural((got, last)))
    stores = []
    for t in range(4):
        rows = slice(t * 128, (t + 1) * 128)
        out[rows] = middle[rows] - mul3((w_ref[0, rows, 256:], w_ref[1, rows, 256:]), proj)
        stores.append(pltpu.make_async_copy(out.at[rows], out_ref.at[rows], sems.at[t]))
        stores[t].start()
    for store in stores:
        store.wait()


def call(kernel, outs, args, scratch=(), scalars=0, inputs=None, out_spec=VMEM):
    single = not isinstance(outs, list)
    return pl.pallas_call(
        kernel,
        out_shape=outs,
        in_specs=inputs or [SMEM] * scalars + [VMEM] * (len(args) - scalars),
        out_specs=out_spec if single else [out_spec] * len(outs),
        scratch_shapes=list(scratch),
        compiler_params=PARAMS,
    )(*args)


def shape(*dims, dtype=F32):
    return jax.ShapeDtypeStruct(dims, dtype)


def exact(left, right):
    dims = (((0,), (0,)), ((), ()))
    return lax.dot_general(left, right, dims, precision=lax.Precision.HIGHEST, preferred_element_type=F32)


def trade(pieces, groups):
    return lax.all_to_all(pieces, ROW + COL, 0, 0, axis_index_groups=groups)


def fetch(value, d):
    def partner(i, n, core):
        return (i + 1) % n if i % 2 == core else (i - 1) % n

    pairs = [
        (device(x, y, z, c), device(partner(x, NX, c) if d & 2 else x, partner(y, NY, c) if d & 1 else y, z, c))
        for x in range(NX)
        for y in range(NY)
        for z in range(NZ)
        for c in range(2)
    ]
    return lax.ppermute(value, ROW + COL, pairs)


def local(vectors, reflectors_first, reflectors_second, factor_first, factor_second):
    core = lax.axis_index("core")
    scalar = core.astype(jnp.int32).reshape(1)
    j = ((lax.axis_index("x") % 2) * 2 + lax.axis_index("y") % 2).astype(jnp.int32).reshape(1)
    shards = jnp.concatenate([reflectors_second, reflectors_first], axis=0)
    mine = lax.all_to_all(jnp.broadcast_to(shards[None], (NZ,) + shards.shape), "z", 0, 0).reshape(256, 512)
    other = lax.ppermute(mine, "core", [(0, 1), (1, 0)])
    block = call(split_kernel, [shape(512, 1024, dtype=BF16)] * 2, (vectors,))
    proj = call(mine_kernel, shape(256, 1024), (mine, *block))
    parts = call(
        other_kernel,
        shape(4, 1056, 128),
        (scalar, mine, other, reflectors_first, proj, *block),
        (pltpu.VMEM((2, 256, 512), F32), pltpu.VMEM((256, 512), F32)),
        scalars=1,
    )
    parts = call(near_kernel, shape(8, 160, 128), (trade(parts, NEAR),))
    share, cross = call(far_kernel, [shape(8, 128, 128), shape(16, 256)], (trade(parts, FAR),))
    share = trade(share, FAR).reshape(1024, 128)
    cross = lax.all_gather(cross, COL, axis=0, tiled=True)
    share = call(pass_kernel, shape(1024, 128), (share, cross), inputs=[VMEM, HBM])
    got = {d: fetch(share, d) for d in (3, 2, 1)}
    both = jnp.stack([jnp.where(core == 0, mine, other), jnp.where(core == 0, other, mine)]).reshape(2, 8, 32, 512)
    by_core = both.transpose(1, 0, 2, 3)
    second = by_core[:, :, :16].reshape(256, 512)
    first = by_core[:, :, 16:].reshape(256, 512)
    w_first = exact(factor_first, first)
    w_second = exact(factor_second, second - exact(cross, w_first))
    square = pltpu.VMEM((512, 512), F32)
    weights = call(
        weight_kernel, shape(2, 512, 512, dtype=BF16), (scalar, j, w_second, w_first), (square, square), scalars=2
    )
    middle = call(middle_kernel, shape(512, 1024), (vectors, weights, share, got[2]))
    return call(
        update_kernel,
        shape(512, 1024),
        (middle, weights, got[1], got[3]),
        (pltpu.VMEM((512, 1024), F32), pltpu.SemaphoreType.DMA((4,))),
        out_spec=HBM,
    )


def solution(mesh):
    fine = Mesh(mesh.devices.reshape(NX, NY, NZ, 2), ROW + COL)
    return jax.shard_map(
        local,
        mesh=fine,
        in_specs=(P(ROW, COL), P(COL, ROW), P(COL, ROW), P(), P()),
        out_specs=P(ROW, COL),
        check_vma=False,
    )
```

time: 133 us -> 134 us (level)
  blocking collectives: 91.3 us -> 66.4 us
  waiting for transfers between devices: 11 us -> 26.8 us
  starting transfers between devices: 13.5 us -> 23.7 us
    all_to_all x2 -> x1, blocking collectives: 48.8 us -> 24 us  [trade(): return lax.all_to_all(pieces, ROW + COL, 0, 0, axis_index_groups=groups)]
    ppermute x0 -> x3, starting transfers between devices: none -> 10.8 us  [fetch(): return lax.ppermute(value, ROW + COL, pairs)]
    all_to_all x2, waiting for transfers between devices: 11 us -> 20.9 us  [trade(): return lax.all_to_all(pieces, ROW + COL, 0, 0, axis_index_groups=groups)]
    ppermute x0 -> x3, waiting for transfers between devices: none -> 5.91 us  [fetch(): return lax.ppermute(value, ROW + COL, pairs)]
    pallas_call x7 -> x9, Pallas kernels: 10 us -> 10.4 us  [call(): pl.pallas_call(kernel, out_shape=outs, in_specs=inputs or [SMEM] * scalar...]
  transfers between devices with their start and end apart: 3 -> 6, of which waited for: 2 -> 3; matrix products, arithmetic and copies ran while one was open for 3% -> 2% of each run, Pallas kernels for 0% -> 3%
where the time goes in v9:
time: 134 us; the launch traced here: 133 us
  blocking collectives  66.4 us (50%)
  waiting for transfers between devices  26.8 us (20%)
  starting transfers between devices  23.7 us (18%)
  Pallas kernels  10.4 us (8%)
  matrix products  2.7 us (2%)
  local copies, waits for them, and re-layouts  1.95 us (1%)
    all_to_all x1, blocking collectives, local(): lax.all_to_all(jnp.broadcast_to(shards[None], (NZ,) + shards.shape), 'z',...  26.7 us
    all_to_all x1, blocking collectives, trade(): return lax.all_to_all(pieces, ROW + COL, 0, 0, axis_index_groups=groups)  24 us
    all_to_all x2, waiting for transfers between devices, trade(): return lax.all_to_all(pieces, ROW + COL, 0, 0, axis_index_groups=groups)  20.9 us
    all_gather x1, blocking collectives, local(): cross = lax.all_gather(cross, COL, axis=0, tiled=True)  15.7 us
    ppermute x3, starting transfers between devices, fetch(): return lax.ppermute(value, ROW + COL, pairs)  10.8 us
    pallas_call x9, Pallas kernels, call(): pl.pallas_call(kernel, out_shape=outs, in_specs=inputs or [SMEM] * scalar...  10.4 us
    all_to_all x2, starting transfers between devices, trade(): return lax.all_to_all(pieces, ROW + COL, 0, 0, axis_index_groups=groups)  8.49 us
    ppermute x3, waiting for transfers between devices, fetch(): return lax.ppermute(value, ROW + COL, pairs)  5.91 us
  transfers between devices with their start and end apart: 6, of which 3 were waited for; matrix products, arithmetic and copies ran while one was open for 2% of the time, Pallas kernels for 3%

profile of v9, /device:TPU:1, one launch (start us, length us, event | category | flops | bytes accessed | tf_op | source)
XLA Modules:
  0.0 133.2 jit_solution(9418173519385223953)
XLA Ops:
  0.0 0.8 pad_maximum_fusion
  0.9 26.7 %all_to_all.20 = f32[8,32,512]{2,1,0:T(8,128)S(1)} all-to-all(f32[8,32,512]{2,1,0:T(8,128)S(1)} %broadcast_in_dim.2), channel_id=1, replica_groups=mesh['x'=4,'y'=8,'z'=8,'core'=2] {'z'}, dimensions={0} | all-to-all | bytes 1048576 | tf_op jit(solution)/shard_map/all_to_all | solution.py:191
  27.5 4.4 %collective-permute-start = (f32[256,512]{1,0:T(8,128)S(1)}, f32[256,512]{1,0:T(8,128)S(1)}, u32[]{:S(2)}, u32[]{:S(2)}) collective-permute-start(f32[256,512]{1,0:T(8,128)S(1)} %bitcast.25), channel_id=1, source_target_pairs={{0,1},{1,0},{2,3},{3,2},{4,5},{5,4},{6,7},{7,6},{8,9},{9,8},{10,11... | collective-permute-start | bytes 1572872 | tf_op jit(solution)/shard_map/ppermute | solution.py:192
  31.9 1.6 %copy-done.1 = f32[512,1024]{1,0:T(8,128)S(1)} copy-done((f32[512,1024]{1,0:T(8,128)S(1)}, f32[512,1024]{1,0:T(8,128)}, u32[]{:S(2)}) %copy-start.1) | copy-done | bytes 2097176
  33.5 0.3 shard_map.55
  33.8 1.0 shard_map.56.proj_ref
  34.8 2.5 %shard_map.57 = f32[4,1056,128]{2,1,0:T(8,128)} custom-call(s32[1]{0:T(128)} %bitcast.core_ref, f32[256,512]{1,0:T(8,128)S(1)} %bitcast.27, f32[256,512]{1,0:T(8,128)S(1)} %collective-permute-done.other_ref, f32[16,512]{1,0:T(8,128)S(1)} %copy-done.2, f32[256,1024]{1,0:T(8,128)S(1)} %shard_map.56.proj_ref, ...), custom_call_target="tpu_custom_call" | custom-call | tf_op jit(solution)/shard_map/pallas_call | solution.py:149
  37.3 24.0 %all_to_all.21.parts = f32[4,1056,128]{2,1,0:T(8,128)S(1)} all-to-all(f32[4,1056,128]{2,1,0:T(8,128)} %shard_map.57), channel_id=1, replica_groups={{0,16,128,144},{32,48,160,176},{64,80,192,208},{96,112,224,240},{256,27..., dimensions={0} | all-to-all | bytes 4325376 | tf_op jit(solution)/shard_map/all_to_all | solution.py:169
  61.3 0.9 shard_map.58
  62.3 5.0 %all-to-all-start.2 = ((f32[8,160,128]{2,1,0:T(8,128)}), f32[8,160,128]{2,1,0:T(8,128)S(1)}, u32[]{:S(2)}, u32[]{:S(2)}) async-start(f32[8,160,128]{2,1,0:T(8,128)} %shard_map.58), calls=%async_computation.2 | async-start | bytes 1310720 | tf_op jit(solution)/shard_map/all_to_all | solution.py:169
  67.3 20.9 %all-to-all-done.2.parts = f32[8,160,128]{2,1,0:T(8,128)S(1)} async-done(((f32[8,160,128]{2,1,0:T(8,128)}), f32[8,160,128]{2,1,0:T(8,128)S(1)}, u32[]{:S(2)}, u32[]{:S(2)}) %all-to-all-start.2) | async-done | bytes 655392 | tf_op jit(solution)/shard_map/all_to_all | solution.py:169
  88.2 0.8 shard_map.59
  89.0 3.5 %all-to-all-start.3 = ((f32[8,128,128]{2,1,0:T(8,128)}), f32[8,128,128]{2,1,0:T(8,128)S(1)}, u32[]{:S(2)}, u32[]{:S(2)}) async-start(f32[8,128,128]{2,1,0:T(8,128)} %get-tuple-element.12), calls=%async_computation.3 | async-start | bytes 1048576 | tf_op jit(solution)/shard_map/all_to_all | solution.py:169
  92.9 1.0 fusion.1
  94.1 15.7 %all_gather.3.after = f32[256,256]{1,0:T(8,128)S(1)} all-gather(f32[16,256]{1,0:T(8,128)S(1)} %get-tuple-element.11), channel_id=1, replica_groups=mesh['x'=4,'y'=8,'z'=8,'core'=2] {'z','core'}, dimensions={0}, use_global_device_ids=true | all-gather | bytes 278528 | tf_op jit(solution)/shard_map/all_gather | solution.py:205
  109.8 4.6 %collective-permute-start.1 = (f32[1024,128]{1,0:T(8,128)S(1)}, f32[1024,128]{1,0:T(8,128)S(1)}, u32[]{:S(2)}, u32[]{:S(2)}) collective-permute-start(f32[1024,128]{1,0:T(8,128)S(1)} %shard_map.61.own), channel_id=1, source_target_pairs={{0,128},{1,385},{2,130},{3,387},{4,132},{5,389},{6,134},{7,391},{8... | collective-permute-start | bytes 1572872 | tf_op jit(solution)/shard_map/ppermute | solution.py:183
  114.5 3.6 %collective-permute-start.2 = (f32[1024,128]{1,0:T(8,128)S(1)}, f32[1024,128]{1,0:T(8,128)S(1)}, u32[]{:S(2)}, u32[]{:S(2)}) collective-permute-start(f32[1024,128]{1,0:T(8,128)S(1)} %shard_map.61.own), channel_id=1, source_target_pairs={{0,16},{1,113},{2,18},{3,115},{4,20},{5,117},{6,22},{7,119},{8,24}... | collective-permute-start | bytes 1572872 | tf_op jit(solution)/shard_map/ppermute | solution.py:183
  118.1 2.6 %collective-permute-start.3 = (f32[1024,128]{1,0:T(8,128)S(1)}, f32[1024,128]{1,0:T(8,128)S(1)}, u32[]{:S(2)}, u32[]{:S(2)}) collective-permute-start(f32[1024,128]{1,0:T(8,128)S(1)} %shard_map.61.own), channel_id=1, source_target_pairs={{0,144},{1,497},{2,146},{3,499},{4,148},{5,501},{6,150},{7,503},{8... | collective-permute-start | bytes 1572872 | tf_op jit(solution)/shard_map/ppermute | solution.py:183
  120.7 1.0 convolution_subtract_fusion
  121.8 0.7 convolution_bitcast_fusion.second_ref
  122.4 0.4 shard_map.60.w_ref
  122.8 2.6 %shard_map.62.middle = f32[512,1024]{1,0:T(8,128)S(1)} custom-call(f32[512,1024]{1,0:T(8,128)} %block.1, bf16[2,512,512]{2,1,0:T(8,128)(2,1)S(1)} %shard_map.60.w_ref, f32[1024,128]{1,0:T(8,128)S(1)} %shard_map.61.own, f32[1024,128]{1,0:T(8,128)S(1)} %collective-permute-done.1.got), custom_call_target="tpu_custom_call" | custom-call | tf_op jit(solution)/shard_map/pallas_call | solution.py:149
  125.7 5.6 %collective-permute-done.3.last = f32[1024,128]{1,0:T(8,128)S(1)} collective-permute-done((f32[1024,128]{1,0:T(8,128)S(1)}, f32[1024,128]{1,0:T(8,128)S(1)}, u32[]{:S(2)}, u32[]{:S(2)}) %collective-permute-start.3) | collective-permute-done | bytes 524320 | tf_op jit(solution)/shard_map/ppermute | solution.py:183
  131.3 1.8 %shard_map.63 = f32[512,1024]{1,0:T(8,128)} custom-call(f32[512,1024]{1,0:T(8,128)S(1)} %shard_map.62.middle, bf16[2,512,512]{2,1,0:T(8,128)(2,1)S(1)} %shard_map.60.w_ref, f32[1024,128]{1,0:T(8,128)S(1)} %collective-permute-done.2.got, f32[1024,128]{1,0:T(8,128)S(1)} %collective-permute-done.3.last), custom_call_target="tpu_custom_call" | custom-call | tf_op jit(solution)/shard_map/pallas_call | solution.py:149
  (17 shorter events, 0.9 us)
Async XLA Ops:
  0.0 92.9 %copy-start = (f32[256,256]{1,0:T(8,128)S(1)}, f32[256,256]{1,0:T(8,128)}, u32[]{:S(2)}) copy-start(f32[256,256]{1,0:T(8,128)} %param.8) | copy-start | bytes 786436
  27.5 7.3 %collective-permute-start = (f32[256,512]{1,0:T(8,128)S(1)}, f32[256,512]{1,0:T(8,128)S(1)}, u32[]{:S(2)}, u32[]{:S(2)}) collective-permute-start(f32[256,512]{1,0:T(8,128)S(1)} %bitcast.25), channel_id=1, source_target_pairs={{0,1},{1,0},{2,3},{3,2},{4,5},{5,4},{6,7},{7,6},{8,9},{9,8},{10,11... | collective-permute-start | bytes 1572872 | tf_op jit(solution)/shard_map/ppermute | solution.py:192
  31.9 1.6 %copy-start.1 = (f32[512,1024]{1,0:T(8,128)S(1)}, f32[512,1024]{1,0:T(8,128)}, u32[]{:S(2)}) copy-start(f32[512,1024]{1,0:T(8,128)} %block.1) | copy-start | bytes 6291460
  33.8 1.0 copy-start.2
  62.3 25.9 %all-to-all-start.2 = ((f32[8,160,128]{2,1,0:T(8,128)}), f32[8,160,128]{2,1,0:T(8,128)S(1)}, u32[]{:S(2)}, u32[]{:S(2)}) async-start(f32[8,160,128]{2,1,0:T(8,128)} %shard_map.58), calls=%async_computation.2 | async-start | bytes 1310720 | tf_op jit(solution)/shard_map/all_to_all | solution.py:169
  89.0 20.8 %all-to-all-start.3 = ((f32[8,128,128]{2,1,0:T(8,128)}), f32[8,128,128]{2,1,0:T(8,128)S(1)}, u32[]{:S(2)}, u32[]{:S(2)}) async-start(f32[8,128,128]{2,1,0:T(8,128)} %get-tuple-element.12), calls=%async_computation.3 | async-start | bytes 1048576 | tf_op jit(solution)/shard_map/all_to_all | solution.py:169
  93.9 27.9 %copy-start.3 = (f32[256,256]{1,0:T(8,128)S(1)}, f32[256,256]{1,0:T(8,128)}, u32[]{:S(2)}) copy-start(f32[256,256]{1,0:T(8,128)} %param.9) | copy-start | bytes 786436
  109.8 13.0 %collective-permute-start.1 = (f32[1024,128]{1,0:T(8,128)S(1)}, f32[1024,128]{1,0:T(8,128)S(1)}, u32[]{:S(2)}, u32[]{:S(2)}) collective-permute-start(f32[1024,128]{1,0:T(8,128)S(1)} %shard_map.61.own), channel_id=1, source_target_pairs={{0,128},{1,385},{2,130},{3,387},{4,132},{5,389},{6,134},{7,391},{8... | collective-permute-start | bytes 1572872 | tf_op jit(solution)/shard_map/ppermute | solution.py:183
  114.5 11.3 %collective-permute-start.2 = (f32[1024,128]{1,0:T(8,128)S(1)}, f32[1024,128]{1,0:T(8,128)S(1)}, u32[]{:S(2)}, u32[]{:S(2)}) collective-permute-start(f32[1024,128]{1,0:T(8,128)S(1)} %shard_map.61.own), channel_id=1, source_target_pairs={{0,16},{1,113},{2,18},{3,115},{4,20},{5,117},{6,22},{7,119},{8,24}... | collective-permute-start | bytes 1572872 | tf_op jit(solution)/shard_map/ppermute | solution.py:183
  118.1 13.2 %collective-permute-start.3 = (f32[1024,128]{1,0:T(8,128)S(1)}, f32[1024,128]{1,0:T(8,128)S(1)}, u32[]{:S(2)}, u32[]{:S(2)}) collective-permute-start(f32[1024,128]{1,0:T(8,128)S(1)} %shard_map.61.own), channel_id=1, source_target_pairs={{0,144},{1,497},{2,146},{3,499},{4,148},{5,501},{6,150},{7,503},{8... | collective-permute-start | bytes 1572872 | tf_op jit(solution)/shard_map/ppermute | solution.py:183

commit v10 on v9

--- a/solution.py
+++ b/solution.py
@@ -52,33 +52,36 @@
     return mul(a[0], b[0]) + (mul(a[0], b[1]) + mul(a[1], b[0]))
 
 
+def shard_kernel(second, first, out):
+    for z in range(8):
+        out[z, :16] = second[...]
+        out[z, 16:] = first[...]
+
+
 def split_kernel(block_ref, high, low):
     high[...], low[...] = split(block_ref[...])
 
 
-def mine_kernel(mine_ref, block_high, block_low, out):
-    out[...] = mul3(split(mine_ref[...]), (block_high[...], block_low[...]))
-
-
-def other_kernel(core_ref, mine_ref, other_ref, own_ref, proj_ref, block_high, block_low, out, both, second):
-    other = split(other_ref[...])
-    for t in range(4):
-        at = slice(t * 256, (t + 1) * 256)
-        proj = mul3(other, (block_high[:, at], block_low[:, at]))
-        for half in range(2):
-            to = slice((2 * t + half) * 128, (2 * t + half + 1) * 128)
-            at = slice(half * 128, (half + 1) * 128)
-            for m in range(2):
-                out[m, to, :] = proj_ref[m * 128 : (m + 1) * 128, to]
-                out[2 + m, to, :] = proj[m * 128 : (m + 1) * 128, at]
+def project_kernel(core_ref, mine_ref, other_ref, own_ref, block_high, block_low, out, high, low, both):
     core = core_ref[0]
     both[0] = mine_ref[...]
     both[1] = other_ref[...]
     for c in range(2):
         from_core = both.at[core ^ c]
         for z in range(8):
-            second[z * 32 + c * 16 : z * 32 + c * 16 + 16, :] = from_core[z * 32 : z * 32 + 16, :]
-    cross = mul3(split(own_ref[...]), split(second[...]), mul_nt)
+            for panel in range(2):
+                h, l = split(from_core[z, panel * 16 : panel * 16 + 16, :])
+                at = panel * 256 + z * 32 + c * 16
+                high[at : at + 16, :] = h
+                low[at : at + 16, :] = l
+    for t in range(4):
+        at = slice(t * 256, (t + 1) * 256)
+        value = mul3((high[...], low[...]), (block_high[:, at], block_low[:, at]))
+        for m in range(4):
+            for half in range(2):
+                to = (2 * t + half) * 128
+                out[m, to : to + 128, :] = value[m * 128 : (m + 1) * 128, half * 128 : (half + 1) * 128]
+    cross = mul3(split(own_ref[...]), (high[:256], low[:256]), mul_nt)
     for m in range(4):
         out[m, 1024:1040, :] = cross[:, :128]
         out[m, 1040:, :] = cross[:, 128:]
@@ -91,7 +94,7 @@
         out[m, 128:, :] = total[1024:]
 
 
-def far_kernel(parts, out, cross):
+def far_kernel(parts, after, out, cross):
     total = ((parts[0] + parts[1]) + (parts[2] + parts[3])) + ((parts[4] + parts[5]) + (parts[6] + parts[7]))
     for m in range(8):
         out[m] = total[:128]
@@ -103,19 +106,16 @@
     out[...] = share[...]
 
 
-ORDER = (0, 2, 1, 3)
-
-
-def weight_kernel(core_ref, j_ref, second_ref, first_ref, out, rows, ordered):
-    core, j = core_ref[0], j_ref[0]
-    for c in range(2):
-        for z in range(8):
-            at = pl.ds(pl.multiple_of(z * 32 + (core ^ c) * 16, 16), 16)
-            to = c * 256 + z * 32
-            rows[to : to + 16, :] = second_ref[at, :]
-            rows[to + 16 : to + 32, :] = first_ref[at, :]
+ORDER = (0, 3, 2, 1)
+
+
+def weight_kernel(j_ref, second_ref, first_ref, out, ordered):
+    j = j_ref[0]
     for place, d in enumerate(ORDER):
-        ordered[place * 128 : (place + 1) * 128, :] = rows[pl.ds(pl.multiple_of((j ^ d) * 128, 128), 128), :]
+        quarter = j ^ d
+        at = pl.ds(pl.multiple_of((quarter & 1) * 128, 128), 128)
+        rows = jnp.where(quarter < 2, second_ref[at, :], first_ref[at, :])
+        ordered[place * 128 : (place + 1) * 128, :] = rows
     out[0], out[1] = split(ordered[...].T)
 
 
@@ -187,39 +187,43 @@
     core = lax.axis_index("core")
     scalar = core.astype(jnp.int32).reshape(1)
     j = ((lax.axis_index("x") % 2) * 2 + lax.axis_index("y") % 2).astype(jnp.int32).reshape(1)
-    shards = jnp.concatenate([reflectors_second, reflectors_first], axis=0)
-    mine = lax.all_to_all(jnp.broadcast_to(shards[None], (NZ,) + shards.shape), "z", 0, 0).reshape(256, 512)
+    shards = call(shard_kernel, shape(NZ, 32, 512), (reflectors_second, reflectors_first))
+    mine = lax.all_to_all(shards, "z", 0, 0)
     other = lax.ppermute(mine, "core", [(0, 1), (1, 0)])
     block = call(split_kernel, [shape(512, 1024, dtype=BF16)] * 2, (vectors,))
-    proj = call(mine_kernel, shape(256, 1024), (mine, *block))
+    wide = pltpu.VMEM((512, 512), BF16)
     parts = call(
-        other_kernel,
+        project_kernel,
         shape(4, 1056, 128),
-        (scalar, mine, other, reflectors_first, proj, *block),
-        (pltpu.VMEM((2, 256, 512), F32), pltpu.VMEM((256, 512), F32)),
+        (scalar, mine, other, reflectors_first, *block),
+        (wide, wide, pltpu.VMEM((2, 8, 32, 512), F32)),
         scalars=1,
     )
+    by_core = jnp.stack([jnp.where(core == 0, mine, other), jnp.where(core == 0, other, mine)], axis=1)
+    second = by_core[:, :, :16].reshape(256, 512)
+    first = by_core[:, :, 16:].reshape(256, 512)
+    w_first = exact(factor_first, first)
     parts = call(near_kernel, shape(8, 160, 128), (trade(parts, NEAR),))
-    share, cross = call(far_kernel, [shape(8, 128, 128), shape(16, 256)], (trade(parts, FAR),))
+    share, cross = call(
+        far_kernel, [shape(8, 128, 128), shape(16, 256)], (trade(parts, FAR), w_first), inputs=[VMEM, HBM]
+    )
     share = trade(share, FAR).reshape(1024, 128)
     cross = lax.all_gather(cross, COL, axis=0, tiled=True)
     share = call(pass_kernel, shape(1024, 128), (share, cross), inputs=[VMEM, HBM])
     got = {d: fetch(share, d) for d in (3, 2, 1)}
-    both = jnp.stack([jnp.where(core == 0, mine, other), jnp.where(core == 0, other, mine)]).reshape(2, 8, 32, 512)
-    by_core = both.transpose(1, 0, 2, 3)
-    second = by_core[:, :, :16].reshape(256, 512)
-    first = by_core[:, :, 16:].reshape(256, 512)
-    w_first = exact(factor_first, first)
     w_second = exact(factor_second, second - exact(cross, w_first))
-    square = pltpu.VMEM((512, 512), F32)
     weights = call(
-        weight_kernel, shape(2, 512, 512, dtype=BF16), (scalar, j, w_second, w_first), (square, square), scalars=2
-    )
-    middle = call(middle_kernel, shape(512, 1024), (vectors, weights, share, got[2]))
+        weight_kernel,
+        shape(2, 512, 512, dtype=BF16),
+        (j, w_second, w_first),
+        (pltpu.VMEM((512, 512), F32),),
+        scalars=1,
+    )
+    middle = call(middle_kernel, shape(512, 1024), (vectors, weights, share, got[3]))
     return call(
         update_kernel,
         shape(512, 1024),
-        (middle, weights, got[1], got[3]),
+        (middle, weights, got[2], got[1]),
         (pltpu.VMEM((512, 1024), F32), pltpu.SemaphoreType.DMA((4,))),
         out_spec=HBM,
     )

time: 134 us -> 129 us (0.963)
  waiting for transfers between devices: 26.8 us -> 23.9 us
  local copies, waits for them, and re-layouts: 1.95 us -> 3.44 us
  Pallas kernels: 10.4 us -> 8.94 us
    ppermute x3, waiting for transfers between devices: 5.91 us -> 3.68 us  [fetch(): return lax.ppermute(value, ROW + COL, pairs)]
    unnamed x8 -> x12, local copies, waits for them, and re-layouts: 1.6 us -> 3.16 us
    pallas_call x9, Pallas kernels: 10.4 us -> 8.94 us  [call(): pl.pallas_call(kernel, out_shape=outs, in_specs=inputs or [SMEM] * scalar...]
  transfers between devices with their start and end apart: 6 -> 6, of which waited for: 3 -> 5; matrix products, arithmetic and copies ran while one was open for 2% -> 3% of each run, Pallas kernels for 3% -> 3%
where the time goes in v10:
time: 129 us; the launch traced here: 128 us
  blocking collectives  66.1 us (51%)
  waiting for transfers between devices  23.9 us (19%)
  starting transfers between devices  22.8 us (18%)
  Pallas kernels  8.94 us (7%)
  local copies, waits for them, and re-layouts  3.44 us (3%)
  matrix products  2.71 us (2%)
    all_to_all x1, blocking collectives, local(): mine = lax.all_to_all(shards, 'z', 0, 0)  26.7 us
    all_to_all x1, blocking collectives, trade(): return lax.all_to_all(pieces, ROW + COL, 0, 0, axis_index_groups=groups)  23.8 us
    all_to_all x2, waiting for transfers between devices, trade(): return lax.all_to_all(pieces, ROW + COL, 0, 0, axis_index_groups=groups)  20.2 us
    all_gather x1, blocking collectives, local(): cross = lax.all_gather(cross, COL, axis=0, tiled=True)  15.7 us
    ppermute x3, starting transfers between devices, fetch(): return lax.ppermute(value, ROW + COL, pairs)  10.9 us
    pallas_call x9, Pallas kernels, call(): pl.pallas_call(kernel, out_shape=outs, in_specs=inputs or [SMEM] * scalar...  8.94 us
    all_to_all x2, starting transfers between devices, trade(): return lax.all_to_all(pieces, ROW + COL, 0, 0, axis_index_groups=groups)  7.58 us
    ppermute x1, starting transfers between devices, local(): other = lax.ppermute(mine, 'core', [(0, 1), (1, 0)])  4.35 us
  transfers between devices with their start and end apart: 6, of which 5 were waited for; matrix products, arithmetic and copies ran while one was open for 3% of the time, Pallas kernels for 3%

profile of v10, /device:TPU:1, one launch (start us, length us, event | category | flops | bytes accessed | tf_op | source)
XLA Modules:
  0.0 128.4 jit_solution(17167475934995035512)
XLA Ops:
  0.0 0.8 copy-done.2
  0.8 0.8 copy-done.4
  1.6 26.7 %all_to_all.20.mine_ref = f32[8,32,512]{2,1,0:T(8,128)S(1)} all-to-all(f32[8,32,512]{2,1,0:T(8,128)S(1)} %shard_map.55), channel_id=1, replica_groups=mesh['x'=4,'y'=8,'z'=8,'core'=2] {'z'}, dimensions={0} | all-to-all | bytes 1048576 | tf_op jit(solution)/shard_map/all_to_all | solution.py:191
  28.3 4.4 %collective-permute-start = (f32[8,32,512]{2,1,0:T(8,128)S(1)}, f32[8,32,512]{2,1,0:T(8,128)S(1)}, u32[]{:S(2)}, u32[]{:S(2)}) collective-permute-start(f32[8,32,512]{2,1,0:T(8,128)S(1)} %all_to_all.20.mine_ref), channel_id=1, source_target_pairs={{0,1},{1,0},{2,3},{3,2},{4,5},{5,4},{6,7},{7,6},{8,9},{9,8},{10,11... | collective-permute-start | bytes 1572872 | tf_op jit(solution)/shard_map/ppermute | solution.py:192
  32.6 1.6 %copy-done.1 = f32[512,1024]{1,0:T(8,128)S(1)} copy-done((f32[512,1024]{1,0:T(8,128)S(1)}, f32[512,1024]{1,0:T(8,128)}, u32[]{:S(2)}) %copy-start.1) | copy-done | bytes 2097176
  34.5 2.0 %shard_map.57 = f32[4,1056,128]{2,1,0:T(8,128)S(1)} custom-call(s32[1]{0:T(128)} %bitcast.4.core_ref, f32[8,32,512]{2,1,0:T(8,128)S(1)} %all_to_all.20.mine_ref, f32[8,32,512]{2,1,0:T(8,128)S(1)} %collective-permute-done.other_ref, f32[16,512]{1,0:T(8,128)S(1)} %copy-done.3, bf16[512,1024]{1,0:T(8,128)(2,1)S(1)} %get-tuple-element.9.block_high, ...), custom_call_target="tpu_custom_call" | custom-call | tf_op jit(solution)/shard_map/pallas_call | solution.py:149
  36.6 23.8 %all_to_all.21.parts = f32[4,1056,128]{2,1,0:T(8,128)S(1)} all-to-all(f32[4,1056,128]{2,1,0:T(8,128)S(1)} %shard_map.57), channel_id=1, replica_groups={{0,16,128,144},{32,48,160,176},{64,80,192,208},{96,112,224,240},{256,27..., dimensions={0} | all-to-all | bytes 4325376 | tf_op jit(solution)/shard_map/all_to_all | solution.py:169
  60.4 0.9 shard_map.58
  61.3 4.1 %all-to-all-start.2 = ((f32[8,160,128]{2,1,0:T(8,128)}), f32[8,160,128]{2,1,0:T(8,128)S(1)}, u32[]{:S(2)}, u32[]{:S(2)}) async-start(f32[8,160,128]{2,1,0:T(8,128)} %shard_map.58), calls=%async_computation.2 | async-start | bytes 1310720 | tf_op jit(solution)/shard_map/all_to_all | solution.py:169
  65.7 1.0 fusion.1
  66.9 19.7 %all-to-all-done.2.parts = f32[8,160,128]{2,1,0:T(8,128)S(1)} async-done(((f32[8,160,128]{2,1,0:T(8,128)}), f32[8,160,128]{2,1,0:T(8,128)S(1)}, u32[]{:S(2)}, u32[]{:S(2)}) %all-to-all-start.2) | async-done | bytes 655392 | tf_op jit(solution)/shard_map/all_to_all | solution.py:169
  86.6 0.8 shard_map.59
  87.5 3.5 %all-to-all-start.3 = ((f32[8,128,128]{2,1,0:T(8,128)}), f32[8,128,128]{2,1,0:T(8,128)S(1)}, u32[]{:S(2)}, u32[]{:S(2)}) async-start(f32[8,128,128]{2,1,0:T(8,128)} %get-tuple-element.12), calls=%async_computation.3 | async-start | bytes 1048576 | tf_op jit(solution)/shard_map/all_to_all | solution.py:169
  91.1 15.7 %all_gather.3.after = f32[256,256]{1,0:T(8,128)S(1)} all-gather(f32[16,256]{1,0:T(8,128)S(1)} %get-tuple-element.11), channel_id=1, replica_groups=mesh['x'=4,'y'=8,'z'=8,'core'=2] {'z','core'}, dimensions={0}, use_global_device_ids=true | all-gather | bytes 278528 | tf_op jit(solution)/shard_map/all_gather | solution.py:211
  106.7 0.5 all-to-all-done.3
  107.3 6.2 %collective-permute-start.1 = (f32[1024,128]{1,0:T(8,128)S(1)}, f32[1024,128]{1,0:T(8,128)S(1)}, u32[]{:S(2)}, u32[]{:S(2)}) collective-permute-start(f32[1024,128]{1,0:T(8,128)S(1)} %shard_map.61.own), channel_id=1, source_target_pairs={{0,144},{1,497},{2,146},{3,499},{4,148},{5,501},{6,150},{7,503},{8... | collective-permute-start | bytes 1572872 | tf_op jit(solution)/shard_map/ppermute | solution.py:183
  113.4 1.9 %collective-permute-start.2 = (f32[1024,128]{1,0:T(8,128)S(1)}, f32[1024,128]{1,0:T(8,128)S(1)}, u32[]{:S(2)}, u32[]{:S(2)}) collective-permute-start(f32[1024,128]{1,0:T(8,128)S(1)} %shard_map.61.own), channel_id=1, source_target_pairs={{0,128},{1,385},{2,130},{3,387},{4,132},{5,389},{6,134},{7,391},{8... | collective-permute-start | bytes 1572872 | tf_op jit(solution)/shard_map/ppermute | solution.py:183
  115.4 2.8 %collective-permute-start.3 = (f32[1024,128]{1,0:T(8,128)S(1)}, f32[1024,128]{1,0:T(8,128)S(1)}, u32[]{:S(2)}, u32[]{:S(2)}) collective-permute-start(f32[1024,128]{1,0:T(8,128)S(1)} %shard_map.61.own), channel_id=1, source_target_pairs={{0,16},{1,113},{2,18},{3,115},{4,20},{5,117},{6,22},{7,119},{8,24}... | collective-permute-start | bytes 1572872 | tf_op jit(solution)/shard_map/ppermute | solution.py:183
  118.2 1.0 convolution_subtract_fusion
  119.3 0.7 convolution_bitcast_fusion.second_ref
  120.6 2.6 %shard_map.62.middle = f32[512,1024]{1,0:T(8,128)S(1)} custom-call(f32[512,1024]{1,0:T(8,128)} %block.1, bf16[2,512,512]{2,1,0:T(8,128)(2,1)S(1)} %shard_map.60.w_ref, f32[1024,128]{1,0:T(8,128)S(1)} %shard_map.61.own, f32[1024,128]{1,0:T(8,128)S(1)} %collective-permute-done.1.got), custom_call_target="tpu_custom_call" | custom-call | tf_op jit(solution)/shard_map/pallas_call | solution.py:149
  123.2 2.9 %collective-permute-done.2.got = f32[1024,128]{1,0:T(8,128)S(1)} collective-permute-done((f32[1024,128]{1,0:T(8,128)S(1)}, f32[1024,128]{1,0:T(8,128)S(1)}, u32[]{:S(2)}, u32[]{:S(2)}) %collective-permute-start.2) | collective-permute-done | bytes 524320 | tf_op jit(solution)/shard_map/ppermute | solution.py:183
  126.1 0.4 collective-permute-done.3.last
  126.6 1.8 %shard_map.63 = f32[512,1024]{1,0:T(8,128)} custom-call(f32[512,1024]{1,0:T(8,128)S(1)} %shard_map.62.middle, bf16[2,512,512]{2,1,0:T(8,128)(2,1)S(1)} %shard_map.60.w_ref, f32[1024,128]{1,0:T(8,128)S(1)} %collective-permute-done.2.got, f32[1024,128]{1,0:T(8,128)S(1)} %collective-permute-done.3.last), custom_call_target="tpu_custom_call" | custom-call | tf_op jit(solution)/shard_map/pallas_call | solution.py:149
  (20 shorter events, 1.6 us)
Async XLA Ops:
  0.0 65.7 %copy-start = (f32[256,256]{1,0:T(8,128)S(1)}, f32[256,256]{1,0:T(8,128)}, u32[]{:S(2)}) copy-start(f32[256,256]{1,0:T(8,128)} %param.8) | copy-start | bytes 786436
  0.0 0.8 copy-start.2
  0.8 0.8 copy-start.4
  1.6 33.0 %copy-start.3 = (f32[16,512]{1,0:T(8,128)S(1)}, f32[16,512]{1,0:T(8,128)}, u32[]{:S(2)}) copy-start(f32[16,512]{1,0:T(8,128)} %own_ref.1) | copy-start | bytes 98308
  28.3 6.3 %collective-permute-start = (f32[8,32,512]{2,1,0:T(8,128)S(1)}, f32[8,32,512]{2,1,0:T(8,128)S(1)}, u32[]{:S(2)}, u32[]{:S(2)}) collective-permute-start(f32[8,32,512]{2,1,0:T(8,128)S(1)} %all_to_all.20.mine_ref), channel_id=1, source_target_pairs={{0,1},{1,0},{2,3},{3,2},{4,5},{5,4},{6,7},{7,6},{8,9},{9,8},{10,11... | collective-permute-start | bytes 1572872 | tf_op jit(solution)/shard_map/ppermute | solution.py:192
  32.6 1.6 %copy-start.1 = (f32[512,1024]{1,0:T(8,128)S(1)}, f32[512,1024]{1,0:T(8,128)}, u32[]{:S(2)}) copy-start(f32[512,1024]{1,0:T(8,128)} %block.1) | copy-start | bytes 6291460
  61.3 25.3 %all-to-all-start.2 = ((f32[8,160,128]{2,1,0:T(8,128)}), f32[8,160,128]{2,1,0:T(8,128)S(1)}, u32[]{:S(2)}, u32[]{:S(2)}) async-start(f32[8,160,128]{2,1,0:T(8,128)} %shard_map.58), calls=%async_computation.2 | async-start | bytes 1310720 | tf_op jit(solution)/shard_map/all_to_all | solution.py:169
  87.5 19.8 %all-to-all-start.3 = ((f32[8,128,128]{2,1,0:T(8,128)}), f32[8,128,128]{2,1,0:T(8,128)S(1)}, u32[]{:S(2)}, u32[]{:S(2)}) async-start(f32[8,128,128]{2,1,0:T(8,128)} %get-tuple-element.12), calls=%async_computation.3 | async-start | bytes 1048576 | tf_op jit(solution)/shard_map/all_to_all | solution.py:169
  91.0 28.3 %copy-start.5 = (f32[256,256]{1,0:T(8,128)S(1)}, f32[256,256]{1,0:T(8,128)}, u32[]{:S(2)}) copy-start(f32[256,256]{1,0:T(8,128)} %param.9) | copy-start | bytes 786436
  107.3 13.3 %collective-permute-start.1 = (f32[1024,128]{1,0:T(8,128)S(1)}, f32[1024,128]{1,0:T(8,128)S(1)}, u32[]{:S(2)}, u32[]{:S(2)}) collective-permute-start(f32[1024,128]{1,0:T(8,128)S(1)} %shard_map.61.own), channel_id=1, source_target_pairs={{0,144},{1,497},{2,146},{3,499},{4,148},{5,501},{6,150},{7,503},{8... | collective-permute-start | bytes 1572872 | tf_op jit(solution)/shard_map/ppermute | solution.py:183
  113.4 12.7 %collective-permute-start.2 = (f32[1024,128]{1,0:T(8,128)S(1)}, f32[1024,128]{1,0:T(8,128)S(1)}, u32[]{:S(2)}, u32[]{:S(2)}) collective-permute-start(f32[1024,128]{1,0:T(8,128)S(1)} %shard_map.61.own), channel_id=1, source_target_pairs={{0,128},{1,385},{2,130},{3,387},{4,132},{5,389},{6,134},{7,391},{8... | collective-permute-start | bytes 1572872 | tf_op jit(solution)/shard_map/ppermute | solution.py:183
  115.4 11.2 %collective-permute-start.3 = (f32[1024,128]{1,0:T(8,128)S(1)}, f32[1024,128]{1,0:T(8,128)S(1)}, u32[]{:S(2)}, u32[]{:S(2)}) collective-permute-start(f32[1024,128]{1,0:T(8,128)S(1)} %shard_map.61.own), channel_id=1, source_target_pairs={{0,16},{1,113},{2,18},{3,115},{4,20},{5,117},{6,22},{7,119},{8,24}... | collective-permute-start | bytes 1572872 | tf_op jit(solution)/shard_map/ppermute | solution.py:183

commit v11 on v10

--- a/solution.py
+++ b/solution.py
@@ -19,13 +19,6 @@
     return ((x % NX * NY + y % NY) * NZ + z) * 2 + core
 
 
-NEAR = [
-    [device(bx + (px ^ core) + core, by + (py ^ core) + core, z, core) for px in range(2) for py in range(2)]
-    for z in range(NZ)
-    for core in range(2)
-    for bx in range(0, NX, 2)
-    for by in range(0, NY, 2)
-]
 FAR = [
     [device(px + dx, py + dy, z, core) for dx in range(0, NX, 2) for dy in range(0, NY, 2)]
     for z in range(NZ)
@@ -52,17 +45,25 @@
     return mul(a[0], b[0]) + (mul(a[0], b[1]) + mul(a[1], b[0]))
 
 
-def shard_kernel(second, first, out):
-    for z in range(8):
-        out[z, :16] = second[...]
-        out[z, 16:] = first[...]
-
-
 def split_kernel(block_ref, high, low):
     high[...], low[...] = split(block_ref[...])
 
 
-def project_kernel(core_ref, mine_ref, other_ref, own_ref, block_high, block_low, out, high, low, both):
+def quarter(rows, block_high, block_low, out):
+    for t in range(4):
+        at = slice(t * 256, (t + 1) * 256)
+        value = mul3(rows, (block_high[:, at], block_low[:, at]))
+        for half in range(2):
+            to = (2 * t + half) * 128
+            out[to : to + 128, :] = value[:, half * 128 : (half + 1) * 128]
+
+
+def rows_of(j, d, high, low):
+    at = pl.ds(pl.multiple_of((j ^ d) * 128, 128), 128)
+    return high[at, :], low[at, :]
+
+
+def diagonal_kernel(core_ref, j_ref, mine_ref, other_ref, own_ref, block_high, block_low, out, high, low, both):
     core = core_ref[0]
     both[0] = mine_ref[...]
     both[1] = other_ref[...]
@@ -74,21 +75,26 @@
                 at = panel * 256 + z * 32 + c * 16
                 high[at : at + 16, :] = h
                 low[at : at + 16, :] = l
-    for t in range(4):
-        at = slice(t * 256, (t + 1) * 256)
-        value = mul3((high[...], low[...]), (block_high[:, at], block_low[:, at]))
-        for m in range(4):
-            for half in range(2):
-                to = (2 * t + half) * 128
-                out[m, to : to + 128, :] = value[m * 128 : (m + 1) * 128, half * 128 : (half + 1) * 128]
+    quarter(rows_of(j_ref[0], 3, high, low), block_high, block_low, out)
     cross = mul3(split(own_ref[...]), (high[:256], low[:256]), mul_nt)
-    for m in range(4):
-        out[m, 1024:1040, :] = cross[:, :128]
-        out[m, 1040:, :] = cross[:, 128:]
-
-
-def near_kernel(parts, out):
-    total = (parts[0] + parts[1]) + (parts[2] + parts[3])
+    out[1024:1040, :] = cross[:, :128]
+    out[1040:, :] = cross[:, 128:]
+
+
+def beside_kernel(j_ref, diagonal, high, low, block_high, block_low, *outs):
+    for d, out in zip((2, 1), outs):
+        quarter(rows_of(j_ref[0], d, high, low), block_high, block_low, out)
+        out[1024:, :] = diagonal[1024:, :]
+
+
+def own_kernel(j_ref, diagonal, got, high, low, block_high, block_low, out):
+    quarter(rows_of(j_ref[0], 0, high, low), block_high, block_low, out)
+    out[1024:, :] = diagonal[1024:, :]
+    out[...] += got[...]
+
+
+def near_kernel(half, got1, got2, out):
+    total = half[...] + (got1[...] + got2[...])
     for m in range(8):
         out[m, :128, :] = total[m * 128 : (m + 1) * 128]
         out[m, 128:, :] = total[1024:]
@@ -165,8 +171,8 @@
     return lax.dot_general(left, right, dims, precision=lax.Precision.HIGHEST, preferred_element_type=F32)
 
 
-def trade(pieces, groups):
-    return lax.all_to_all(pieces, ROW + COL, 0, 0, axis_index_groups=groups)
+def trade(pieces):
+    return lax.all_to_all(pieces, ROW + COL, 0, 0, axis_index_groups=FAR)
 
 
 def fetch(value, d):
@@ -187,27 +193,29 @@
     core = lax.axis_index("core")
     scalar = core.astype(jnp.int32).reshape(1)
     j = ((lax.axis_index("x") % 2) * 2 + lax.axis_index("y") % 2).astype(jnp.int32).reshape(1)
-    shards = call(shard_kernel, shape(NZ, 32, 512), (reflectors_second, reflectors_first))
-    mine = lax.all_to_all(shards, "z", 0, 0)
+    shards = jnp.concatenate([reflectors_second, reflectors_first], axis=0)
+    mine = lax.all_to_all(jnp.broadcast_to(shards[None], (NZ,) + shards.shape), "z", 0, 0)
     other = lax.ppermute(mine, "core", [(0, 1), (1, 0)])
     block = call(split_kernel, [shape(512, 1024, dtype=BF16)] * 2, (vectors,))
-    wide = pltpu.VMEM((512, 512), BF16)
-    parts = call(
-        project_kernel,
-        shape(4, 1056, 128),
-        (scalar, mine, other, reflectors_first, *block),
-        (wide, wide, pltpu.VMEM((2, 8, 32, 512), F32)),
-        scalars=1,
-    )
+    wide = shape(512, 512, dtype=BF16)
+    diagonal, *panels = call(
+        diagonal_kernel,
+        [shape(1056, 128), wide, wide],
+        (scalar, j, mine, other, reflectors_first, *block),
+        (pltpu.VMEM((2, 8, 32, 512), F32),),
+        scalars=2,
+    )
+    along_x, along_y = call(beside_kernel, [shape(1056, 128)] * 2, (j, diagonal, *panels, *block), scalars=1)
+    half = call(own_kernel, shape(1056, 128), (j, diagonal, fetch(diagonal, 3), *panels, *block), scalars=1)
     by_core = jnp.stack([jnp.where(core == 0, mine, other), jnp.where(core == 0, other, mine)], axis=1)
     second = by_core[:, :, :16].reshape(256, 512)
     first = by_core[:, :, 16:].reshape(256, 512)
     w_first = exact(factor_first, first)
-    parts = call(near_kernel, shape(8, 160, 128), (trade(parts, NEAR),))
+    parts = call(near_kernel, shape(8, 160, 128), (half, fetch(along_y, 1), fetch(along_x, 2)))
     share, cross = call(
-        far_kernel, [shape(8, 128, 128), shape(16, 256)], (trade(parts, FAR), w_first), inputs=[VMEM, HBM]
-    )
-    share = trade(share, FAR).reshape(1024, 128)
+        far_kernel, [shape(8, 128, 128), shape(16, 256)], (trade(parts), w_first), inputs=[VMEM, HBM]
+    )
+    share = trade(share).reshape(1024, 128)
     cross = lax.all_gather(cross, COL, axis=0, tiled=True)
     share = call(pass_kernel, shape(1024, 128), (share, cross), inputs=[VMEM, HBM])
     got = {d: fetch(share, d) for d in (3, 2, 1)}

time: 129 us -> 128 us (level)
  blocking collectives: 66.1 us -> 42.4 us
  starting transfers between devices: 22.8 us -> 36.9 us
  waiting for transfers between devices: 23.9 us -> 32.4 us
  local copies, waits for them, and re-layouts: 3.44 us -> 1.93 us
    all_to_all x2 -> x1, blocking collectives: 50.5 us -> 26.7 us  [local(): lax.all_to_all(jnp.broadcast_to(shards[None], (NZ,) + shards.shape), 'z',...]
    ppermute x3 -> x6, starting transfers between devices: 10.9 us -> 22.7 us  [fetch(): return lax.ppermute(value, ROW + COL, pairs)]
    ppermute x3 -> x6, waiting for transfers between devices: 3.68 us -> 12.2 us  [fetch(): return lax.ppermute(value, ROW + COL, pairs)]
    all_to_all x2, starting transfers between devices: 7.58 us -> 9.79 us  [trade(): return lax.all_to_all(pieces, ROW + COL, 0, 0, axis_index_groups=FAR)]
    unnamed x12 -> x8, local copies, waits for them, and re-layouts: 3.16 us -> 1.6 us
    pallas_call x9 -> x10, Pallas kernels: 8.94 us -> 9.37 us  [call(): pl.pallas_call(kernel, out_shape=outs, in_specs=inputs or [SMEM] * scalar...]
  transfers between devices with their start and end apart: 6 -> 9, of which waited for: 5 -> 7; matrix products, arithmetic and copies ran while one was open for 3% -> 3% of each run, Pallas kernels for 3% -> 4%
where the time goes in v11:
time: 128 us; the launch traced here: 127 us
  blocking collectives  42.4 us (33%)
  starting transfers between devices  36.9 us (29%)
  waiting for transfers between devices  32.4 us (25%)
  Pallas kernels  9.37 us (7%)
  matrix products  2.7 us (2%)
  local copies, waits for them, and re-layouts  1.93 us (2%)
    all_to_all x1, blocking collectives, local(): lax.all_to_all(jnp.broadcast_to(shards[None], (NZ,) + shards.shape), 'z',...  26.7 us
    ppermute x6, starting transfers between devices, fetch(): return lax.ppermute(value, ROW + COL, pairs)  22.7 us
    all_to_all x2, waiting for transfers between devices, trade(): return lax.all_to_all(pieces, ROW + COL, 0, 0, axis_index_groups=FAR)  20.2 us
    all_gather x1, blocking collectives, local(): cross = lax.all_gather(cross, COL, axis=0, tiled=True)  15.7 us
    ppermute x6, waiting for transfers between devices, fetch(): return lax.ppermute(value, ROW + COL, pairs)  12.2 us
    all_to_all x2, starting transfers between devices, trade(): return lax.all_to_all(pieces, ROW + COL, 0, 0, axis_index_groups=FAR)  9.79 us
    pallas_call x10, Pallas kernels, call(): pl.pallas_call(kernel, out_shape=outs, in_specs=inputs or [SMEM] * scalar...  9.37 us
    ppermute x1, starting transfers between devices, local(): other = lax.ppermute(mine, 'core', [(0, 1), (1, 0)])  4.35 us
  transfers between devices with their start and end apart: 9, of which 7 were waited for; matrix products, arithmetic and copies ran while one was open for 3% of the time, Pallas kernels for 4%

profile of v11, /device:TPU:1, one launch (start us, length us, event | category | flops | bytes accessed | tf_op | source)
XLA Modules:
  0.0 127.0 jit_solution(17820483737486202976)
XLA Ops:
  0.9 26.7 %all_to_all.15.mine_ref = f32[8,32,512]{2,1,0:T(8,128)S(1)} all-to-all(f32[8,32,512]{2,1,0:T(8,128)S(1)} %broadcast_in_dim.2), channel_id=1, replica_groups=mesh['x'=4,'y'=8,'z'=8,'core'=2] {'z'}, dimensions={0} | all-to-all | bytes 1048576 | tf_op jit(solution)/shard_map/all_to_all | solution.py:197
  27.6 4.4 %collective-permute-start = (f32[8,32,512]{2,1,0:T(8,128)S(1)}, f32[8,32,512]{2,1,0:T(8,128)S(1)}, u32[]{:S(2)}, u32[]{:S(2)}) collective-permute-start(f32[8,32,512]{2,1,0:T(8,128)S(1)} %all_to_all.15.mine_ref), channel_id=1, source_target_pairs={{0,1},{1,0},{2,3},{3,2},{4,5},{5,4},{6,7},{7,6},{8,9},{9,8},{10,11... | collective-permute-start | bytes 1572872 | tf_op jit(solution)/shard_map/ppermute | solution.py:198
  31.9 1.6 %copy-done.1 = f32[512,1024]{1,0:T(8,128)S(1)} copy-done((f32[512,1024]{1,0:T(8,128)S(1)}, f32[512,1024]{1,0:T(8,128)}, u32[]{:S(2)}) %copy-start.1) | copy-done | bytes 2097176
  33.9 0.9 shard_map.56
  34.8 7.3 %collective-permute-start.1 = (f32[1056,128]{1,0:T(8,128)S(1)}, f32[1056,128]{1,0:T(8,128)S(1)}, u32[]{:S(2)}, u32[]{:S(2)}) collective-permute-start(f32[1056,128]{1,0:T(8,128)S(1)} %get-tuple-element.16.diagonal), channel_id=1, source_target_pairs={{0,144},{1,497},{2,146},{3,499},{4,148},{5,501},{6,150},{7,503},{8... | collective-permute-start | bytes 1622024 | tf_op jit(solution)/shard_map/ppermute | solution.py:189
  42.1 1.0 shard_map.58
  43.1 1.9 %collective-permute-start.2 = (f32[1056,128]{1,0:T(8,128)S(1)}, f32[1056,128]{1,0:T(8,128)S(1)}, u32[]{:S(2)}, u32[]{:S(2)}) collective-permute-start(f32[1056,128]{1,0:T(8,128)S(1)} %get-tuple-element.19), channel_id=1, source_target_pairs={{0,16},{1,113},{2,18},{3,115},{4,20},{5,117},{6,22},{7,119},{8,24}... | collective-permute-start | bytes 1622024 | tf_op jit(solution)/shard_map/ppermute | solution.py:189
  45.0 2.2 %collective-permute-start.3 = (f32[1056,128]{1,0:T(8,128)S(1)}, f32[1056,128]{1,0:T(8,128)S(1)}, u32[]{:S(2)}, u32[]{:S(2)}) collective-permute-start(f32[1056,128]{1,0:T(8,128)S(1)} %get-tuple-element.20), channel_id=1, source_target_pairs={{0,128},{1,385},{2,130},{3,387},{4,132},{5,389},{6,134},{7,391},{8... | collective-permute-start | bytes 1622024 | tf_op jit(solution)/shard_map/ppermute | solution.py:189
  47.2 1.6 %collective-permute-done.1.got = f32[1056,128]{1,0:T(8,128)S(1)} collective-permute-done((f32[1056,128]{1,0:T(8,128)S(1)}, f32[1056,128]{1,0:T(8,128)S(1)}, u32[]{:S(2)}, u32[]{:S(2)}) %collective-permute-start.1) | collective-permute-done | bytes 540704 | tf_op jit(solution)/shard_map/ppermute | solution.py:189
  49.4 5.0 %collective-permute-done.2.got1 = f32[1056,128]{1,0:T(8,128)S(1)} collective-permute-done((f32[1056,128]{1,0:T(8,128)S(1)}, f32[1056,128]{1,0:T(8,128)S(1)}, u32[]{:S(2)}, u32[]{:S(2)}) %collective-permute-start.2) | collective-permute-done | bytes 540704 | tf_op jit(solution)/shard_map/ppermute | solution.py:189
  54.4 1.9 %collective-permute-done.3.got2 = f32[1056,128]{1,0:T(8,128)S(1)} collective-permute-done((f32[1056,128]{1,0:T(8,128)S(1)}, f32[1056,128]{1,0:T(8,128)S(1)}, u32[]{:S(2)}, u32[]{:S(2)}) %collective-permute-start.3) | collective-permute-done | bytes 540704 | tf_op jit(solution)/shard_map/ppermute | solution.py:189
  56.3 0.9 shard_map.59
  57.3 6.3 %all-to-all-start.1 = ((f32[8,160,128]{2,1,0:T(8,128)}), f32[8,160,128]{2,1,0:T(8,128)S(1)}, u32[]{:S(2)}, u32[]{:S(2)}) async-start(f32[8,160,128]{2,1,0:T(8,128)} %shard_map.59), calls=%async_computation.1 | async-start | bytes 1310720 | tf_op jit(solution)/shard_map/all_to_all | solution.py:175
  63.8 1.0 fusion.1
  65.1 19.7 %all-to-all-done.1.parts = f32[8,160,128]{2,1,0:T(8,128)S(1)} async-done(((f32[8,160,128]{2,1,0:T(8,128)}), f32[8,160,128]{2,1,0:T(8,128)S(1)}, u32[]{:S(2)}, u32[]{:S(2)}) %all-to-all-start.1) | async-done | bytes 655392 | tf_op jit(solution)/shard_map/all_to_all | solution.py:175
  85.6 3.5 %all-to-all-start.2 = ((f32[8,128,128]{2,1,0:T(8,128)}), f32[8,128,128]{2,1,0:T(8,128)S(1)}, u32[]{:S(2)}, u32[]{:S(2)}) async-start(f32[8,128,128]{2,1,0:T(8,128)} %get-tuple-element.22), calls=%async_computation.2 | async-start | bytes 1048576 | tf_op jit(solution)/shard_map/all_to_all | solution.py:175
  89.2 15.7 %all_gather.3.after = f32[256,256]{1,0:T(8,128)S(1)} all-gather(f32[16,256]{1,0:T(8,128)S(1)} %get-tuple-element.21), channel_id=1, replica_groups=mesh['x'=4,'y'=8,'z'=8,'core'=2] {'z','core'}, dimensions={0}, use_global_device_ids=true | all-gather | bytes 278528 | tf_op jit(solution)/shard_map/all_gather | solution.py:219
  105.4 6.6 %collective-permute-start.4 = (f32[1024,128]{1,0:T(8,128)S(1)}, f32[1024,128]{1,0:T(8,128)S(1)}, u32[]{:S(2)}, u32[]{:S(2)}) collective-permute-start(f32[1024,128]{1,0:T(8,128)S(1)} %shard_map.62.own), channel_id=1, source_target_pairs={{0,144},{1,497},{2,146},{3,499},{4,148},{5,501},{6,150},{7,503},{8... | collective-permute-start | bytes 1572872 | tf_op jit(solution)/shard_map/ppermute | solution.py:189
  112.0 1.9 %collective-permute-start.5 = (f32[1024,128]{1,0:T(8,128)S(1)}, f32[1024,128]{1,0:T(8,128)S(1)}, u32[]{:S(2)}, u32[]{:S(2)}) collective-permute-start(f32[1024,128]{1,0:T(8,128)S(1)} %shard_map.62.own), channel_id=1, source_target_pairs={{0,128},{1,385},{2,130},{3,387},{4,132},{5,389},{6,134},{7,391},{8... | collective-permute-start | bytes 1572872 | tf_op jit(solution)/shard_map/ppermute | solution.py:189
  113.9 2.8 %collective-permute-start.6 = (f32[1024,128]{1,0:T(8,128)S(1)}, f32[1024,128]{1,0:T(8,128)S(1)}, u32[]{:S(2)}, u32[]{:S(2)}) collective-permute-start(f32[1024,128]{1,0:T(8,128)S(1)} %shard_map.62.own), channel_id=1, source_target_pairs={{0,16},{1,113},{2,18},{3,115},{4,20},{5,117},{6,22},{7,119},{8,24}... | collective-permute-start | bytes 1572872 | tf_op jit(solution)/shard_map/ppermute | solution.py:189
  116.7 1.0 convolution_subtract_fusion
  118.8 2.6 %shard_map.63.middle = f32[512,1024]{1,0:T(8,128)S(1)} custom-call(f32[512,1024]{1,0:T(8,128)} %block.1, bf16[2,512,512]{2,1,0:T(8,128)(2,1)S(1)} %shard_map.61.w_ref, f32[1024,128]{1,0:T(8,128)S(1)} %shard_map.62.own, f32[1024,128]{1,0:T(8,128)S(1)} %collective-permute-done.4.got), custom_call_target="tpu_custom_call" | custom-call | tf_op jit(solution)/shard_map/pallas_call | solution.py:155
  121.4 2.9 %collective-permute-done.5.got = f32[1024,128]{1,0:T(8,128)S(1)} collective-permute-done((f32[1024,128]{1,0:T(8,128)S(1)}, f32[1024,128]{1,0:T(8,128)S(1)}, u32[]{:S(2)}, u32[]{:S(2)}) %collective-permute-start.5) | collective-permute-done | bytes 524320 | tf_op jit(solution)/shard_map/ppermute | solution.py:189
  125.1 1.9 %shard_map.64 = f32[512,1024]{1,0:T(8,128)} custom-call(f32[512,1024]{1,0:T(8,128)S(1)} %shard_map.63.middle, bf16[2,512,512]{2,1,0:T(8,128)(2,1)S(1)} %shard_map.61.w_ref, f32[1024,128]{1,0:T(8,128)S(1)} %collective-permute-done.5.got, f32[1024,128]{1,0:T(8,128)S(1)} %collective-permute-done.6.last), custom_call_target="tpu_custom_call" | custom-call | tf_op jit(solution)/shard_map/pallas_call | solution.py:155
  (24 shorter events, 5.4 us)
Async XLA Ops:
  0.0 63.8 %copy-start = (f32[256,256]{1,0:T(8,128)S(1)}, f32[256,256]{1,0:T(8,128)}, u32[]{:S(2)}) copy-start(f32[256,256]{1,0:T(8,128)} %param.8) | copy-start | bytes 786436
  0.0 33.8 %copy-start.2 = (f32[16,512]{1,0:T(8,128)S(1)}, f32[16,512]{1,0:T(8,128)}, u32[]{:S(2)}) copy-start(f32[16,512]{1,0:T(8,128)} %own_ref.1) | copy-start | bytes 98308
  27.6 6.3 %collective-permute-start = (f32[8,32,512]{2,1,0:T(8,128)S(1)}, f32[8,32,512]{2,1,0:T(8,128)S(1)}, u32[]{:S(2)}, u32[]{:S(2)}) collective-permute-start(f32[8,32,512]{2,1,0:T(8,128)S(1)} %all_to_all.15.mine_ref), channel_id=1, source_target_pairs={{0,1},{1,0},{2,3},{3,2},{4,5},{5,4},{6,7},{7,6},{8,9},{9,8},{10,11... | collective-permute-start | bytes 1572872 | tf_op jit(solution)/shard_map/ppermute | solution.py:198
  31.9 1.6 %copy-start.1 = (f32[512,1024]{1,0:T(8,128)S(1)}, f32[512,1024]{1,0:T(8,128)}, u32[]{:S(2)}) copy-start(f32[512,1024]{1,0:T(8,128)} %block.1) | copy-start | bytes 6291460
  34.8 14.1 %collective-permute-start.1 = (f32[1056,128]{1,0:T(8,128)S(1)}, f32[1056,128]{1,0:T(8,128)S(1)}, u32[]{:S(2)}, u32[]{:S(2)}) collective-permute-start(f32[1056,128]{1,0:T(8,128)S(1)} %get-tuple-element.16.diagonal), channel_id=1, source_target_pairs={{0,144},{1,497},{2,146},{3,499},{4,148},{5,501},{6,150},{7,503},{8... | collective-permute-start | bytes 1622024 | tf_op jit(solution)/shard_map/ppermute | solution.py:189
  43.1 11.3 %collective-permute-start.2 = (f32[1056,128]{1,0:T(8,128)S(1)}, f32[1056,128]{1,0:T(8,128)S(1)}, u32[]{:S(2)}, u32[]{:S(2)}) collective-permute-start(f32[1056,128]{1,0:T(8,128)S(1)} %get-tuple-element.19), channel_id=1, source_target_pairs={{0,16},{1,113},{2,18},{3,115},{4,20},{5,117},{6,22},{7,119},{8,24}... | collective-permute-start | bytes 1622024 | tf_op jit(solution)/shard_map/ppermute | solution.py:189
  45.0 11.3 %collective-permute-start.3 = (f32[1056,128]{1,0:T(8,128)S(1)}, f32[1056,128]{1,0:T(8,128)S(1)}, u32[]{:S(2)}, u32[]{:S(2)}) collective-permute-start(f32[1056,128]{1,0:T(8,128)S(1)} %get-tuple-element.20), channel_id=1, source_target_pairs={{0,128},{1,385},{2,130},{3,387},{4,132},{5,389},{6,134},{7,391},{8... | collective-permute-start | bytes 1622024 | tf_op jit(solution)/shard_map/ppermute | solution.py:189
  57.3 27.5 %all-to-all-start.1 = ((f32[8,160,128]{2,1,0:T(8,128)}), f32[8,160,128]{2,1,0:T(8,128)S(1)}, u32[]{:S(2)}, u32[]{:S(2)}) async-start(f32[8,160,128]{2,1,0:T(8,128)} %shard_map.59), calls=%async_computation.1 | async-start | bytes 1310720 | tf_op jit(solution)/shard_map/all_to_all | solution.py:175
  85.6 19.8 %all-to-all-start.2 = ((f32[8,128,128]{2,1,0:T(8,128)}), f32[8,128,128]{2,1,0:T(8,128)S(1)}, u32[]{:S(2)}, u32[]{:S(2)}) async-start(f32[8,128,128]{2,1,0:T(8,128)} %get-tuple-element.22), calls=%async_computation.2 | async-start | bytes 1048576 | tf_op jit(solution)/shard_map/all_to_all | solution.py:175
  89.1 28.7 %copy-start.3 = (f32[256,256]{1,0:T(8,128)S(1)}, f32[256,256]{1,0:T(8,128)}, u32[]{:S(2)}) copy-start(f32[256,256]{1,0:T(8,128)} %param.9) | copy-start | bytes 786436
  105.4 13.4 %collective-permute-start.4 = (f32[1024,128]{1,0:T(8,128)S(1)}, f32[1024,128]{1,0:T(8,128)S(1)}, u32[]{:S(2)}, u32[]{:S(2)}) collective-permute-start(f32[1024,128]{1,0:T(8,128)S(1)} %shard_map.62.own), channel_id=1, source_target_pairs={{0,144},{1,497},{2,146},{3,499},{4,148},{5,501},{6,150},{7,503},{8... | collective-permute-start | bytes 1572872 | tf_op jit(solution)/shard_map/ppermute | solution.py:189
  112.0 12.3 %collective-permute-start.5 = (f32[1024,128]{1,0:T(8,128)S(1)}, f32[1024,128]{1,0:T(8,128)S(1)}, u32[]{:S(2)}, u32[]{:S(2)}) collective-permute-start(f32[1024,128]{1,0:T(8,128)S(1)} %shard_map.62.own), channel_id=1, source_target_pairs={{0,128},{1,385},{2,130},{3,387},{4,132},{5,389},{6,134},{7,391},{8... | collective-permute-start | bytes 1572872 | tf_op jit(solution)/shard_map/ppermute | solution.py:189
  113.9 11.2 %collective-permute-start.6 = (f32[1024,128]{1,0:T(8,128)S(1)}, f32[1024,128]{1,0:T(8,128)S(1)}, u32[]{:S(2)}, u32[]{:S(2)}) collective-permute-start(f32[1024,128]{1,0:T(8,128)S(1)} %shard_map.62.own), channel_id=1, source_target_pairs={{0,16},{1,113},{2,18},{3,115},{4,20},{5,117},{6,22},{7,119},{8,24}... | collective-permute-start | bytes 1572872 | tf_op jit(solution)/shard_map/ppermute | solution.py:189

commit v12 on v11

--- a/solution.py
+++ b/solution.py
@@ -19,8 +19,22 @@
     return ((x % NX * NY + y % NY) * NZ + z) * 2 + core
 
 
+def label_x(x, core):
+    return (x >> 1) ^ (x & 1 & ~core)
+
+
+def label_y(y, core):
+    y = (y - core) & 7
+    return (y & 1) ^ (y >> 2)
+
+
 FAR = [
-    [device(px + dx, py + dy, z, core) for dx in range(0, NX, 2) for dy in range(0, NY, 2)]
+    [
+        device(x, y, z, core)
+        for x in range(NX)
+        for y in range(NY)
+        if (label_x(x, core), label_y(y, core)) == (px, py)
+    ]
     for z in range(NZ)
     for core in range(2)
     for px in range(2)
@@ -192,7 +206,8 @@
 def local(vectors, reflectors_first, reflectors_second, factor_first, factor_second):
     core = lax.axis_index("core")
     scalar = core.astype(jnp.int32).reshape(1)
-    j = ((lax.axis_index("x") % 2) * 2 + lax.axis_index("y") % 2).astype(jnp.int32).reshape(1)
+    j = label_x(lax.axis_index("x"), core) * 2 + label_y(lax.axis_index("y"), core)
+    j = j.astype(jnp.int32).reshape(1)
     shards = jnp.concatenate([reflectors_second, reflectors_first], axis=0)
     mine = lax.all_to_all(jnp.broadcast_to(shards[None], (NZ,) + shards.shape), "z", 0, 0)
     other = lax.ppermute(mine, "core", [(0, 1), (1, 0)])

time: 128 us -> 123 us (0.961)
  waiting for transfers between devices: 32.4 us -> 25.2 us
  blocking collectives: 42.4 us -> 44.3 us
    all_to_all x2, waiting for transfers between devices: 20.2 us -> 12.2 us  [trade(): return lax.all_to_all(pieces, ROW + COL, 0, 0, axis_index_groups=FAR)]
    all_gather x1, blocking collectives: 15.7 us -> 17.6 us  [local(): cross = lax.all_gather(cross, COL, axis=0, tiled=True)]
where the time goes in v12:
time: 123 us; the launch traced here: 122 us
  blocking collectives  44.3 us (36%)
  starting transfers between devices  37.6 us (31%)
  waiting for transfers between devices  25.2 us (20%)
  Pallas kernels  9.36 us (8%)
  matrix products  2.7 us (2%)
  local copies, waits for them, and re-layouts  1.93 us (2%)
    all_to_all x1, blocking collectives, local(): lax.all_to_all(jnp.broadcast_to(shards[None], (NZ,) + shards.shape), 'z',...  26.7 us
    ppermute x6, starting transfers between devices, fetch(): return lax.ppermute(value, ROW + COL, pairs)  22.5 us
    all_gather x1, blocking collectives, local(): cross = lax.all_gather(cross, COL, axis=0, tiled=True)  17.6 us
    ppermute x6, waiting for transfers between devices, fetch(): return lax.ppermute(value, ROW + COL, pairs)  13 us
    all_to_all x2, waiting for transfers between devices, trade(): return lax.all_to_all(pieces, ROW + COL, 0, 0, axis_index_groups=FAR)  12.2 us
    all_to_all x2, starting transfers between devices, trade(): return lax.all_to_all(pieces, ROW + COL, 0, 0, axis_index_groups=FAR)  10.8 us
    pallas_call x10, Pallas kernels, call(): pl.pallas_call(kernel, out_shape=outs, in_specs=inputs or [SMEM] * scalar...  9.36 us
    ppermute x1, starting transfers between devices, local(): other = lax.ppermute(mine, 'core', [(0, 1), (1, 0)])  4.35 us
  transfers between devices with their start and end apart: 9, of which 7 were waited for; matrix products, arithmetic and copies ran while one was open for 3% of the time, Pallas kernels for 4%

profile of v12, /device:TPU:1, one launch (start us, length us, event | category | flops | bytes accessed | tf_op | source)
XLA Modules:
  0.0 122.4 jit_solution(10440473162504178895)
XLA Ops:
  0.9 26.7 %all_to_all.15.mine_ref = f32[8,32,512]{2,1,0:T(8,128)S(1)} all-to-all(f32[8,32,512]{2,1,0:T(8,128)S(1)} %broadcast_in_dim.2), channel_id=1, replica_groups=mesh['x'=4,'y'=8,'z'=8,'core'=2] {'z'}, dimensions={0} | all-to-all | bytes 1048576 | tf_op jit(solution)/shard_map/all_to_all | solution.py:212
  27.6 4.4 %collective-permute-start = (f32[8,32,512]{2,1,0:T(8,128)S(1)}, f32[8,32,512]{2,1,0:T(8,128)S(1)}, u32[]{:S(2)}, u32[]{:S(2)}) collective-permute-start(f32[8,32,512]{2,1,0:T(8,128)S(1)} %all_to_all.15.mine_ref), channel_id=1, source_target_pairs={{0,1},{1,0},{2,3},{3,2},{4,5},{5,4},{6,7},{7,6},{8,9},{9,8},{10,11... | collective-permute-start | bytes 1572872 | tf_op jit(solution)/shard_map/ppermute | solution.py:213
  31.9 1.6 %copy-done.1 = f32[512,1024]{1,0:T(8,128)S(1)} copy-done((f32[512,1024]{1,0:T(8,128)S(1)}, f32[512,1024]{1,0:T(8,128)}, u32[]{:S(2)}) %copy-start.1) | copy-done | bytes 2097176
  34.8 7.3 %collective-permute-start.1 = (f32[1056,128]{1,0:T(8,128)S(1)}, f32[1056,128]{1,0:T(8,128)S(1)}, u32[]{:S(2)}, u32[]{:S(2)}) collective-permute-start(f32[1056,128]{1,0:T(8,128)S(1)} %get-tuple-element.16.diagonal), channel_id=1, source_target_pairs={{0,144},{1,497},{2,146},{3,499},{4,148},{5,501},{6,150},{7,503},{8... | collective-permute-start | bytes 1622024 | tf_op jit(solution)/shard_map/ppermute | solution.py:203
  42.1 1.0 shard_map.58
  43.1 1.9 %collective-permute-start.2 = (f32[1056,128]{1,0:T(8,128)S(1)}, f32[1056,128]{1,0:T(8,128)S(1)}, u32[]{:S(2)}, u32[]{:S(2)}) collective-permute-start(f32[1056,128]{1,0:T(8,128)S(1)} %get-tuple-element.19), channel_id=1, source_target_pairs={{0,16},{1,113},{2,18},{3,115},{4,20},{5,117},{6,22},{7,119},{8,24}... | collective-permute-start | bytes 1622024 | tf_op jit(solution)/shard_map/ppermute | solution.py:203
  45.0 2.2 %collective-permute-start.3 = (f32[1056,128]{1,0:T(8,128)S(1)}, f32[1056,128]{1,0:T(8,128)S(1)}, u32[]{:S(2)}, u32[]{:S(2)}) collective-permute-start(f32[1056,128]{1,0:T(8,128)S(1)} %get-tuple-element.20), channel_id=1, source_target_pairs={{0,128},{1,385},{2,130},{3,387},{4,132},{5,389},{6,134},{7,391},{8... | collective-permute-start | bytes 1622024 | tf_op jit(solution)/shard_map/ppermute | solution.py:203
  47.2 1.6 %collective-permute-done.1.got = f32[1056,128]{1,0:T(8,128)S(1)} collective-permute-done((f32[1056,128]{1,0:T(8,128)S(1)}, f32[1056,128]{1,0:T(8,128)S(1)}, u32[]{:S(2)}, u32[]{:S(2)}) %collective-permute-start.1) | collective-permute-done | bytes 540704 | tf_op jit(solution)/shard_map/ppermute | solution.py:203
  49.4 5.0 %collective-permute-done.2.got1 = f32[1056,128]{1,0:T(8,128)S(1)} collective-permute-done((f32[1056,128]{1,0:T(8,128)S(1)}, f32[1056,128]{1,0:T(8,128)S(1)}, u32[]{:S(2)}, u32[]{:S(2)}) %collective-permute-start.2) | collective-permute-done | bytes 540704 | tf_op jit(solution)/shard_map/ppermute | solution.py:203
  54.4 1.9 %collective-permute-done.3.got2 = f32[1056,128]{1,0:T(8,128)S(1)} collective-permute-done((f32[1056,128]{1,0:T(8,128)S(1)}, f32[1056,128]{1,0:T(8,128)S(1)}, u32[]{:S(2)}, u32[]{:S(2)}) %collective-permute-start.3) | collective-permute-done | bytes 540704 | tf_op jit(solution)/shard_map/ppermute | solution.py:203
  56.3 0.9 shard_map.59
  57.3 4.1 %all-to-all-start.1 = ((f32[8,160,128]{2,1,0:T(8,128)}), f32[8,160,128]{2,1,0:T(8,128)S(1)}, u32[]{:S(2)}, u32[]{:S(2)}) async-start(f32[8,160,128]{2,1,0:T(8,128)} %shard_map.59), calls=%async_computation.1 | async-start | bytes 1310720 | tf_op jit(solution)/shard_map/all_to_all | solution.py:189
  61.6 1.0 fusion.1
  62.8 12.2 %all-to-all-done.1.parts = f32[8,160,128]{2,1,0:T(8,128)S(1)} async-done(((f32[8,160,128]{2,1,0:T(8,128)}), f32[8,160,128]{2,1,0:T(8,128)S(1)}, u32[]{:S(2)}, u32[]{:S(2)}) %all-to-all-start.1) | async-done | bytes 655392 | tf_op jit(solution)/shard_map/all_to_all | solution.py:189
  75.8 6.7 %all-to-all-start.2 = ((f32[8,128,128]{2,1,0:T(8,128)}), f32[8,128,128]{2,1,0:T(8,128)S(1)}, u32[]{:S(2)}, u32[]{:S(2)}) async-start(f32[8,128,128]{2,1,0:T(8,128)} %get-tuple-element.22), calls=%async_computation.2 | async-start | bytes 1048576 | tf_op jit(solution)/shard_map/all_to_all | solution.py:189
  82.6 17.6 %all_gather.3.after = f32[256,256]{1,0:T(8,128)S(1)} all-gather(f32[16,256]{1,0:T(8,128)S(1)} %get-tuple-element.21), channel_id=1, replica_groups=mesh['x'=4,'y'=8,'z'=8,'core'=2] {'z','core'}, dimensions={0}, use_global_device_ids=true | all-gather | bytes 278528 | tf_op jit(solution)/shard_map/all_gather | solution.py:234
  100.3 7.0 %collective-permute-start.4 = (f32[1024,128]{1,0:T(8,128)S(1)}, f32[1024,128]{1,0:T(8,128)S(1)}, u32[]{:S(2)}, u32[]{:S(2)}) collective-permute-start(f32[1024,128]{1,0:T(8,128)S(1)} %shard_map.62.own), channel_id=1, source_target_pairs={{0,144},{1,497},{2,146},{3,499},{4,148},{5,501},{6,150},{7,503},{8... | collective-permute-start | bytes 1572872 | tf_op jit(solution)/shard_map/ppermute | solution.py:203
  107.3 2.2 %collective-permute-start.5 = (f32[1024,128]{1,0:T(8,128)S(1)}, f32[1024,128]{1,0:T(8,128)S(1)}, u32[]{:S(2)}, u32[]{:S(2)}) collective-permute-start(f32[1024,128]{1,0:T(8,128)S(1)} %shard_map.62.own), channel_id=1, source_target_pairs={{0,128},{1,385},{2,130},{3,387},{4,132},{5,389},{6,134},{7,391},{8... | collective-permute-start | bytes 1572872 | tf_op jit(solution)/shard_map/ppermute | solution.py:203
  109.4 1.9 %collective-permute-start.6 = (f32[1024,128]{1,0:T(8,128)S(1)}, f32[1024,128]{1,0:T(8,128)S(1)}, u32[]{:S(2)}, u32[]{:S(2)}) collective-permute-start(f32[1024,128]{1,0:T(8,128)S(1)} %shard_map.62.own), channel_id=1, source_target_pairs={{0,16},{1,113},{2,18},{3,115},{4,20},{5,117},{6,22},{7,119},{8,24}... | collective-permute-start | bytes 1572872 | tf_op jit(solution)/shard_map/ppermute | solution.py:203
  111.4 1.0 convolution_subtract_fusion
  113.9 2.6 %shard_map.63.middle = f32[512,1024]{1,0:T(8,128)S(1)} custom-call(f32[512,1024]{1,0:T(8,128)} %block.1, bf16[2,512,512]{2,1,0:T(8,128)(2,1)S(1)} %shard_map.61.w_ref, f32[1024,128]{1,0:T(8,128)S(1)} %shard_map.62.own, f32[1024,128]{1,0:T(8,128)S(1)} %collective-permute-done.4.got), custom_call_target="tpu_custom_call" | custom-call | tf_op jit(solution)/shard_map/pallas_call | solution.py:169
  116.5 2.9 %collective-permute-done.5.got = f32[1024,128]{1,0:T(8,128)S(1)} collective-permute-done((f32[1024,128]{1,0:T(8,128)S(1)}, f32[1024,128]{1,0:T(8,128)S(1)}, u32[]{:S(2)}, u32[]{:S(2)}) %collective-permute-start.5) | collective-permute-done | bytes 524320 | tf_op jit(solution)/shard_map/ppermute | solution.py:203
  119.4 1.2 collective-permute-done.6.last
  120.6 1.8 %shard_map.64 = f32[512,1024]{1,0:T(8,128)} custom-call(f32[512,1024]{1,0:T(8,128)S(1)} %shard_map.63.middle, bf16[2,512,512]{2,1,0:T(8,128)(2,1)S(1)} %shard_map.61.w_ref, f32[1024,128]{1,0:T(8,128)S(1)} %collective-permute-done.5.got, f32[1024,128]{1,0:T(8,128)S(1)} %collective-permute-done.6.last), custom_call_target="tpu_custom_call" | custom-call | tf_op jit(solution)/shard_map/pallas_call | solution.py:169
  (24 shorter events, 5.5 us)
Async XLA Ops:
  0.0 61.6 %copy-start = (f32[256,256]{1,0:T(8,128)S(1)}, f32[256,256]{1,0:T(8,128)}, u32[]{:S(2)}) copy-start(f32[256,256]{1,0:T(8,128)} %param.8) | copy-start | bytes 786436
  0.0 33.8 %copy-start.2 = (f32[16,512]{1,0:T(8,128)S(1)}, f32[16,512]{1,0:T(8,128)}, u32[]{:S(2)}) copy-start(f32[16,512]{1,0:T(8,128)} %own_ref.1) | copy-start | bytes 98308
  27.6 6.3 %collective-permute-start = (f32[8,32,512]{2,1,0:T(8,128)S(1)}, f32[8,32,512]{2,1,0:T(8,128)S(1)}, u32[]{:S(2)}, u32[]{:S(2)}) collective-permute-start(f32[8,32,512]{2,1,0:T(8,128)S(1)} %all_to_all.15.mine_ref), channel_id=1, source_target_pairs={{0,1},{1,0},{2,3},{3,2},{4,5},{5,4},{6,7},{7,6},{8,9},{9,8},{10,11... | collective-permute-start | bytes 1572872 | tf_op jit(solution)/shard_map/ppermute | solution.py:213
  31.9 1.6 %copy-start.1 = (f32[512,1024]{1,0:T(8,128)S(1)}, f32[512,1024]{1,0:T(8,128)}, u32[]{:S(2)}) copy-start(f32[512,1024]{1,0:T(8,128)} %block.1) | copy-start | bytes 6291460
  34.8 14.1 %collective-permute-start.1 = (f32[1056,128]{1,0:T(8,128)S(1)}, f32[1056,128]{1,0:T(8,128)S(1)}, u32[]{:S(2)}, u32[]{:S(2)}) collective-permute-start(f32[1056,128]{1,0:T(8,128)S(1)} %get-tuple-element.16.diagonal), channel_id=1, source_target_pairs={{0,144},{1,497},{2,146},{3,499},{4,148},{5,501},{6,150},{7,503},{8... | collective-permute-start | bytes 1622024 | tf_op jit(solution)/shard_map/ppermute | solution.py:203
  43.1 11.3 %collective-permute-start.2 = (f32[1056,128]{1,0:T(8,128)S(1)}, f32[1056,128]{1,0:T(8,128)S(1)}, u32[]{:S(2)}, u32[]{:S(2)}) collective-permute-start(f32[1056,128]{1,0:T(8,128)S(1)} %get-tuple-element.19), channel_id=1, source_target_pairs={{0,16},{1,113},{2,18},{3,115},{4,20},{5,117},{6,22},{7,119},{8,24}... | collective-permute-start | bytes 1622024 | tf_op jit(solution)/shard_map/ppermute | solution.py:203
  45.0 11.3 %collective-permute-start.3 = (f32[1056,128]{1,0:T(8,128)S(1)}, f32[1056,128]{1,0:T(8,128)S(1)}, u32[]{:S(2)}, u32[]{:S(2)}) collective-permute-start(f32[1056,128]{1,0:T(8,128)S(1)} %get-tuple-element.20), channel_id=1, source_target_pairs={{0,128},{1,385},{2,130},{3,387},{4,132},{5,389},{6,134},{7,391},{8... | collective-permute-start | bytes 1622024 | tf_op jit(solution)/shard_map/ppermute | solution.py:203
  57.3 17.7 %all-to-all-start.1 = ((f32[8,160,128]{2,1,0:T(8,128)}), f32[8,160,128]{2,1,0:T(8,128)S(1)}, u32[]{:S(2)}, u32[]{:S(2)}) async-start(f32[8,160,128]{2,1,0:T(8,128)} %shard_map.59), calls=%async_computation.1 | async-start | bytes 1310720 | tf_op jit(solution)/shard_map/all_to_all | solution.py:189
  75.8 24.4 %all-to-all-start.2 = ((f32[8,128,128]{2,1,0:T(8,128)}), f32[8,128,128]{2,1,0:T(8,128)S(1)}, u32[]{:S(2)}, u32[]{:S(2)}) async-start(f32[8,128,128]{2,1,0:T(8,128)} %get-tuple-element.22), calls=%async_computation.2 | async-start | bytes 1048576 | tf_op jit(solution)/shard_map/all_to_all | solution.py:189
  82.6 29.9 %copy-start.3 = (f32[256,256]{1,0:T(8,128)S(1)}, f32[256,256]{1,0:T(8,128)}, u32[]{:S(2)}) copy-start(f32[256,256]{1,0:T(8,128)} %param.9) | copy-start | bytes 786436
  100.3 13.6 %collective-permute-start.4 = (f32[1024,128]{1,0:T(8,128)S(1)}, f32[1024,128]{1,0:T(8,128)S(1)}, u32[]{:S(2)}, u32[]{:S(2)}) collective-permute-start(f32[1024,128]{1,0:T(8,128)S(1)} %shard_map.62.own), channel_id=1, source_target_pairs={{0,144},{1,497},{2,146},{3,499},{4,148},{5,501},{6,150},{7,503},{8... | collective-permute-start | bytes 1572872 | tf_op jit(solution)/shard_map/ppermute | solution.py:203
  107.3 12.2 %collective-permute-start.5 = (f32[1024,128]{1,0:T(8,128)S(1)}, f32[1024,128]{1,0:T(8,128)S(1)}, u32[]{:S(2)}, u32[]{:S(2)}) collective-permute-start(f32[1024,128]{1,0:T(8,128)S(1)} %shard_map.62.own), channel_id=1, source_target_pairs={{0,128},{1,385},{2,130},{3,387},{4,132},{5,389},{6,134},{7,391},{8... | collective-permute-start | bytes 1572872 | tf_op jit(solution)/shard_map/ppermute | solution.py:203
  109.4 11.1 %collective-permute-start.6 = (f32[1024,128]{1,0:T(8,128)S(1)}, f32[1024,128]{1,0:T(8,128)S(1)}, u32[]{:S(2)}, u32[]{:S(2)}) collective-permute-start(f32[1024,128]{1,0:T(8,128)S(1)} %shard_map.62.own), channel_id=1, source_target_pairs={{0,16},{1,113},{2,18},{3,115},{4,20},{5,117},{6,22},{7,119},{8,24}... | collective-permute-start | bytes 1572872 | tf_op jit(solution)/shard_map/ppermute | solution.py:203

commit v13 on v12

--- a/solution.py
+++ b/solution.py
@@ -42,6 +42,15 @@
 ]
 
 
+PARITY = [
+    [device(x, y, z, core) for x in range(px, NX, 2) for y in range(py, NY, 2)]
+    for z in range(NZ)
+    for core in range(2)
+    for px in range(2)
+    for py in range(2)
+]
+
+
 def split(value):
     high = value.astype(BF16)
     return high, (value - high.astype(F32)).astype(BF16)
@@ -77,7 +86,7 @@
     return high[at, :], low[at, :]
 
 
-def diagonal_kernel(core_ref, j_ref, mine_ref, other_ref, own_ref, block_high, block_low, out, high, low, both):
+def diagonal_kernel(core_ref, j_ref, mine_ref, other_ref, own_ref, block_high, block_low, out, cross_out, high, low, both):
     core = core_ref[0]
     both[0] = mine_ref[...]
     both[1] = other_ref[...]
@@ -91,35 +100,45 @@
                 low[at : at + 16, :] = l
     quarter(rows_of(j_ref[0], 3, high, low), block_high, block_low, out)
     cross = mul3(split(own_ref[...]), (high[:256], low[:256]), mul_nt)
-    out[1024:1040, :] = cross[:, :128]
-    out[1040:, :] = cross[:, 128:]
-
-
-def beside_kernel(j_ref, diagonal, high, low, block_high, block_low, *outs):
+    for m in range(8):
+        cross_out[m, :16, :] = cross[:, :128]
+        cross_out[m, 16:, :] = cross[:, 128:]
+
+
+def beside_kernel(j_ref, high, low, block_high, block_low, *outs):
     for d, out in zip((2, 1), outs):
         quarter(rows_of(j_ref[0], d, high, low), block_high, block_low, out)
-        out[1024:, :] = diagonal[1024:, :]
-
-
-def own_kernel(j_ref, diagonal, got, high, low, block_high, block_low, out):
+
+
+def own_kernel(j_ref, got, high, low, block_high, block_low, out):
     quarter(rows_of(j_ref[0], 0, high, low), block_high, block_low, out)
-    out[1024:, :] = diagonal[1024:, :]
     out[...] += got[...]
 
 
-def near_kernel(half, got1, got2, out):
+def sum8(parts):
+    return ((parts[0] + parts[1]) + (parts[2] + parts[3])) + ((parts[4] + parts[5]) + (parts[6] + parts[7]))
+
+
+def cross_kernel(parts, out):
+    total = sum8(parts)
+    out[:, :128] = total[:16]
+    out[:, 128:] = total[16:]
+
+
+def cross_sum_kernel(own, got1, got2, got3, out):
+    out[...] = (own[...] + got1[...]) + (got2[...] + got3[...])
+
+
+def near_kernel(half, got1, got2, after, out):
     total = half[...] + (got1[...] + got2[...])
     for m in range(8):
-        out[m, :128, :] = total[m * 128 : (m + 1) * 128]
-        out[m, 128:, :] = total[1024:]
-
-
-def far_kernel(parts, after, out, cross):
-    total = ((parts[0] + parts[1]) + (parts[2] + parts[3])) + ((parts[4] + parts[5]) + (parts[6] + parts[7]))
+        out[m] = total[m * 128 : (m + 1) * 128]
+
+
+def far_kernel(parts, after1, after2, out):
+    total = sum8(parts)
     for m in range(8):
-        out[m] = total[:128]
-    cross[:, :128] = total[128:144]
-    cross[:, 128:] = total[144:]
+        out[m] = total
 
 
 def pass_kernel(share, after, out):
@@ -185,8 +204,8 @@
     return lax.dot_general(left, right, dims, precision=lax.Precision.HIGHEST, preferred_element_type=F32)
 
 
-def trade(pieces):
-    return lax.all_to_all(pieces, ROW + COL, 0, 0, axis_index_groups=FAR)
+def trade(pieces, groups):
+    return lax.all_to_all(pieces, ROW + COL, 0, 0, axis_index_groups=groups)
 
 
 def fetch(value, d):
@@ -213,25 +232,26 @@
     other = lax.ppermute(mine, "core", [(0, 1), (1, 0)])
     block = call(split_kernel, [shape(512, 1024, dtype=BF16)] * 2, (vectors,))
     wide = shape(512, 512, dtype=BF16)
-    diagonal, *panels = call(
+    diagonal, cross, *panels = call(
         diagonal_kernel,
-        [shape(1056, 128), wide, wide],
+        [shape(1024, 128), shape(8, 32, 128), wide, wide],
         (scalar, j, mine, other, reflectors_first, *block),
         (pltpu.VMEM((2, 8, 32, 512), F32),),
         scalars=2,
     )
-    along_x, along_y = call(beside_kernel, [shape(1056, 128)] * 2, (j, diagonal, *panels, *block), scalars=1)
-    half = call(own_kernel, shape(1056, 128), (j, diagonal, fetch(diagonal, 3), *panels, *block), scalars=1)
+    along_x, along_y = call(beside_kernel, [shape(1024, 128)] * 2, (j, *panels, *block), scalars=1)
+    half = call(own_kernel, shape(1024, 128), (j, fetch(diagonal, 3), *panels, *block), scalars=1)
     by_core = jnp.stack([jnp.where(core == 0, mine, other), jnp.where(core == 0, other, mine)], axis=1)
     second = by_core[:, :, :16].reshape(256, 512)
     first = by_core[:, :, 16:].reshape(256, 512)
     w_first = exact(factor_first, first)
-    parts = call(near_kernel, shape(8, 160, 128), (half, fetch(along_y, 1), fetch(along_x, 2)))
-    share, cross = call(
-        far_kernel, [shape(8, 128, 128), shape(16, 256)], (trade(parts), w_first), inputs=[VMEM, HBM]
-    )
-    share = trade(share).reshape(1024, 128)
+    cross = call(cross_kernel, shape(16, 256), (trade(cross, PARITY),))
+    parts = (half, fetch(along_y, 1), fetch(along_x, 2), cross)
+    parts = call(near_kernel, shape(8, 128, 128), parts, inputs=[VMEM, VMEM, VMEM, HBM])
     cross = lax.all_gather(cross, COL, axis=0, tiled=True)
+    share = call(far_kernel, shape(8, 128, 128), (trade(parts, FAR), w_first, cross), inputs=[VMEM, HBM, HBM])
+    share = trade(share, FAR).reshape(1024, 128)
+    cross = call(cross_sum_kernel, shape(256, 256), (cross, *(fetch(cross, d) for d in (1, 2, 3))))
     share = call(pass_kernel, shape(1024, 128), (share, cross), inputs=[VMEM, HBM])
     got = {d: fetch(share, d) for d in (3, 2, 1)}
     w_second = exact(factor_second, second - exact(cross, w_first))

time: 123 us -> 138 us (1.12)
  blocking collectives: 44.3 us -> 60.1 us
  waiting for transfers between devices: 25.2 us -> 12.8 us
  starting transfers between devices: 37.6 us -> 48.9 us
    all_to_all x0 -> x1, blocking collectives: none -> 16.6 us  [trade(): return lax.all_to_all(pieces, ROW + COL, 0, 0, axis_index_groups=groups)]
    ppermute x6 -> x9, starting transfers between devices: 22.5 us -> 34.9 us  [fetch(): return lax.ppermute(value, ROW + COL, pairs)]
    all_to_all x2, waiting for transfers between devices: 12.2 us -> 0.01 us  [trade(): return lax.all_to_all(pieces, ROW + COL, 0, 0, axis_index_groups=groups)]
    ppermute x6 -> x9, waiting for transfers between devices: 13 us -> 12.8 us  [fetch(): return lax.ppermute(value, ROW + COL, pairs)]
    pallas_call x10 -> x12, Pallas kernels: 9.36 us -> 9.41 us  [call(): pl.pallas_call(kernel, out_shape=outs, in_specs=inputs or [SMEM] * scalar...]
  transfers between devices with their start and end apart: 9 -> 12, of which waited for: 7 -> 4; matrix products, arithmetic and copies ran while one was open for 3% -> 2% of each run, Pallas kernels for 4% -> 4%
where the time goes in v13:
time: 138 us; the launch traced here: 137 us
  blocking collectives  60.1 us (44%)
  starting transfers between devices  48.9 us (35%)
  waiting for transfers between devices  12.8 us (9%)
  Pallas kernels  9.41 us (7%)
  matrix products  2.7 us (2%)
  local copies, waits for them, and re-layouts  1.93 us (1%)
    ppermute x9, starting transfers between devices, fetch(): return lax.ppermute(value, ROW + COL, pairs)  34.9 us
    all_to_all x1, blocking collectives, local(): lax.all_to_all(jnp.broadcast_to(shards[None], (NZ,) + shards.shape), 'z',...  26.7 us
    all_gather x1, blocking collectives, local(): cross = lax.all_gather(cross, COL, axis=0, tiled=True)  16.9 us
    all_to_all x1, blocking collectives, trade(): return lax.all_to_all(pieces, ROW + COL, 0, 0, axis_index_groups=groups)  16.6 us
    ppermute x9, waiting for transfers between devices, fetch(): return lax.ppermute(value, ROW + COL, pairs)  12.8 us
    all_to_all x2, starting transfers between devices, trade(): return lax.all_to_all(pieces, ROW + COL, 0, 0, axis_index_groups=groups)  9.72 us
    pallas_call x12, Pallas kernels, call(): pl.pallas_call(kernel, out_shape=outs, in_specs=inputs or [SMEM] * scalar...  9.41 us
    ppermute x1, starting transfers between devices, local(): other = lax.ppermute(mine, 'core', [(0, 1), (1, 0)])  4.35 us
  transfers between devices with their start and end apart: 12, of which 4 were waited for; matrix products, arithmetic and copies ran while one was open for 2% of the time, Pallas kernels for 4%

profile of v13, /device:TPU:1, one launch (start us, length us, event | category | flops | bytes accessed | tf_op | source)
XLA Modules:
  0.0 137.3 jit_solution(4659597869075242850)
XLA Ops:
  0.9 26.7 %all_to_all.20.mine_ref = f32[8,32,512]{2,1,0:T(8,128)S(1)} all-to-all(f32[8,32,512]{2,1,0:T(8,128)S(1)} %broadcast_in_dim.2), channel_id=1, replica_groups=mesh['x'=4,'y'=8,'z'=8,'core'=2] {'z'}, dimensions={0} | all-to-all | bytes 1048576 | tf_op jit(solution)/shard_map/all_to_all | solution.py:231
  27.6 4.4 %collective-permute-start = (f32[8,32,512]{2,1,0:T(8,128)S(1)}, f32[8,32,512]{2,1,0:T(8,128)S(1)}, u32[]{:S(2)}, u32[]{:S(2)}) collective-permute-start(f32[8,32,512]{2,1,0:T(8,128)S(1)} %all_to_all.20.mine_ref), channel_id=1, source_target_pairs={{0,1},{1,0},{2,3},{3,2},{4,5},{5,4},{6,7},{7,6},{8,9},{9,8},{10,11... | collective-permute-start | bytes 1572872 | tf_op jit(solution)/shard_map/ppermute | solution.py:232
  31.9 1.6 %copy-done.1 = f32[512,1024]{1,0:T(8,128)S(1)} copy-done((f32[512,1024]{1,0:T(8,128)S(1)}, f32[512,1024]{1,0:T(8,128)}, u32[]{:S(2)}) %copy-start.1) | copy-done | bytes 2097176
  34.8 7.3 %collective-permute-start.4 = (f32[1024,128]{1,0:T(8,128)S(1)}, f32[1024,128]{1,0:T(8,128)S(1)}, u32[]{:S(2)}, u32[]{:S(2)}) collective-permute-start(f32[1024,128]{1,0:T(8,128)S(1)} %get-tuple-element.16), channel_id=1, source_target_pairs={{0,144},{1,497},{2,146},{3,499},{4,148},{5,501},{6,150},{7,503},{8... | collective-permute-start | bytes 1572872 | tf_op jit(solution)/shard_map/ppermute | solution.py:222
  42.1 1.0 shard_map.61
  43.1 1.9 %collective-permute-start.5 = (f32[1024,128]{1,0:T(8,128)S(1)}, f32[1024,128]{1,0:T(8,128)S(1)}, u32[]{:S(2)}, u32[]{:S(2)}) collective-permute-start(f32[1024,128]{1,0:T(8,128)S(1)} %get-tuple-element.19), channel_id=1, source_target_pairs={{0,16},{1,113},{2,18},{3,115},{4,20},{5,117},{6,22},{7,119},{8,24}... | collective-permute-start | bytes 1572872 | tf_op jit(solution)/shard_map/ppermute | solution.py:222
  45.0 2.2 %collective-permute-start.6 = (f32[1024,128]{1,0:T(8,128)S(1)}, f32[1024,128]{1,0:T(8,128)S(1)}, u32[]{:S(2)}, u32[]{:S(2)}) collective-permute-start(f32[1024,128]{1,0:T(8,128)S(1)} %get-tuple-element.20), channel_id=1, source_target_pairs={{0,128},{1,385},{2,130},{3,387},{4,132},{5,389},{6,134},{7,391},{8... | collective-permute-start | bytes 1572872 | tf_op jit(solution)/shard_map/ppermute | solution.py:222
  47.2 16.6 %all_to_all.21.parts = f32[8,32,128]{2,1,0:T(8,128)S(1)} all-to-all(f32[8,32,128]{2,1,0:T(8,128)S(1)} %get-tuple-element.15), channel_id=1, replica_groups={{0,32,64,96,256,288,320,352},{16,48,80,112,272,304,336,368},{128,160,19..., dimensions={0} | all-to-all | bytes 262144 | tf_op jit(solution)/shard_map/all_to_all | solution.py:208
  65.3 3.8 %all-to-all-start.2 = ((f32[8,128,128]{2,1,0:T(8,128)}), f32[8,128,128]{2,1,0:T(8,128)S(1)}, u32[]{:S(2)}, u32[]{:S(2)}) async-start(f32[8,128,128]{2,1,0:T(8,128)} %shard_map.62), calls=%async_computation.2 | async-start | bytes 1048576 | tf_op jit(solution)/shard_map/all_to_all | solution.py:208
  69.5 1.0 fusion.1
  70.7 16.9 %all_gather.3.own.after2 = f32[256,256]{1,0:T(8,128)S(1)} all-gather(f32[16,256]{1,0:T(8,128)S(1)} %shard_map.57.after), channel_id=1, replica_groups=mesh['x'=4,'y'=8,'z'=8,'core'=2] {'z','core'}, dimensions={0}, use_global_device_ids=true | all-gather | bytes 278528 | tf_op jit(solution)/shard_map/all_gather | solution.py:251
  88.4 5.9 %all-to-all-start.3 = ((f32[8,128,128]{2,1,0:T(8,128)}), f32[8,128,128]{2,1,0:T(8,128)S(1)}, u32[]{:S(2)}, u32[]{:S(2)}) async-start(f32[8,128,128]{2,1,0:T(8,128)} %shard_map.63), calls=%async_computation.3 | async-start | bytes 1048576 | tf_op jit(solution)/shard_map/all_to_all | solution.py:208
  94.3 5.5 %collective-permute-start.1 = (f32[256,256]{1,0:T(8,128)S(1)}, f32[256,256]{1,0:T(8,128)S(1)}, u32[]{:S(2)}, u32[]{:S(2)}) collective-permute-start(f32[256,256]{1,0:T(8,128)S(1)} %all_gather.3.own.after2), channel_id=1, source_target_pairs={{0,16},{1,113},{2,18},{3,115},{4,20},{5,117},{6,22},{7,119},{8,24}... | collective-permute-start | bytes 786440 | tf_op jit(solution)/shard_map/ppermute | solution.py:222
  99.8 5.2 %collective-permute-start.2 = (f32[256,256]{1,0:T(8,128)S(1)}, f32[256,256]{1,0:T(8,128)S(1)}, u32[]{:S(2)}, u32[]{:S(2)}) collective-permute-start(f32[256,256]{1,0:T(8,128)S(1)} %all_gather.3.own.after2), channel_id=1, source_target_pairs={{0,128},{1,385},{2,130},{3,387},{4,132},{5,389},{6,134},{7,391},{8... | collective-permute-start | bytes 786440 | tf_op jit(solution)/shard_map/ppermute | solution.py:222
  105.0 1.9 %collective-permute-start.3 = (f32[256,256]{1,0:T(8,128)S(1)}, f32[256,256]{1,0:T(8,128)S(1)}, u32[]{:S(2)}, u32[]{:S(2)}) collective-permute-start(f32[256,256]{1,0:T(8,128)S(1)} %all_gather.3.own.after2), channel_id=1, source_target_pairs={{0,144},{1,497},{2,146},{3,499},{4,148},{5,501},{6,150},{7,503},{8... | collective-permute-start | bytes 786440 | tf_op jit(solution)/shard_map/ppermute | solution.py:222
  107.0 5.0 %collective-permute-done.1.got1 = f32[256,256]{1,0:T(8,128)S(1)} collective-permute-done((f32[256,256]{1,0:T(8,128)S(1)}, f32[256,256]{1,0:T(8,128)S(1)}, u32[]{:S(2)}, u32[]{:S(2)}) %collective-permute-start.1) | collective-permute-done | bytes 262176 | tf_op jit(solution)/shard_map/ppermute | solution.py:222
  112.0 4.6 %collective-permute-done.3.got3 = f32[256,256]{1,0:T(8,128)S(1)} collective-permute-done((f32[256,256]{1,0:T(8,128)S(1)}, f32[256,256]{1,0:T(8,128)S(1)}, u32[]{:S(2)}, u32[]{:S(2)}) %collective-permute-start.3) | collective-permute-done | bytes 262176 | tf_op jit(solution)/shard_map/ppermute | solution.py:222
  116.7 1.9 %collective-permute-start.7 = (f32[1024,128]{1,0:T(8,128)S(1)}, f32[1024,128]{1,0:T(8,128)S(1)}, u32[]{:S(2)}, u32[]{:S(2)}) collective-permute-start(f32[1024,128]{1,0:T(8,128)S(1)} %shard_map.64.own), channel_id=1, source_target_pairs={{0,144},{1,497},{2,146},{3,499},{4,148},{5,501},{6,150},{7,503},{8... | collective-permute-start | bytes 1572872 | tf_op jit(solution)/shard_map/ppermute | solution.py:222
  118.7 4.3 %collective-permute-start.8 = (f32[1024,128]{1,0:T(8,128)S(1)}, f32[1024,128]{1,0:T(8,128)S(1)}, u32[]{:S(2)}, u32[]{:S(2)}) collective-permute-start(f32[1024,128]{1,0:T(8,128)S(1)} %shard_map.64.own), channel_id=1, source_target_pairs={{0,128},{1,385},{2,130},{3,387},{4,132},{5,389},{6,134},{7,391},{8... | collective-permute-start | bytes 1572872 | tf_op jit(solution)/shard_map/ppermute | solution.py:222
  122.9 4.6 %collective-permute-start.9 = (f32[1024,128]{1,0:T(8,128)S(1)}, f32[1024,128]{1,0:T(8,128)S(1)}, u32[]{:S(2)}, u32[]{:S(2)}) collective-permute-start(f32[1024,128]{1,0:T(8,128)S(1)} %shard_map.64.own), channel_id=1, source_target_pairs={{0,16},{1,113},{2,18},{3,115},{4,20},{5,117},{6,22},{7,119},{8,24}... | collective-permute-start | bytes 1572872 | tf_op jit(solution)/shard_map/ppermute | solution.py:222
  127.5 1.0 convolution_subtract_fusion
  130.1 2.6 %shard_map.65.middle = f32[512,1024]{1,0:T(8,128)S(1)} custom-call(f32[512,1024]{1,0:T(8,128)} %block.1, bf16[2,512,512]{2,1,0:T(8,128)(2,1)S(1)} %shard_map.59.w_ref, f32[1024,128]{1,0:T(8,128)S(1)} %shard_map.64.own, f32[1024,128]{1,0:T(8,128)S(1)} %collective-permute-done.7.got), custom_call_target="tpu_custom_call" | custom-call | tf_op jit(solution)/shard_map/pallas_call | solution.py:188
  132.7 2.7 %collective-permute-done.8.got = f32[1024,128]{1,0:T(8,128)S(1)} collective-permute-done((f32[1024,128]{1,0:T(8,128)S(1)}, f32[1024,128]{1,0:T(8,128)S(1)}, u32[]{:S(2)}, u32[]{:S(2)}) %collective-permute-start.8) | collective-permute-done | bytes 524320 | tf_op jit(solution)/shard_map/ppermute | solution.py:222
  135.4 1.9 %shard_map.66 = f32[512,1024]{1,0:T(8,128)} custom-call(f32[512,1024]{1,0:T(8,128)S(1)} %shard_map.65.middle, bf16[2,512,512]{2,1,0:T(8,128)(2,1)S(1)} %shard_map.59.w_ref, f32[1024,128]{1,0:T(8,128)S(1)} %collective-permute-done.8.got, f32[1024,128]{1,0:T(8,128)S(1)} %collective-permute-done.9.last), custom_call_target="tpu_custom_call" | custom-call | tf_op jit(solution)/shard_map/pallas_call | solution.py:188
  (33 shorter events, 6.5 us)
Async XLA Ops:
  0.0 69.5 %copy-start = (f32[256,256]{1,0:T(8,128)S(1)}, f32[256,256]{1,0:T(8,128)}, u32[]{:S(2)}) copy-start(f32[256,256]{1,0:T(8,128)} %param.8) | copy-start | bytes 786436
  0.0 33.8 %copy-start.2 = (f32[16,512]{1,0:T(8,128)S(1)}, f32[16,512]{1,0:T(8,128)}, u32[]{:S(2)}) copy-start(f32[16,512]{1,0:T(8,128)} %own_ref.1) | copy-start | bytes 98308
  27.6 6.3 %collective-permute-start = (f32[8,32,512]{2,1,0:T(8,128)S(1)}, f32[8,32,512]{2,1,0:T(8,128)S(1)}, u32[]{:S(2)}, u32[]{:S(2)}) collective-permute-start(f32[8,32,512]{2,1,0:T(8,128)S(1)} %all_to_all.20.mine_ref), channel_id=1, source_target_pairs={{0,1},{1,0},{2,3},{3,2},{4,5},{5,4},{6,7},{7,6},{8,9},{9,8},{10,11... | collective-permute-start | bytes 1572872 | tf_op jit(solution)/shard_map/ppermute | solution.py:232
  31.9 1.6 %copy-start.1 = (f32[512,1024]{1,0:T(8,128)S(1)}, f32[512,1024]{1,0:T(8,128)}, u32[]{:S(2)}) copy-start(f32[512,1024]{1,0:T(8,128)} %block.1) | copy-start | bytes 6291460
  34.8 29.0 %collective-permute-start.4 = (f32[1024,128]{1,0:T(8,128)S(1)}, f32[1024,128]{1,0:T(8,128)S(1)}, u32[]{:S(2)}, u32[]{:S(2)}) collective-permute-start(f32[1024,128]{1,0:T(8,128)S(1)} %get-tuple-element.16), channel_id=1, source_target_pairs={{0,144},{1,497},{2,146},{3,499},{4,148},{5,501},{6,150},{7,503},{8... | collective-permute-start | bytes 1572872 | tf_op jit(solution)/shard_map/ppermute | solution.py:222
  43.1 21.3 %collective-permute-start.5 = (f32[1024,128]{1,0:T(8,128)S(1)}, f32[1024,128]{1,0:T(8,128)S(1)}, u32[]{:S(2)}, u32[]{:S(2)}) collective-permute-start(f32[1024,128]{1,0:T(8,128)S(1)} %get-tuple-element.19), channel_id=1, source_target_pairs={{0,16},{1,113},{2,18},{3,115},{4,20},{5,117},{6,22},{7,119},{8,24}... | collective-permute-start | bytes 1572872 | tf_op jit(solution)/shard_map/ppermute | solution.py:222
  45.0 19.4 %collective-permute-start.6 = (f32[1024,128]{1,0:T(8,128)S(1)}, f32[1024,128]{1,0:T(8,128)S(1)}, u32[]{:S(2)}, u32[]{:S(2)}) collective-permute-start(f32[1024,128]{1,0:T(8,128)S(1)} %get-tuple-element.20), channel_id=1, source_target_pairs={{0,128},{1,385},{2,130},{3,387},{4,132},{5,389},{6,134},{7,391},{8... | collective-permute-start | bytes 1572872 | tf_op jit(solution)/shard_map/ppermute | solution.py:222
  65.3 22.2 %all-to-all-start.2 = ((f32[8,128,128]{2,1,0:T(8,128)}), f32[8,128,128]{2,1,0:T(8,128)S(1)}, u32[]{:S(2)}, u32[]{:S(2)}) async-start(f32[8,128,128]{2,1,0:T(8,128)} %shard_map.62), calls=%async_computation.2 | async-start | bytes 1048576 | tf_op jit(solution)/shard_map/all_to_all | solution.py:208
  88.4 28.3 %all-to-all-start.3 = ((f32[8,128,128]{2,1,0:T(8,128)}), f32[8,128,128]{2,1,0:T(8,128)S(1)}, u32[]{:S(2)}, u32[]{:S(2)}) async-start(f32[8,128,128]{2,1,0:T(8,128)} %shard_map.63), calls=%async_computation.3 | async-start | bytes 1048576 | tf_op jit(solution)/shard_map/all_to_all | solution.py:208
  94.3 17.7 %collective-permute-start.1 = (f32[256,256]{1,0:T(8,128)S(1)}, f32[256,256]{1,0:T(8,128)S(1)}, u32[]{:S(2)}, u32[]{:S(2)}) collective-permute-start(f32[256,256]{1,0:T(8,128)S(1)} %all_gather.3.own.after2), channel_id=1, source_target_pairs={{0,16},{1,113},{2,18},{3,115},{4,20},{5,117},{6,22},{7,119},{8,24}... | collective-permute-start | bytes 786440 | tf_op jit(solution)/shard_map/ppermute | solution.py:222
  99.8 12.2 %collective-permute-start.2 = (f32[256,256]{1,0:T(8,128)S(1)}, f32[256,256]{1,0:T(8,128)S(1)}, u32[]{:S(2)}, u32[]{:S(2)}) collective-permute-start(f32[256,256]{1,0:T(8,128)S(1)} %all_gather.3.own.after2), channel_id=1, source_target_pairs={{0,128},{1,385},{2,130},{3,387},{4,132},{5,389},{6,134},{7,391},{8... | collective-permute-start | bytes 786440 | tf_op jit(solution)/shard_map/ppermute | solution.py:222
  105.0 11.6 %collective-permute-start.3 = (f32[256,256]{1,0:T(8,128)S(1)}, f32[256,256]{1,0:T(8,128)S(1)}, u32[]{:S(2)}, u32[]{:S(2)}) collective-permute-start(f32[256,256]{1,0:T(8,128)S(1)} %all_gather.3.own.after2), channel_id=1, source_target_pairs={{0,144},{1,497},{2,146},{3,499},{4,148},{5,501},{6,150},{7,503},{8... | collective-permute-start | bytes 786440 | tf_op jit(solution)/shard_map/ppermute | solution.py:222
  107.0 21.6 %copy-start.3 = (f32[256,256]{1,0:T(8,128)S(1)}, f32[256,256]{1,0:T(8,128)}, u32[]{:S(2)}) copy-start(f32[256,256]{1,0:T(8,128)} %param.9) | copy-start | bytes 786436
  116.7 13.4 %collective-permute-start.7 = (f32[1024,128]{1,0:T(8,128)S(1)}, f32[1024,128]{1,0:T(8,128)S(1)}, u32[]{:S(2)}, u32[]{:S(2)}) collective-permute-start(f32[1024,128]{1,0:T(8,128)S(1)} %shard_map.64.own), channel_id=1, source_target_pairs={{0,144},{1,497},{2,146},{3,499},{4,148},{5,501},{6,150},{7,503},{8... | collective-permute-start | bytes 1572872 | tf_op jit(solution)/shard_map/ppermute | solution.py:222
  118.7 16.8 %collective-permute-start.8 = (f32[1024,128]{1,0:T(8,128)S(1)}, f32[1024,128]{1,0:T(8,128)S(1)}, u32[]{:S(2)}, u32[]{:S(2)}) collective-permute-start(f32[1024,128]{1,0:T(8,128)S(1)} %shard_map.64.own), channel_id=1, source_target_pairs={{0,128},{1,385},{2,130},{3,387},{4,132},{5,389},{6,134},{7,391},{8... | collective-permute-start | bytes 1572872 | tf_op jit(solution)/shard_map/ppermute | solution.py:222
  122.9 12.5 %collective-permute-start.9 = (f32[1024,128]{1,0:T(8,128)S(1)}, f32[1024,128]{1,0:T(8,128)S(1)}, u32[]{:S(2)}, u32[]{:S(2)}) collective-permute-start(f32[1024,128]{1,0:T(8,128)S(1)} %shard_map.64.own), channel_id=1, source_target_pairs={{0,16},{1,113},{2,18},{3,115},{4,20},{5,117},{6,22},{7,119},{8,24}... | collective-permute-start | bytes 1572872 | tf_op jit(solution)/shard_map/ppermute | solution.py:222

commit v14 on v12

v14 whole, which is shorter than its diff:
```python
import jax
import jax.numpy as jnp
from jax import lax
from jax.experimental import pallas as pl
from jax.experimental.pallas import tpu as pltpu
from jax.sharding import Mesh, PartitionSpec as P

ROW = ("x", "y")
COL = ("z", "core")
NX, NY, NZ = 4, 8, 8
F32, BF16 = jnp.float32, jnp.bfloat16
VMEM = pl.BlockSpec(memory_space=pltpu.VMEM)
SMEM = pl.BlockSpec(memory_space=pltpu.SMEM)
HBM = pl.BlockSpec(memory_space=pltpu.HBM)
PARAMS = pltpu.CompilerParams(vmem_limit_bytes=48 * 2**20)


def device(x, y, z, core):
    return ((x % NX * NY + y % NY) * NZ + z) * 2 + core


def label_x(x, core):
    return (x >> 1) ^ (x & 1 & ~core)


def label_y(y, core):
    y = (y - core) & 7
    return (y & 1) ^ (y >> 2)


FAR = [
    [
        device(x, y, z, core)
        for x in range(NX)
        for y in range(NY)
        if (label_x(x, core), label_y(y, core)) == (px, py)
    ]
    for z in range(NZ)
    for core in range(2)
    for px in range(2)
    for py in range(2)
]


def split(value):
    high = value.astype(BF16)
    return high, (value - high.astype(F32)).astype(BF16)


def mul(a, b):
    return jnp.dot(a, b, preferred_element_type=F32)


def mul_nt(a, b):
    return lax.dot_general(a, b, (((1,), (1,)), ((), ())), preferred_element_type=F32)


def mul3(a, b, mul=mul):
    return mul(a[0], b[0]) + (mul(a[0], b[1]) + mul(a[1], b[0]))


def split_kernel(block_ref, high, low):
    high[...], low[...] = split(block_ref[...])


def quarter(j, d, high, low, cross, block_high, block_low, out):
    at = pl.ds(pl.multiple_of((j ^ d) * 128, 128), 128)
    rows = high[at, :], low[at, :]
    for t in range(4):
        at = slice(t * 256, (t + 1) * 256)
        value = mul3(rows, (block_high[:, at], block_low[:, at]))
        for half in range(2):
            to = (2 * t + half) * 128
            out[to : to + 128, :] = value[:, half * 128 : (half + 1) * 128]
    at = pl.ds(pl.multiple_of((j ^ d) * 64, 64), 64)
    out[1024:1088, :] = cross[at, :128]
    out[1088:, :] = cross[at, 128:]


def diagonal_kernel(core_ref, j_ref, mine_ref, other_ref, block_high, block_low, out, cross, high, low, both):
    core = core_ref[0]
    both[0] = mine_ref[...]
    both[1] = other_ref[...]
    for c in range(2):
        from_core = both.at[core ^ c]
        for z in range(8):
            for panel in range(2):
                h, l = split(from_core[z, panel * 16 : panel * 16 + 16, :])
                at = (z // 2) * 128 + panel * 64 + (z % 2) * 32 + c * 16
                high[at : at + 16, :] = h
                low[at : at + 16, :] = l

    def whole(panel, ref):
        return jnp.concatenate([ref[q * 128 + panel * 64 : q * 128 + panel * 64 + 64, :] for q in range(4)], axis=0)

    cross[...] = mul3((whole(1, high), whole(1, low)), (whole(0, high), whole(0, low)), mul_nt)
    quarter(j_ref[0], 3, high, low, cross, block_high, block_low, out)


def beside_kernel(j_ref, cross, high, low, block_high, block_low, *outs):
    for d, out in zip((2, 1), outs):
        quarter(j_ref[0], d, high, low, cross, block_high, block_low, out)


def own_kernel(j_ref, got, cross, high, low, block_high, block_low, out):
    quarter(j_ref[0], 0, high, low, cross, block_high, block_low, out)
    out[...] += got[...]


def near_kernel(half, got1, got2, out):
    total = half[...] + (got1[...] + got2[...])
    for m in range(8):
        out[m, :128, :] = total[m * 128 : (m + 1) * 128]
        out[m, 128:, :] = total[1024 + m * 16 : 1040 + m * 16]


def far_kernel(parts, after, out):
    total = ((parts[0] + parts[1]) + (parts[2] + parts[3])) + ((parts[4] + parts[5]) + (parts[6] + parts[7]))
    for m in range(8):
        out[m] = total


def share_kernel(parts, out):
    for m in range(8):
        out[m * 128 : (m + 1) * 128, :] = parts[m, :128]
        out[1024 + m * 16 : 1040 + m * 16, :] = parts[m, 128:]


ORDER = (0, 3, 2, 1)


def prepare_kernel(j_ref, second_ref, w_ref, factor_ref, panel, weights, factor, turned):
    panel[...] = second_ref[...].T
    turned[...] = factor_ref[...].T
    at = [pl.ds(pl.multiple_of((j_ref[0] ^ d) * 64, 64), 64) for d in ORDER]
    weights[0], weights[1] = split(jnp.concatenate([w_ref[rows, :] for rows in at], axis=0).T)
    factor[0], factor[1] = split(jnp.concatenate([turned[rows, :] for rows in at], axis=0).T)


def natural(part):
    return jnp.concatenate([part[t * 128 : (t + 1) * 128, :] for t in range(8)], axis=1)


def cross_of(part):
    return jnp.concatenate([part[1024:1088, :], part[1088:, :]], axis=1)


def middle_kernel(block, weights, own, got, out):
    proj = split(jnp.concatenate([natural(own)[64:], natural(got)[64:]], axis=0))
    for t in range(2):
        rows = slice(t * 256, (t + 1) * 256)
        out[rows] = block[rows] - mul3((weights[0, rows, :128], weights[1, rows, :128]), proj)


def update_kernel(middle, panel, weights, factor, own, got3, got2, got1, out_ref, out, sems):
    parts = (own, got3, got2, got1)
    cross = split(jnp.concatenate([cross_of(part) for part in parts], axis=0))
    rest = panel[...] - mul3((weights[0], weights[1]), cross)
    second = split(mul3(split(rest), (factor[0], factor[1])))
    quarters = [natural(part) for part in parts]
    left = [jnp.concatenate([second[i], weights[i, :, 128:]], axis=1) for i in range(2)]
    rows = [quarter[:64] for quarter in quarters] + [quarter[64:] for quarter in quarters[2:]]
    right = split(jnp.concatenate(rows, axis=0))
    stores = []
    for t in range(4):
        at = slice(t * 128, (t + 1) * 128)
        out[at] = middle[at] - mul3((left[0][at], left[1][at]), right)
        stores.append(pltpu.make_async_copy(out.at[at], out_ref.at[at], sems.at[t]))
        stores[t].start()
    for store in stores:
        store.wait()


def call(kernel, outs, args, scratch=(), scalars=0, inputs=None, out_spec=VMEM):
    single = not isinstance(outs, list)
    return pl.pallas_call(
        kernel,
        out_shape=outs,
        in_specs=inputs or [SMEM] * scalars + [VMEM] * (len(args) - scalars),
        out_specs=out_spec if single else [out_spec] * len(outs),
        scratch_shapes=list(scratch),
        compiler_params=PARAMS,
    )(*args)


def shape(*dims, dtype=F32):
    return jax.ShapeDtypeStruct(dims, dtype)


def exact(left, right):
    dims = (((0,), (0,)), ((), ()))
    return lax.dot_general(left, right, dims, precision=lax.Precision.HIGHEST, preferred_element_type=F32)


def trade(pieces):
    return lax.all_to_all(pieces, ROW + COL, 0, 0, axis_index_groups=FAR)


def fetch(value, d):
    def partner(i, n, core):
        return (i + 1) % n if i % 2 == core else (i - 1) % n

    pairs = [
        (device(x, y, z, c), device(partner(x, NX, c) if d & 2 else x, partner(y, NY, c) if d & 1 else y, z, c))
        for x in range(NX)
        for y in range(NY)
        for z in range(NZ)
        for c in range(2)
    ]
    return lax.ppermute(value, ROW + COL, pairs)


def local(vectors, reflectors_first, reflectors_second, factor_first, factor_second):
    core = lax.axis_index("core")
    scalar = core.astype(jnp.int32).reshape(1)
    j = label_x(lax.axis_index("x"), core) * 2 + label_y(lax.axis_index("y"), core)
    j = j.astype(jnp.int32).reshape(1)
    shards = jnp.concatenate([reflectors_second, reflectors_first], axis=0)
    mine = lax.all_to_all(jnp.broadcast_to(shards[None], (NZ,) + shards.shape), "z", 0, 0)
    other = lax.ppermute(mine, "core", [(0, 1), (1, 0)])
    block = call(split_kernel, [shape(512, 1024, dtype=BF16)] * 2, (vectors,))
    wide = shape(512, 512, dtype=BF16)
    diagonal, *panels = call(
        diagonal_kernel,
        [shape(1152, 128), shape(256, 256), wide, wide],
        (scalar, j, mine, other, *block),
        (pltpu.VMEM((2, 8, 32, 512), F32),),
        scalars=2,
    )
    along_x, along_y = call(beside_kernel, [shape(1152, 128)] * 2, (j, *panels, *block), scalars=1)
    half = call(own_kernel, shape(1152, 128), (j, fetch(diagonal, 3), *panels, *block), scalars=1)
    by_core = jnp.stack([jnp.where(core == 0, mine, other), jnp.where(core == 0, other, mine)], axis=1)
    second = by_core[:, :, :16].reshape(256, 512)
    first = by_core[:, :, 16:].reshape(256, 512)
    w_first = exact(factor_first, first)
    parts = call(near_kernel, shape(8, 144, 128), (half, fetch(along_y, 1), fetch(along_x, 2)))
    parts = call(far_kernel, shape(8, 144, 128), (trade(parts), w_first), inputs=[VMEM, HBM])
    share = call(share_kernel, shape(1152, 128), (trade(parts),))
    got = {d: fetch(share, d) for d in (3, 2, 1)}
    panel, weights, factor = call(
        prepare_kernel,
        [shape(512, 256), shape(2, 512, 256, dtype=BF16), shape(2, 256, 256, dtype=BF16)],
        (j, second, w_first, factor_second),
        (pltpu.VMEM((256, 256), F32),),
        scalars=1,
    )
    middle = call(middle_kernel, shape(512, 1024), (vectors, weights, share, got[3]))
    return call(
        update_kernel,
        shape(512, 1024),
        (middle, panel, weights, factor, share, got[3], got[2], got[1]),
        (pltpu.VMEM((512, 1024), F32), pltpu.SemaphoreType.DMA((4,))),
        out_spec=HBM,
    )


def solution(mesh):
    fine = Mesh(mesh.devices.reshape(NX, NY, NZ, 2), ROW + COL)
    return jax.shard_map(
        local,
        mesh=fine,
        in_specs=(P(ROW, COL), P(COL, ROW), P(COL, ROW), P(), P()),
        out_specs=P(ROW, COL),
        check_vma=False,
    )
```

time: 123 us -> 121 us (0.984)
  starting transfers between devices: 37.6 us -> 31.6 us
  blocking collectives: 44.3 us -> 47.9 us
  waiting for transfers between devices: 25.2 us -> 27.5 us
  matrix products: 2.7 us -> 0.67 us
    all_to_all x0 -> x1, blocking collectives: none -> 21.3 us  [trade(): return lax.all_to_all(pieces, ROW + COL, 0, 0, axis_index_groups=FAR)]
    all_gather x1 -> x0, blocking collectives: 17.6 us -> none  [local(): cross = lax.all_gather(cross, COL, axis=0, tiled=True)]
    all_to_all x2 -> x1, starting transfers between devices: 10.8 us -> 4.07 us  [trade(): return lax.all_to_all(pieces, ROW + COL, 0, 0, axis_index_groups=FAR)]
    ppermute x6, waiting for transfers between devices: 13 us -> 15.9 us  [fetch(): return lax.ppermute(value, ROW + COL, pairs)]
    dot_general x3 -> x1, matrix products: 2.7 us -> 0.67 us  [exact(): lax.dot_general(left, right, dims, precision=lax.Precision.HIGHEST, prefe...]
    all_to_all x2 -> x1, waiting for transfers between devices: 12.2 us -> 11.6 us  [trade(): return lax.all_to_all(pieces, ROW + COL, 0, 0, axis_index_groups=FAR)]
  transfers between devices with their start and end apart: 9 -> 8, of which waited for: 7 -> 7; matrix products, arithmetic and copies ran while one was open for 3% -> 1% of each run, Pallas kernels for 4% -> 3%
where the time goes in v14:
time: 121 us; the launch traced here: 120 us
  blocking collectives  47.9 us (40%)
  starting transfers between devices  31.6 us (26%)
  waiting for transfers between devices  27.5 us (23%)
  Pallas kernels  8.86 us (7%)
  local copies, waits for them, and re-layouts  1.72 us (1%)
    all_to_all x1, blocking collectives, local(): lax.all_to_all(jnp.broadcast_to(shards[None], (NZ,) + shards.shape), 'z',...  26.7 us
    ppermute x6, starting transfers between devices, fetch(): return lax.ppermute(value, ROW + COL, pairs)  23.2 us
    all_to_all x1, blocking collectives, trade(): return lax.all_to_all(pieces, ROW + COL, 0, 0, axis_index_groups=FAR)  21.3 us
    ppermute x6, waiting for transfers between devices, fetch(): return lax.ppermute(value, ROW + COL, pairs)  15.9 us
    all_to_all x1, waiting for transfers between devices, trade(): return lax.all_to_all(pieces, ROW + COL, 0, 0, axis_index_groups=FAR)  11.6 us
    pallas_call x10, Pallas kernels, call(): pl.pallas_call(kernel, out_shape=outs, in_specs=inputs or [SMEM] * scalar...  8.86 us
    ppermute x1, starting transfers between devices, local(): other = lax.ppermute(mine, 'core', [(0, 1), (1, 0)])  4.35 us
    all_to_all x1, starting transfers between devices, trade(): return lax.all_to_all(pieces, ROW + COL, 0, 0, axis_index_groups=FAR)  4.07 us
  transfers between devices with their start and end apart: 8, of which 7 were waited for; matrix products, arithmetic and copies ran while one was open for 1% of the time, Pallas kernels for 3%

profile of v14, /device:TPU:1, one launch (start us, length us, event | category | flops | bytes accessed | tf_op | source)
XLA Modules:
  0.0 119.6 jit_solution(1667803288805492062)
XLA Ops:
  0.0 0.8 pad_maximum_fusion.1
  0.9 26.7 %all_to_all.15.mine_ref = f32[8,32,512]{2,1,0:T(8,128)S(1)} all-to-all(f32[8,32,512]{2,1,0:T(8,128)S(1)} %broadcast_in_dim.2), channel_id=1, replica_groups=mesh['x'=4,'y'=8,'z'=8,'core'=2] {'z'}, dimensions={0} | all-to-all | bytes 1048576 | tf_op jit(solution)/shard_map/all_to_all | solution.py:219
  27.5 4.4 %collective-permute-start = (f32[8,32,512]{2,1,0:T(8,128)S(1)}, f32[8,32,512]{2,1,0:T(8,128)S(1)}, u32[]{:S(2)}, u32[]{:S(2)}) collective-permute-start(f32[8,32,512]{2,1,0:T(8,128)S(1)} %all_to_all.15.mine_ref), channel_id=1, source_target_pairs={{0,1},{1,0},{2,3},{3,2},{4,5},{5,4},{6,7},{7,6},{8,9},{9,8},{10,11... | collective-permute-start | bytes 1572872 | tf_op jit(solution)/shard_map/ppermute | solution.py:220
  31.9 1.6 %copy-done.1 = f32[512,1024]{1,0:T(8,128)S(1)} copy-done((f32[512,1024]{1,0:T(8,128)S(1)}, f32[512,1024]{1,0:T(8,128)}, u32[]{:S(2)}) %copy-start.1) | copy-done | bytes 2097176
  33.8 1.0 shard_map.57
  34.8 7.3 %collective-permute-start.1 = (f32[1152,128]{1,0:T(8,128)S(1)}, f32[1152,128]{1,0:T(8,128)S(1)}, u32[]{:S(2)}, u32[]{:S(2)}) collective-permute-start(f32[1152,128]{1,0:T(8,128)S(1)} %get-tuple-element.19), channel_id=1, source_target_pairs={{0,144},{1,497},{2,146},{3,499},{4,148},{5,501},{6,150},{7,503},{8... | collective-permute-start | bytes 1769480 | tf_op jit(solution)/shard_map/ppermute | solution.py:210
  42.1 1.0 shard_map.59
  43.2 1.9 %collective-permute-start.2 = (f32[1152,128]{1,0:T(8,128)S(1)}, f32[1152,128]{1,0:T(8,128)S(1)}, u32[]{:S(2)}, u32[]{:S(2)}) collective-permute-start(f32[1152,128]{1,0:T(8,128)S(1)} %get-tuple-element.23), channel_id=1, source_target_pairs={{0,16},{1,113},{2,18},{3,115},{4,20},{5,117},{6,22},{7,119},{8,24}... | collective-permute-start | bytes 1769480 | tf_op jit(solution)/shard_map/ppermute | solution.py:210
  45.1 2.2 %collective-permute-start.3 = (f32[1152,128]{1,0:T(8,128)S(1)}, f32[1152,128]{1,0:T(8,128)S(1)}, u32[]{:S(2)}, u32[]{:S(2)}) collective-permute-start(f32[1152,128]{1,0:T(8,128)S(1)} %get-tuple-element.24), channel_id=1, source_target_pairs={{0,128},{1,385},{2,130},{3,387},{4,132},{5,389},{6,134},{7,391},{8... | collective-permute-start | bytes 1769480 | tf_op jit(solution)/shard_map/ppermute | solution.py:210
  47.3 2.1 %collective-permute-done.1.got = f32[1152,128]{1,0:T(8,128)S(1)} collective-permute-done((f32[1152,128]{1,0:T(8,128)S(1)}, f32[1152,128]{1,0:T(8,128)S(1)}, u32[]{:S(2)}, u32[]{:S(2)}) %collective-permute-start.1) | collective-permute-done | bytes 589856 | tf_op jit(solution)/shard_map/ppermute | solution.py:210
  50.0 5.2 %collective-permute-done.2.got1 = f32[1152,128]{1,0:T(8,128)S(1)} collective-permute-done((f32[1152,128]{1,0:T(8,128)S(1)}, f32[1152,128]{1,0:T(8,128)S(1)}, u32[]{:S(2)}, u32[]{:S(2)}) %collective-permute-start.2) | collective-permute-done | bytes 589856 | tf_op jit(solution)/shard_map/ppermute | solution.py:210
  55.3 1.7 %collective-permute-done.3.got2 = f32[1152,128]{1,0:T(8,128)S(1)} collective-permute-done((f32[1152,128]{1,0:T(8,128)S(1)}, f32[1152,128]{1,0:T(8,128)S(1)}, u32[]{:S(2)}, u32[]{:S(2)}) %collective-permute-start.3) | collective-permute-done | bytes 589856 | tf_op jit(solution)/shard_map/ppermute | solution.py:210
  56.9 0.9 shard_map.60
  57.8 4.1 %all-to-all-start.1 = ((f32[8,144,128]{2,1,0:T(8,128)}), f32[8,144,128]{2,1,0:T(8,128)S(1)}, u32[]{:S(2)}, u32[]{:S(2)}) async-start(f32[8,144,128]{2,1,0:T(8,128)} %shard_map.60), calls=%async_computation.1 | async-start | bytes 1179648 | tf_op jit(solution)/shard_map/all_to_all | solution.py:196
  62.9 11.6 %all-to-all-done.1.parts = f32[8,144,128]{2,1,0:T(8,128)S(1)} async-done(((f32[8,144,128]{2,1,0:T(8,128)}), f32[8,144,128]{2,1,0:T(8,128)S(1)}, u32[]{:S(2)}, u32[]{:S(2)}) %all-to-all-start.1) | async-done | bytes 589856 | tf_op jit(solution)/shard_map/all_to_all | solution.py:196
  74.5 21.3 %all_to_all.16.parts = f32[8,144,128]{2,1,0:T(8,128)S(1)} all-to-all(f32[8,144,128]{2,1,0:T(8,128)S(1)} %shard_map.61), channel_id=1, replica_groups={{0,32,80,112,384,416,464,496},{16,48,64,96,400,432,448,480},{128,160,20..., dimensions={0} | all-to-all | bytes 1179648 | tf_op jit(solution)/shard_map/all_to_all | solution.py:196
  95.8 6.4 %collective-permute-start.4 = (f32[1152,128]{1,0:T(8,128)S(1)}, f32[1152,128]{1,0:T(8,128)S(1)}, u32[]{:S(2)}, u32[]{:S(2)}) collective-permute-start(f32[1152,128]{1,0:T(8,128)S(1)} %shard_map.62.own), channel_id=1, source_target_pairs={{0,144},{1,497},{2,146},{3,499},{4,148},{5,501},{6,150},{7,503},{8... | collective-permute-start | bytes 1769480 | tf_op jit(solution)/shard_map/ppermute | solution.py:210
  102.2 1.9 %collective-permute-start.6 = (f32[1152,128]{1,0:T(8,128)S(1)}, f32[1152,128]{1,0:T(8,128)S(1)}, u32[]{:S(2)}, u32[]{:S(2)}) collective-permute-start(f32[1152,128]{1,0:T(8,128)S(1)} %shard_map.62.own), channel_id=1, source_target_pairs={{0,16},{1,113},{2,18},{3,115},{4,20},{5,117},{6,22},{7,119},{8,24}... | collective-permute-start | bytes 1769480 | tf_op jit(solution)/shard_map/ppermute | solution.py:210
  104.2 3.5 %collective-permute-start.5 = (f32[1152,128]{1,0:T(8,128)S(1)}, f32[1152,128]{1,0:T(8,128)S(1)}, u32[]{:S(2)}, u32[]{:S(2)}) collective-permute-start(f32[1152,128]{1,0:T(8,128)S(1)} %shard_map.62.own), channel_id=1, source_target_pairs={{0,128},{1,385},{2,130},{3,387},{4,132},{5,389},{6,134},{7,391},{8... | collective-permute-start | bytes 1769480 | tf_op jit(solution)/shard_map/ppermute | solution.py:210
  108.2 1.6 %collective-permute-done.4.got.got3 = f32[1152,128]{1,0:T(8,128)S(1)} collective-permute-done((f32[1152,128]{1,0:T(8,128)S(1)}, f32[1152,128]{1,0:T(8,128)S(1)}, u32[]{:S(2)}, u32[]{:S(2)}) %collective-permute-start.4) | collective-permute-done | bytes 589856 | tf_op jit(solution)/shard_map/ppermute | solution.py:210
  109.8 1.0 shard_map.63.middle
  110.8 4.6 %collective-permute-done.6.got1 = f32[1152,128]{1,0:T(8,128)S(1)} collective-permute-done((f32[1152,128]{1,0:T(8,128)S(1)}, f32[1152,128]{1,0:T(8,128)S(1)}, u32[]{:S(2)}, u32[]{:S(2)}) %collective-permute-start.6) | collective-permute-done | bytes 589856 | tf_op jit(solution)/shard_map/ppermute | solution.py:210
  115.4 0.7 collective-permute-done.5.got2
  116.1 3.5 %shard_map.64 = f32[512,1024]{1,0:T(8,128)} custom-call(f32[512,1024]{1,0:T(8,128)S(1)} %shard_map.63.middle, f32[512,256]{1,0:T(8,128)S(1)} %get-tuple-element.25.panel, bf16[2,512,256]{2,1,0:T(8,128)(2,1)S(1)} %get-tuple-element.16.weights, bf16[2,256,256]{2,1,0:T(8,128)(2,1)S(1)} %get-tuple-element.26.factor, f32[1152,128]{1,0:T(8,128)S(1)} %shard_map.62.own, ...), custom_call_target="tpu_custom_call" | custom-call | tf_op jit(solution)/shard_map/pallas_call | solution.py:176
  (19 shorter events, 2.5 us)
Async XLA Ops:
  0.0 62.2 %copy-start = (f32[256,256]{1,0:T(8,128)S(1)}, f32[256,256]{1,0:T(8,128)}, u32[]{:S(2)}) copy-start(f32[256,256]{1,0:T(8,128)} %param.8) | copy-start | bytes 786436
  27.5 6.3 %collective-permute-start = (f32[8,32,512]{2,1,0:T(8,128)S(1)}, f32[8,32,512]{2,1,0:T(8,128)S(1)}, u32[]{:S(2)}, u32[]{:S(2)}) collective-permute-start(f32[8,32,512]{2,1,0:T(8,128)S(1)} %all_to_all.15.mine_ref), channel_id=1, source_target_pairs={{0,1},{1,0},{2,3},{3,2},{4,5},{5,4},{6,7},{7,6},{8,9},{9,8},{10,11... | collective-permute-start | bytes 1572872 | tf_op jit(solution)/shard_map/ppermute | solution.py:220
  31.9 1.6 %copy-start.1 = (f32[512,1024]{1,0:T(8,128)S(1)}, f32[512,1024]{1,0:T(8,128)}, u32[]{:S(2)}) copy-start(f32[512,1024]{1,0:T(8,128)} %block.1) | copy-start | bytes 6291460
  34.8 14.6 %collective-permute-start.1 = (f32[1152,128]{1,0:T(8,128)S(1)}, f32[1152,128]{1,0:T(8,128)S(1)}, u32[]{:S(2)}, u32[]{:S(2)}) collective-permute-start(f32[1152,128]{1,0:T(8,128)S(1)} %get-tuple-element.19), channel_id=1, source_target_pairs={{0,144},{1,497},{2,146},{3,499},{4,148},{5,501},{6,150},{7,503},{8... | collective-permute-start | bytes 1769480 | tf_op jit(solution)/shard_map/ppermute | solution.py:210
  43.2 12.1 %collective-permute-start.2 = (f32[1152,128]{1,0:T(8,128)S(1)}, f32[1152,128]{1,0:T(8,128)S(1)}, u32[]{:S(2)}, u32[]{:S(2)}) collective-permute-start(f32[1152,128]{1,0:T(8,128)S(1)} %get-tuple-element.23), channel_id=1, source_target_pairs={{0,16},{1,113},{2,18},{3,115},{4,20},{5,117},{6,22},{7,119},{8,24}... | collective-permute-start | bytes 1769480 | tf_op jit(solution)/shard_map/ppermute | solution.py:210
  45.1 11.8 %collective-permute-start.3 = (f32[1152,128]{1,0:T(8,128)S(1)}, f32[1152,128]{1,0:T(8,128)S(1)}, u32[]{:S(2)}, u32[]{:S(2)}) collective-permute-start(f32[1152,128]{1,0:T(8,128)S(1)} %get-tuple-element.24), channel_id=1, source_target_pairs={{0,128},{1,385},{2,130},{3,387},{4,132},{5,389},{6,134},{7,391},{8... | collective-permute-start | bytes 1769480 | tf_op jit(solution)/shard_map/ppermute | solution.py:210
  57.8 16.6 %all-to-all-start.1 = ((f32[8,144,128]{2,1,0:T(8,128)}), f32[8,144,128]{2,1,0:T(8,128)S(1)}, u32[]{:S(2)}, u32[]{:S(2)}) async-start(f32[8,144,128]{2,1,0:T(8,128)} %shard_map.60), calls=%async_computation.1 | async-start | bytes 1179648 | tf_op jit(solution)/shard_map/all_to_all | solution.py:196
  74.5 33.2 %copy-start.3 = (f32[256,256]{1,0:T(8,128)S(1)}, f32[256,256]{1,0:T(8,128)}, u32[]{:S(2)}) copy-start(f32[256,256]{1,0:T(8,128)} %factor_ref.1) | copy-start | bytes 786436
  74.5 35.3 %copy-start.2 = (f32[512,1024]{1,0:T(8,128)S(1)}, f32[512,1024]{1,0:T(8,128)}, u32[]{:S(2)}) copy-start(f32[512,1024]{1,0:T(8,128)} %block.1) | copy-start | bytes 6291460
  95.8 14.0 %collective-permute-start.4 = (f32[1152,128]{1,0:T(8,128)S(1)}, f32[1152,128]{1,0:T(8,128)S(1)}, u32[]{:S(2)}, u32[]{:S(2)}) collective-permute-start(f32[1152,128]{1,0:T(8,128)S(1)} %shard_map.62.own), channel_id=1, source_target_pairs={{0,144},{1,497},{2,146},{3,499},{4,148},{5,501},{6,150},{7,503},{8... | collective-permute-start | bytes 1769480 | tf_op jit(solution)/shard_map/ppermute | solution.py:210
  102.2 13.1 %collective-permute-start.6 = (f32[1152,128]{1,0:T(8,128)S(1)}, f32[1152,128]{1,0:T(8,128)S(1)}, u32[]{:S(2)}, u32[]{:S(2)}) collective-permute-start(f32[1152,128]{1,0:T(8,128)S(1)} %shard_map.62.own), channel_id=1, source_target_pairs={{0,16},{1,113},{2,18},{3,115},{4,20},{5,117},{6,22},{7,119},{8,24}... | collective-permute-start | bytes 1769480 | tf_op jit(solution)/shard_map/ppermute | solution.py:210
  104.2 11.9 %collective-permute-start.5 = (f32[1152,128]{1,0:T(8,128)S(1)}, f32[1152,128]{1,0:T(8,128)S(1)}, u32[]{:S(2)}, u32[]{:S(2)}) collective-permute-start(f32[1152,128]{1,0:T(8,128)S(1)} %shard_map.62.own), channel_id=1, source_target_pairs={{0,128},{1,385},{2,130},{3,387},{4,132},{5,389},{6,134},{7,391},{8... | collective-permute-start | bytes 1769480 | tf_op jit(solution)/shard_map/ppermute | solution.py:210

commit v15 on v14

--- a/solution.py
+++ b/solution.py
@@ -114,7 +114,7 @@
         out[m, 128:, :] = total[1024 + m * 16 : 1040 + m * 16]
 
 
-def far_kernel(parts, after, out):
+def far_kernel(parts, out):
     total = ((parts[0] + parts[1]) + (parts[2] + parts[3])) + ((parts[4] + parts[5]) + (parts[6] + parts[7]))
     for m in range(8):
         out[m] = total
@@ -129,12 +129,16 @@
 ORDER = (0, 3, 2, 1)
 
 
-def prepare_kernel(j_ref, second_ref, w_ref, factor_ref, panel, weights, factor, turned):
+def prepare_kernel(j_ref, second_ref, first_ref, second_factor, first_factor, panel, weights, factor, turned):
+    at = [pl.ds(pl.multiple_of((j_ref[0] ^ d) * 64, 64), 64) for d in ORDER]
+
+    def ordered(ref):
+        turned[...] = ref[...].T
+        return split(jnp.concatenate([turned[rows, :] for rows in at], axis=0).T)
+
     panel[...] = second_ref[...].T
-    turned[...] = factor_ref[...].T
-    at = [pl.ds(pl.multiple_of((j_ref[0] ^ d) * 64, 64), 64) for d in ORDER]
-    weights[0], weights[1] = split(jnp.concatenate([w_ref[rows, :] for rows in at], axis=0).T)
-    factor[0], factor[1] = split(jnp.concatenate([turned[rows, :] for rows in at], axis=0).T)
+    weights[0], weights[1] = split(mul3(split(first_ref[...].T), ordered(first_factor)))
+    factor[0], factor[1] = ordered(second_factor)
 
 
 def natural(part):
@@ -187,11 +191,6 @@
     return jax.ShapeDtypeStruct(dims, dtype)
 
 
-def exact(left, right):
-    dims = (((0,), (0,)), ((), ()))
-    return lax.dot_general(left, right, dims, precision=lax.Precision.HIGHEST, preferred_element_type=F32)
-
-
 def trade(pieces):
     return lax.all_to_all(pieces, ROW + COL, 0, 0, axis_index_groups=FAR)
 
@@ -232,15 +231,14 @@
     by_core = jnp.stack([jnp.where(core == 0, mine, other), jnp.where(core == 0, other, mine)], axis=1)
     second = by_core[:, :, :16].reshape(256, 512)
     first = by_core[:, :, 16:].reshape(256, 512)
-    w_first = exact(factor_first, first)
     parts = call(near_kernel, shape(8, 144, 128), (half, fetch(along_y, 1), fetch(along_x, 2)))
-    parts = call(far_kernel, shape(8, 144, 128), (trade(parts), w_first), inputs=[VMEM, HBM])
+    parts = call(far_kernel, shape(8, 144, 128), (trade(parts),))
     share = call(share_kernel, shape(1152, 128), (trade(parts),))
     got = {d: fetch(share, d) for d in (3, 2, 1)}
     panel, weights, factor = call(
         prepare_kernel,
         [shape(512, 256), shape(2, 512, 256, dtype=BF16), shape(2, 256, 256, dtype=BF16)],
-        (j, second, w_first, factor_second),
+        (j, second, first, factor_second, factor_first),
         (pltpu.VMEM((256, 256), F32),),
         scalars=1,
     )

time: 121 us -> 121 us (level)
  blocking collectives: 47.9 us -> 61.9 us
  waiting for transfers between devices: 27.5 us -> 14.4 us
  starting transfers between devices: 31.6 us -> 30.1 us
    all_to_all x1 -> x2, blocking collectives: 21.3 us -> 35.3 us  [trade(): return lax.all_to_all(pieces, ROW + COL, 0, 0, axis_index_groups=FAR)]
    all_to_all x1 -> x0, waiting for transfers between devices: 11.6 us -> none  [trade(): return lax.all_to_all(pieces, ROW + COL, 0, 0, axis_index_groups=FAR)]
    all_to_all x1 -> x0, starting transfers between devices: 4.07 us -> none  [trade(): return lax.all_to_all(pieces, ROW + COL, 0, 0, axis_index_groups=FAR)]
    ppermute x6, starting transfers between devices: 23.2 us -> 25.7 us  [fetch(): return lax.ppermute(value, ROW + COL, pairs)]
    ppermute x6, waiting for transfers between devices: 15.9 us -> 14.4 us  [fetch(): return lax.ppermute(value, ROW + COL, pairs)]
  transfers between devices with their start and end apart: 8 -> 7, of which waited for: 7 -> 5; matrix products, arithmetic and copies ran while one was open for 1% -> 0% of each run, Pallas kernels for 3% -> 3%
where the time goes in v15:
time: 121 us; the launch traced here: 120 us
  blocking collectives  61.9 us (51%)
  starting transfers between devices  30.1 us (25%)
  waiting for transfers between devices  14.4 us (12%)
  Pallas kernels  9.43 us (8%)
  local copies, waits for them, and re-layouts  2.52 us (2%)
    all_to_all x2, blocking collectives, trade(): return lax.all_to_all(pieces, ROW + COL, 0, 0, axis_index_groups=FAR)  35.3 us
    all_to_all x1, blocking collectives, local(): lax.all_to_all(jnp.broadcast_to(shards[None], (NZ,) + shards.shape), 'z',...  26.7 us
    ppermute x6, starting transfers between devices, fetch(): return lax.ppermute(value, ROW + COL, pairs)  25.7 us
    ppermute x6, waiting for transfers between devices, fetch(): return lax.ppermute(value, ROW + COL, pairs)  14.4 us
    pallas_call x10, Pallas kernels, call(): pl.pallas_call(kernel, out_shape=outs, in_specs=inputs or [SMEM] * scalar...  9.43 us
    ppermute x1, starting transfers between devices, local(): other = lax.ppermute(mine, 'core', [(0, 1), (1, 0)])  4.35 us
  transfers between devices with their start and end apart: 7, of which 5 were waited for; matrix products, arithmetic and copies ran while one was open for 0% of the time, Pallas kernels for 3%

profile of v15, /device:TPU:1, one launch (start us, length us, event | category | flops | bytes accessed | tf_op | source)
XLA Modules:
  0.0 119.5 jit_solution(7757802481535438185)
XLA Ops:
  0.0 0.8 pad_maximum_fusion.1
  0.8 26.7 %all_to_all.15.mine_ref = f32[8,32,512]{2,1,0:T(8,128)S(1)} all-to-all(f32[8,32,512]{2,1,0:T(8,128)S(1)} %broadcast_in_dim.2), channel_id=1, replica_groups=mesh['x'=4,'y'=8,'z'=8,'core'=2] {'z'}, dimensions={0} | all-to-all | bytes 1048576 | tf_op jit(solution)/shard_map/all_to_all | solution.py:218
  27.5 4.4 %collective-permute-start = (f32[8,32,512]{2,1,0:T(8,128)S(1)}, f32[8,32,512]{2,1,0:T(8,128)S(1)}, u32[]{:S(2)}, u32[]{:S(2)}) collective-permute-start(f32[8,32,512]{2,1,0:T(8,128)S(1)} %all_to_all.15.mine_ref), channel_id=1, source_target_pairs={{0,1},{1,0},{2,3},{3,2},{4,5},{5,4},{6,7},{7,6},{8,9},{9,8},{10,11... | collective-permute-start | bytes 1572872 | tf_op jit(solution)/shard_map/ppermute | solution.py:219
  31.9 1.6 %copy-done = f32[512,1024]{1,0:T(8,128)S(1)} copy-done((f32[512,1024]{1,0:T(8,128)S(1)}, f32[512,1024]{1,0:T(8,128)}, u32[]{:S(2)}) %copy-start) | copy-done | bytes 2097176
  33.8 1.0 shard_map.57
  34.8 7.3 %collective-permute-start.1 = (f32[1152,128]{1,0:T(8,128)S(1)}, f32[1152,128]{1,0:T(8,128)S(1)}, u32[]{:S(2)}, u32[]{:S(2)}) collective-permute-start(f32[1152,128]{1,0:T(8,128)S(1)} %get-tuple-element.19), channel_id=1, source_target_pairs={{0,144},{1,497},{2,146},{3,499},{4,148},{5,501},{6,150},{7,503},{8... | collective-permute-start | bytes 1769480 | tf_op jit(solution)/shard_map/ppermute | solution.py:209
  42.1 1.0 shard_map.59
  43.1 1.9 %collective-permute-start.2 = (f32[1152,128]{1,0:T(8,128)S(1)}, f32[1152,128]{1,0:T(8,128)S(1)}, u32[]{:S(2)}, u32[]{:S(2)}) collective-permute-start(f32[1152,128]{1,0:T(8,128)S(1)} %get-tuple-element.23), channel_id=1, source_target_pairs={{0,16},{1,113},{2,18},{3,115},{4,20},{5,117},{6,22},{7,119},{8,24}... | collective-permute-start | bytes 1769480 | tf_op jit(solution)/shard_map/ppermute | solution.py:209
  45.1 2.2 %collective-permute-start.3 = (f32[1152,128]{1,0:T(8,128)S(1)}, f32[1152,128]{1,0:T(8,128)S(1)}, u32[]{:S(2)}, u32[]{:S(2)}) collective-permute-start(f32[1152,128]{1,0:T(8,128)S(1)} %get-tuple-element.24), channel_id=1, source_target_pairs={{0,128},{1,385},{2,130},{3,387},{4,132},{5,389},{6,134},{7,391},{8... | collective-permute-start | bytes 1769480 | tf_op jit(solution)/shard_map/ppermute | solution.py:209
  47.3 2.1 %collective-permute-done.1.got = f32[1152,128]{1,0:T(8,128)S(1)} collective-permute-done((f32[1152,128]{1,0:T(8,128)S(1)}, f32[1152,128]{1,0:T(8,128)S(1)}, u32[]{:S(2)}, u32[]{:S(2)}) %collective-permute-start.1) | collective-permute-done | bytes 589856 | tf_op jit(solution)/shard_map/ppermute | solution.py:209
  49.4 0.6 shard_map.58.half
  50.0 5.3 %collective-permute-done.2.got1 = f32[1152,128]{1,0:T(8,128)S(1)} collective-permute-done((f32[1152,128]{1,0:T(8,128)S(1)}, f32[1152,128]{1,0:T(8,128)S(1)}, u32[]{:S(2)}, u32[]{:S(2)}) %collective-permute-start.2) | collective-permute-done | bytes 589856 | tf_op jit(solution)/shard_map/ppermute | solution.py:209
  55.2 1.7 %collective-permute-done.3.got2 = f32[1152,128]{1,0:T(8,128)S(1)} collective-permute-done((f32[1152,128]{1,0:T(8,128)S(1)}, f32[1152,128]{1,0:T(8,128)S(1)}, u32[]{:S(2)}, u32[]{:S(2)}) %collective-permute-start.3) | collective-permute-done | bytes 589856 | tf_op jit(solution)/shard_map/ppermute | solution.py:209
  57.0 17.3 %all_to_all.16.parts = f32[8,144,128]{2,1,0:T(8,128)S(1)} all-to-all(f32[8,144,128]{2,1,0:T(8,128)S(1)} %shard_map.60), channel_id=1, replica_groups={{0,32,80,112,384,416,464,496},{16,48,64,96,400,432,448,480},{128,160,20..., dimensions={0} | all-to-all | bytes 1179648 | tf_op jit(solution)/shard_map/all_to_all | solution.py:195
  74.4 17.9 %all_to_all.17.parts = f32[8,144,128]{2,1,0:T(8,128)S(1)} all-to-all(f32[8,144,128]{2,1,0:T(8,128)S(1)} %shard_map.61), channel_id=1, replica_groups={{0,32,80,112,384,416,464,496},{16,48,64,96,400,432,448,480},{128,160,20..., dimensions={0} | all-to-all | bytes 1179648 | tf_op jit(solution)/shard_map/all_to_all | solution.py:195
  92.3 8.8 %collective-permute-start.4 = (f32[1152,128]{1,0:T(8,128)S(1)}, f32[1152,128]{1,0:T(8,128)S(1)}, u32[]{:S(2)}, u32[]{:S(2)}) collective-permute-start(f32[1152,128]{1,0:T(8,128)S(1)} %shard_map.62.own), channel_id=1, source_target_pairs={{0,144},{1,497},{2,146},{3,499},{4,148},{5,501},{6,150},{7,503},{8... | collective-permute-start | bytes 1769480 | tf_op jit(solution)/shard_map/ppermute | solution.py:209
  101.1 1.9 %collective-permute-start.6 = (f32[1152,128]{1,0:T(8,128)S(1)}, f32[1152,128]{1,0:T(8,128)S(1)}, u32[]{:S(2)}, u32[]{:S(2)}) collective-permute-start(f32[1152,128]{1,0:T(8,128)S(1)} %shard_map.62.own), channel_id=1, source_target_pairs={{0,16},{1,113},{2,18},{3,115},{4,20},{5,117},{6,22},{7,119},{8,24}... | collective-permute-start | bytes 1769480 | tf_op jit(solution)/shard_map/ppermute | solution.py:209
  103.1 3.6 %collective-permute-start.5 = (f32[1152,128]{1,0:T(8,128)S(1)}, f32[1152,128]{1,0:T(8,128)}, u32[]{:S(2)}, u32[]{:S(2)}) collective-permute-start(f32[1152,128]{1,0:T(8,128)S(1)} %shard_map.62.own), channel_id=1, source_target_pairs={{0,128},{1,385},{2,130},{3,387},{4,132},{5,389},{6,134},{7,391},{8... | collective-permute-start | bytes 1769480 | tf_op jit(solution)/shard_map/ppermute | solution.py:209
  107.0 0.7 copy-done.2
  107.8 0.8 shard_map.55
  108.7 1.0 shard_map.63.middle
  109.7 4.6 %collective-permute-done.6.got1 = f32[1152,128]{1,0:T(8,128)S(1)} collective-permute-done((f32[1152,128]{1,0:T(8,128)S(1)}, f32[1152,128]{1,0:T(8,128)S(1)}, u32[]{:S(2)}, u32[]{:S(2)}) %collective-permute-start.6) | collective-permute-done | bytes 589856 | tf_op jit(solution)/shard_map/ppermute | solution.py:209
  114.3 0.7 collective-permute-done.5.got2
  115.0 4.5 %shard_map.64 = f32[512,1024]{1,0:T(8,128)} custom-call(f32[512,1024]{1,0:T(8,128)S(1)} %shard_map.63.middle, f32[512,256]{1,0:T(8,128)S(1)} %get-tuple-element.25.panel, bf16[2,512,256]{2,1,0:T(8,128)(2,1)S(1)} %get-tuple-element.16.weights, bf16[2,256,256]{2,1,0:T(8,128)(2,1)S(1)} %get-tuple-element.26.factor, f32[1152,128]{1,0:T(8,128)S(1)} %shard_map.62.own, ...), custom_call_target="tpu_custom_call" | custom-call | tf_op jit(solution)/shard_map/pallas_call | solution.py:180
  (17 shorter events, 0.9 us)
Async XLA Ops:
  27.5 6.3 %collective-permute-start = (f32[8,32,512]{2,1,0:T(8,128)S(1)}, f32[8,32,512]{2,1,0:T(8,128)S(1)}, u32[]{:S(2)}, u32[]{:S(2)}) collective-permute-start(f32[8,32,512]{2,1,0:T(8,128)S(1)} %all_to_all.15.mine_ref), channel_id=1, source_target_pairs={{0,1},{1,0},{2,3},{3,2},{4,5},{5,4},{6,7},{7,6},{8,9},{9,8},{10,11... | collective-permute-start | bytes 1572872 | tf_op jit(solution)/shard_map/ppermute | solution.py:219
  31.9 1.6 %copy-start = (f32[512,1024]{1,0:T(8,128)S(1)}, f32[512,1024]{1,0:T(8,128)}, u32[]{:S(2)}) copy-start(f32[512,1024]{1,0:T(8,128)} %block.1) | copy-start | bytes 6291460
  34.8 14.6 %collective-permute-start.1 = (f32[1152,128]{1,0:T(8,128)S(1)}, f32[1152,128]{1,0:T(8,128)S(1)}, u32[]{:S(2)}, u32[]{:S(2)}) collective-permute-start(f32[1152,128]{1,0:T(8,128)S(1)} %get-tuple-element.19), channel_id=1, source_target_pairs={{0,144},{1,497},{2,146},{3,499},{4,148},{5,501},{6,150},{7,503},{8... | collective-permute-start | bytes 1769480 | tf_op jit(solution)/shard_map/ppermute | solution.py:209
  43.1 12.1 %collective-permute-start.2 = (f32[1152,128]{1,0:T(8,128)S(1)}, f32[1152,128]{1,0:T(8,128)S(1)}, u32[]{:S(2)}, u32[]{:S(2)}) collective-permute-start(f32[1152,128]{1,0:T(8,128)S(1)} %get-tuple-element.23), channel_id=1, source_target_pairs={{0,16},{1,113},{2,18},{3,115},{4,20},{5,117},{6,22},{7,119},{8,24}... | collective-permute-start | bytes 1769480 | tf_op jit(solution)/shard_map/ppermute | solution.py:209
  45.1 11.8 %collective-permute-start.3 = (f32[1152,128]{1,0:T(8,128)S(1)}, f32[1152,128]{1,0:T(8,128)S(1)}, u32[]{:S(2)}, u32[]{:S(2)}) collective-permute-start(f32[1152,128]{1,0:T(8,128)S(1)} %get-tuple-element.24), channel_id=1, source_target_pairs={{0,128},{1,385},{2,130},{3,387},{4,132},{5,389},{6,134},{7,391},{8... | collective-permute-start | bytes 1769480 | tf_op jit(solution)/shard_map/ppermute | solution.py:209
  92.3 16.3 %collective-permute-start.4 = (f32[1152,128]{1,0:T(8,128)S(1)}, f32[1152,128]{1,0:T(8,128)S(1)}, u32[]{:S(2)}, u32[]{:S(2)}) collective-permute-start(f32[1152,128]{1,0:T(8,128)S(1)} %shard_map.62.own), channel_id=1, source_target_pairs={{0,144},{1,497},{2,146},{3,499},{4,148},{5,501},{6,150},{7,503},{8... | collective-permute-start | bytes 1769480 | tf_op jit(solution)/shard_map/ppermute | solution.py:209
  101.1 13.1 %collective-permute-start.6 = (f32[1152,128]{1,0:T(8,128)S(1)}, f32[1152,128]{1,0:T(8,128)S(1)}, u32[]{:S(2)}, u32[]{:S(2)}) collective-permute-start(f32[1152,128]{1,0:T(8,128)S(1)} %shard_map.62.own), channel_id=1, source_target_pairs={{0,16},{1,113},{2,18},{3,115},{4,20},{5,117},{6,22},{7,119},{8,24}... | collective-permute-start | bytes 1769480 | tf_op jit(solution)/shard_map/ppermute | solution.py:209
  103.1 11.9 %collective-permute-start.5 = (f32[1152,128]{1,0:T(8,128)S(1)}, f32[1152,128]{1,0:T(8,128)}, u32[]{:S(2)}, u32[]{:S(2)}) collective-permute-start(f32[1152,128]{1,0:T(8,128)S(1)} %shard_map.62.own), channel_id=1, source_target_pairs={{0,128},{1,385},{2,130},{3,387},{4,132},{5,389},{6,134},{7,391},{8... | collective-permute-start | bytes 1769480 | tf_op jit(solution)/shard_map/ppermute | solution.py:209
  106.8 1.0 copy-start.2
  106.8 1.0 copy-start.3
  106.9 1.7 %copy-start.1 = (f32[512,1024]{1,0:T(8,128)S(1)}, f32[512,1024]{1,0:T(8,128)}, u32[]{:S(2)}) copy-start(f32[512,1024]{1,0:T(8,128)} %block.1) | copy-start | bytes 6291460

commit v16 on v15

--- a/solution.py
+++ b/solution.py
@@ -129,15 +129,25 @@
 ORDER = (0, 3, 2, 1)
 
 
-def prepare_kernel(j_ref, second_ref, first_ref, second_factor, first_factor, panel, weights, factor, turned):
+def prepare_kernel(
+    core_ref, j_ref, mine_ref, other_ref, second_factor, first_factor, panel, weights, factor, turned, both, panels
+):
+    both[0] = mine_ref[...]
+    both[1] = other_ref[...]
+    for c in range(2):
+        from_core = both.at[core_ref[0] ^ c]
+        for z in range(8):
+            to = slice(z * 32 + c * 16, z * 32 + c * 16 + 16)
+            panels[0, to, :] = from_core[z, :16, :]
+            panels[1, to, :] = from_core[z, 16:, :]
     at = [pl.ds(pl.multiple_of((j_ref[0] ^ d) * 64, 64), 64) for d in ORDER]
 
     def ordered(ref):
         turned[...] = ref[...].T
         return split(jnp.concatenate([turned[rows, :] for rows in at], axis=0).T)
 
-    panel[...] = second_ref[...].T
-    weights[0], weights[1] = split(mul3(split(first_ref[...].T), ordered(first_factor)))
+    panel[...] = panels[0].T
+    weights[0], weights[1] = split(mul3(split(panels[1].T), ordered(first_factor)))
     factor[0], factor[1] = ordered(second_factor)
 
 
@@ -228,9 +238,6 @@
     )
     along_x, along_y = call(beside_kernel, [shape(1152, 128)] * 2, (j, *panels, *block), scalars=1)
     half = call(own_kernel, shape(1152, 128), (j, fetch(diagonal, 3), *panels, *block), scalars=1)
-    by_core = jnp.stack([jnp.where(core == 0, mine, other), jnp.where(core == 0, other, mine)], axis=1)
-    second = by_core[:, :, :16].reshape(256, 512)
-    first = by_core[:, :, 16:].reshape(256, 512)
     parts = call(near_kernel, shape(8, 144, 128), (half, fetch(along_y, 1), fetch(along_x, 2)))
     parts = call(far_kernel, shape(8, 144, 128), (trade(parts),))
     share = call(share_kernel, shape(1152, 128), (trade(parts),))
@@ -238,9 +245,9 @@
     panel, weights, factor = call(
         prepare_kernel,
         [shape(512, 256), shape(2, 512, 256, dtype=BF16), shape(2, 256, 256, dtype=BF16)],
-        (j, second, first, factor_second, factor_first),
-        (pltpu.VMEM((256, 256), F32),),
-        scalars=1,
+        (scalar, j, mine, other, factor_second, factor_first),
+        (pltpu.VMEM((256, 256), F32), pltpu.VMEM((2, 8, 32, 512), F32), pltpu.VMEM((2, 256, 512), F32)),
+        scalars=2,
     )
     middle = call(middle_kernel, shape(512, 1024), (vectors, weights, share, got[3]))
     return call(

time: 121 us -> 120 us (level)
  transfers between devices with their start and end apart: 7 -> 7, of which waited for: 5 -> 6; matrix products, arithmetic and copies ran while one was open for 0% -> 0% of each run, Pallas kernels for 3% -> 3%
where the time goes in v16:
time: 120 us; the launch traced here: 119 us
  blocking collectives  62.5 us (52%)
  starting transfers between devices  29.7 us (25%)
  waiting for transfers between devices  15.4 us (13%)
  Pallas kernels  8.41 us (7%)
  local copies, waits for them, and re-layouts  1.65 us (1%)
    all_to_all x2, blocking collectives, trade(): return lax.all_to_all(pieces, ROW + COL, 0, 0, axis_index_groups=FAR)  35.9 us
    all_to_all x1, blocking collectives, local(): lax.all_to_all(jnp.broadcast_to(shards[None], (NZ,) + shards.shape), 'z',...  26.7 us
    ppermute x6, starting transfers between devices, fetch(): return lax.ppermute(value, ROW + COL, pairs)  25.4 us
    ppermute x6, waiting for transfers between devices, fetch(): return lax.ppermute(value, ROW + COL, pairs)  15.4 us
    pallas_call x10, Pallas kernels, call(): pl.pallas_call(kernel, out_shape=outs, in_specs=inputs or [SMEM] * scalar...  8.41 us
    ppermute x1, starting transfers between devices, local(): other = lax.ppermute(mine, 'core', [(0, 1), (1, 0)])  4.35 us
  transfers between devices with their start and end apart: 7, of which 6 were waited for; matrix products, arithmetic and copies ran while one was open for 0% of the time, Pallas kernels for 3%

profile of v16, /device:TPU:1, one launch (start us, length us, event | category | flops | bytes accessed | tf_op | source)
XLA Modules:
  0.0 118.7 jit_solution(15886622235274200687)
XLA Ops:
  0.0 0.8 pad_maximum_fusion
  0.8 26.7 %all_to_all.15.mine_ref = f32[8,32,512]{2,1,0:T(8,128)S(1)} all-to-all(f32[8,32,512]{2,1,0:T(8,128)S(1)} %broadcast_in_dim.2), channel_id=1, replica_groups=mesh['x'=4,'y'=8,'z'=8,'core'=2] {'z'}, dimensions={0} | all-to-all | bytes 1048576 | tf_op jit(solution)/shard_map/all_to_all | solution.py:228
  27.5 4.4 %collective-permute-start = (f32[8,32,512]{2,1,0:T(8,128)S(1)}, f32[8,32,512]{2,1,0:T(8,128)S(1)}, u32[]{:S(2)}, u32[]{:S(2)}) collective-permute-start(f32[8,32,512]{2,1,0:T(8,128)S(1)} %all_to_all.15.mine_ref), channel_id=1, source_target_pairs={{0,1},{1,0},{2,3},{3,2},{4,5},{5,4},{6,7},{7,6},{8,9},{9,8},{10,11... | collective-permute-start | bytes 1572872 | tf_op jit(solution)/shard_map/ppermute | solution.py:229
  31.9 1.6 %copy-done = f32[512,1024]{1,0:T(8,128)S(1)} copy-done((f32[512,1024]{1,0:T(8,128)S(1)}, f32[512,1024]{1,0:T(8,128)}, u32[]{:S(2)}) %copy-start) | copy-done | bytes 2097176
  33.8 1.0 shard_map.57
  34.8 7.3 %collective-permute-start.1 = (f32[1152,128]{1,0:T(8,128)S(1)}, f32[1152,128]{1,0:T(8,128)S(1)}, u32[]{:S(2)}, u32[]{:S(2)}) collective-permute-start(f32[1152,128]{1,0:T(8,128)S(1)} %get-tuple-element.19), channel_id=1, source_target_pairs={{0,144},{1,497},{2,146},{3,499},{4,148},{5,501},{6,150},{7,503},{8... | collective-permute-start | bytes 1769480 | tf_op jit(solution)/shard_map/ppermute | solution.py:219
  42.1 1.0 shard_map.59
  43.1 1.9 %collective-permute-start.2 = (f32[1152,128]{1,0:T(8,128)S(1)}, f32[1152,128]{1,0:T(8,128)S(1)}, u32[]{:S(2)}, u32[]{:S(2)}) collective-permute-start(f32[1152,128]{1,0:T(8,128)S(1)} %get-tuple-element.23), channel_id=1, source_target_pairs={{0,16},{1,113},{2,18},{3,115},{4,20},{5,117},{6,22},{7,119},{8,24}... | collective-permute-start | bytes 1769480 | tf_op jit(solution)/shard_map/ppermute | solution.py:219
  45.0 2.2 %collective-permute-start.3 = (f32[1152,128]{1,0:T(8,128)S(1)}, f32[1152,128]{1,0:T(8,128)S(1)}, u32[]{:S(2)}, u32[]{:S(2)}) collective-permute-start(f32[1152,128]{1,0:T(8,128)S(1)} %get-tuple-element.24), channel_id=1, source_target_pairs={{0,128},{1,385},{2,130},{3,387},{4,132},{5,389},{6,134},{7,391},{8... | collective-permute-start | bytes 1769480 | tf_op jit(solution)/shard_map/ppermute | solution.py:219
  47.2 2.1 %collective-permute-done.1.got = f32[1152,128]{1,0:T(8,128)S(1)} collective-permute-done((f32[1152,128]{1,0:T(8,128)S(1)}, f32[1152,128]{1,0:T(8,128)S(1)}, u32[]{:S(2)}, u32[]{:S(2)}) %collective-permute-start.1) | collective-permute-done | bytes 589856 | tf_op jit(solution)/shard_map/ppermute | solution.py:219
  49.3 0.6 shard_map.58.half
  49.9 5.3 %collective-permute-done.2.got1 = f32[1152,128]{1,0:T(8,128)S(1)} collective-permute-done((f32[1152,128]{1,0:T(8,128)S(1)}, f32[1152,128]{1,0:T(8,128)S(1)}, u32[]{:S(2)}, u32[]{:S(2)}) %collective-permute-start.2) | collective-permute-done | bytes 589856 | tf_op jit(solution)/shard_map/ppermute | solution.py:219
  55.2 1.7 %collective-permute-done.3.got2 = f32[1152,128]{1,0:T(8,128)S(1)} collective-permute-done((f32[1152,128]{1,0:T(8,128)S(1)}, f32[1152,128]{1,0:T(8,128)S(1)}, u32[]{:S(2)}, u32[]{:S(2)}) %collective-permute-start.3) | collective-permute-done | bytes 589856 | tf_op jit(solution)/shard_map/ppermute | solution.py:219
  57.0 17.5 %all_to_all.16.parts = f32[8,144,128]{2,1,0:T(8,128)S(1)} all-to-all(f32[8,144,128]{2,1,0:T(8,128)S(1)} %shard_map.60), channel_id=1, replica_groups={{0,32,80,112,384,416,464,496},{16,48,64,96,400,432,448,480},{128,160,20..., dimensions={0} | all-to-all | bytes 1179648 | tf_op jit(solution)/shard_map/all_to_all | solution.py:205
  74.5 18.4 %all_to_all.17.parts = f32[8,144,128]{2,1,0:T(8,128)S(1)} all-to-all(f32[8,144,128]{2,1,0:T(8,128)S(1)} %shard_map.61), channel_id=1, replica_groups={{0,32,80,112,384,416,464,496},{16,48,64,96,400,432,448,480},{128,160,20..., dimensions={0} | all-to-all | bytes 1179648 | tf_op jit(solution)/shard_map/all_to_all | solution.py:205
  92.9 8.5 %collective-permute-start.4 = (f32[1152,128]{1,0:T(8,128)S(1)}, f32[1152,128]{1,0:T(8,128)S(1)}, u32[]{:S(2)}, u32[]{:S(2)}) collective-permute-start(f32[1152,128]{1,0:T(8,128)S(1)} %shard_map.62.own), channel_id=1, source_target_pairs={{0,144},{1,497},{2,146},{3,499},{4,148},{5,501},{6,150},{7,503},{8... | collective-permute-start | bytes 1769480 | tf_op jit(solution)/shard_map/ppermute | solution.py:219
  101.4 1.9 %collective-permute-start.6 = (f32[1152,128]{1,0:T(8,128)S(1)}, f32[1152,128]{1,0:T(8,128)S(1)}, u32[]{:S(2)}, u32[]{:S(2)}) collective-permute-start(f32[1152,128]{1,0:T(8,128)S(1)} %shard_map.62.own), channel_id=1, source_target_pairs={{0,16},{1,113},{2,18},{3,115},{4,20},{5,117},{6,22},{7,119},{8,24}... | collective-permute-start | bytes 1769480 | tf_op jit(solution)/shard_map/ppermute | solution.py:219
  103.3 3.6 %collective-permute-start.5 = (f32[1152,128]{1,0:T(8,128)S(1)}, f32[1152,128]{1,0:T(8,128)S(1)}, u32[]{:S(2)}, u32[]{:S(2)}) collective-permute-start(f32[1152,128]{1,0:T(8,128)S(1)} %shard_map.62.own), channel_id=1, source_target_pairs={{0,128},{1,385},{2,130},{3,387},{4,132},{5,389},{6,134},{7,391},{8... | collective-permute-start | bytes 1769480 | tf_op jit(solution)/shard_map/ppermute | solution.py:219
  107.0 0.9 shard_map.55
  107.9 0.8 collective-permute-done.4.got.got3
  108.7 1.0 shard_map.63.middle
  109.6 4.9 %collective-permute-done.6.got1 = f32[1152,128]{1,0:T(8,128)S(1)} collective-permute-done((f32[1152,128]{1,0:T(8,128)S(1)}, f32[1152,128]{1,0:T(8,128)S(1)}, u32[]{:S(2)}, u32[]{:S(2)}) %collective-permute-start.6) | collective-permute-done | bytes 589856 | tf_op jit(solution)/shard_map/ppermute | solution.py:219
  114.5 0.6 collective-permute-done.5.got2
  115.2 3.5 %shard_map.64 = f32[512,1024]{1,0:T(8,128)} custom-call(f32[512,1024]{1,0:T(8,128)S(1)} %shard_map.63.middle, f32[512,256]{1,0:T(8,128)S(1)} %get-tuple-element.25.panel, bf16[2,512,256]{2,1,0:T(8,128)(2,1)S(1)} %get-tuple-element.16.weights, bf16[2,256,256]{2,1,0:T(8,128)(2,1)S(1)} %get-tuple-element.26.factor, f32[1152,128]{1,0:T(8,128)S(1)} %shard_map.62.own, ...), custom_call_target="tpu_custom_call" | custom-call | tf_op jit(solution)/shard_map/pallas_call | solution.py:190
  (13 shorter events, 0.5 us)
Async XLA Ops:
  27.5 6.3 %collective-permute-start = (f32[8,32,512]{2,1,0:T(8,128)S(1)}, f32[8,32,512]{2,1,0:T(8,128)S(1)}, u32[]{:S(2)}, u32[]{:S(2)}) collective-permute-start(f32[8,32,512]{2,1,0:T(8,128)S(1)} %all_to_all.15.mine_ref), channel_id=1, source_target_pairs={{0,1},{1,0},{2,3},{3,2},{4,5},{5,4},{6,7},{7,6},{8,9},{9,8},{10,11... | collective-permute-start | bytes 1572872 | tf_op jit(solution)/shard_map/ppermute | solution.py:229
  31.9 1.6 %copy-start = (f32[512,1024]{1,0:T(8,128)S(1)}, f32[512,1024]{1,0:T(8,128)}, u32[]{:S(2)}) copy-start(f32[512,1024]{1,0:T(8,128)} %block.1) | copy-start | bytes 6291460
  34.8 14.6 %collective-permute-start.1 = (f32[1152,128]{1,0:T(8,128)S(1)}, f32[1152,128]{1,0:T(8,128)S(1)}, u32[]{:S(2)}, u32[]{:S(2)}) collective-permute-start(f32[1152,128]{1,0:T(8,128)S(1)} %get-tuple-element.19), channel_id=1, source_target_pairs={{0,144},{1,497},{2,146},{3,499},{4,148},{5,501},{6,150},{7,503},{8... | collective-permute-start | bytes 1769480 | tf_op jit(solution)/shard_map/ppermute | solution.py:219
  43.1 12.1 %collective-permute-start.2 = (f32[1152,128]{1,0:T(8,128)S(1)}, f32[1152,128]{1,0:T(8,128)S(1)}, u32[]{:S(2)}, u32[]{:S(2)}) collective-permute-start(f32[1152,128]{1,0:T(8,128)S(1)} %get-tuple-element.23), channel_id=1, source_target_pairs={{0,16},{1,113},{2,18},{3,115},{4,20},{5,117},{6,22},{7,119},{8,24}... | collective-permute-start | bytes 1769480 | tf_op jit(solution)/shard_map/ppermute | solution.py:219
  45.0 11.8 %collective-permute-start.3 = (f32[1152,128]{1,0:T(8,128)S(1)}, f32[1152,128]{1,0:T(8,128)S(1)}, u32[]{:S(2)}, u32[]{:S(2)}) collective-permute-start(f32[1152,128]{1,0:T(8,128)S(1)} %get-tuple-element.24), channel_id=1, source_target_pairs={{0,128},{1,385},{2,130},{3,387},{4,132},{5,389},{6,134},{7,391},{8... | collective-permute-start | bytes 1769480 | tf_op jit(solution)/shard_map/ppermute | solution.py:219
  56.9 50.0 %copy-start.2 = (f32[256,256]{1,0:T(8,128)S(1)}, f32[256,256]{1,0:T(8,128)}, u32[]{:S(2)}) copy-start(f32[256,256]{1,0:T(8,128)} %second_factor.1) | copy-start | bytes 786436
  57.0 50.0 %copy-start.3 = (f32[256,256]{1,0:T(8,128)S(1)}, f32[256,256]{1,0:T(8,128)}, u32[]{:S(2)}) copy-start(f32[256,256]{1,0:T(8,128)} %first_factor.1) | copy-start | bytes 786436
  74.5 34.2 %copy-start.1 = (f32[512,1024]{1,0:T(8,128)S(1)}, f32[512,1024]{1,0:T(8,128)}, u32[]{:S(2)}) copy-start(f32[512,1024]{1,0:T(8,128)} %block.1) | copy-start | bytes 6291460
  92.9 15.7 %collective-permute-start.4 = (f32[1152,128]{1,0:T(8,128)S(1)}, f32[1152,128]{1,0:T(8,128)S(1)}, u32[]{:S(2)}, u32[]{:S(2)}) collective-permute-start(f32[1152,128]{1,0:T(8,128)S(1)} %shard_map.62.own), channel_id=1, source_target_pairs={{0,144},{1,497},{2,146},{3,499},{4,148},{5,501},{6,150},{7,503},{8... | collective-permute-start | bytes 1769480 | tf_op jit(solution)/shard_map/ppermute | solution.py:219
  101.4 13.1 %collective-permute-start.6 = (f32[1152,128]{1,0:T(8,128)S(1)}, f32[1152,128]{1,0:T(8,128)S(1)}, u32[]{:S(2)}, u32[]{:S(2)}) collective-permute-start(f32[1152,128]{1,0:T(8,128)S(1)} %shard_map.62.own), channel_id=1, source_target_pairs={{0,16},{1,113},{2,18},{3,115},{4,20},{5,117},{6,22},{7,119},{8,24}... | collective-permute-start | bytes 1769480 | tf_op jit(solution)/shard_map/ppermute | solution.py:219
  103.3 11.8 %collective-permute-start.5 = (f32[1152,128]{1,0:T(8,128)S(1)}, f32[1152,128]{1,0:T(8,128)S(1)}, u32[]{:S(2)}, u32[]{:S(2)}) collective-permute-start(f32[1152,128]{1,0:T(8,128)S(1)} %shard_map.62.own), channel_id=1, source_target_pairs={{0,128},{1,385},{2,130},{3,387},{4,132},{5,389},{6,134},{7,391},{8... | collective-permute-start | bytes 1769480 | tf_op jit(solution)/shard_map/ppermute | solution.py:219

commit v17 on v16

--- a/solution.py
+++ b/solution.py
@@ -12,7 +12,7 @@
 VMEM = pl.BlockSpec(memory_space=pltpu.VMEM)
 SMEM = pl.BlockSpec(memory_space=pltpu.SMEM)
 HBM = pl.BlockSpec(memory_space=pltpu.HBM)
-PARAMS = pltpu.CompilerParams(vmem_limit_bytes=48 * 2**20)
+PARAMS = pltpu.CompilerParams(vmem_limit_bytes=28 * 2**20)
 
 
 def device(x, y, z, core):
@@ -77,7 +77,9 @@
     out[1088:, :] = cross[at, 128:]
 
 
-def diagonal_kernel(core_ref, j_ref, mine_ref, other_ref, block_high, block_low, out, cross, high, low, both):
+def project_kernel(
+    core_ref, j_ref, mine_ref, other_ref, block_high, block_low, out3, out2, out1, cross, high, low, both
+):
     core = core_ref[0]
     both[0] = mine_ref[...]
     both[1] = other_ref[...]
@@ -94,11 +96,7 @@
         return jnp.concatenate([ref[q * 128 + panel * 64 : q * 128 + panel * 64 + 64, :] for q in range(4)], axis=0)
 
     cross[...] = mul3((whole(1, high), whole(1, low)), (whole(0, high), whole(0, low)), mul_nt)
-    quarter(j_ref[0], 3, high, low, cross, block_high, block_low, out)
-
-
-def beside_kernel(j_ref, cross, high, low, block_high, block_low, *outs):
-    for d, out in zip((2, 1), outs):
+    for d, out in ((3, out3), (2, out2), (1, out1)):
         quarter(j_ref[0], d, high, low, cross, block_high, block_low, out)
 
 
@@ -159,17 +157,19 @@
     return jnp.concatenate([part[1024:1088, :], part[1088:, :]], axis=1)
 
 
-def middle_kernel(block, weights, own, got, out):
+def middle_kernel(block, panel, weights, own, got, out, rest):
+    cross = split(jnp.concatenate([cross_of(own), cross_of(got)], axis=0))
+    rest[...] = panel[...] - mul3((weights[0, :, :128], weights[1, :, :128]), cross)
     proj = split(jnp.concatenate([natural(own)[64:], natural(got)[64:]], axis=0))
     for t in range(2):
         rows = slice(t * 256, (t + 1) * 256)
         out[rows] = block[rows] - mul3((weights[0, rows, :128], weights[1, rows, :128]), proj)
 
 
-def update_kernel(middle, panel, weights, factor, own, got3, got2, got1, out_ref, out, sems):
+def update_kernel(middle, rest_ref, weights, factor, own, got3, got2, got1, out_ref, out, sems):
     parts = (own, got3, got2, got1)
-    cross = split(jnp.concatenate([cross_of(part) for part in parts], axis=0))
-    rest = panel[...] - mul3((weights[0], weights[1]), cross)
+    cross = split(jnp.concatenate([cross_of(got2), cross_of(got1)], axis=0))
+    rest = rest_ref[...] - mul3((weights[0, :, 128:], weights[1, :, 128:]), cross)
     second = split(mul3(split(rest), (factor[0], factor[1])))
     quarters = [natural(part) for part in parts]
     left = [jnp.concatenate([second[i], weights[i, :, 128:]], axis=1) for i in range(2)]
@@ -229,14 +229,13 @@
     other = lax.ppermute(mine, "core", [(0, 1), (1, 0)])
     block = call(split_kernel, [shape(512, 1024, dtype=BF16)] * 2, (vectors,))
     wide = shape(512, 512, dtype=BF16)
-    diagonal, *panels = call(
-        diagonal_kernel,
-        [shape(1152, 128), shape(256, 256), wide, wide],
+    diagonal, along_x, along_y, *panels = call(
+        project_kernel,
+        [shape(1152, 128)] * 3 + [shape(256, 256), wide, wide],
         (scalar, j, mine, other, *block),
         (pltpu.VMEM((2, 8, 32, 512), F32),),
         scalars=2,
     )
-    along_x, along_y = call(beside_kernel, [shape(1152, 128)] * 2, (j, *panels, *block), scalars=1)
     half = call(own_kernel, shape(1152, 128), (j, fetch(diagonal, 3), *panels, *block), scalars=1)
     parts = call(near_kernel, shape(8, 144, 128), (half, fetch(along_y, 1), fetch(along_x, 2)))
     parts = call(far_kernel, shape(8, 144, 128), (trade(parts),))
@@ -249,11 +248,13 @@
         (pltpu.VMEM((256, 256), F32), pltpu.VMEM((2, 8, 32, 512), F32), pltpu.VMEM((2, 256, 512), F32)),
         scalars=2,
     )
-    middle = call(middle_kernel, shape(512, 1024), (vectors, weights, share, got[3]))
+    middle, rest = call(
+        middle_kernel, [shape(512, 1024), shape(512, 256)], (vectors, panel, weights, share, got[3])
+    )
     return call(
         update_kernel,
         shape(512, 1024),
-        (middle, panel, weights, factor, share, got[3], got[2], got[1]),
+        (middle, rest, weights, factor, share, got[3], got[2], got[1]),
         (pltpu.VMEM((512, 1024), F32), pltpu.SemaphoreType.DMA((4,))),
         out_spec=HBM,
     )

time: 120 us -> 121 us (level)
    pallas_call x10 -> x9, Pallas kernels: 8.41 us -> 8.46 us  [call(): pl.pallas_call(kernel, out_shape=outs, in_specs=inputs or [SMEM] * scalar...]
where the time goes in v17:
time: 121 us; the launch traced here: 119 us
  blocking collectives  62.9 us (52%)
  starting transfers between devices  29.2 us (24%)
  waiting for transfers between devices  15.9 us (13%)
  Pallas kernels  8.46 us (7%)
  local copies, waits for them, and re-layouts  1.65 us (1%)
    all_to_all x2, blocking collectives, trade(): return lax.all_to_all(pieces, ROW + COL, 0, 0, axis_index_groups=FAR)  36.2 us
    all_to_all x1, blocking collectives, local(): lax.all_to_all(jnp.broadcast_to(shards[None], (NZ,) + shards.shape), 'z',...  26.7 us
    ppermute x6, starting transfers between devices, fetch(): return lax.ppermute(value, ROW + COL, pairs)  24.9 us
    ppermute x6, waiting for transfers between devices, fetch(): return lax.ppermute(value, ROW + COL, pairs)  15.9 us
    pallas_call x9, Pallas kernels, call(): pl.pallas_call(kernel, out_shape=outs, in_specs=inputs or [SMEM] * scalar...  8.46 us
    ppermute x1, starting transfers between devices, local(): other = lax.ppermute(mine, 'core', [(0, 1), (1, 0)])  4.35 us
  transfers between devices with their start and end apart: 7, of which 6 were waited for; matrix products, arithmetic and copies ran while one was open for 0% of the time, Pallas kernels for 3%

profile of v17, /device:TPU:1, one launch (start us, length us, event | category | flops | bytes accessed | tf_op | source)
XLA Modules:
  0.0 119.1 jit_solution(6676507754724431876)
XLA Ops:
  0.0 0.8 pad_maximum_fusion
  0.8 26.7 %all_to_all.15.mine_ref = f32[8,32,512]{2,1,0:T(8,128)S(1)} all-to-all(f32[8,32,512]{2,1,0:T(8,128)S(1)} %broadcast_in_dim.2), channel_id=1, replica_groups=mesh['x'=4,'y'=8,'z'=8,'core'=2] {'z'}, dimensions={0} | all-to-all | bytes 1048576 | tf_op jit(solution)/shard_map/all_to_all | solution.py:228
  27.5 4.4 %collective-permute-start = (f32[8,32,512]{2,1,0:T(8,128)S(1)}, f32[8,32,512]{2,1,0:T(8,128)S(1)}, u32[]{:S(2)}, u32[]{:S(2)}) collective-permute-start(f32[8,32,512]{2,1,0:T(8,128)S(1)} %all_to_all.15.mine_ref), channel_id=1, source_target_pairs={{0,1},{1,0},{2,3},{3,2},{4,5},{5,4},{6,7},{7,6},{8,9},{9,8},{10,11... | collective-permute-start | bytes 1572872 | tf_op jit(solution)/shard_map/ppermute | solution.py:229
  31.9 1.6 %copy-done = f32[512,1024]{1,0:T(8,128)S(1)} copy-done((f32[512,1024]{1,0:T(8,128)S(1)}, f32[512,1024]{1,0:T(8,128)}, u32[]{:S(2)}) %copy-start) | copy-done | bytes 2097176
  33.5 0.3 shard_map.56
  33.8 1.9 %shard_map.57 = (f32[1152,128]{1,0:T(8,128)S(1)}, f32[1152,128]{1,0:T(8,128)S(1)}, f32[1152,128]{1,0:T(8,128)S(1)}, f32[256,256]{1,0:T(8,128)S(1)}, bf16[512,512...) custom-call(s32[1]{0:T(128)} %bitcast.core_ref, s32[1]{0:T(128)} %bitcast.1.j_ref, f32[8,32,512]{2,1,0:T(8,128)S(1)} %all_to_all.15.mine_ref, ...), custom_call_target="tpu_custom_call" | custom-call | tf_op jit(solution)/shard_map/pallas_call | solution.py:190
  35.7 7.3 %collective-permute-start.1 = (f32[1152,128]{1,0:T(8,128)S(1)}, f32[1152,128]{1,0:T(8,128)S(1)}, u32[]{:S(2)}, u32[]{:S(2)}) collective-permute-start(f32[1152,128]{1,0:T(8,128)S(1)} %get-tuple-element.22), channel_id=1, source_target_pairs={{0,144},{1,497},{2,146},{3,499},{4,148},{5,501},{6,150},{7,503},{8... | collective-permute-start | bytes 1769480 | tf_op jit(solution)/shard_map/ppermute | solution.py:219
  43.0 1.9 %collective-permute-start.2 = (f32[1152,128]{1,0:T(8,128)S(1)}, f32[1152,128]{1,0:T(8,128)S(1)}, u32[]{:S(2)}, u32[]{:S(2)}) collective-permute-start(f32[1152,128]{1,0:T(8,128)S(1)} %get-tuple-element.26), channel_id=1, source_target_pairs={{0,16},{1,113},{2,18},{3,115},{4,20},{5,117},{6,22},{7,119},{8,24}... | collective-permute-start | bytes 1769480 | tf_op jit(solution)/shard_map/ppermute | solution.py:219
  44.9 2.2 %collective-permute-start.3 = (f32[1152,128]{1,0:T(8,128)S(1)}, f32[1152,128]{1,0:T(8,128)S(1)}, u32[]{:S(2)}, u32[]{:S(2)}) collective-permute-start(f32[1152,128]{1,0:T(8,128)S(1)} %get-tuple-element.27), channel_id=1, source_target_pairs={{0,128},{1,385},{2,130},{3,387},{4,132},{5,389},{6,134},{7,391},{8... | collective-permute-start | bytes 1769480 | tf_op jit(solution)/shard_map/ppermute | solution.py:219
  47.1 3.1 %collective-permute-done.1.got = f32[1152,128]{1,0:T(8,128)S(1)} collective-permute-done((f32[1152,128]{1,0:T(8,128)S(1)}, f32[1152,128]{1,0:T(8,128)S(1)}, u32[]{:S(2)}, u32[]{:S(2)}) %collective-permute-start.1) | collective-permute-done | bytes 589856 | tf_op jit(solution)/shard_map/ppermute | solution.py:219
  50.2 0.6 shard_map.58.half
  50.9 5.2 %collective-permute-done.2.got1 = f32[1152,128]{1,0:T(8,128)S(1)} collective-permute-done((f32[1152,128]{1,0:T(8,128)S(1)}, f32[1152,128]{1,0:T(8,128)S(1)}, u32[]{:S(2)}, u32[]{:S(2)}) %collective-permute-start.2) | collective-permute-done | bytes 589856 | tf_op jit(solution)/shard_map/ppermute | solution.py:219
  56.1 0.6 collective-permute-done.3.got2
  56.9 17.8 %all_to_all.16.parts = f32[8,144,128]{2,1,0:T(8,128)S(1)} all-to-all(f32[8,144,128]{2,1,0:T(8,128)S(1)} %shard_map.59), channel_id=1, replica_groups={{0,32,80,112,384,416,464,496},{16,48,64,96,400,432,448,480},{128,160,20..., dimensions={0} | all-to-all | bytes 1179648 | tf_op jit(solution)/shard_map/all_to_all | solution.py:205
  74.7 18.4 %all_to_all.17.parts = f32[8,144,128]{2,1,0:T(8,128)S(1)} all-to-all(f32[8,144,128]{2,1,0:T(8,128)S(1)} %shard_map.60), channel_id=1, replica_groups={{0,32,80,112,384,416,464,496},{16,48,64,96,400,432,448,480},{128,160,20..., dimensions={0} | all-to-all | bytes 1179648 | tf_op jit(solution)/shard_map/all_to_all | solution.py:205
  93.2 8.7 %collective-permute-start.4 = (f32[1152,128]{1,0:T(8,128)S(1)}, f32[1152,128]{1,0:T(8,128)S(1)}, u32[]{:S(2)}, u32[]{:S(2)}) collective-permute-start(f32[1152,128]{1,0:T(8,128)S(1)} %shard_map.61.own), channel_id=1, source_target_pairs={{0,144},{1,497},{2,146},{3,499},{4,148},{5,501},{6,150},{7,503},{8... | collective-permute-start | bytes 1769480 | tf_op jit(solution)/shard_map/ppermute | solution.py:219
  101.9 1.9 %collective-permute-start.6 = (f32[1152,128]{1,0:T(8,128)S(1)}, f32[1152,128]{1,0:T(8,128)S(1)}, u32[]{:S(2)}, u32[]{:S(2)}) collective-permute-start(f32[1152,128]{1,0:T(8,128)S(1)} %shard_map.61.own), channel_id=1, source_target_pairs={{0,16},{1,113},{2,18},{3,115},{4,20},{5,117},{6,22},{7,119},{8,24}... | collective-permute-start | bytes 1769480 | tf_op jit(solution)/shard_map/ppermute | solution.py:219
  103.8 2.8 %collective-permute-start.5 = (f32[1152,128]{1,0:T(8,128)S(1)}, f32[1152,128]{1,0:T(8,128)S(1)}, u32[]{:S(2)}, u32[]{:S(2)}) collective-permute-start(f32[1152,128]{1,0:T(8,128)S(1)} %shard_map.61.own), channel_id=1, source_target_pairs={{0,128},{1,385},{2,130},{3,387},{4,132},{5,389},{6,134},{7,391},{8... | collective-permute-start | bytes 1769480 | tf_op jit(solution)/shard_map/ppermute | solution.py:219
  106.7 0.9 shard_map.55
  107.6 1.6 %collective-permute-done.4.got.got3 = f32[1152,128]{1,0:T(8,128)S(1)} collective-permute-done((f32[1152,128]{1,0:T(8,128)S(1)}, f32[1152,128]{1,0:T(8,128)S(1)}, u32[]{:S(2)}, u32[]{:S(2)}) %collective-permute-start.4) | collective-permute-done | bytes 589856 | tf_op jit(solution)/shard_map/ppermute | solution.py:219
  109.2 1.2 shard_map.62
  110.4 4.7 %collective-permute-done.6.got1 = f32[1152,128]{1,0:T(8,128)S(1)} collective-permute-done((f32[1152,128]{1,0:T(8,128)S(1)}, f32[1152,128]{1,0:T(8,128)S(1)}, u32[]{:S(2)}, u32[]{:S(2)}) %collective-permute-start.6) | collective-permute-done | bytes 589856 | tf_op jit(solution)/shard_map/ppermute | solution.py:219
  115.0 0.6 collective-permute-done.5.got2
  115.7 3.4 %shard_map.63 = f32[512,1024]{1,0:T(8,128)} custom-call(f32[512,1024]{1,0:T(8,128)S(1)} %get-tuple-element.28.middle, f32[512,256]{1,0:T(8,128)S(1)} %get-tuple-element.29.rest_ref, bf16[2,512,256]{2,1,0:T(8,128)(2,1)S(1)} %get-tuple-element.19.weights, bf16[2,256,256]{2,1,0:T(8,128)(2,1)S(1)} %get-tuple-element.30.factor, f32[1152,128]{1,0:T(8,128)S(1)} %shard_map.61.own, ...), custom_call_target="tpu_custom_call" | custom-call | tf_op jit(solution)/shard_map/pallas_call | solution.py:190
  (12 shorter events, 0.2 us)
Async XLA Ops:
  27.5 6.3 %collective-permute-start = (f32[8,32,512]{2,1,0:T(8,128)S(1)}, f32[8,32,512]{2,1,0:T(8,128)S(1)}, u32[]{:S(2)}, u32[]{:S(2)}) collective-permute-start(f32[8,32,512]{2,1,0:T(8,128)S(1)} %all_to_all.15.mine_ref), channel_id=1, source_target_pairs={{0,1},{1,0},{2,3},{3,2},{4,5},{5,4},{6,7},{7,6},{8,9},{9,8},{10,11... | collective-permute-start | bytes 1572872 | tf_op jit(solution)/shard_map/ppermute | solution.py:229
  31.9 1.6 %copy-start = (f32[512,1024]{1,0:T(8,128)S(1)}, f32[512,1024]{1,0:T(8,128)}, u32[]{:S(2)}) copy-start(f32[512,1024]{1,0:T(8,128)} %block.1) | copy-start | bytes 6291460
  35.7 14.6 %collective-permute-start.1 = (f32[1152,128]{1,0:T(8,128)S(1)}, f32[1152,128]{1,0:T(8,128)S(1)}, u32[]{:S(2)}, u32[]{:S(2)}) collective-permute-start(f32[1152,128]{1,0:T(8,128)S(1)} %get-tuple-element.22), channel_id=1, source_target_pairs={{0,144},{1,497},{2,146},{3,499},{4,148},{5,501},{6,150},{7,503},{8... | collective-permute-start | bytes 1769480 | tf_op jit(solution)/shard_map/ppermute | solution.py:219
  43.0 13.1 %collective-permute-start.2 = (f32[1152,128]{1,0:T(8,128)S(1)}, f32[1152,128]{1,0:T(8,128)S(1)}, u32[]{:S(2)}, u32[]{:S(2)}) collective-permute-start(f32[1152,128]{1,0:T(8,128)S(1)} %get-tuple-element.26), channel_id=1, source_target_pairs={{0,16},{1,113},{2,18},{3,115},{4,20},{5,117},{6,22},{7,119},{8,24}... | collective-permute-start | bytes 1769480 | tf_op jit(solution)/shard_map/ppermute | solution.py:219
  44.9 11.8 %collective-permute-start.3 = (f32[1152,128]{1,0:T(8,128)S(1)}, f32[1152,128]{1,0:T(8,128)S(1)}, u32[]{:S(2)}, u32[]{:S(2)}) collective-permute-start(f32[1152,128]{1,0:T(8,128)S(1)} %get-tuple-element.27), channel_id=1, source_target_pairs={{0,128},{1,385},{2,130},{3,387},{4,132},{5,389},{6,134},{7,391},{8... | collective-permute-start | bytes 1769480 | tf_op jit(solution)/shard_map/ppermute | solution.py:219
  56.8 49.8 %copy-start.2 = (f32[256,256]{1,0:T(8,128)S(1)}, f32[256,256]{1,0:T(8,128)}, u32[]{:S(2)}) copy-start(f32[256,256]{1,0:T(8,128)} %second_factor.1) | copy-start | bytes 786436
  56.8 49.8 %copy-start.3 = (f32[256,256]{1,0:T(8,128)S(1)}, f32[256,256]{1,0:T(8,128)}, u32[]{:S(2)}) copy-start(f32[256,256]{1,0:T(8,128)} %first_factor.1) | copy-start | bytes 786436
  74.7 34.4 %copy-start.1 = (f32[512,1024]{1,0:T(8,128)S(1)}, f32[512,1024]{1,0:T(8,128)}, u32[]{:S(2)}) copy-start(f32[512,1024]{1,0:T(8,128)} %block.1) | copy-start | bytes 6291460
  93.2 16.0 %collective-permute-start.4 = (f32[1152,128]{1,0:T(8,128)S(1)}, f32[1152,128]{1,0:T(8,128)S(1)}, u32[]{:S(2)}, u32[]{:S(2)}) collective-permute-start(f32[1152,128]{1,0:T(8,128)S(1)} %shard_map.61.own), channel_id=1, source_target_pairs={{0,144},{1,497},{2,146},{3,499},{4,148},{5,501},{6,150},{7,503},{8... | collective-permute-start | bytes 1769480 | tf_op jit(solution)/shard_map/ppermute | solution.py:219
  101.9 13.1 %collective-permute-start.6 = (f32[1152,128]{1,0:T(8,128)S(1)}, f32[1152,128]{1,0:T(8,128)S(1)}, u32[]{:S(2)}, u32[]{:S(2)}) collective-permute-start(f32[1152,128]{1,0:T(8,128)S(1)} %shard_map.61.own), channel_id=1, source_target_pairs={{0,16},{1,113},{2,18},{3,115},{4,20},{5,117},{6,22},{7,119},{8,24}... | collective-permute-start | bytes 1769480 | tf_op jit(solution)/shard_map/ppermute | solution.py:219
  103.8 11.8 %collective-permute-start.5 = (f32[1152,128]{1,0:T(8,128)S(1)}, f32[1152,128]{1,0:T(8,128)S(1)}, u32[]{:S(2)}, u32[]{:S(2)}) collective-permute-start(f32[1152,128]{1,0:T(8,128)S(1)} %shard_map.61.own), channel_id=1, source_target_pairs={{0,128},{1,385},{2,130},{3,387},{4,132},{5,389},{6,134},{7,391},{8... | collective-permute-start | bytes 1769480 | tf_op jit(solution)/shard_map/ppermute | solution.py:219

commit v18 on v16

--- a/solution.py
+++ b/solution.py
@@ -159,26 +159,31 @@
     return jnp.concatenate([part[1024:1088, :], part[1088:, :]], axis=1)
 
 
-def middle_kernel(block, weights, own, got, out):
+def middle_kernel(block, panel, weights, own, got, out, rest):
+    cross = split(jnp.concatenate([cross_of(own), cross_of(got)], axis=0))
+    rest[...] = panel[...] - mul3((weights[0, :, :128], weights[1, :, :128]), cross)
     proj = split(jnp.concatenate([natural(own)[64:], natural(got)[64:]], axis=0))
     for t in range(2):
         rows = slice(t * 256, (t + 1) * 256)
         out[rows] = block[rows] - mul3((weights[0, rows, :128], weights[1, rows, :128]), proj)
 
 
-def update_kernel(middle, panel, weights, factor, own, got3, got2, got1, out_ref, out, sems):
+def update_kernel(middle, rest_ref, weights, factor, own, got3, got2, got1, out_ref, out, sems):
     parts = (own, got3, got2, got1)
-    cross = split(jnp.concatenate([cross_of(part) for part in parts], axis=0))
-    rest = panel[...] - mul3((weights[0], weights[1]), cross)
+    cross = split(jnp.concatenate([cross_of(got2), cross_of(got1)], axis=0))
+    rest = rest_ref[...] - mul3((weights[0, :, 128:], weights[1, :, 128:]), cross)
     second = split(mul3(split(rest), (factor[0], factor[1])))
     quarters = [natural(part) for part in parts]
     left = [jnp.concatenate([second[i], weights[i, :, 128:]], axis=1) for i in range(2)]
     rows = [quarter[:64] for quarter in quarters] + [quarter[64:] for quarter in quarters[2:]]
     right = split(jnp.concatenate(rows, axis=0))
     stores = []
-    for t in range(4):
-        at = slice(t * 128, (t + 1) * 128)
-        out[at] = middle[at] - mul3((left[0][at], left[1][at]), right)
+    for t in range(2):
+        at = slice(t * 256, (t + 1) * 256)
+        tile = left[0][at], left[1][at]
+        for half in range(2):
+            columns = slice(half * 512, (half + 1) * 512)
+            out[at, columns] = middle[at, columns] - mul3(tile, (right[0][:, columns], right[1][:, columns]))
         stores.append(pltpu.make_async_copy(out.at[at], out_ref.at[at], sems.at[t]))
         stores[t].start()
     for store in stores:
@@ -249,12 +254,14 @@
         (pltpu.VMEM((256, 256), F32), pltpu.VMEM((2, 8, 32, 512), F32), pltpu.VMEM((2, 256, 512), F32)),
         scalars=2,
     )
-    middle = call(middle_kernel, shape(512, 1024), (vectors, weights, share, got[3]))
+    middle, rest = call(
+        middle_kernel, [shape(512, 1024), shape(512, 256)], (vectors, panel, weights, share, got[3])
+    )
     return call(
         update_kernel,
         shape(512, 1024),
-        (middle, panel, weights, factor, share, got[3], got[2], got[1]),
-        (pltpu.VMEM((512, 1024), F32), pltpu.SemaphoreType.DMA((4,))),
+        (middle, rest, weights, factor, share, got[3], got[2], got[1]),
+        (pltpu.VMEM((512, 1024), F32), pltpu.SemaphoreType.DMA((2,))),
         out_spec=HBM,
     )
 

time: 120 us -> 120 us (level)
  Pallas kernels: 8.41 us -> 10.3 us
  waiting for transfers between devices: 15.4 us -> 13.6 us
    pallas_call x10, Pallas kernels: 8.41 us -> 10.3 us  [call(): pl.pallas_call(kernel, out_shape=outs, in_specs=inputs or [SMEM] * scalar...]
    ppermute x6, waiting for transfers between devices: 15.4 us -> 13.6 us  [fetch(): return lax.ppermute(value, ROW + COL, pairs)]
  transfers between devices with their start and end apart: 7 -> 7, of which waited for: 6 -> 6; matrix products, arithmetic and copies ran while one was open for 0% -> 0% of each run, Pallas kernels for 3% -> 5%
where the time goes in v18:
time: 120 us; the launch traced here: 119 us
  blocking collectives  62.4 us (52%)
  starting transfers between devices  29.7 us (25%)
  waiting for transfers between devices  13.6 us (11%)
  Pallas kernels  10.3 us (9%)
  local copies, waits for them, and re-layouts  1.65 us (1%)
    all_to_all x2, blocking collectives, trade(): return lax.all_to_all(pieces, ROW + COL, 0, 0, axis_index_groups=FAR)  35.7 us
    all_to_all x1, blocking collectives, local(): lax.all_to_all(jnp.broadcast_to(shards[None], (NZ,) + shards.shape), 'z',...  26.7 us
    ppermute x6, starting transfers between devices, fetch(): return lax.ppermute(value, ROW + COL, pairs)  25.4 us
    ppermute x6, waiting for transfers between devices, fetch(): return lax.ppermute(value, ROW + COL, pairs)  13.6 us
    pallas_call x10, Pallas kernels, call(): pl.pallas_call(kernel, out_shape=outs, in_specs=inputs or [SMEM] * scalar...  10.3 us
    ppermute x1, starting transfers between devices, local(): other = lax.ppermute(mine, 'core', [(0, 1), (1, 0)])  4.35 us
  transfers between devices with their start and end apart: 7, of which 6 were waited for; matrix products, arithmetic and copies ran while one was open for 0% of the time, Pallas kernels for 5%

profile of v18, /device:TPU:1, one launch (start us, length us, event | category | flops | bytes accessed | tf_op | source)
XLA Modules:
  0.0 118.6 jit_solution(1266708244691300908)
XLA Ops:
  0.0 0.8 pad_maximum_fusion
  0.8 26.7 %all_to_all.15.mine_ref = f32[8,32,512]{2,1,0:T(8,128)S(1)} all-to-all(f32[8,32,512]{2,1,0:T(8,128)S(1)} %broadcast_in_dim.2), channel_id=1, replica_groups=mesh['x'=4,'y'=8,'z'=8,'core'=2] {'z'}, dimensions={0} | all-to-all | bytes 1048576 | tf_op jit(solution)/shard_map/all_to_all | solution.py:233
  27.5 4.4 %collective-permute-start = (f32[8,32,512]{2,1,0:T(8,128)S(1)}, f32[8,32,512]{2,1,0:T(8,128)S(1)}, u32[]{:S(2)}, u32[]{:S(2)}) collective-permute-start(f32[8,32,512]{2,1,0:T(8,128)S(1)} %all_to_all.15.mine_ref), channel_id=1, source_target_pairs={{0,1},{1,0},{2,3},{3,2},{4,5},{5,4},{6,7},{7,6},{8,9},{9,8},{10,11... | collective-permute-start | bytes 1572872 | tf_op jit(solution)/shard_map/ppermute | solution.py:234
  31.9 1.6 %copy-done = f32[512,1024]{1,0:T(8,128)S(1)} copy-done((f32[512,1024]{1,0:T(8,128)S(1)}, f32[512,1024]{1,0:T(8,128)}, u32[]{:S(2)}) %copy-start) | copy-done | bytes 2097176
  33.8 1.0 shard_map.57
  34.8 7.3 %collective-permute-start.1 = (f32[1152,128]{1,0:T(8,128)S(1)}, f32[1152,128]{1,0:T(8,128)S(1)}, u32[]{:S(2)}, u32[]{:S(2)}) collective-permute-start(f32[1152,128]{1,0:T(8,128)S(1)} %get-tuple-element.22), channel_id=1, source_target_pairs={{0,144},{1,497},{2,146},{3,499},{4,148},{5,501},{6,150},{7,503},{8... | collective-permute-start | bytes 1769480 | tf_op jit(solution)/shard_map/ppermute | solution.py:224
  42.1 1.0 shard_map.59
  43.1 1.9 %collective-permute-start.2 = (f32[1152,128]{1,0:T(8,128)S(1)}, f32[1152,128]{1,0:T(8,128)S(1)}, u32[]{:S(2)}, u32[]{:S(2)}) collective-permute-start(f32[1152,128]{1,0:T(8,128)S(1)} %get-tuple-element.26), channel_id=1, source_target_pairs={{0,16},{1,113},{2,18},{3,115},{4,20},{5,117},{6,22},{7,119},{8,24}... | collective-permute-start | bytes 1769480 | tf_op jit(solution)/shard_map/ppermute | solution.py:224
  45.0 2.2 %collective-permute-start.3 = (f32[1152,128]{1,0:T(8,128)S(1)}, f32[1152,128]{1,0:T(8,128)S(1)}, u32[]{:S(2)}, u32[]{:S(2)}) collective-permute-start(f32[1152,128]{1,0:T(8,128)S(1)} %get-tuple-element.27), channel_id=1, source_target_pairs={{0,128},{1,385},{2,130},{3,387},{4,132},{5,389},{6,134},{7,391},{8... | collective-permute-start | bytes 1769480 | tf_op jit(solution)/shard_map/ppermute | solution.py:224
  47.2 2.1 %collective-permute-done.1.got = f32[1152,128]{1,0:T(8,128)S(1)} collective-permute-done((f32[1152,128]{1,0:T(8,128)S(1)}, f32[1152,128]{1,0:T(8,128)S(1)}, u32[]{:S(2)}, u32[]{:S(2)}) %collective-permute-start.1) | collective-permute-done | bytes 589856 | tf_op jit(solution)/shard_map/ppermute | solution.py:224
  49.3 0.6 shard_map.58.half
  49.9 5.3 %collective-permute-done.2.got1 = f32[1152,128]{1,0:T(8,128)S(1)} collective-permute-done((f32[1152,128]{1,0:T(8,128)S(1)}, f32[1152,128]{1,0:T(8,128)S(1)}, u32[]{:S(2)}, u32[]{:S(2)}) %collective-permute-start.2) | collective-permute-done | bytes 589856 | tf_op jit(solution)/shard_map/ppermute | solution.py:224
  55.2 1.7 %collective-permute-done.3.got2 = f32[1152,128]{1,0:T(8,128)S(1)} collective-permute-done((f32[1152,128]{1,0:T(8,128)S(1)}, f32[1152,128]{1,0:T(8,128)S(1)}, u32[]{:S(2)}, u32[]{:S(2)}) %collective-permute-start.3) | collective-permute-done | bytes 589856 | tf_op jit(solution)/shard_map/ppermute | solution.py:224
  57.0 17.5 %all_to_all.16.parts = f32[8,144,128]{2,1,0:T(8,128)S(1)} all-to-all(f32[8,144,128]{2,1,0:T(8,128)S(1)} %shard_map.60), channel_id=1, replica_groups={{0,32,80,112,384,416,464,496},{16,48,64,96,400,432,448,480},{128,160,20..., dimensions={0} | all-to-all | bytes 1179648 | tf_op jit(solution)/shard_map/all_to_all | solution.py:210
  74.5 18.2 %all_to_all.17.parts = f32[8,144,128]{2,1,0:T(8,128)S(1)} all-to-all(f32[8,144,128]{2,1,0:T(8,128)S(1)} %shard_map.61), channel_id=1, replica_groups={{0,32,80,112,384,416,464,496},{16,48,64,96,400,432,448,480},{128,160,20..., dimensions={0} | all-to-all | bytes 1179648 | tf_op jit(solution)/shard_map/all_to_all | solution.py:210
  92.8 8.5 %collective-permute-start.4 = (f32[1152,128]{1,0:T(8,128)S(1)}, f32[1152,128]{1,0:T(8,128)S(1)}, u32[]{:S(2)}, u32[]{:S(2)}) collective-permute-start(f32[1152,128]{1,0:T(8,128)S(1)} %shard_map.62.own), channel_id=1, source_target_pairs={{0,144},{1,497},{2,146},{3,499},{4,148},{5,501},{6,150},{7,503},{8... | collective-permute-start | bytes 1769480 | tf_op jit(solution)/shard_map/ppermute | solution.py:224
  101.2 1.9 %collective-permute-start.6 = (f32[1152,128]{1,0:T(8,128)S(1)}, f32[1152,128]{1,0:T(8,128)S(1)}, u32[]{:S(2)}, u32[]{:S(2)}) collective-permute-start(f32[1152,128]{1,0:T(8,128)S(1)} %shard_map.62.own), channel_id=1, source_target_pairs={{0,16},{1,113},{2,18},{3,115},{4,20},{5,117},{6,22},{7,119},{8,24}... | collective-permute-start | bytes 1769480 | tf_op jit(solution)/shard_map/ppermute | solution.py:224
  103.2 3.6 %collective-permute-start.5 = (f32[1152,128]{1,0:T(8,128)S(1)}, f32[1152,128]{1,0:T(8,128)S(1)}, u32[]{:S(2)}, u32[]{:S(2)}) collective-permute-start(f32[1152,128]{1,0:T(8,128)S(1)} %shard_map.62.own), channel_id=1, source_target_pairs={{0,128},{1,385},{2,130},{3,387},{4,132},{5,389},{6,134},{7,391},{8... | collective-permute-start | bytes 1769480 | tf_op jit(solution)/shard_map/ppermute | solution.py:224
  106.8 0.9 shard_map.55
  107.7 0.8 collective-permute-done.4.got.got3
  108.5 2.8 %shard_map.63 = (f32[512,1024]{1,0:T(8,128)S(1)}, f32[512,256]{1,0:T(8,128)S(1)}) custom-call(f32[512,1024]{1,0:T(8,128)} %block.1, f32[512,256]{1,0:T(8,128)S(1)} %get-tuple-element.18.panel, bf16[2,512,256]{2,1,0:T(8,128)(2,1)S(1)} %get-tuple-element.19.weights, f32[1152,128]{1,0:T(8,128)S(1)} %shard_map.62.own, ...), custom_call_target="tpu_custom_call" | custom-call | tf_op jit(solution)/shard_map/pallas_call | solution.py:195
  111.3 3.1 %collective-permute-done.6.got1 = f32[1152,128]{1,0:T(8,128)S(1)} collective-permute-done((f32[1152,128]{1,0:T(8,128)S(1)}, f32[1152,128]{1,0:T(8,128)S(1)}, u32[]{:S(2)}, u32[]{:S(2)}) %collective-permute-start.6) | collective-permute-done | bytes 589856 | tf_op jit(solution)/shard_map/ppermute | solution.py:224
  114.4 0.6 collective-permute-done.5.got2
  115.0 3.6 %shard_map.64 = f32[512,1024]{1,0:T(8,128)} custom-call(f32[512,1024]{1,0:T(8,128)S(1)} %get-tuple-element.28.middle, f32[512,256]{1,0:T(8,128)S(1)} %get-tuple-element.29.rest_ref, bf16[2,512,256]{2,1,0:T(8,128)(2,1)S(1)} %get-tuple-element.19.weights, bf16[2,256,256]{2,1,0:T(8,128)(2,1)S(1)} %get-tuple-element.30.factor, f32[1152,128]{1,0:T(8,128)S(1)} %shard_map.62.own, ...), custom_call_target="tpu_custom_call" | custom-call | tf_op jit(solution)/shard_map/pallas_call | solution.py:195
  (11 shorter events, 0.5 us)
Async XLA Ops:
  27.5 6.3 %collective-permute-start = (f32[8,32,512]{2,1,0:T(8,128)S(1)}, f32[8,32,512]{2,1,0:T(8,128)S(1)}, u32[]{:S(2)}, u32[]{:S(2)}) collective-permute-start(f32[8,32,512]{2,1,0:T(8,128)S(1)} %all_to_all.15.mine_ref), channel_id=1, source_target_pairs={{0,1},{1,0},{2,3},{3,2},{4,5},{5,4},{6,7},{7,6},{8,9},{9,8},{10,11... | collective-permute-start | bytes 1572872 | tf_op jit(solution)/shard_map/ppermute | solution.py:234
  31.9 1.6 %copy-start = (f32[512,1024]{1,0:T(8,128)S(1)}, f32[512,1024]{1,0:T(8,128)}, u32[]{:S(2)}) copy-start(f32[512,1024]{1,0:T(8,128)} %block.1) | copy-start | bytes 6291460
  34.8 14.6 %collective-permute-start.1 = (f32[1152,128]{1,0:T(8,128)S(1)}, f32[1152,128]{1,0:T(8,128)S(1)}, u32[]{:S(2)}, u32[]{:S(2)}) collective-permute-start(f32[1152,128]{1,0:T(8,128)S(1)} %get-tuple-element.22), channel_id=1, source_target_pairs={{0,144},{1,497},{2,146},{3,499},{4,148},{5,501},{6,150},{7,503},{8... | collective-permute-start | bytes 1769480 | tf_op jit(solution)/shard_map/ppermute | solution.py:224
  43.1 12.1 %collective-permute-start.2 = (f32[1152,128]{1,0:T(8,128)S(1)}, f32[1152,128]{1,0:T(8,128)S(1)}, u32[]{:S(2)}, u32[]{:S(2)}) collective-permute-start(f32[1152,128]{1,0:T(8,128)S(1)} %get-tuple-element.26), channel_id=1, source_target_pairs={{0,16},{1,113},{2,18},{3,115},{4,20},{5,117},{6,22},{7,119},{8,24}... | collective-permute-start | bytes 1769480 | tf_op jit(solution)/shard_map/ppermute | solution.py:224
  45.0 11.8 %collective-permute-start.3 = (f32[1152,128]{1,0:T(8,128)S(1)}, f32[1152,128]{1,0:T(8,128)S(1)}, u32[]{:S(2)}, u32[]{:S(2)}) collective-permute-start(f32[1152,128]{1,0:T(8,128)S(1)} %get-tuple-element.27), channel_id=1, source_target_pairs={{0,128},{1,385},{2,130},{3,387},{4,132},{5,389},{6,134},{7,391},{8... | collective-permute-start | bytes 1769480 | tf_op jit(solution)/shard_map/ppermute | solution.py:224
  56.9 49.9 %copy-start.1 = (f32[256,256]{1,0:T(8,128)S(1)}, f32[256,256]{1,0:T(8,128)}, u32[]{:S(2)}) copy-start(f32[256,256]{1,0:T(8,128)} %second_factor.1) | copy-start | bytes 786436
  57.0 49.9 %copy-start.2 = (f32[256,256]{1,0:T(8,128)S(1)}, f32[256,256]{1,0:T(8,128)}, u32[]{:S(2)}) copy-start(f32[256,256]{1,0:T(8,128)} %first_factor.1) | copy-start | bytes 786436
  92.8 15.7 %collective-permute-start.4 = (f32[1152,128]{1,0:T(8,128)S(1)}, f32[1152,128]{1,0:T(8,128)S(1)}, u32[]{:S(2)}, u32[]{:S(2)}) collective-permute-start(f32[1152,128]{1,0:T(8,128)S(1)} %shard_map.62.own), channel_id=1, source_target_pairs={{0,144},{1,497},{2,146},{3,499},{4,148},{5,501},{6,150},{7,503},{8... | collective-permute-start | bytes 1769480 | tf_op jit(solution)/shard_map/ppermute | solution.py:224
  101.2 13.1 %collective-permute-start.6 = (f32[1152,128]{1,0:T(8,128)S(1)}, f32[1152,128]{1,0:T(8,128)S(1)}, u32[]{:S(2)}, u32[]{:S(2)}) collective-permute-start(f32[1152,128]{1,0:T(8,128)S(1)} %shard_map.62.own), channel_id=1, source_target_pairs={{0,16},{1,113},{2,18},{3,115},{4,20},{5,117},{6,22},{7,119},{8,24}... | collective-permute-start | bytes 1769480 | tf_op jit(solution)/shard_map/ppermute | solution.py:224
  103.2 11.8 %collective-permute-start.5 = (f32[1152,128]{1,0:T(8,128)S(1)}, f32[1152,128]{1,0:T(8,128)S(1)}, u32[]{:S(2)}, u32[]{:S(2)}) collective-permute-start(f32[1152,128]{1,0:T(8,128)S(1)} %shard_map.62.own), channel_id=1, source_target_pairs={{0,128},{1,385},{2,130},{3,387},{4,132},{5,389},{6,134},{7,391},{8... | collective-permute-start | bytes 1769480 | tf_op jit(solution)/shard_map/ppermute | solution.py:224
